TPU v7x, 32 devices: a whole 2x2x4 slice. The times are simulated.
32 devices in a mesh: coarse: 8 (over z, x), fine: 4 (over y, core).
Axes of the slice: x: 2, y: 2, z: 4, core: 2. Of those that a mesh axis runs over, the one named last changes fastest.
Arguments:
- node_feats: bfloat16 [65536, 256], P(('coarse', 'fine')), may hold values from -6 to 6
- grad_out: bfloat16 [65536, 256], P(('coarse', 'fine')), may hold values from -6 to 6
- cluster_ids: int32 [65536], P(('coarse', 'fine')), may hold values from 0 to 8191, as said below
- halo_lists: int32 [1024], P('coarse'), may hold values from 0 to 1023, as said below
- edge_sources: int32 [32768], P('coarse'), may hold values from 0 to 1151, as said below
- w_edge_in: bfloat16 [512, 256], replicated, may hold values from -0.25 to 0.25
- b_edge_in: bfloat16 [256], replicated, may hold values from -4 to 4
- w_edge_out: bfloat16 [256, 256], replicated, may hold values from -0.375 to 0.375
- w_unpool: bfloat16 [256, 256], replicated, may hold values from -0.375 to 0.375
Outputs:
- grad_feats: bfloat16 [65536, 256], P(('coarse', 'fine'))
- grad_w_in: float32 [512, 256], replicated
- grad_b_in: float32 [256], replicated
- grad_w_out: float32 [256, 256], replicated
- grad_unpool: float32 [256, 256], replicated
Inputs may be any that keep to these rules, and one draw needn't show every extreme that they name: `cluster_ids`: the fine nodes on the devices of coarse index g lie in cells g*1024 to (g+1)*1024 - 1. `halo_lists`: each owner's block of 128 entries holds distinct indices. `edge_sources`: each owner's block of 4096 entries takes every value of its range at least once.
All inputs are finite; a program needn't handle non-finite values.
Results may differ from a plain program's by a relative error of at most 0.0065.
Values may be sent and summed in bfloat16 or wider, within the bound.
No kernel may reach another device: no remote copies, remote signals or barrier semaphores. Data moves between devices by JAX's collectives and lax.ppermute only.
A program may use at most 128 MiB of HBM per device.

v0:
```python
import jax
import jax.numpy as jnp
from jax import lax
from jax.sharding import PartitionSpec as P

K = 4


def with_halo(cells, sides, width):
    for axis, dim in sides:
        count = lax.axis_size(axis)
        head = lax.slice_in_dim(cells, 0, width, axis=dim)
        tail = lax.slice_in_dim(cells, cells.shape[dim] - width, cells.shape[dim], axis=dim)
        cells = jnp.concatenate(
            [
                lax.ppermute(tail, axis, [(i, (i + 1) % count) for i in range(count)]),
                cells,
                lax.ppermute(head, axis, [((i + 1) % count, i) for i in range(count)]),
            ],
            axis=dim,
        )
    return cells


def edge_work(
    dst_bf, dst_full, extended, sources, grad_sum_bf, w_edge_in, b_edge_in, w_edge_out, w_unpool
):
    row_count = dst_bf.shape[0]
    feature_width = dst_bf.shape[1]
    fan_count = sources.shape[0] // row_count
    dst_rep = jnp.repeat(dst_bf, fan_count, axis=0)
    src_feats = jnp.take(extended, sources, axis=0)
    joined = jnp.concatenate([dst_rep, src_feats], axis=1)
    pre_act = jnp.dot(joined, w_edge_in, preferred_element_type=jnp.float32) + b_edge_in.astype(
        jnp.float32
    )
    sigmoid_act = jax.nn.sigmoid(pre_act)
    hidden = (pre_act * sigmoid_act).astype(jnp.bfloat16)
    messages = jnp.dot(hidden, w_edge_out, preferred_element_type=jnp.float32)
    aggregate = messages.reshape(row_count, fan_count, feature_width).sum(axis=1)
    new_coarse = (dst_full + aggregate).astype(jnp.bfloat16)
    grad_new = jnp.dot(grad_sum_bf, w_unpool.T, preferred_element_type=jnp.float32).astype(
        jnp.bfloat16
    )
    grad_up = jnp.dot(new_coarse.T, grad_sum_bf, preferred_element_type=jnp.float32)
    grad_msg = jnp.repeat(grad_new, fan_count, axis=0)
    grad_w2 = jnp.dot(hidden.T, grad_msg, preferred_element_type=jnp.float32)
    grad_hidden = jnp.dot(grad_msg, w_edge_out.T, preferred_element_type=jnp.float32)
    grad_act = (grad_hidden * sigmoid_act * (1.0 + pre_act * (1.0 - sigmoid_act))).astype(
        jnp.bfloat16
    )
    grad_w1 = jnp.dot(joined.T, grad_act, preferred_element_type=jnp.float32)
    grad_b1 = jnp.sum(grad_act.astype(jnp.float32), axis=0)
    grad_joined = jnp.dot(grad_act, w_edge_in.T, preferred_element_type=jnp.float32)
    grad_dst = grad_new.astype(jnp.float32) + grad_joined[:, :feature_width].reshape(
        row_count, fan_count, feature_width
    ).sum(axis=1)
    grad_src = jax.ops.segment_sum(
        grad_joined[:, feature_width:], sources, num_segments=extended.shape[0]
    )
    return (grad_dst, grad_src, grad_up, grad_w2, grad_w1, grad_b1)


def extend_rows(pooled_bf, right_ids, left_ids):
    half_rows = right_ids.shape[0]
    outgoing = jnp.concatenate(
        [jnp.take(pooled_bf, left_ids, axis=0), jnp.take(pooled_bf, right_ids, axis=0)], axis=0
    )
    arrived = with_halo(outgoing, (("coarse", 0),), half_rows)
    return jnp.concatenate([pooled_bf, arrived[:half_rows], arrived[3 * half_rows :]], axis=0)


def return_rows(grad_src, right_ids, left_ids, cell_count):
    half_rows = right_ids.shape[0]
    arrived = with_halo(
        grad_src[cell_count:].astype(jnp.bfloat16), (("coarse", 0),), half_rows
    ).astype(jnp.float32)
    for_left = arrived[:half_rows]
    for_right = arrived[3 * half_rows :]
    return jax.ops.segment_sum(for_left, left_ids, num_segments=cell_count) + jax.ops.segment_sum(
        for_right, right_ids, num_segments=cell_count
    )


def local(
    node_feats,
    grad_out,
    cluster_ids,
    halo_lists,
    edge_sources,
    w_edge_in,
    b_edge_in,
    w_edge_out,
    w_unpool,
):
    fan_count = K
    cell_count = edge_sources.shape[0] // fan_count
    half_rows = halo_lists.shape[0] // 2
    owner_index = lax.axis_index("coarse")
    local_ids = cluster_ids - owner_index * cell_count
    part_feats = jax.ops.segment_sum(
        node_feats.astype(jnp.float32), local_ids, num_segments=cell_count
    )
    part_grads = jax.ops.segment_sum(
        grad_out.astype(jnp.float32), local_ids, num_segments=cell_count
    )
    right_ids = halo_lists[:half_rows]
    left_ids = halo_lists[half_rows:]
    pooled, grad_sum = lax.psum((part_feats, part_grads), "fine")
    pooled_bf = pooled.astype(jnp.bfloat16)
    extended = extend_rows(pooled_bf, right_ids, left_ids)
    grad_dst, grad_src, grad_up, grad_w2, grad_w1, grad_b1 = edge_work(
        pooled_bf,
        pooled,
        extended,
        edge_sources,
        grad_sum.astype(jnp.bfloat16),
        w_edge_in,
        b_edge_in,
        w_edge_out,
        w_unpool,
    )
    grad_pool = (
        grad_dst + grad_src[:cell_count] + return_rows(grad_src, right_ids, left_ids, cell_count)
    )
    grad_w1, grad_b1, grad_w2, grad_up = lax.psum((grad_w1, grad_b1, grad_w2, grad_up), "coarse")
    grad_feats = (grad_out.astype(jnp.float32) + jnp.take(grad_pool, local_ids, axis=0)).astype(
        jnp.bfloat16
    )
    total_cells = cell_count * lax.axis_size("coarse")
    total_edges = total_cells * fan_count
    edge_scale = float(total_edges) ** (-0.5)
    cell_scale = float(total_cells) ** (-0.5)
    return (
        grad_feats,
        grad_w1 * edge_scale,
        grad_b1 * edge_scale,
        grad_w2 * edge_scale,
        grad_up * cell_scale,
    )


def solution(mesh):
    return jax.shard_map(
        local,
        mesh=mesh,
        in_specs=(
            P(("coarse", "fine"), None),
            P(("coarse", "fine"), None),
            P(("coarse", "fine")),
            P("coarse"),
            P("coarse"),
            P(),
            P(),
            P(),
            P(),
        ),
        out_specs=(P(("coarse", "fine"), None), P(), P(), P(), P()),
        check_vma=False,
    )
```

profile of v0, /device:TPU:0, one launch (start us, length us, event | category | flops | bytes accessed | tf_op | source)
XLA Modules:
  0.0 256.0 jit_solution(16022169368157409763)
XLA Ops:
  8.1 11.9 %scatter_custom_fusion.1 = f32[1024,256]{1,0:T(8,128)} fusion(s32[2048]{0:T(1024)S(1)} %get-tuple-element.10, bf16[2048,256]{1,0:T(8,128)(2,1)} %param.11, f32[]{:T(128)} %constant.35.clone.1), kind=kCustom, calls=%fused_computation.23 | custom fusion | flops 1048576 | bytes 2097156 | tf_op jit(solution)/shard_map/scatter-add | solution.py:101
  20.3 11.9 %scatter_custom_fusion = f32[1024,256]{1,0:T(8,128)S(1)} fusion(s32[2048]{0:T(1024)S(1)} %get-tuple-element.10, bf16[2048,256]{1,0:T(8,128)(2,1)S(1)} %copy-done.5, f32[]{:T(128)} %constant.35.clone.1), kind=kCustom, calls=%fused_computation.20 | custom fusion | flops 1048576 | bytes 2097156 | tf_op jit(solution)/shard_map/scatter-add | solution.py:104
  32.2 35.3 %all-reduce.8 = bf16[1024,256]{1,0:T(8,128)(2,1)S(1)} all-reduce(f32[1024,256]{1,0:T(8,128)S(1)} %scatter_custom_fusion), channel_id=1, replica_groups=mesh['coarse'=8,'fine'=4] {'fine'}, use_global_device_ids=true, to_apply=%region_1.0 | all-reduce | flops 262144 | bytes 1572864 | tf_op jit(solution)/shard_map/psum | solution.py:109
  68.3 1.5 convert_element_type.46
  71.8 1.9 collective-permute-start
  73.8 3.0 %collective-permute-start.1 = (bf16[64,256]{1,0:T(8,128)(2,1)S(1)}, bf16[64,256]{1,0:T(8,128)(2,1)}, u32[]{:S(2)}, u32[]{:S(2)}) collective-permute-start(bf16[64,256]{1,0:T(8,128)(2,1)S(1)} %broadcast_select_fusion.1), channel_id=1, source_target_pairs={{4,0},{8,4},{12,8},{16,12},{20,16},{24,20},{28,24},{0,28},{5,1},{9... | collective-permute-start | bytes 98312 | tf_op jit(solution)/shard_map/ppermute | solution.py:18
  78.6 2.1 reshape.38
  81.3 2.1 reshape.39
  84.1 14.6 %gather_fusion = bf16[4096,256]{1,0:T(8,128)(2,1)S(1)} fusion(bf16[1152,256]{1,0:T(8,128)(2,1)S(1)} %pad_maximum_fusion.3, s32[4096]{0:T(1024)S(1)} %fusion.21), kind=kCustom, calls=%fused_computation.2 | custom fusion | bytes 4210688 | tf_op jit(solution)/shard_map/jit(_take)/gather | solution.py:32
  98.8 2.1 broadcast_select_fusion
  101.0 1.3 multiply_convert_fusion
  102.6 1.4 fusion.27
  104.0 2.6 %fusion.28 = f32[4096,256]{1,0:T(8,128)} fusion(bf16[4096,256]{1,0:T(8,128)(2,1)S(1)} %get-tuple-element.23, bf16[256,256]{1,0:T(8,128)(2,1)S(1)} %copy-done.11), kind=kOutput, calls=%fused_computation.71 | convolution fusion | flops 536870912 | bytes 6422528 | tf_op jit(solution)/shard_map/dot_general | solution.py:39
  106.7 2.4 convert_reduce_fusion
  109.0 2.1 fusion.4
  111.1 4.5 %fusion.26 = f32[4096,512]{1,0:T(8,128)} fusion(bf16[4096,256]{1,0:T(8,128)(2,1)S(1)} %get-tuple-element.26, bf16[512,256]{1,0:T(8,128)(2,1)S(1)} %copy-done), kind=kOutput, calls=%fused_computation.69 | convolution fusion | flops 1073741824 | bytes 10747904 | tf_op jit(solution)/shard_map/dot_general | solution.py:54
  115.7 23.6 %scatter_custom_fusion.2 = f32[1152,256]{1,0:T(8,128)S(1)} fusion(s32[4096]{0:T(1024)S(1)} %copy-done.13, f32[4096,512]{1,0:T(8,128)} %fusion.26, f32[]{:T(128)} %constant.35.clone.1), kind=kCustom, calls=%fused_computation.12 | custom fusion | flops 1048576 | bytes 5374464 | tf_op jit(solution)/shard_map/scatter-add | solution.py:58
  139.3 4.4 %slice.51 = f32[4096,256]{1,0:T(8,128)} slice(f32[4096,512]{1,0:T(8,128)} %fusion.26), slice={[0:4096], [0:256]} | slice | bytes 8388608 | tf_op jit(solution)/shard_map/slice | solution.py:55
  143.7 5.2 %reshape.41 = f32[1024,4,256]{2,1,0:T(4,128)} reshape(f32[4096,256]{1,0:T(8,128)} %fusion.28) | data formatting | bytes 8388608 | tf_op jit(solution)/shard_map/reshape | solution.py:40
  148.9 5.6 %reduce_sum.29 = f32[1024,256]{1,0:T(8,128)} reduce(f32[1024,4,256]{2,1,0:T(4,128)} %reshape.41, f32[]{:T(128)} %constant.35.clone.1), dimensions={1}, to_apply=%region_11.13 | reduce | flops 786432 | bytes 5242884 | tf_op jit(solution)/shard_map/reduce_sum | solution.py:40
  154.5 5.2 %reshape.40 = f32[1024,4,256]{2,1,0:T(4,128)} reshape(f32[4096,256]{1,0:T(8,128)} %slice.51) | data formatting | bytes 8388608 | tf_op jit(solution)/shard_map/reshape | solution.py:55
  159.7 4.7 %reduce_sum.27 = f32[1024,256]{1,0:T(8,128)S(1)} reduce(f32[1024,4,256]{2,1,0:T(4,128)} %reshape.40, f32[]{:T(128)} %constant.35.clone.1), dimensions={1}, to_apply=%region_4.0 | reduce | flops 786432 | bytes 5242884 | tf_op jit(solution)/shard_map/reduce_sum | solution.py:57
  164.4 0.9 convert.3
  167.3 1.0 fusion.11
  168.5 4.7 %collective-permute-start.3 = (bf16[64,256]{1,0:T(8,128)(2,1)S(1)}, bf16[64,256]{1,0:T(8,128)(2,1)S(1)}, u32[]{:S(2)}, u32[]{:S(2)}) collective-permute-start(bf16[64,256]{1,0:T(8,128)(2,1)S(1)} %get-tuple-element.16), channel_id=1, source_target_pairs={{4,0},{8,4},{12,8},{16,12},{20,16},{24,20},{28,24},{0,28},{5,1},{9... | collective-permute-start | bytes 98312 | tf_op jit(solution)/shard_map/ppermute | solution.py:18
  173.2 17.2 %psum.45 = f32[256]{0:T(256)S(1)} all-reduce(f32[256]{0:T(256)S(1)} %copy-done.15), channel_id=1, replica_groups=mesh['coarse'=8,'fine'=4] {'coarse'}, use_global_device_ids=true, to_apply=%region_9.11 | all-reduce | flops 256 | bytes 2048 | tf_op jit(solution)/shard_map/psum | solution.py:126
  191.0 1.8 scatter_custom_fusion.3
  192.9 6.6 %gather_fusion.1 = f32[2048,256]{1,0:T(8,128)S(1)} fusion(f32[1024,256]{1,0:T(8,128)S(1)} %scatter_custom_fusion.3, s32[2048]{0:T(1024)S(1)} %fusion.22), kind=kCustom, calls=%fused_computation.3 | custom fusion | bytes 4202496 | tf_op jit(solution)/shard_map/jit(_take)/gather | solution.py:127
  199.5 2.3 fusion.7
  201.8 43.6 %all-reduce.7.cloned.1.call-done = (f32[512,256]{1,0:T(8,128)}, f32[256,256]{1,0:T(8,128)}, f32[256,256]{1,0:T(8,128)}) async-done(((f32[512,256]{1,0:T(8,128)}, f32[256,256]{1,0:T(8,128)}, f32[256,256]{1,0:T(8,128)}), (f32[512,256]{1,0:T(8,128)}, f32[256,256]{1,0:T(8,128)}, f32[256,256]{1,0:T(8,128)})) %all-reduce.7.cloned.1.call-update) | async-done | bytes 1048592 | tf_op jit(solution)/shard_map/psum | solution.py:126
  245.4 1.9 broadcast_multiply_fusion
  247.3 1.9 broadcast_multiply_fusion.1
  (70 shorter events, 10.2 us)
Async XLA Ops:
  7.2 93.8 %copy-start = (bf16[512,256]{1,0:T(8,128)(2,1)S(1)}, bf16[512,256]{1,0:T(8,128)(2,1)}, u32[]{:S(2)}) copy-start(bf16[512,256]{1,0:T(8,128)(2,1)} %param.16) | copy-start | bytes 786436
  7.2 12.9 %copy-start.14 = (s32[128]{0:T(128)S(1)}, s32[128]{0:T(128)}, u32[]{:S(2)}) copy-start(s32[128]{0:T(128)} %param.14) | copy-start | bytes 1540
  7.2 13.1 %copy-start.13 = (s32[4096]{0:T(1024)S(1)}, s32[4096]{0:T(1024)}, u32[]{:S(2)}) copy-start(s32[4096]{0:T(1024)} %param.15) | copy-start | bytes 49156
  7.2 13.1 %copy-start.5 = (bf16[2048,256]{1,0:T(8,128)(2,1)S(1)}, bf16[2048,256]{1,0:T(8,128)(2,1)}, u32[]{:S(2)}) copy-start(bf16[2048,256]{1,0:T(8,128)(2,1)} %param.12) | copy-start | bytes 3145732
  7.2 61.1 %all-reduce.5.cloned.1.call-start = ((), (), s32[]{:S(2)}) async-start(), calls=%async_computation | async-start | bytes 2097152 | tf_op jit(solution)/shard_map/psum | solution.py:109
  20.0 47.5 %copy-start.12 = (bf16[256,256]{1,0:T(8,128)(2,1)S(1)}, bf16[256,256]{1,0:T(8,128)(2,1)}, u32[]{:S(2)}) copy-start(bf16[256,256]{1,0:T(8,128)(2,1)} %param.19) | copy-start | bytes 393220
  20.0 225.4 %all-reduce.7.cloned.1.call-start = ((), (), s32[]{:S(2)}) async-start(), calls=%async_computation.1 | async-start | bytes 2097152 | tf_op jit(solution)/shard_map/psum | solution.py:126
  67.5 0.8 copy-start.3
  67.5 10.1 %copy-start.16 = (bf16[256]{0:T(256)(128)(2,1)S(1)}, bf16[256]{0:T(256)(128)(2,1)}, u32[]{:S(2)}) copy-start(bf16[256]{0:T(256)(128)(2,1)} %param.17) | copy-start | bytes 1540
  68.3 10.4 %copy-start.1 = (bf16[1024,256]{1,0:T(8,128)(2,1)}, bf16[1024,256]{1,0:T(8,128)(2,1)S(1)}, u32[]{:S(2)}) copy-start(bf16[1024,256]{1,0:T(8,128)(2,1)S(1)} %convolution_convert_fusion) | copy-start | bytes 1572868
  71.8 11.5 %collective-permute-start = (bf16[64,256]{1,0:T(8,128)(2,1)}, bf16[64,256]{1,0:T(8,128)(2,1)S(1)}, u32[]{:S(2)}, u32[]{:S(2)}) collective-permute-start(bf16[64,256]{1,0:T(8,128)(2,1)} %broadcast_select_fusion.2), channel_id=1, source_target_pairs={{0,4},{4,8},{8,12},{12,16},{16,20},{20,24},{24,28},{28,0},{1,5},{5... | collective-permute-start | bytes 98312 | tf_op jit(solution)/shard_map/ppermute | solution.py:16
  73.8 9.5 %collective-permute-start.1 = (bf16[64,256]{1,0:T(8,128)(2,1)S(1)}, bf16[64,256]{1,0:T(8,128)(2,1)}, u32[]{:S(2)}, u32[]{:S(2)}) collective-permute-start(bf16[64,256]{1,0:T(8,128)(2,1)S(1)} %broadcast_select_fusion.1), channel_id=1, source_target_pairs={{4,0},{8,4},{12,8},{16,12},{20,16},{24,20},{28,24},{0,28},{5,1},{9... | collective-permute-start | bytes 98312 | tf_op jit(solution)/shard_map/ppermute | solution.py:18
  98.8 2.2 copy-start.9
  98.8 2.2 copy-start.17
  101.0 1.6 copy-start.8
  102.6 1.4 copy-start.11
  164.4 1.2 copy-start.2
  165.6 1.0 copy-start.4
  165.6 1.4 copy-start.6
  165.6 1.7 copy-start.7
  167.3 1.1 copy-start.10
  167.3 5.9 %copy-start.15 = (f32[256]{0:T(256)S(1)}, f32[256]{0:T(256)}, u32[]{:S(2)}) copy-start(f32[256]{0:T(256)} %get-tuple-element.25) | copy-start | bytes 3076
  167.3 23.7 %slice-start = ((bf16[1152,256]{1,0:T(8,128)(2,1)}), bf16[128,256]{1,0:T(8,128)(2,1)S(1)}, s32[]{:S(2)}) async-start(bf16[1152,256]{1,0:T(8,128)(2,1)} %convert.3), calls=%async_computation.2 | async-start | bytes 131072 | tf_op jit(solution)/shard_map/slice | solution.py:76
  168.4 22.6 %collective-permute-start.2 = (bf16[64,256]{1,0:T(8,128)(2,1)S(1)}, bf16[64,256]{1,0:T(8,128)(2,1)S(1)}, u32[]{:S(2)}, u32[]{:S(2)}) collective-permute-start(bf16[64,256]{1,0:T(8,128)(2,1)S(1)} %get-tuple-element.15), channel_id=1, source_target_pairs={{0,4},{4,8},{8,12},{12,16},{16,20},{20,24},{24,28},{28,0},{1,5},{5... | collective-permute-start | bytes 98312 | tf_op jit(solution)/shard_map/ppermute | solution.py:16
  168.5 22.5 %collective-permute-start.3 = (bf16[64,256]{1,0:T(8,128)(2,1)S(1)}, bf16[64,256]{1,0:T(8,128)(2,1)S(1)}, u32[]{:S(2)}, u32[]{:S(2)}) collective-permute-start(bf16[64,256]{1,0:T(8,128)(2,1)S(1)} %get-tuple-element.16), channel_id=1, source_target_pairs={{4,0},{8,4},{12,8},{16,12},{20,16},{24,20},{28,24},{0,28},{5,1},{9... | collective-permute-start | bytes 98312 | tf_op jit(solution)/shard_map/ppermute | solution.py:18
Sparse Core Ops, SparseCore 0:
  20.1 47.1 all-reduce.4
  168.5 76.8 all-reduce.6
where the time goes:
time: 257 us; the launch traced here: 256 us
  other arithmetic  74.5 us (29%)
  blocking collectives  52.5 us (20%)
  local copies, waits for them, and re-layouts  45.4 us (18%)
  waiting for transfers between devices  43.6 us (17%)
  matrix products  15.7 us (6%)
  between operations  14.4 us (6%)
  starting transfers between devices  9.8 us (4%)
    psum x1, waiting for transfers between devices, local(): lax.psum((grad_w1, grad_b1, grad_w2, grad_up), 'coarse')  43.6 us
    psum x1, blocking collectives, local(): pooled, grad_sum = lax.psum((part_feats, part_grads), 'fine')  35.3 us
    scatter-add x1, other arithmetic, edge_work(): jax.ops.segment_sum(grad_joined[:, feature_width:], sources, num_segments...  23.6 us
    psum x1, blocking collectives, local(): lax.psum((grad_w1, grad_b1, grad_w2, grad_up), 'coarse')  17.2 us
    gather x1, local copies, waits for them, and re-layouts, edge_work(): src_feats = jnp.take(extended, sources, axis=0)  14.6 us
    scatter-add x1, other arithmetic, local(): jax.ops.segment_sum(node_feats.astype(jnp.float32), local_ids, num_segmen...  11.9 us
    scatter-add x1, other arithmetic, local(): jax.ops.segment_sum(grad_out.astype(jnp.float32), local_ids, num_segments...  11.9 us
    ppermute x2, starting transfers between devices, with_halo(): lax.ppermute(head, axis, [((i + 1) % count, i) for i in range(count)])  7.73 us
  transfers between devices with their start and end apart: 6, of which 1 were waited for; matrix products, arithmetic and copies ran while one was open for 12% of the time, Pallas kernels for 0%

commit v1 on v0

v1 whole, which is shorter than its diff:
```python
import functools

import jax
import jax.numpy as jnp
from jax import lax
from jax.experimental import pallas as pl
from jax.experimental.pallas import tpu as pltpu
from jax.sharding import PartitionSpec as P

K = 4
BF = jnp.bfloat16
F32 = jnp.float32
LANES = 128
PACK = 16
MIB = 1 << 20


def dot(a, b):
    return jnp.dot(a, b, preferred_element_type=F32)


def dot_nt(a, b):
    return lax.dot_general(a, b, (((1,), (1,)), ((), ())), preferred_element_type=F32)


def dot_tn(a, b):
    return lax.dot_general(a, b, (((0,), (0,)), ((), ())), preferred_element_type=F32)


def bits_of(count):
    assert count > 1 and count & (count - 1) == 0
    return count.bit_length() - 1


def swap(x, axis, bit):
    count = lax.axis_size(axis)
    return lax.ppermute(x, axis, [(i, i ^ (1 << bit)) for i in range(count)])


def shift(x, axis, step):
    count = lax.axis_size(axis)
    return lax.ppermute(x, axis, [(i, (i + step) % count) for i in range(count)])


def send_owner(x, step, flip):
    owners, fines = lax.axis_size("coarse"), lax.axis_size("fine")
    pairs = [
        (g * fines + f, (g + step) % owners * fines + (f ^ (2 * flip)))
        for g in range(owners)
        for f in range(fines)
    ]
    return lax.ppermute(x, ("coarse", "fine"), pairs)


def call(body, outs, args, flops, vmem=16, scratch=(), anywhere=0):
    moved = sum(a.size * a.dtype.itemsize for a in (*args, *outs))
    spaces = [pltpu.HBM] * anywhere + [pltpu.VMEM] * (len(args) - anywhere)
    return pl.pallas_call(
        body,
        out_shape=outs,
        in_specs=[pl.BlockSpec(memory_space=space) for space in spaces],
        scratch_shapes=scratch,
        compiler_params=pltpu.CompilerParams(vmem_limit_bytes=vmem * MIB),
        cost_estimate=pl.CostEstimate(flops=int(flops), bytes_accessed=int(moved), transcendentals=0),
    )(*args)


def sds(shape, dtype):
    return jax.ShapeDtypeStruct(shape, dtype)


def column(row):
    blocks = [
        jnp.broadcast_to(row[:, i : i + LANES], (LANES, LANES)).T
        for i in range(0, row.shape[1], LANES)
    ]
    return blocks[0] if len(blocks) == 1 else jnp.concatenate(blocks, axis=0)


def hot_rows(row, width):
    ids = column(row)
    ids = jnp.concatenate([ids] * (width // LANES), axis=1)
    lane = lax.broadcasted_iota(jnp.int32, ids.shape, 1)
    return jnp.where(lane == ids, 1.0, 0.0).astype(BF)


def hot_columns(row, height, start=0):
    shape = (height, row.shape[1])
    at = lax.broadcasted_iota(jnp.int32, shape, 0)
    return jnp.where(at == row - start, 1.0, 0.0).astype(BF)


def pool_body(ids_hbm, x_hbm, keep_ref, send_ref, ids_ref, x_ref, sems):
    copies = [
        pltpu.make_async_copy(ids_hbm, ids_ref, sems.at[0]),
        pltpu.make_async_copy(x_hbm, x_ref, sems.at[1]),
    ]
    for copy in copies:
        copy.start()
    for copy in copies:
        copy.wait()
    half = keep_ref.shape[0]
    core = lax.axis_index("fine") % 2
    ids = lax.rem(ids_ref[...], 2 * half)
    x = x_ref[...]
    step = min(256, half)
    for out_ref, base in ((send_ref, (1 - core) * half), (keep_ref, core * half)):
        for t in range(0, half, step):
            out_ref[t : t + step, :] = dot(hot_columns(ids, step, base + t), x)


def halo_body(part_ref, lists_ref, right_ref, left_ref):
    half = part_ref.shape[0]
    width = right_ref.shape[0]
    core = lax.axis_index("fine") % 2
    picked = dot(hot_rows(lists_ref[...] - core * half, half), part_ref[...]).astype(BF)
    right_ref[...] = picked[:width]
    left_ref[...] = picked[width:]


def halo_sum_body(*refs):
    *parts, out_ref, slots = refs
    count = len(parts) // 2
    side = parts[0].shape[0]
    chip = lax.axis_index("fine") // 2
    for first, pieces in ((0, parts[:count]), (side, parts[count:])):
        for offset, piece in enumerate(pieces):
            slots[chip ^ offset] = piece[...].astype(F32)
        total = slots[0]
        for i in range(1, count):
            total = total + slots[i]
        out_ref[first : first + side, :] = total.astype(BF)


def core_order(half):
    core = lax.axis_index("fine") % 2
    at_own = pl.ds(pl.multiple_of(core * half, half), half)
    at_other = pl.ds(pl.multiple_of((1 - core) * half, half), half)
    return at_own, at_other


def forward_body(
    own_p, other_p, own_halo, other_halo, src_ref, w1_ref, b_ref,
    ext, hid, slope, feats,
):
    half, width = own_p.shape
    cells = 2 * half
    rows = ext.shape[0]
    at_own, at_other = core_order(half)
    ext[at_own, :] = own_p[...]
    ext[at_other, :] = other_p[...]
    ext[cells:, :] = own_halo[...] + other_halo[...]
    base = dot(ext[0:cells, :], w1_ref[0:width, :]) + b_ref[...].astype(F32)
    block = 256
    for k in range(K):
        for t in range(0, cells, block):
            part = src_ref[k : k + 1, t : t + block]
            feats[t : t + block, :] = dot(hot_rows(part, rows), ext[...]).astype(BF)
        pre = base + dot(feats[...], w1_ref[width : 2 * width, :])
        sig = 0.5 * jnp.tanh(0.5 * pre) + 0.5
        hidden = pre * sig
        hid[...] = hidden if k == 0 else hid[...] + hidden
        slope[k * cells : (k + 1) * cells, :] = sig + hidden * (1.0 - sig)


def split(x):
    high = x.astype(BF)
    return high, (x - high.astype(F32)).astype(BF)


def bias_rows(bias):
    high, low = split(bias)
    at = lax.broadcasted_iota(jnp.int32, (PACK, bias.shape[1]), 0)
    return jnp.where(at == 0, high.astype(F32), jnp.where(at == 1, low.astype(F32), 0.0))


def backward_body(
    own_g, other_g, ext, hid, slope, src_ref, w1_ref, wo_ref, wu_ref,
    gs_ref, ga_ref, gn_ref, back_l, back_r, send_ref,
    gsum, act, total,
):
    half, width = own_g.shape
    cells = 2 * half
    rows = ext.shape[0]
    side = back_l.shape[0]
    fine = lax.axis_index("fine")
    at_own, at_other = core_order(half)
    gsum[at_own, :] = own_g[...]
    gsum[at_other, :] = other_g[...]
    gn = dot_nt(gsum[...], wu_ref[...]).astype(BF)
    gn_ref[...] = gn
    grad = dot_nt(gn, wo_ref[...])
    for k in range(K):
        at = slice(k * cells, (k + 1) * cells)
        part = (grad * slope[at, :]).astype(BF)
        act[at, :] = part
        ga_ref[...] = part.astype(F32) if k == 0 else ga_ref[...] + part.astype(F32)
    step = LANES
    for r in range(0, rows, step):
        out = jnp.zeros((step, width), F32)
        for k in range(K):
            at = slice(k * cells, (k + 1) * cells)
            out += dot(hot_columns(src_ref[k : k + 1, :], step, r), act[at, :])
        gs_ref[r : r + step, :] = out
    back = dot_nt(gs_ref[cells:, :].astype(BF), w1_ref[width : 2 * width, :]).astype(BF)
    back_l[...] = back[:side]
    back_r[...] = back[side:]

    fines, coarses = lax.axis_size("fine"), lax.axis_size("coarse")
    per = 4 * width // fines
    n = min(per, width)
    for index in range(fines):

        @pl.when(fine == index)
        def _():
            for r in range(0, per, n):
                which, first = divmod(index * per + r, width)
                cols = slice(first, first + n)
                if which == 0:
                    high, low = split(ga_ref[...])
                    left = ext[0:cells, cols]
                    out = dot_tn(left, high) + dot_tn(left, low)
                elif which == 1:
                    high, low = split(gs_ref[...])
                    left = ext[:, cols]
                    out = dot_tn(left, high) + dot_tn(left, low)
                elif which == 2:
                    high, low = split(hid[:, cols])
                    out = dot_tn(high, gn_ref[...]) + dot_tn(low, gn_ref[...])
                else:
                    high, low = split(hid[...])
                    agg = dot(high, wo_ref[:, cols]) + dot(low, wo_ref[:, cols])
                    new = (ext[0:cells, cols].astype(F32) + agg).astype(BF)
                    out = dot_tn(new, gsum[...])
                total[r : r + n, :] = out

    bias = bias_rows(jnp.sum(ga_ref[...], axis=0, keepdims=True))
    share = per // coarses
    block = send_ref.shape[0] // coarses
    for g in range(coarses):
        parts = [total[g * share : (g + 1) * share, :], bias[: block - share]]
        send_ref[g * block : (g + 1) * block, :] = jnp.concatenate(parts, axis=0).astype(BF)


def share_body(recv, out_ref, bias_ref, *, share):
    count = lax.axis_size("coarse")
    block = recv.shape[0] // count
    total = recv[0:block, :].astype(F32)
    for g in range(1, count):
        total = total + recv[g * block : (g + 1) * block, :].astype(F32)
    each = out_ref.shape[0] // count
    rows = total[0:each].astype(BF)
    for g in range(count):
        out_ref[g * each : (g + 1) * each, :] = rows
    bias_ref[...] = bias_rows(total[share : share + 1] + total[share + 1 : share + 2]).astype(BF)


def join_body(parts, bias, out_ref):
    n = parts.shape[0]
    out_ref[0:n, :] = parts[...]
    out_ref[n : n + PACK, :] = bias[...]


def merge_body(own, other, out_ref, *, axis, bit):
    n = own.shape[0]
    side = lax.rem(lax.axis_index(axis) // (1 << bit), 2)
    out_ref[pl.ds(pl.multiple_of(side * n, n), n), :] = own[...]
    out_ref[pl.ds(pl.multiple_of((1 - side) * n, n), n), :] = other[...]


def merge(own, axis, bit):
    other = swap(own, axis, bit)
    n, width = own.shape
    body = functools.partial(merge_body, axis=axis, bit=bit)
    return call(body, (sds((2 * n, width), BF),), (own, other), 0)[0]


def weights_body(own, other, w1_ref, gb_ref, wo_ref, up_ref, *, per, share, edge_scale, cell_scale):
    width = own.shape[1]
    core = lax.axis_index("fine") % 2
    coarses = lax.axis_size("coarse")
    pieces = lax.axis_size("fine") // 2
    size = own.shape[0] // pieces
    each = (size - PACK) // coarses
    outs = ((w1_ref, 0, edge_scale), (w1_ref, width, edge_scale), (wo_ref, 0, edge_scale), (up_ref, 0, cell_scale))
    for index in range(2 * pieces):
        first = (index // 2) * size
        mine, theirs = own[first : first + size, :].astype(F32), other[first : first + size, :].astype(F32)
        value = jnp.where(core == index % 2, mine, theirs)
        if index == 0:
            at = size - PACK
            gb_ref[...] = (value[at : at + 1] + value[at + 1 : at + 2]) * edge_scale
        n = min(share, each)
        for g in range(coarses):
            which, row = divmod(index * per + g * n, width)
            out_ref, start, scale = outs[which]
            out_ref[start + row : start + row + n, :] = value[g * each : g * each + n] * scale


def pooled_grad_body(gs_ref, ga_ref, gn_ref, w1_ref, out_ref):
    cells, width = ga_ref.shape
    out_ref[...] = (
        gn_ref[...].astype(F32)
        + dot_nt(ga_ref[...].astype(BF), w1_ref[0:width, :])
        + dot_nt(gs_ref[0:cells, :].astype(BF), w1_ref[width : 2 * width, :])
    )


def feats_body(pool_ref, from_r, from_l, lists_ref, ids_ref, grad_ref, out_ref, table):
    cells = pool_ref.shape[0]
    nodes = grad_ref.shape[0]
    side = from_r.shape[0]
    lists = lists_ref[...]
    returned = jnp.concatenate([from_r[...], from_l[...]], axis=0)
    step = min(256, cells)
    for t in range(0, cells, step):
        add = dot(hot_columns(lists, step, t), returned)
        table[t : t + step, :] = (pool_ref[t : t + step, :] + add).astype(BF)
    block = 256
    for t in range(0, nodes, block):
        ids = lax.rem(ids_ref[:, t : t + block], cells)
        rows = dot(hot_rows(ids, cells), table[...])
        out_ref[t : t + block, :] = (grad_ref[t : t + block, :].astype(F32) + rows).astype(BF)


def local(
    node_feats, grad_out, cluster_ids, halo_lists, edge_sources, w_edge_in, b_edge_in, w_edge_out, w_unpool,
):
    nodes, width = node_feats.shape
    cells = edge_sources.shape[0] // K
    half = cells // 2
    side = halo_lists.shape[0] // 2
    rows = cells + 2 * side
    fines, coarses = lax.axis_size("fine"), lax.axis_size("coarse")
    fine_bits = bits_of(fines)
    ids = cluster_ids.reshape(1, nodes)
    lists = halo_lists.reshape(1, 2 * side)
    src = edge_sources.reshape(cells, K).T
    bias = b_edge_in.reshape(1, width)

    def pool(x):
        keep, send = call(
            pool_body, (sds((half, width), F32),) * 2, (ids, x), 2 * nodes * cells * width,
            scratch=(pltpu.VMEM(ids.shape, jnp.int32), pltpu.VMEM(x.shape, BF), pltpu.SemaphoreType.DMA((2,))),
            anywhere=2,
        )
        return keep + swap(send, "fine", 0)

    def across(part):
        for bit in range(1, fine_bits):
            part = part + swap(part.astype(BF), "fine", bit).astype(F32)
        return part.astype(BF)

    def halos(part):
        to_right, to_left = call(
            halo_body, (sds((side, width), BF),) * 2, (part.astype(BF), lists), 4 * side * half * width
        )
        arrived = [send_owner(to_right, 1, d) for d in range(fines // 2)]
        arrived += [send_owner(to_left, -1, d) for d in range(fines // 2)]
        own = call(
            halo_sum_body, (sds((2 * side, width), BF),), arrived, 0,
            scratch=(pltpu.VMEM((fines // 2, side, width), F32),),
        )[0]
        return own, swap(own, "fine", 0)

    part_p = pool(node_feats)
    own_p = across(part_p)
    own_halo, other_halo = halos(part_p)
    own_g = across(pool(grad_out))
    other_p = swap(own_p, "fine", 0)
    other_g = swap(own_g, "fine", 0)
    ext, hid, slope = call(
        forward_body,
        (sds((rows, width), BF), sds((cells, width), F32), sds((K * cells, width), F32)),
        (own_p, other_p, own_halo, other_halo, src, w_edge_in, bias),
        2 * K * cells * width * (rows + width),
        vmem=40,
        scratch=(pltpu.VMEM((cells, width), BF),),
    )
    per = 4 * width // fines
    share = per // coarses
    block = -(-(share + 2) // PACK) * PACK
    each = -(-share // PACK) * PACK
    gs, ga, gn, back_l, back_r, send = call(
        backward_body,
        (
            sds((rows, width), F32), sds((cells, width), F32), sds((cells, width), BF),
            sds((side, width), BF), sds((side, width), BF), sds((coarses * block, width), BF),
        ),
        (own_g, other_g, ext, hid, slope, src, w_edge_in, w_edge_out, w_unpool),
        2 * K * cells * width * rows,
        vmem=40,
        scratch=(
            pltpu.VMEM((cells, width), BF), pltpu.VMEM((cells * K, width), BF), pltpu.VMEM((per, width), F32),
        ),
    )
    recv = lax.all_to_all(send, "coarse", 0, 0, tiled=True)
    spread, bias_sum = call(
        functools.partial(share_body, share=share),
        (sds((coarses * each, width), BF), sds((PACK, width), BF)),
        (recv,),
        0,
    )
    part = lax.all_to_all(spread, "coarse", 0, 0, tiled=True)
    part = call(join_body, (sds((coarses * each + PACK, width), BF),), (part, bias_sum), 0)[0]

    from_r = shift(back_l, "coarse", -1)
    from_l = shift(back_r, "coarse", 1)
    pool_grad = call(
        pooled_grad_body, (sds((cells, width), F32),), (gs, ga, gn, w_edge_in), 4 * cells * width * width
    )[0]
    grad_feats = call(
        feats_body,
        (sds((nodes, width), BF),),
        (pool_grad, from_r, from_l, lists, ids, grad_out),
        2 * nodes * cells * width,
        vmem=24,
        scratch=(pltpu.VMEM((cells, width), BF),),
    )[0]

    for bit in range(1, fine_bits):
        part = merge(part, "fine", bit)
    other = swap(part, "fine", 0)
    total_cells = cells * coarses
    scales = dict(edge_scale=float(total_cells * K) ** -0.5, cell_scale=float(total_cells) ** -0.5)
    grad_w1, grad_b, grad_wo, grad_up = call(
        functools.partial(weights_body, per=per, share=share, **scales),
        (
            sds((2 * width, width), F32), sds((1, width), F32), sds((width, width), F32), sds((width, width), F32),
        ),
        (part, other),
        0,
    )
    return grad_feats, grad_w1, grad_b.reshape(width), grad_wo, grad_up


def solution(mesh):
    both = ("coarse", "fine")
    return jax.shard_map(
        local,
        mesh=mesh,
        in_specs=(P(both, None), P(both, None), P(both), P("coarse"), P("coarse"), P(), P(), P(), P()),
        out_specs=(P(both, None), P(), P(), P(), P()),
        check_vma=False,
    )
```

time: 257 us -> 79.8 us (0.31)
  other arithmetic: 74.5 us -> 0.26 us
  local copies, waits for them, and re-layouts: 45.4 us -> 3.9 us
  waiting for transfers between devices: 43.6 us -> 15.4 us
  blocking collectives: 52.5 us -> 24.9 us
  Pallas kernels: 0 us -> 15.9 us
  matrix products: 15.7 us -> 0 us
  between operations: 14.4 us -> 0.86 us
  starting transfers between devices: 9.8 us -> 18.3 us
    psum x2 -> x0, blocking collectives: 52.5 us -> none  [the longest x1 35.3 us: local(): pooled, grad_sum = lax.psum((part_feats, part_grads), 'fine')]
    scatter-add x3 -> x0, other arithmetic: 47.4 us -> none  [the longest x1 23.6 us: edge_work(): jax.ops.segment_sum(grad_joined[:, feature_width:], sources, num_segments...]
    psum x2 -> x0, waiting for transfers between devices: 43.6 us -> none  [the longest x1 43.6 us: local(): lax.psum((grad_w1, grad_b1, grad_w2, grad_up), 'coarse')]
    all_to_all x0 -> x2, blocking collectives: none -> 24.9 us  [the longest x1 14.6 us: local(): recv = lax.all_to_all(send, 'coarse', 0, 0, tiled=True)]
    gather x4 -> x0, local copies, waits for them, and re-layouts: 22.7 us -> none  [the longest x1 14.6 us: edge_work(): src_feats = jnp.take(extended, sources, axis=0)]
    pallas_call x0 -> x12, Pallas kernels: none -> 15.9 us  [call(): pl.pallas_call(body, out_shape=outs, in_specs=[pl.BlockSpec(memory_space=...]
    dot_general x8 -> x0, matrix products: 15.7 us -> none  [the longest x1 4.52 us: edge_work(): jnp.dot(grad_act, w_edge_in.T, preferred_element_type=jnp.float32)]
    ppermute x4 -> x15, waiting for transfers between devices: 0.01 us -> 15.4 us  [the longest x9 9.52 us: swap(): return lax.ppermute(x, axis, [(i, i ^ 1 << bit) for i in range(count)])]
  transfers between devices with their start and end apart: 6 -> 15, of which waited for: 1 -> 6; matrix products, arithmetic and copies ran while one was open for 12% -> 1% of each run, Pallas kernels for 0% -> 11%
where the time goes in v1:
time: 79.8 us; the launch traced here: 79.5 us
  blocking collectives  24.9 us (31%)
  starting transfers between devices  18.3 us (23%)
  Pallas kernels  15.9 us (20%)
  waiting for transfers between devices  15.4 us (19%)
  local copies, waits for them, and re-layouts  3.9 us (5%)
  between operations  0.86 us (1%)
    pallas_call x12, Pallas kernels, call(): pl.pallas_call(body, out_shape=outs, in_specs=[pl.BlockSpec(memory_space=...  15.9 us
    all_to_all x1, blocking collectives, local(): recv = lax.all_to_all(send, 'coarse', 0, 0, tiled=True)  14.6 us
    ppermute x4, starting transfers between devices, send_owner(): return lax.ppermute(x, ('coarse', 'fine'), pairs)  12.9 us
    all_to_all x1, blocking collectives, local(): part = lax.all_to_all(spread, 'coarse', 0, 0, tiled=True)  10.3 us
    ppermute x9, waiting for transfers between devices, swap(): return lax.ppermute(x, axis, [(i, i ^ 1 << bit) for i in range(count)])  9.52 us
    ppermute x2, waiting for transfers between devices, shift(): lax.ppermute(x, axis, [(i, (i + step) % count) for i in range(count)])  5.2 us
    ppermute x9, starting transfers between devices, swap(): return lax.ppermute(x, axis, [(i, i ^ 1 << bit) for i in range(count)])  3.31 us
    unnamed x22, local copies, waits for them, and re-layouts  3.18 us
  transfers between devices with their start and end apart: 15, of which 6 were waited for; matrix products, arithmetic and copies ran while one was open for 1% of the time, Pallas kernels for 11%

profile of v1, /device:TPU:0, one launch (start us, length us, event | category | flops | bytes accessed | tf_op | source)
XLA Modules:
  0.0 79.5 jit_solution(8492355614660691845)
XLA Ops:
  0.6 1.2 %copy-done.2 = bf16[2048,256]{1,0:T(8,128)(2,1)S(1)} copy-done((bf16[2048,256]{1,0:T(8,128)(2,1)S(1)}, bf16[2048,256]{1,0:T(8,128)(2,1)}, u32[]{:S(2)}) %copy-start.2) | copy-done | bytes 1048600
  1.9 0.7 copy-done.7
  2.6 1.3 %shard_map.129 = (f32[512,256]{1,0:T(8,128)S(1)}, f32[512,256]{1,0:T(8,128)S(1)}) custom-call(s32[1,2048]{1,0:T(1,128)S(1)} %bitcast.16, bf16[2048,256]{1,0:T(8,128)(2,1)S(1)} %copy-done.2), custom_call_target="tpu_custom_call" | custom-call | flops 1073741824 | bytes 2105344 | tf_op jit(solution)/shard_map/pallas_call | solution.py:58
  3.9 0.5 collective-permute-start.3
  4.4 1.2 %copy-done.3 = bf16[2048,256]{1,0:T(8,128)(2,1)S(1)} copy-done((bf16[2048,256]{1,0:T(8,128)(2,1)S(1)}, bf16[2048,256]{1,0:T(8,128)(2,1)}, u32[]{:S(2)}) %copy-start.3) | copy-done | bytes 1048600
  5.7 1.3 %shard_map.128 = (f32[512,256]{1,0:T(8,128)S(1)}, f32[512,256]{1,0:T(8,128)S(1)}) custom-call(s32[1,2048]{1,0:T(1,128)S(1)} %bitcast.17, bf16[2048,256]{1,0:T(8,128)(2,1)S(1)} %copy-done.3), custom_call_target="tpu_custom_call" | custom-call | flops 1073741824 | bytes 2105344 | tf_op jit(solution)/shard_map/pallas_call | solution.py:58
  7.2 0.2 shard_map.130
  7.5 3.9 %collective-permute-start.7 = (bf16[64,256]{1,0:T(8,128)(2,1)S(1)}, bf16[64,256]{1,0:T(8,128)(2,1)S(1)}, u32[]{:S(2)}, u32[]{:S(2)}) collective-permute-start(bf16[64,256]{1,0:T(8,128)(2,1)S(1)} %get-tuple-element.30), channel_id=1, source_target_pairs={{0,6},{1,7},{2,4},{3,5},{4,10},{5,11},{6,8},{7,9},{8,14},{9,15},{1... | collective-permute-start | bytes 98312 | tf_op jit(solution)/shard_map/ppermute | solution.py:52
  11.4 1.5 %collective-permute-start.6 = (bf16[64,256]{1,0:T(8,128)(2,1)S(1)}, bf16[64,256]{1,0:T(8,128)(2,1)S(1)}, u32[]{:S(2)}, u32[]{:S(2)}) collective-permute-start(bf16[64,256]{1,0:T(8,128)(2,1)S(1)} %get-tuple-element.30), channel_id=1, source_target_pairs={{0,4},{1,5},{2,6},{3,7},{4,8},{5,9},{6,10},{7,11},{8,12},{9,13},{1... | collective-permute-start | bytes 98312 | tf_op jit(solution)/shard_map/ppermute | solution.py:52
  13.0 0.5 collective-permute-start.4
  13.5 4.1 %collective-permute-start.9 = (bf16[64,256]{1,0:T(8,128)(2,1)S(1)}, bf16[64,256]{1,0:T(8,128)(2,1)S(1)}, u32[]{:S(2)}, u32[]{:S(2)}) collective-permute-start(bf16[64,256]{1,0:T(8,128)(2,1)S(1)} %get-tuple-element.31), channel_id=1, source_target_pairs={{0,30},{1,31},{2,28},{3,29},{4,2},{5,3},{6,0},{7,1},{8,6},{9,7},{1... | collective-permute-start | bytes 98312 | tf_op jit(solution)/shard_map/ppermute | solution.py:52
  17.7 0.6 collective-permute-start.1
  18.3 4.6 %collective-permute-done.4 = bf16[512,256]{1,0:T(8,128)(2,1)S(1)} collective-permute-done((bf16[512,256]{1,0:T(8,128)(2,1)S(1)}, bf16[512,256]{1,0:T(8,128)(2,1)S(1)}, u32[]{:S(2)}, u32[]{:S(2)}) %collective-permute-start.4) | collective-permute-done | bytes 262176 | tf_op jit(solution)/shard_map/ppermute | solution.py:37
  22.9 3.2 %collective-permute-start.8 = (bf16[64,256]{1,0:T(8,128)(2,1)S(1)}, bf16[64,256]{1,0:T(8,128)(2,1)S(1)}, u32[]{:S(2)}, u32[]{:S(2)}) collective-permute-start(bf16[64,256]{1,0:T(8,128)(2,1)S(1)} %get-tuple-element.31), channel_id=1, source_target_pairs={{0,28},{1,29},{2,30},{3,31},{4,0},{5,1},{6,2},{7,3},{8,4},{9,5},{1... | collective-permute-start | bytes 98312 | tf_op jit(solution)/shard_map/ppermute | solution.py:52
  26.3 0.5 reshape.31
  26.8 0.2 copy.14
  27.0 0.7 collective-permute-done.8.refs_2_
  27.9 0.6 collective-permute-start.2
  28.4 0.6 collective-permute-done.10.other_halo
  29.1 4.3 %shard_map.132 = (bf16[1152,256]{1,0:T(8,128)(2,1)S(1)}, f32[1024,256]{1,0:T(8,128)S(1)}, f32[4096,256]{1,0:T(8,128)S(1)}) custom-call(bf16[512,256]{1,0:T(8,128)(2,1)S(1)} %add_convert_fusion.own_p, bf16[512,256]{1,0:T(8,128)(2,1)S(1)} %collective-permute-done.5.other_p, bf16[128,256]{1,0:T(8,128)(2,1)S(1)} %shard_map.131.own_halo, ...), custom_call_target="tpu_custom_call" | custom-call | flops 2952790016 | bytes 6767104 | tf_op jit(solution)/shard_map/pallas_call | solution.py:58
  33.4 4.6 %shard_map.133 = (f32[1152,256]{1,0:T(8,128)S(1)}, f32[1024,256]{1,0:T(8,128)S(1)}, bf16[1024,256]{1,0:T(8,128)(2,1)S(1)}, bf16[64,256]{1,0:T(8,128)(2,1)S(1)}, ...) custom-call(bf16[512,256]{1,0:T(8,128)(2,1)S(1)} %add_convert_fusion.1.own_g, ...), custom_call_target="tpu_custom_call" | custom-call | flops 2415919104 | bytes 9912320 | tf_op jit(solution)/shard_map/pallas_call | solution.py:58
  38.0 14.6 %all_to_all.22 = bf16[8,48,256]{2,1,0:T(8,128)(2,1)S(1)} all-to-all(bf16[8,48,256]{2,1,0:T(8,128)(2,1)S(1)} %bitcast.10), channel_id=1, replica_groups=mesh['coarse'=8,'fine'=4] {'coarse'}, dimensions={0} | all-to-all | bytes 393216 | tf_op jit(solution)/shard_map/all_to_all | solution.py:397
  52.7 10.3 %all_to_all.23 = bf16[8,32,256]{2,1,0:T(8,128)(2,1)S(1)} all-to-all(bf16[8,32,256]{2,1,0:T(8,128)(2,1)S(1)} %bitcast.11), channel_id=1, replica_groups=mesh['coarse'=8,'fine'=4] {'coarse'}, dimensions={0} | all-to-all | bytes 262144 | tf_op jit(solution)/shard_map/all_to_all | solution.py:404
  63.0 0.8 %collective-permute-start.13 = (bf16[272,256]{1,0:T(8,128)(2,1)S(1)}, bf16[272,256]{1,0:T(8,128)(2,1)S(1)}, u32[]{:S(2)}, u32[]{:S(2)}) collective-permute-start(bf16[272,256]{1,0:T(8,128)(2,1)S(1)} %shard_map.137.own), channel_id=1, source_target_pairs={{0,2},{1,3},{2,0},{3,1},{4,6},{5,7},{6,4},{7,5},{8,10},{9,11},{10,... | collective-permute-start | bytes 417800 | tf_op jit(solution)/shard_map/ppermute | solution.py:37
  63.8 4.3 %collective-permute-done.13.other = bf16[272,256]{1,0:T(8,128)(2,1)S(1)} collective-permute-done((bf16[272,256]{1,0:T(8,128)(2,1)S(1)}, bf16[272,256]{1,0:T(8,128)(2,1)S(1)}, u32[]{:S(2)}, u32[]{:S(2)}) %collective-permute-start.13) | collective-permute-done | bytes 139296 | tf_op jit(solution)/shard_map/ppermute | solution.py:37
  68.2 1.1 %collective-permute-start.11 = (bf16[64,256]{1,0:T(8,128)(2,1)S(1)}, bf16[64,256]{1,0:T(8,128)(2,1)S(1)}, u32[]{:S(2)}, u32[]{:S(2)}) collective-permute-start(bf16[64,256]{1,0:T(8,128)(2,1)S(1)} %get-tuple-element.38), channel_id=1, source_target_pairs={{0,28},{4,0},{8,4},{12,8},{16,12},{20,16},{24,20},{28,24},{1,29},{... | collective-permute-start | bytes 98312 | tf_op jit(solution)/shard_map/ppermute | solution.py:42
  69.3 0.9 %collective-permute-start.12 = (bf16[64,256]{1,0:T(8,128)(2,1)S(1)}, bf16[64,256]{1,0:T(8,128)(2,1)S(1)}, u32[]{:S(2)}, u32[]{:S(2)}) collective-permute-start(bf16[64,256]{1,0:T(8,128)(2,1)S(1)} %get-tuple-element.39), channel_id=1, source_target_pairs={{0,4},{4,8},{8,12},{12,16},{16,20},{20,24},{24,28},{28,0},{1,5},{5... | collective-permute-start | bytes 98312 | tf_op jit(solution)/shard_map/ppermute | solution.py:42
  70.3 0.5 shard_map.134.pool_ref
  70.7 1.4 %collective-permute-done.11.from_r = bf16[64,256]{1,0:T(8,128)(2,1)S(1)} collective-permute-done((bf16[64,256]{1,0:T(8,128)(2,1)S(1)}, bf16[64,256]{1,0:T(8,128)(2,1)S(1)}, u32[]{:S(2)}, u32[]{:S(2)}) %collective-permute-start.11) | collective-permute-done | bytes 32800 | tf_op jit(solution)/shard_map/ppermute | solution.py:42
  72.2 3.8 %collective-permute-done.12.from_l = bf16[64,256]{1,0:T(8,128)(2,1)S(1)} collective-permute-done((bf16[64,256]{1,0:T(8,128)(2,1)S(1)}, bf16[64,256]{1,0:T(8,128)(2,1)S(1)}, u32[]{:S(2)}, u32[]{:S(2)}) %collective-permute-start.12) | collective-permute-done | bytes 32800 | tf_op jit(solution)/shard_map/ppermute | solution.py:42
  76.0 2.5 %shard_map.135 = bf16[2048,256]{1,0:T(8,128)(2,1)} custom-call(f32[1024,256]{1,0:T(8,128)S(1)} %shard_map.134.pool_ref, bf16[64,256]{1,0:T(8,128)(2,1)S(1)} %collective-permute-done.11.from_r, bf16[64,256]{1,0:T(8,128)(2,1)S(1)} %collective-permute-done.12.from_l, s32[1,128]{1,0:T(1,128)S(1)} %bitcast.15, s32[1,2048]{1,0:T(1,128)S(1)} %bitcast.18, ...), custom_call_target="tpu_custom_call" | custom-call | flops 1073741824 | bytes 3219968 | tf_op jit(solution)/shard_map/pallas_call | solution.py:58
  78.4 1.0 %shard_map.139 = (f32[512,256]{1,0:T(8,128)}, f32[1,256]{1,0:T(1,128)}, f32[256,256]{1,0:T(8,128)}, f32[256,256]{1,0:T(8,128)}) custom-call(bf16[544,256]{1,0:T(8,128)(2,1)S(1)} %shard_map.138.own, bf16[544,256]{1,0:T(8,128)(2,1)S(1)} %collective-permute-done.14.other), custom_call_target="tpu_custom_call" | custom-call | bytes 1606656 | tf_op jit(solution)/shard_map/pallas_call | solution.py:58
  (41 shorter events, 0.8 us)
Async XLA Ops:
  0.6 1.2 %copy-start.2 = (bf16[2048,256]{1,0:T(8,128)(2,1)S(1)}, bf16[2048,256]{1,0:T(8,128)(2,1)}, u32[]{:S(2)}) copy-start(bf16[2048,256]{1,0:T(8,128)(2,1)} %x_hbm.3) | copy-start | bytes 3145732
  1.9 0.7 copy-start.7
  2.6 4.7 %copy-start.1 = (s32[128]{0:T(128)S(1)}, s32[128]{0:T(128)}, u32[]{:S(2)}) copy-start(s32[128]{0:T(128)} %param.12) | copy-start | bytes 1540
  3.9 3.2 %collective-permute-start.3 = (f32[512,256]{1,0:T(8,128)S(1)}, f32[512,256]{1,0:T(8,128)S(1)}, u32[]{:S(2)}, u32[]{:S(2)}) collective-permute-start(f32[512,256]{1,0:T(8,128)S(1)} %get-tuple-element.29), channel_id=1, source_target_pairs={{0,1},{1,0},{2,3},{3,2},{4,5},{5,4},{6,7},{7,6},{8,9},{9,8},{10,11... | collective-permute-start | bytes 1572872 | tf_op jit(solution)/shard_map/ppermute | solution.py:37
  4.4 1.2 %copy-start.3 = (bf16[2048,256]{1,0:T(8,128)(2,1)S(1)}, bf16[2048,256]{1,0:T(8,128)(2,1)}, u32[]{:S(2)}) copy-start(bf16[2048,256]{1,0:T(8,128)(2,1)} %grad_ref.1) | copy-start | bytes 3145732
  5.6 20.6 %copy-start.10 = (bf16[256]{0:T(256)(128)(2,1)S(1)}, bf16[256]{0:T(256)(128)(2,1)}, u32[]{:S(2)}) copy-start(bf16[256]{0:T(256)(128)(2,1)} %param.15) | copy-start | bytes 1540
  5.7 20.6 %copy-start.9 = (s32[4096]{0:T(1024)S(1)}, s32[4096]{0:T(1024)}, u32[]{:S(2)}) copy-start(s32[4096]{0:T(1024)} %param.13) | copy-start | bytes 49156
  7.0 22.1 %copy-start = (bf16[512,256]{1,0:T(8,128)(2,1)S(1)}, bf16[512,256]{1,0:T(8,128)(2,1)}, u32[]{:S(2)}) copy-start(bf16[512,256]{1,0:T(8,128)(2,1)} %w1_ref.5) | copy-start | bytes 786436
  7.0 10.6 %collective-permute-start = (f32[512,256]{1,0:T(8,128)S(1)}, f32[512,256]{1,0:T(8,128)S(1)}, u32[]{:S(2)}, u32[]{:S(2)}) collective-permute-start(f32[512,256]{1,0:T(8,128)S(1)} %get-tuple-element.27), channel_id=1, source_target_pairs={{0,1},{1,0},{2,3},{3,2},{4,5},{5,4},{6,7},{7,6},{8,9},{9,8},{10,11... | collective-permute-start | bytes 1572872 | tf_op jit(solution)/shard_map/ppermute | solution.py:37
  7.5 18.7 %collective-permute-start.7 = (bf16[64,256]{1,0:T(8,128)(2,1)S(1)}, bf16[64,256]{1,0:T(8,128)(2,1)S(1)}, u32[]{:S(2)}, u32[]{:S(2)}) collective-permute-start(bf16[64,256]{1,0:T(8,128)(2,1)S(1)} %get-tuple-element.30), channel_id=1, source_target_pairs={{0,6},{1,7},{2,4},{3,5},{4,10},{5,11},{6,8},{7,9},{8,14},{9,15},{1... | collective-permute-start | bytes 98312 | tf_op jit(solution)/shard_map/ppermute | solution.py:52
  11.4 15.6 %collective-permute-start.6 = (bf16[64,256]{1,0:T(8,128)(2,1)S(1)}, bf16[64,256]{1,0:T(8,128)(2,1)S(1)}, u32[]{:S(2)}, u32[]{:S(2)}) collective-permute-start(bf16[64,256]{1,0:T(8,128)(2,1)S(1)} %get-tuple-element.30), channel_id=1, source_target_pairs={{0,4},{1,5},{2,6},{3,7},{4,8},{5,9},{6,10},{7,11},{8,12},{9,13},{1... | collective-permute-start | bytes 98312 | tf_op jit(solution)/shard_map/ppermute | solution.py:52
  13.0 9.9 %collective-permute-start.4 = (bf16[512,256]{1,0:T(8,128)(2,1)S(1)}, bf16[512,256]{1,0:T(8,128)(2,1)S(1)}, u32[]{:S(2)}, u32[]{:S(2)}) collective-permute-start(bf16[512,256]{1,0:T(8,128)(2,1)S(1)} %get-tuple-element.47.part_ref), channel_id=1, source_target_pairs={{0,2},{1,3},{2,0},{3,1},{4,6},{5,7},{6,4},{7,5},{8,10},{9,11},{10,... | collective-permute-start | bytes 786440 | tf_op jit(solution)/shard_map/ppermute | solution.py:37
  13.5 13.5 %collective-permute-start.9 = (bf16[64,256]{1,0:T(8,128)(2,1)S(1)}, bf16[64,256]{1,0:T(8,128)(2,1)S(1)}, u32[]{:S(2)}, u32[]{:S(2)}) collective-permute-start(bf16[64,256]{1,0:T(8,128)(2,1)S(1)} %get-tuple-element.31), channel_id=1, source_target_pairs={{0,30},{1,31},{2,28},{3,29},{4,2},{5,3},{6,0},{7,1},{8,6},{9,7},{1... | collective-permute-start | bytes 98312 | tf_op jit(solution)/shard_map/ppermute | solution.py:52
  17.7 10.1 %collective-permute-start.1 = (bf16[512,256]{1,0:T(8,128)(2,1)S(1)}, bf16[512,256]{1,0:T(8,128)(2,1)S(1)}, u32[]{:S(2)}, u32[]{:S(2)}) collective-permute-start(bf16[512,256]{1,0:T(8,128)(2,1)S(1)} %get-tuple-element.49), channel_id=1, source_target_pairs={{0,2},{1,3},{2,0},{3,1},{4,6},{5,7},{6,4},{7,5},{8,10},{9,11},{10,... | collective-permute-start | bytes 786440 | tf_op jit(solution)/shard_map/ppermute | solution.py:37
  22.9 4.8 %collective-permute-start.8 = (bf16[64,256]{1,0:T(8,128)(2,1)S(1)}, bf16[64,256]{1,0:T(8,128)(2,1)S(1)}, u32[]{:S(2)}, u32[]{:S(2)}) collective-permute-start(bf16[64,256]{1,0:T(8,128)(2,1)S(1)} %get-tuple-element.31), channel_id=1, source_target_pairs={{0,28},{1,29},{2,30},{3,31},{4,0},{5,1},{6,2},{7,3},{8,4},{9,5},{1... | collective-permute-start | bytes 98312 | tf_op jit(solution)/shard_map/ppermute | solution.py:52
  26.2 2.9 %collective-permute-start.5 = (bf16[512,256]{1,0:T(8,128)(2,1)S(1)}, bf16[512,256]{1,0:T(8,128)(2,1)S(1)}, u32[]{:S(2)}, u32[]{:S(2)}) collective-permute-start(bf16[512,256]{1,0:T(8,128)(2,1)S(1)} %add_convert_fusion.own_p), channel_id=1, source_target_pairs={{0,1},{1,0},{2,3},{3,2},{4,5},{5,4},{6,7},{7,6},{8,9},{9,8},{10,11... | collective-permute-start | bytes 786440 | tf_op jit(solution)/shard_map/ppermute | solution.py:37
  27.7 1.3 %collective-permute-start.10 = (bf16[128,256]{1,0:T(8,128)(2,1)S(1)}, bf16[128,256]{1,0:T(8,128)(2,1)S(1)}, u32[]{:S(2)}, u32[]{:S(2)}) collective-permute-start(bf16[128,256]{1,0:T(8,128)(2,1)S(1)} %shard_map.131.own_halo), channel_id=1, source_target_pairs={{0,1},{1,0},{2,3},{3,2},{4,5},{5,4},{6,7},{7,6},{8,9},{9,8},{10,11... | collective-permute-start | bytes 196616 | tf_op jit(solution)/shard_map/ppermute | solution.py:37
  27.9 5.5 %collective-permute-start.2 = (bf16[512,256]{1,0:T(8,128)(2,1)S(1)}, bf16[512,256]{1,0:T(8,128)(2,1)S(1)}, u32[]{:S(2)}, u32[]{:S(2)}) collective-permute-start(bf16[512,256]{1,0:T(8,128)(2,1)S(1)} %add_convert_fusion.1.own_g), channel_id=1, source_target_pairs={{0,1},{1,0},{2,3},{3,2},{4,5},{5,4},{6,7},{7,6},{8,9},{9,8},{10,11... | collective-permute-start | bytes 786440 | tf_op jit(solution)/shard_map/ppermute | solution.py:37
  29.1 4.3 %copy-start.5 = (bf16[256,256]{1,0:T(8,128)(2,1)S(1)}, bf16[256,256]{1,0:T(8,128)(2,1)}, u32[]{:S(2)}) copy-start(bf16[256,256]{1,0:T(8,128)(2,1)} %wo_ref.1) | copy-start | bytes 393220
  29.1 4.4 %copy-start.6 = (bf16[256,256]{1,0:T(8,128)(2,1)S(1)}, bf16[256,256]{1,0:T(8,128)(2,1)}, u32[]{:S(2)}) copy-start(bf16[256,256]{1,0:T(8,128)(2,1)} %wu_ref.1) | copy-start | bytes 393220
  38.0 37.9 %copy-start.4 = (bf16[2048,256]{1,0:T(8,128)(2,1)S(1)}, bf16[2048,256]{1,0:T(8,128)(2,1)}, u32[]{:S(2)}) copy-start(bf16[2048,256]{1,0:T(8,128)(2,1)} %grad_ref.1) | copy-start | bytes 3145732
  38.0 37.9 %copy-start.8 = (s32[2048]{0:T(1024)S(1)}, s32[2048]{0:T(1024)}, u32[]{:S(2)}) copy-start(s32[2048]{0:T(1024)} %param.11) | copy-start | bytes 24580
  63.0 5.1 %collective-permute-start.13 = (bf16[272,256]{1,0:T(8,128)(2,1)S(1)}, bf16[272,256]{1,0:T(8,128)(2,1)S(1)}, u32[]{:S(2)}, u32[]{:S(2)}) collective-permute-start(bf16[272,256]{1,0:T(8,128)(2,1)S(1)} %shard_map.137.own), channel_id=1, source_target_pairs={{0,2},{1,3},{2,0},{3,1},{4,6},{5,7},{6,4},{7,5},{8,10},{9,11},{10,... | collective-permute-start | bytes 417800 | tf_op jit(solution)/shard_map/ppermute | solution.py:37
  68.1 10.3 %collective-permute-start.14 = (bf16[544,256]{1,0:T(8,128)(2,1)S(1)}, bf16[544,256]{1,0:T(8,128)(2,1)S(1)}, u32[]{:S(2)}, u32[]{:S(2)}) collective-permute-start(bf16[544,256]{1,0:T(8,128)(2,1)S(1)} %shard_map.138.own), channel_id=1, source_target_pairs={{0,1},{1,0},{2,3},{3,2},{4,5},{5,4},{6,7},{7,6},{8,9},{9,8},{10,11... | collective-permute-start | bytes 835592 | tf_op jit(solution)/shard_map/ppermute | solution.py:37
  68.2 4.0 %collective-permute-start.11 = (bf16[64,256]{1,0:T(8,128)(2,1)S(1)}, bf16[64,256]{1,0:T(8,128)(2,1)S(1)}, u32[]{:S(2)}, u32[]{:S(2)}) collective-permute-start(bf16[64,256]{1,0:T(8,128)(2,1)S(1)} %get-tuple-element.38), channel_id=1, source_target_pairs={{0,28},{4,0},{8,4},{12,8},{16,12},{20,16},{24,20},{28,24},{1,29},{... | collective-permute-start | bytes 98312 | tf_op jit(solution)/shard_map/ppermute | solution.py:42
  69.3 6.6 %collective-permute-start.12 = (bf16[64,256]{1,0:T(8,128)(2,1)S(1)}, bf16[64,256]{1,0:T(8,128)(2,1)S(1)}, u32[]{:S(2)}, u32[]{:S(2)}) collective-permute-start(bf16[64,256]{1,0:T(8,128)(2,1)S(1)} %get-tuple-element.39), channel_id=1, source_target_pairs={{0,4},{4,8},{8,12},{12,16},{16,20},{20,24},{24,28},{28,0},{1,5},{5... | collective-permute-start | bytes 98312 | tf_op jit(solution)/shard_map/ppermute | solution.py:42

commit v2 on v1

v2 whole, which is shorter than its diff:
```python
import functools

import jax
import jax.numpy as jnp
from jax import lax
from jax.experimental import pallas as pl
from jax.experimental.pallas import tpu as pltpu
from jax.sharding import PartitionSpec as P

K = 4
BF = jnp.bfloat16
F32 = jnp.float32
LANES = 128
PACK = 16
MIB = 1 << 20


def dot(a, b):
    return jnp.dot(a, b, preferred_element_type=F32)


def dot_nt(a, b):
    return lax.dot_general(a, b, (((1,), (1,)), ((), ())), preferred_element_type=F32)


def dot_tn(a, b):
    return lax.dot_general(a, b, (((0,), (0,)), ((), ())), preferred_element_type=F32)


def bits_of(count):
    assert count > 1 and count & (count - 1) == 0
    return count.bit_length() - 1


def swap(x, axis, bit):
    count = lax.axis_size(axis)
    return lax.ppermute(x, axis, [(i, i ^ (1 << bit)) for i in range(count)])


def swap_both(x):
    owners, fines = lax.axis_size("coarse"), lax.axis_size("fine")
    pairs = [(g * fines + f, (g ^ 1) * fines + (f ^ 2)) for g in range(owners) for f in range(fines)]
    return lax.ppermute(x, ("coarse", "fine"), pairs)


def send_sides(x, flip=0):
    owners, fines = lax.axis_size("coarse"), lax.axis_size("fine")
    pairs = [
        (g * fines + f, (g + 1 - 2 * (f % 2)) % owners * fines + (f ^ (2 * flip)))
        for g in range(owners)
        for f in range(fines)
    ]
    return lax.ppermute(x, ("coarse", "fine"), pairs)


def call(body, outs, args, flops, vmem=16, scratch=(), after=()):
    moved = sum(a.size * a.dtype.itemsize for a in (*args, *outs))
    count, waited = len(args), len(after)

    def kernel(*refs):
        body(*refs[:count], *refs[count + waited :])

    specs = [pl.BlockSpec(memory_space=pltpu.VMEM)] * count + [pl.BlockSpec(memory_space=pl.ANY)] * waited
    return pl.pallas_call(
        kernel,
        out_shape=outs,
        in_specs=specs,
        scratch_shapes=scratch,
        compiler_params=pltpu.CompilerParams(vmem_limit_bytes=vmem * MIB),
        cost_estimate=pl.CostEstimate(flops=int(flops), bytes_accessed=int(moved), transcendentals=0),
    )(*args, *after)


def sds(shape, dtype):
    return jax.ShapeDtypeStruct(shape, dtype)


def column(row):
    blocks = [
        jnp.broadcast_to(row[:, i : i + LANES], (LANES, LANES)).T
        for i in range(0, row.shape[1], LANES)
    ]
    return blocks[0] if len(blocks) == 1 else jnp.concatenate(blocks, axis=0)


def hot_rows(row, width):
    ids = column(row)
    ids = jnp.concatenate([ids] * (width // LANES), axis=1)
    lane = lax.broadcasted_iota(jnp.int32, ids.shape, 1)
    return jnp.where(lane == ids, 1.0, 0.0).astype(BF)


def hot_columns(row, height, start=0):
    shape = (height, row.shape[1])
    at = lax.broadcasted_iota(jnp.int32, shape, 0)
    return jnp.where(at == row - start, 1.0, 0.0).astype(BF)


def pool_body(ids_ref, x_ref, keep_ref, send_ref):
    half = keep_ref.shape[0]
    core = lax.axis_index("fine") % 2
    ids = ids_ref[...]
    x = x_ref[...]
    step = min(256, half)
    for out_ref, base in ((send_ref, (1 - core) * half), (keep_ref, core * half)):
        for t in range(0, half, step):
            out_ref[t : t + step, :] = dot(hot_columns(ids, step, base + t), x)


def pick_body(part_ref, lists_ref, out_ref):
    half = part_ref.shape[0]
    core = lax.axis_index("fine") % 2
    out_ref[...] = dot(hot_rows(lists_ref[...] - core * half, half), part_ref[...]).astype(BF)


def side_body(own, other, out_ref):
    side = out_ref.shape[0]
    core = lax.axis_index("fine") % 2
    at = pl.ds(pl.multiple_of(core * side, side), side)
    out_ref[...] = own[at, :] + other[at, :]


def halo_sum_body(*refs):
    *parts, out_ref, slots = refs
    chip = lax.axis_index("fine") // 2
    for offset, part in enumerate(parts):
        slots[chip ^ offset] = part[...].astype(F32)
    total = slots[0]
    for i in range(1, len(parts)):
        total = total + slots[i]
    out_ref[...] = total.astype(BF)


def chip_body(keep, recv, part_ref, send_ref):
    total = keep[...] + recv[...]
    part_ref[...] = total
    send_ref[...] = total.astype(BF)


def across_body(part, recv, *out_refs):
    total = part[...] + recv[...].astype(F32)
    for ref in out_refs:
        ref[...] = total.astype(ref.dtype)


def core_order(half):
    core = lax.axis_index("fine") % 2
    at_own = pl.ds(pl.multiple_of(core * half, half), half)
    at_other = pl.ds(pl.multiple_of((1 - core) * half, half), half)
    return at_own, at_other


def forward_body(
    own_p, other_p, own_halo, other_halo, src_ref, w1_ref, b_ref,
    ext, hid, slope, feats, token_ref,
):
    half, width = own_p.shape
    cells = 2 * half
    rows = ext.shape[0]
    at_own, at_other = core_order(half)
    ext[at_own, :] = own_p[...]
    ext[at_other, :] = other_p[...]
    side = own_halo.shape[0]
    core = lax.axis_index("fine") % 2
    ext[pl.ds(pl.multiple_of(cells + core * side, PACK), side), :] = own_halo[...]
    ext[pl.ds(pl.multiple_of(cells + (1 - core) * side, PACK), side), :] = other_halo[...]
    token_ref[...] = jnp.zeros_like(token_ref)
    base = dot(ext[0:cells, :], w1_ref[0:width, :]) + b_ref[...].astype(F32)
    block = 512
    for k in range(K):
        for t in range(0, cells, block):
            part = src_ref[k : k + 1, t : t + block]
            at = k * cells + t
            feats[at : at + block, :] = dot(hot_rows(part, rows), ext[...]).astype(BF)
        at = slice(k * cells, (k + 1) * cells)
        pre = base + dot(feats[at, :], w1_ref[width : 2 * width, :])
        sig = 0.5 * jnp.tanh(0.5 * pre) + 0.5
        hidden = pre * sig
        hid[...] = hidden if k == 0 else hid[...] + hidden
        slope[at, :] = sig + hidden * (1.0 - sig)


def split(x):
    high = x.astype(BF)
    return high, (x - high.astype(F32)).astype(BF)


def bias_rows(bias):
    high, low = (part.astype(F32) for part in split(bias))
    at = lax.broadcasted_iota(jnp.int32, (PACK, bias.shape[1]), 0)
    return jnp.where(at == 0, high, jnp.where(at == 1, low, 0.0)).astype(BF), high + low


def axis_bit(axis, bit):
    return lax.rem(lax.axis_index(axis) // (1 << bit), 2)


def emit(total_ref, bias, bit, keep_ref, send_ref, bias_ref):
    n = keep_ref.shape[0]
    if n == total_ref.shape[0]:
        sent = total_ref[...].astype(BF)
        keep_ref[...] = sent.astype(F32)
    else:
        side = axis_bit("coarse", bit)
        keep_ref[...] = total_ref[pl.ds(pl.multiple_of(side * n, n), n), :]
        sent = total_ref[pl.ds(pl.multiple_of((1 - side) * n, n), n), :].astype(BF)
    rows, bias = bias_rows(bias)
    send_ref[0:n, :] = sent
    send_ref[n : n + PACK, :] = rows
    bias_ref[...] = jnp.broadcast_to(bias, bias_ref.shape)


def backward_body(
    own_g, other_g, ext, feats, hid, slope, wo_ref, wu_ref,
    act, ga_ref, gn_ref, keep_ref, send_ref, bias_ref,
    gsum, total,
):
    half, width = own_g.shape
    cells = 2 * half
    fine = lax.axis_index("fine")
    at_own, at_other = core_order(half)
    gsum[at_own, :] = own_g[...]
    gsum[at_other, :] = other_g[...]
    gn = dot_nt(gsum[...], wu_ref[...]).astype(BF)
    gn_ref[...] = gn
    grad = dot_nt(gn, wo_ref[...])
    ga = jnp.zeros((cells, width), F32)
    for k in range(K):
        at = slice(k * cells, (k + 1) * cells)
        part = (grad * slope[at, :]).astype(BF)
        act[at, :] = part
        ga = ga + part.astype(F32)
    ga_ref[...] = ga

    fines = lax.axis_size("fine")
    per = 4 * width // fines
    n = min(per, width)
    for index in range(fines):

        @pl.when(fine == index)
        def _():
            for r in range(0, per, n):
                which, first = divmod(index * per + r, width)
                cols = slice(first, first + n)
                if which == 0:
                    high, low = split(ga_ref[...])
                    left = ext[0:cells, cols]
                    out = dot_tn(left, high) + dot_tn(left, low)
                elif which == 1:
                    out = dot_tn(feats[:, cols], act[...])
                elif which == 2:
                    high, low = split(hid[:, cols])
                    out = dot_tn(high, gn_ref[...]) + dot_tn(low, gn_ref[...])
                else:
                    high, low = split(hid[...])
                    agg = dot(high, wo_ref[:, cols]) + dot(low, wo_ref[:, cols])
                    new = (ext[0:cells, cols].astype(F32) + agg).astype(BF)
                    out = dot_tn(new, gsum[...])
                total[r : r + n, :] = out

    emit(total, jnp.sum(ga_ref[...], axis=0, keepdims=True), 0, keep_ref, send_ref, bias_ref)


def received_bias(recv, n):
    return recv[n : n + 1, :].astype(F32) + recv[n + 1 : n + 2, :].astype(F32)


def stage_body(keep_in, recv, bias_in, keep_ref, send_ref, bias_ref, total, *, bit):
    n = keep_in.shape[0]
    total[...] = keep_in[...] + recv[0:n, :].astype(F32)
    emit(total, bias_in[0:1, :] + received_bias(recv, n), bit, keep_ref, send_ref, bias_ref)


def end_body(keep_in, recv, bias_in, out_ref):
    n = keep_in.shape[0]
    out_ref[0:n, :] = (keep_in[...] + recv[0:n, :].astype(F32)).astype(BF)
    out_ref[n : n + PACK, :] = bias_rows(bias_in[0:1, :] + received_bias(recv, n))[0]


def scatter(act, src_ref, first, count):
    cells = src_ref.shape[1]
    out = jnp.zeros((count, act.shape[1]), F32)
    for k in range(K):
        hot = hot_columns(src_ref[k : k + 1, :], count, first)
        out += dot(hot, act[k * cells : (k + 1) * cells, :])
    return out


def back_body(act, src_ref, w1_ref, out_ref, both):
    side, width = out_ref.shape
    rows = scatter(act, src_ref, src_ref.shape[1], 2 * side)
    both[...] = dot_nt(rows.astype(BF), w1_ref[width : 2 * width, :])
    core = lax.axis_index("fine") % 2
    out_ref[...] = both[pl.ds(pl.multiple_of((1 - core) * side, side), side), :].astype(BF)


def cell_grad_body(act, src_ref, ga_ref, gn_ref, w1_ref, out_ref, *, first):
    count, width = out_ref.shape
    step = min(512, count)
    for r in range(0, count, step):
        at = slice(first + r, first + r + step)
        rows = scatter(act, src_ref, first + r, step)
        out_ref[r : r + step, :] = (
            gn_ref[at, :].astype(F32)
            + dot_nt(ga_ref[at, :].astype(BF), w1_ref[0:width, :])
            + dot_nt(rows.astype(BF), w1_ref[width : 2 * width, :])
        )


def merge_body(own, other, *rest, bit):
    n = own.shape[0]
    out_ref = rest[-1]
    side = axis_bit("fine", bit)
    out_ref[pl.ds(pl.multiple_of(side * n, PACK), n), :] = own[...]
    out_ref[pl.ds(pl.multiple_of((1 - side) * n, PACK), n), :] = other[...]


def square_body(own, by_owner, by_chip, by_both, out_ref):
    size = out_ref.shape[0] // 2
    n = own.shape[0] - PACK
    half, chip = axis_bit("coarse", 0), axis_bit("fine", 1)
    for block, i, j in ((own, half, chip), (by_owner, 1 - half, chip), (by_chip, half, 1 - chip), (by_both, 1 - half, 1 - chip)):
        out_ref[pl.ds(pl.multiple_of(j * size + i * n, PACK), n), :] = block[0:n, :]
    for block, j in ((own, chip), (by_chip, 1 - chip)):
        out_ref[pl.ds(pl.multiple_of(j * size + 2 * n, PACK), PACK), :] = block[n:, :]


def weights_body(own, other, w1_ref, gb_ref, wo_ref, up_ref, *, per, edge_scale, cell_scale):
    width = own.shape[1]
    core = lax.axis_index("fine") % 2
    outs = ((w1_ref, 0, edge_scale), (w1_ref, width, edge_scale), (wo_ref, 0, edge_scale), (up_ref, 0, cell_scale))
    size = per + PACK
    n = min(per, width)
    for index in range(lax.axis_size("fine")):
        at = slice((index // 2) * size, (index // 2 + 1) * size)
        value = jnp.where(core == index % 2, own[at, :].astype(F32), other[at, :].astype(F32))
        if index == 0:
            gb_ref[...] = (value[per : per + 1] + value[per + 1 : per + 2]) * edge_scale
        for r in range(0, per, n):
            which, row = divmod(index * per + r, width)
            out_ref, start, scale = outs[which]
            out_ref[start + row : start + row + n, :] = value[r : r + n] * scale


def feats_body(*refs):
    *pool_refs, own_back, other_back, lists_ref, ids_ref, grad_ref, out_ref, token_ref, table = refs
    token_ref[...] = jnp.zeros_like(token_ref)
    cells = table.shape[0]
    nodes = grad_ref.shape[0]
    lists = lists_ref[...]
    core = lax.axis_index("fine") % 2
    side = own_back.shape[0]
    returned = jnp.concatenate([own_back[...], other_back[...]], axis=0)
    first, second = lists[:, :side], lists[:, side:]
    lists = jnp.where(core == 0, jnp.concatenate([second, first], axis=1), lists)
    step = pool_refs[0].shape[0]
    for i, pool_ref in enumerate(pool_refs):
        add = dot(hot_columns(lists, step, i * step), returned)
        table[i * step : (i + 1) * step, :] = (pool_ref[...] + add).astype(BF)
    block = 256
    for t in range(0, nodes, block):
        rows = dot(hot_rows(ids_ref[:, t : t + block], cells), table[...])
        out_ref[t : t + block, :] = (grad_ref[t : t + block, :].astype(F32) + rows).astype(BF)


def local(
    node_feats, grad_out, cluster_ids, halo_lists, edge_sources, w_edge_in, b_edge_in, w_edge_out, w_unpool,
):
    nodes, width = node_feats.shape
    cells = edge_sources.shape[0] // K
    half = cells // 2
    side = halo_lists.shape[0] // 2
    rows = cells + 2 * side
    fines, coarses = lax.axis_size("fine"), lax.axis_size("coarse")
    fine_bits, coarse_bits = bits_of(fines), bits_of(coarses)
    ids = lax.rem(cluster_ids, cells).reshape(1, nodes)
    lists = halo_lists.reshape(1, 2 * side)
    src = edge_sources.reshape(cells, K).T
    bias = b_edge_in.reshape(1, width)

    def pool(x):
        keep, send = call(pool_body, (sds((half, width), F32),) * 2, (ids, x), 2 * nodes * cells * width)
        outs = (sds((half, width), F32), sds((half, width), BF))
        return call(chip_body, outs, (keep, swap(send, "fine", 0)), 0)

    def across(part, send, after=()):
        for bit in range(1, fine_bits):
            recv = swap(send, "fine", bit)
            last = bit == fine_bits - 1
            outs = (sds((half, width), BF),) if last else (sds((half, width), F32), sds((half, width), BF))
            part, send = (*call(across_body, outs, (part, recv), 0, after=after), None)[:2]
        return part

    part_p, send_p = pool(node_feats)
    part_g, send_g = pool(grad_out)
    picked = call(pick_body, (sds((2 * side, width), BF),), (send_p, lists), 0, after=(send_g,))[0]
    sent = call(side_body, (sds((side, width), BF),), (picked, swap(picked, "fine", 0)), 0)[0]
    own_halo = call(
        halo_sum_body, (sds((side, width), BF),), [send_sides(sent, d) for d in range(fines // 2)], 0,
        scratch=(pltpu.VMEM((fines // 2, side, width), F32),),
    )[0]
    own_p = across(part_p, send_p, after=(own_halo,))
    other_halo = swap(own_halo, "fine", 0)
    other_p = swap(own_p, "fine", 0)
    ext, hid, slope, feats, forward_token = call(
        forward_body,
        (
            sds((rows, width), BF), sds((cells, width), F32),
            sds((K * cells, width), F32), sds((K * cells, width), BF), sds((8, LANES), F32),
        ),
        (own_p, other_p, own_halo, other_halo, src, w_edge_in, bias),
        2 * K * cells * width * (rows + width),
        vmem=32,
    )
    own_g = across(part_g, send_g, after=(forward_token,))
    other_g = swap(own_g, "fine", 0)
    per = 4 * width // fines
    first = per // 2
    act, ga, gn, keep, send, bias_sum = call(
        backward_body,
        (
            sds((K * cells, width), BF), sds((cells, width), F32), sds((cells, width), BF),
            sds((first, width), F32), sds((first + PACK, width), BF), sds((8, width), F32),
        ),
        (own_g, other_g, ext, feats, hid, slope, w_edge_out, w_unpool),
        2 * K * cells * width * width,
        vmem=32,
        scratch=(pltpu.VMEM((cells, width), BF), pltpu.VMEM((per, width), F32)),
    )

    back = call(
        back_body, (sds((side, width), BF),), (act, src, w_edge_in), 4 * K * side * cells * width,
        scratch=(pltpu.VMEM((2 * side, width), F32),),
    )[0]
    own_back = send_sides(back)
    other_back = swap(own_back, "fine", 0)
    cell_grads = [
        call(
            functools.partial(cell_grad_body, first=at),
            (sds((half, width), F32),),
            (act, src, ga, gn, w_edge_in),
            2 * K * half * cells * width,
        )[0]
        for at in (0, half)
    ]
    grad_feats, feats_token = call(
        feats_body,
        (sds((nodes, width), BF), sds((8, LANES), F32)),
        (*cell_grads, own_back, other_back, lists, ids, grad_out),
        2 * nodes * cells * width,
        vmem=24,
        scratch=(pltpu.VMEM((cells, width), BF),),
    )

    after = {1: (back,), 2: (cell_grads[0],)}
    for bit in range(1, coarse_bits):
        recv = swap(send, "coarse", bit - 1)
        keep, send, bias_sum = call(
            functools.partial(stage_body, bit=bit),
            (sds((first, width), F32), sds((first + PACK, width), BF), sds((8, width), F32)),
            (keep, recv, bias_sum),
            0,
            scratch=(pltpu.VMEM((first, width), F32),),
            after=after.get(bit, ()),
        )
    recv = swap(send, "coarse", coarse_bits - 1)
    part = call(
        end_body, (sds((first + PACK, width), BF),), (keep, recv, bias_sum), 0,
        after=(cell_grads[1], other_back),
    )[0]
    near = [swap(part, "coarse", 0), swap(part, "fine", 1), swap_both(part)]
    part = call(
        square_body, (sds((2 * (per + PACK), width), BF),), (part, *near), 0, after=(feats_token,)
    )[0]
    for bit in range(2, fine_bits):
        other = swap(part, "fine", bit)
        body = functools.partial(merge_body, bit=bit)
        part = call(body, (sds((2 * part.shape[0], width), BF),), (part, other), 0)[0]
    other = swap(part, "fine", 0)
    total_cells = cells * coarses
    scales = dict(edge_scale=float(total_cells * K) ** -0.5, cell_scale=float(total_cells) ** -0.5)
    grad_w1, grad_b, grad_wo, grad_up = call(
        functools.partial(weights_body, per=per, **scales),
        (
            sds((2 * width, width), F32), sds((1, width), F32), sds((width, width), F32), sds((width, width), F32),
        ),
        (part, other),
        0,
    )
    return grad_feats, grad_w1, grad_b.reshape(width), grad_wo, grad_up


def solution(mesh):
    both = ("coarse", "fine")
    return jax.shard_map(
        local,
        mesh=mesh,
        in_specs=(P(both, None), P(both, None), P(both), P("coarse"), P("coarse"), P(), P(), P(), P()),
        out_specs=(P(both, None), P(), P(), P(), P()),
        check_vma=False,
    )
```

time: 79.8 us -> 56.6 us (0.71)
  blocking collectives: 24.9 us -> 0 us
  waiting for transfers between devices: 15.4 us -> 21 us
  starting transfers between devices: 18.3 us -> 15.7 us
  local copies, waits for them, and re-layouts: 3.9 us -> 1.99 us
    all_to_all x2 -> x0, blocking collectives: 24.9 us -> none  [the longest x1 14.6 us: local(): recv = lax.all_to_all(send, 'coarse', 0, 0, tiled=True)]
    ppermute x6 -> x4, starting transfers between devices: 14.9 us -> 6.77 us  [the longest x3 6.07 us: send_sides(): return lax.ppermute(x, ('coarse', 'fine'), pairs)]
    ppermute x9 -> x15, starting transfers between devices: 3.31 us -> 8.91 us  [swap(): return lax.ppermute(x, axis, [(i, i ^ 1 << bit) for i in range(count)])]
    ppermute x9 -> x15, waiting for transfers between devices: 9.52 us -> 14.9 us  [swap(): return lax.ppermute(x, axis, [(i, i ^ 1 << bit) for i in range(count)])]
    unnamed x22 -> x16, local copies, waits for them, and re-layouts: 3.18 us -> 1.27 us
    pallas_call x12 -> x20, Pallas kernels: 15.9 us -> 16.2 us  [call(): pl.pallas_call(kernel, out_shape=outs, in_specs=specs, scratch_shapes=scr...]
    ppermute x6 -> x4, waiting for transfers between devices: 5.89 us -> 6.05 us  [the longest x3 6.05 us: send_sides(): return lax.ppermute(x, ('coarse', 'fine'), pairs)]
  transfers between devices with their start and end apart: 15 -> 19, of which waited for: 6 -> 12; matrix products, arithmetic and copies ran while one was open for 1% -> 1% of each run, Pallas kernels for 11% -> 22%
where the time goes in v2:
time: 56.6 us; the launch traced here: 56.4 us
  waiting for transfers between devices  21 us (37%)
  Pallas kernels  16.2 us (29%)
  starting transfers between devices  15.7 us (28%)
  local copies, waits for them, and re-layouts  1.99 us (4%)
  between operations  0.86 us (2%)
  other arithmetic  0.7 us (1%)
    pallas_call x20, Pallas kernels, call(): pl.pallas_call(kernel, out_shape=outs, in_specs=specs, scratch_shapes=scr...  16.2 us
    ppermute x15, waiting for transfers between devices, swap(): return lax.ppermute(x, axis, [(i, i ^ 1 << bit) for i in range(count)])  14.9 us
    ppermute x15, starting transfers between devices, swap(): return lax.ppermute(x, axis, [(i, i ^ 1 << bit) for i in range(count)])  8.91 us
    ppermute x3, starting transfers between devices, send_sides(): return lax.ppermute(x, ('coarse', 'fine'), pairs)  6.07 us
    ppermute x3, waiting for transfers between devices, send_sides(): return lax.ppermute(x, ('coarse', 'fine'), pairs)  6.05 us
    unnamed x16, local copies, waits for them, and re-layouts  1.27 us
  transfers between devices with their start and end apart: 19, of which 12 were waited for; matrix products, arithmetic and copies ran while one was open for 1% of the time, Pallas kernels for 22%

profile of v2, /device:TPU:0, one launch (start us, length us, event | category | flops | bytes accessed | tf_op | source)
XLA Modules:
  0.0 56.4 jit_solution(11649883698091310150)
XLA Ops:
  0.6 0.7 %negate_select_fusion = s32[2048]{0:T(1024)S(1)} fusion(s32[2048]{0:T(1024)} %param.11), kind=kLoop, calls=%fused_computation | loop fusion | flops 12288 | bytes 16384 | tf_op jit(solution)/shard_map/rem | solution.py:376
  1.3 1.2 %copy-done.4 = bf16[2048,256]{1,0:T(8,128)(2,1)S(1)} copy-done((bf16[2048,256]{1,0:T(8,128)(2,1)S(1)}, bf16[2048,256]{1,0:T(8,128)(2,1)}, u32[]{:S(2)}) %copy-start.4) | copy-done | bytes 1048600
  2.6 1.2 %shard_map.130 = (f32[512,256]{1,0:T(8,128)S(1)}, f32[512,256]{1,0:T(8,128)S(1)}) custom-call(s32[1,2048]{1,0:T(1,128)S(1)} %bitcast.8, bf16[2048,256]{1,0:T(8,128)(2,1)S(1)} %copy-done.4), custom_call_target="tpu_custom_call" | custom-call | flops 1073741824 | bytes 2105344 | tf_op jit(solution)/shard_map/pallas_call | solution.py:64
  3.8 0.5 collective-permute-start.2
  4.3 1.2 %shard_map.128 = (f32[512,256]{1,0:T(8,128)S(1)}, f32[512,256]{1,0:T(8,128)S(1)}) custom-call(s32[1,2048]{1,0:T(1,128)S(1)} %bitcast.9, bf16[2048,256]{1,0:T(8,128)(2,1)S(1)} %copy-done.5), custom_call_target="tpu_custom_call" | custom-call | flops 1073741824 | bytes 2105344 | tf_op jit(solution)/shard_map/pallas_call | solution.py:64
  6.0 3.0 %collective-permute-start.3 = (bf16[512,256]{1,0:T(8,128)(2,1)S(1)}, bf16[512,256]{1,0:T(8,128)(2,1)S(1)}, u32[]{:S(2)}, u32[]{:S(2)}) collective-permute-start(bf16[512,256]{1,0:T(8,128)(2,1)S(1)} %get-tuple-element.43.refs_0_), channel_id=1, source_target_pairs={{0,2},{1,3},{2,0},{3,1},{4,6},{5,7},{6,4},{7,5},{8,10},{9,11},{10,... | collective-permute-start | bytes 786440 | tf_op jit(solution)/shard_map/ppermute | solution.py:37
  9.3 1.2 %collective-permute-done.4.refs_1_ = bf16[128,256]{1,0:T(8,128)(2,1)S(1)} collective-permute-done((bf16[128,256]{1,0:T(8,128)(2,1)S(1)}, bf16[128,256]{1,0:T(8,128)(2,1)S(1)}, u32[]{:S(2)}, u32[]{:S(2)}) %collective-permute-start.4) | collective-permute-done | bytes 65568 | tf_op jit(solution)/shard_map/ppermute | solution.py:37
  10.6 2.3 %collective-permute-start.6 = (bf16[64,256]{1,0:T(8,128)(2,1)S(1)}, bf16[64,256]{1,0:T(8,128)(2,1)S(1)}, u32[]{:S(2)}, u32[]{:S(2)}) collective-permute-start(bf16[64,256]{1,0:T(8,128)(2,1)S(1)} %shard_map.133), channel_id=1, source_target_pairs={{0,6},{1,31},{2,4},{3,29},{4,10},{5,3},{6,8},{7,1},{8,14},{9,7},{1... | collective-permute-start | bytes 98312 | tf_op jit(solution)/shard_map/ppermute | solution.py:53
  12.8 1.5 %collective-permute-start.5 = (bf16[64,256]{1,0:T(8,128)(2,1)S(1)}, bf16[64,256]{1,0:T(8,128)(2,1)S(1)}, u32[]{:S(2)}, u32[]{:S(2)}) collective-permute-start(bf16[64,256]{1,0:T(8,128)(2,1)S(1)} %shard_map.133), channel_id=1, source_target_pairs={{0,4},{1,29},{2,6},{3,31},{4,8},{5,1},{6,10},{7,3},{8,12},{9,5},{1... | collective-permute-start | bytes 98312 | tf_op jit(solution)/shard_map/ppermute | solution.py:53
  14.4 3.7 %collective-permute-done.6.refs_1_ = bf16[64,256]{1,0:T(8,128)(2,1)S(1)} collective-permute-done((bf16[64,256]{1,0:T(8,128)(2,1)S(1)}, bf16[64,256]{1,0:T(8,128)(2,1)S(1)}, u32[]{:S(2)}, u32[]{:S(2)}) %collective-permute-start.6) | collective-permute-done | bytes 32800 | tf_op jit(solution)/shard_map/ppermute | solution.py:53
  18.1 1.4 %collective-permute-done.5.refs_0_ = bf16[64,256]{1,0:T(8,128)(2,1)S(1)} collective-permute-done((bf16[64,256]{1,0:T(8,128)(2,1)S(1)}, bf16[64,256]{1,0:T(8,128)(2,1)S(1)}, u32[]{:S(2)}, u32[]{:S(2)}) %collective-permute-start.5) | collective-permute-done | bytes 32800 | tf_op jit(solution)/shard_map/ppermute | solution.py:53
  20.1 0.5 reshape.27
  20.9 0.7 %collective-permute-start.1 = (bf16[512,256]{1,0:T(8,128)(2,1)S(1)}, bf16[512,256]{1,0:T(8,128)(2,1)S(1)}, u32[]{:S(2)}, u32[]{:S(2)}) collective-permute-start(bf16[512,256]{1,0:T(8,128)(2,1)S(1)} %get-tuple-element.39.refs_2_), channel_id=1, source_target_pairs={{0,2},{1,3},{2,0},{3,1},{4,6},{5,7},{6,4},{7,5},{8,10},{9,11},{10,... | collective-permute-start | bytes 786440 | tf_op jit(solution)/shard_map/ppermute | solution.py:37
  21.6 4.4 %shard_map.136 = (bf16[1152,256]{1,0:T(8,128)(2,1)S(1)}, f32[1024,256]{1,0:T(8,128)S(1)}, f32[4096,256]{1,0:T(8,128)S(1)}, bf16[4096,256]{1,0:T(8,128)(2,1)S(1)}, f32[8,128]{1,0:T(8,128)S(1)}) custom-call(bf16[512,256]{1,0:T(8,128)(2,1)S(1)} %shard_map.135.refs_0_, bf16[512,256]{1,0:T(8,128)(2,1)S(1)} %collective-permute-done.7.refs_1_, ...), custom_call_target="tpu_custom_call" | custom-call | flops 2952790016 | bytes 8802816 | tf_op jit(solution)/shard_map/pallas_call | solution.py:64
  26.0 3.2 %collective-permute-done.1.refs_1_ = bf16[512,256]{1,0:T(8,128)(2,1)S(1)} collective-permute-done((bf16[512,256]{1,0:T(8,128)(2,1)S(1)}, bf16[512,256]{1,0:T(8,128)(2,1)S(1)}, u32[]{:S(2)}, u32[]{:S(2)}) %collective-permute-start.1) | collective-permute-done | bytes 262176 | tf_op jit(solution)/shard_map/ppermute | solution.py:37
  29.3 1.5 %collective-permute-done.9.refs_1_ = bf16[512,256]{1,0:T(8,128)(2,1)S(1)} collective-permute-done((bf16[512,256]{1,0:T(8,128)(2,1)S(1)}, bf16[512,256]{1,0:T(8,128)(2,1)S(1)}, u32[]{:S(2)}, u32[]{:S(2)}) %collective-permute-start.9) | collective-permute-done | bytes 262176 | tf_op jit(solution)/shard_map/ppermute | solution.py:37
  30.8 1.5 %shard_map.138 = (bf16[4096,256]{1,0:T(8,128)(2,1)S(1)}, f32[1024,256]{1,0:T(8,128)S(1)}, bf16[1024,256]{1,0:T(8,128)(2,1)S(1)}, f32[128,256]{1,0:T(8,128)S(1)},...) custom-call(bf16[512,256]{1,0:T(8,128)(2,1)S(1)} %shard_map.137.refs_0_, ...), custom_call_target="tpu_custom_call" | custom-call | flops 536870912 | bytes 12599296 | tf_op jit(solution)/shard_map/pallas_call | solution.py:64
  32.4 0.6 %shard_map.141.refs_3_ = bf16[64,256]{1,0:T(8,128)(2,1)S(1)} custom-call(bf16[4096,256]{1,0:T(8,128)(2,1)S(1)} %get-tuple-element.49.refs_0_, s32[4,1024]{1,0:T(4,128)S(1)} %bitcast.5, bf16[512,256]{1,0:T(8,128)(2,1)S(1)} %copy-done), custom_call_target="tpu_custom_call" | custom-call | flops 268435456 | bytes 2408448 | tf_op jit(solution)/shard_map/pallas_call | solution.py:64
  33.0 2.2 %collective-permute-start.10 = (bf16[64,256]{1,0:T(8,128)(2,1)S(1)}, bf16[64,256]{1,0:T(8,128)(2,1)S(1)}, u32[]{:S(2)}, u32[]{:S(2)}) collective-permute-start(bf16[64,256]{1,0:T(8,128)(2,1)S(1)} %shard_map.141.refs_3_), channel_id=1, source_target_pairs={{0,4},{1,29},{2,6},{3,31},{4,8},{5,1},{6,10},{7,3},{8,12},{9,5},{1... | collective-permute-start | bytes 98312 | tf_op jit(solution)/shard_map/ppermute | solution.py:53
  35.3 2.1 %collective-permute-done.12.refs_1_ = bf16[144,256]{1,0:T(8,128)(2,1)S(1)} collective-permute-done((bf16[144,256]{1,0:T(8,128)(2,1)S(1)}, bf16[144,256]{1,0:T(8,128)(2,1)S(1)}, u32[]{:S(2)}, u32[]{:S(2)}) %collective-permute-start.12) | collective-permute-done | bytes 73760 | tf_op jit(solution)/shard_map/ppermute | solution.py:37
  37.5 1.5 %shard_map.139.refs_0_.refs_3_ = f32[512,256]{1,0:T(8,128)S(1)} custom-call(bf16[4096,256]{1,0:T(8,128)(2,1)S(1)} %get-tuple-element.49.refs_0_, s32[4,1024]{1,0:T(4,128)S(1)} %bitcast.6, f32[1024,256]{1,0:T(8,128)S(1)} %get-tuple-element.50.refs_2_, bf16[1024,256]{1,0:T(8,128)(2,1)S(1)} %get-tuple-element.51.refs_3_, bf16[512,256]{1,0:T(8,128)(2,1)S(1)} %copy-done), custom_call_target="tpu_custom_call" | custom-call | flops 1073741824 | bytes 4472832 | tf_op jit(solution)/shard_map/pallas_call | solution.py:64
  39.0 1.0 %collective-permute-done.10.refs_2_ = bf16[64,256]{1,0:T(8,128)(2,1)S(1)} collective-permute-done((bf16[64,256]{1,0:T(8,128)(2,1)S(1)}, bf16[64,256]{1,0:T(8,128)(2,1)S(1)}, u32[]{:S(2)}, u32[]{:S(2)}) %collective-permute-start.10) | collective-permute-done | bytes 32800 | tf_op jit(solution)/shard_map/ppermute | solution.py:53
  40.0 1.8 %collective-permute-done.13.refs_1_ = bf16[144,256]{1,0:T(8,128)(2,1)S(1)} collective-permute-done((bf16[144,256]{1,0:T(8,128)(2,1)S(1)}, bf16[144,256]{1,0:T(8,128)(2,1)S(1)}, u32[]{:S(2)}, u32[]{:S(2)}) %collective-permute-start.13) | collective-permute-done | bytes 73760 | tf_op jit(solution)/shard_map/ppermute | solution.py:37
  41.9 0.8 %collective-permute-start.14 = (bf16[144,256]{1,0:T(8,128)(2,1)S(1)}, bf16[144,256]{1,0:T(8,128)(2,1)S(1)}, u32[]{:S(2)}, u32[]{:S(2)}) collective-permute-start(bf16[144,256]{1,0:T(8,128)(2,1)S(1)} %get-tuple-element.60), channel_id=1, source_target_pairs={{0,16},{4,20},{8,24},{12,28},{16,0},{20,4},{24,8},{28,12},{1,17},{... | collective-permute-start | bytes 221192 | tf_op jit(solution)/shard_map/ppermute | solution.py:37
  42.7 1.5 %shard_map.140.refs_1_.refs_3_ = f32[512,256]{1,0:T(8,128)S(1)} custom-call(bf16[4096,256]{1,0:T(8,128)(2,1)S(1)} %get-tuple-element.49.refs_0_, s32[4,1024]{1,0:T(4,128)S(1)} %bitcast.7, f32[1024,256]{1,0:T(8,128)S(1)} %get-tuple-element.50.refs_2_, bf16[1024,256]{1,0:T(8,128)(2,1)S(1)} %get-tuple-element.51.refs_3_, bf16[512,256]{1,0:T(8,128)(2,1)S(1)} %copy-done), custom_call_target="tpu_custom_call" | custom-call | flops 1073741824 | bytes 4472832 | tf_op jit(solution)/shard_map/pallas_call | solution.py:64
  44.2 3.2 %collective-permute-done.14.refs_1_ = bf16[144,256]{1,0:T(8,128)(2,1)S(1)} collective-permute-done((bf16[144,256]{1,0:T(8,128)(2,1)S(1)}, bf16[144,256]{1,0:T(8,128)(2,1)S(1)}, u32[]{:S(2)}, u32[]{:S(2)}) %collective-permute-start.14) | collective-permute-done | bytes 73760 | tf_op jit(solution)/shard_map/ppermute | solution.py:37
  47.4 0.7 %collective-permute-start.17 = (bf16[144,256]{1,0:T(8,128)(2,1)S(1)}, bf16[144,256]{1,0:T(8,128)(2,1)S(1)}, u32[]{:S(2)}, u32[]{:S(2)}) collective-permute-start(bf16[144,256]{1,0:T(8,128)(2,1)S(1)} %shard_map.145.refs_0_), channel_id=1, source_target_pairs={{0,6},{1,7},{2,4},{3,5},{4,2},{5,3},{6,0},{7,1},{8,14},{9,15},{10,... | collective-permute-start | bytes 221192 | tf_op jit(solution)/shard_map/ppermute | solution.py:43
  48.2 1.2 %collective-permute-start.16 = (bf16[144,256]{1,0:T(8,128)(2,1)S(1)}, bf16[144,256]{1,0:T(8,128)(2,1)S(1)}, u32[]{:S(2)}, u32[]{:S(2)}) collective-permute-start(bf16[144,256]{1,0:T(8,128)(2,1)S(1)} %shard_map.145.refs_0_), channel_id=1, source_target_pairs={{0,2},{1,3},{2,0},{3,1},{4,6},{5,7},{6,4},{7,5},{8,10},{9,11},{10,... | collective-permute-start | bytes 221192 | tf_op jit(solution)/shard_map/ppermute | solution.py:37
  49.3 1.7 %collective-permute-start.15 = (bf16[144,256]{1,0:T(8,128)(2,1)S(1)}, bf16[144,256]{1,0:T(8,128)(2,1)S(1)}, u32[]{:S(2)}, u32[]{:S(2)}) collective-permute-start(bf16[144,256]{1,0:T(8,128)(2,1)S(1)} %shard_map.145.refs_0_), channel_id=1, source_target_pairs={{0,4},{4,0},{8,12},{12,8},{16,20},{20,16},{24,28},{28,24},{1,5},{5... | collective-permute-start | bytes 221192 | tf_op jit(solution)/shard_map/ppermute | solution.py:37
  51.0 2.5 %shard_map.142 = (bf16[2048,256]{1,0:T(8,128)(2,1)}, f32[8,128]{1,0:T(8,128)S(1)}) custom-call(f32[512,256]{1,0:T(8,128)S(1)} %shard_map.139.refs_0_.refs_3_, f32[512,256]{1,0:T(8,128)S(1)} %shard_map.140.refs_1_.refs_3_, bf16[64,256]{1,0:T(8,128)(2,1)S(1)} %collective-permute-done.10.refs_2_, bf16[64,256]{1,0:T(8,128)(2,1)S(1)} %collective-permute-done.11.refs_3_.refs_4_, ...), custom_call_target="tpu_custom_call" | custom-call | flops 1073741824 | bytes 3224064 | tf_op jit(solution)/shard_map/pallas_call | solution.py:64
  53.8 1.5 %collective-permute-done.18.refs_1_ = bf16[544,256]{1,0:T(8,128)(2,1)S(1)} collective-permute-done((bf16[544,256]{1,0:T(8,128)(2,1)S(1)}, bf16[544,256]{1,0:T(8,128)(2,1)S(1)}, u32[]{:S(2)}, u32[]{:S(2)}) %collective-permute-start.18) | collective-permute-done | bytes 278560 | tf_op jit(solution)/shard_map/ppermute | solution.py:37
  55.4 1.0 %shard_map.147 = (f32[512,256]{1,0:T(8,128)}, f32[1,256]{1,0:T(1,128)}, f32[256,256]{1,0:T(8,128)}, f32[256,256]{1,0:T(8,128)}) custom-call(bf16[544,256]{1,0:T(8,128)(2,1)S(1)} %shard_map.146.refs_0_, bf16[544,256]{1,0:T(8,128)(2,1)S(1)} %collective-permute-done.18.refs_1_), custom_call_target="tpu_custom_call" | custom-call | bytes 1606656 | tf_op jit(solution)/shard_map/pallas_call | solution.py:64
  (46 shorter events, 2.3 us)
Async XLA Ops:
  1.3 1.2 %copy-start.4 = (bf16[2048,256]{1,0:T(8,128)(2,1)S(1)}, bf16[2048,256]{1,0:T(8,128)(2,1)}, u32[]{:S(2)}) copy-start(bf16[2048,256]{1,0:T(8,128)(2,1)} %refs_1_.3) | copy-start | bytes 3145732
  2.6 1.8 %copy-start.5 = (bf16[2048,256]{1,0:T(8,128)(2,1)S(1)}, bf16[2048,256]{1,0:T(8,128)(2,1)}, u32[]{:S(2)}) copy-start(bf16[2048,256]{1,0:T(8,128)(2,1)} %refs_6_.3) | copy-start | bytes 3145732
  3.8 5.2 %copy-start.3 = (s32[128]{0:T(128)S(1)}, s32[128]{0:T(128)}, u32[]{:S(2)}) copy-start(s32[128]{0:T(128)} %param.12) | copy-start | bytes 1540
  3.8 2.1 %collective-permute-start.2 = (f32[512,256]{1,0:T(8,128)S(1)}, f32[512,256]{1,0:T(8,128)S(1)}, u32[]{:S(2)}, u32[]{:S(2)}) collective-permute-start(f32[512,256]{1,0:T(8,128)S(1)} %get-tuple-element.41), channel_id=1, source_target_pairs={{0,1},{1,0},{2,3},{3,2},{4,5},{5,4},{6,7},{7,6},{8,9},{9,8},{10,11... | collective-permute-start | bytes 1572872 | tf_op jit(solution)/shard_map/ppermute | solution.py:37
  5.6 14.5 %copy-start.7 = (bf16[256]{0:T(256)(128)(2,1)S(1)}, bf16[256]{0:T(256)(128)(2,1)}, u32[]{:S(2)}) copy-start(bf16[256]{0:T(256)(128)(2,1)} %param.15) | copy-start | bytes 1540
  5.6 14.5 %copy-start.6 = (s32[4096]{0:T(1024)S(1)}, s32[4096]{0:T(1024)}, u32[]{:S(2)}) copy-start(s32[4096]{0:T(1024)} %param.13) | copy-start | bytes 49156
  5.6 3.3 %collective-permute-start = (f32[512,256]{1,0:T(8,128)S(1)}, f32[512,256]{1,0:T(8,128)S(1)}, u32[]{:S(2)}, u32[]{:S(2)}) collective-permute-start(f32[512,256]{1,0:T(8,128)S(1)} %get-tuple-element.37), channel_id=1, source_target_pairs={{0,1},{1,0},{2,3},{3,2},{4,5},{5,4},{6,7},{7,6},{8,9},{9,8},{10,11... | collective-permute-start | bytes 1572872 | tf_op jit(solution)/shard_map/ppermute | solution.py:37
  5.9 15.6 %copy-start = (bf16[512,256]{1,0:T(8,128)(2,1)S(1)}, bf16[512,256]{1,0:T(8,128)(2,1)}, u32[]{:S(2)}) copy-start(bf16[512,256]{1,0:T(8,128)(2,1)} %refs_2_.1) | copy-start | bytes 786436
  6.0 13.5 %collective-permute-start.3 = (bf16[512,256]{1,0:T(8,128)(2,1)S(1)}, bf16[512,256]{1,0:T(8,128)(2,1)S(1)}, u32[]{:S(2)}, u32[]{:S(2)}) collective-permute-start(bf16[512,256]{1,0:T(8,128)(2,1)S(1)} %get-tuple-element.43.refs_0_), channel_id=1, source_target_pairs={{0,2},{1,3},{2,0},{3,1},{4,6},{5,7},{6,4},{7,5},{8,10},{9,11},{10,... | collective-permute-start | bytes 786440 | tf_op jit(solution)/shard_map/ppermute | solution.py:37
  9.2 1.3 %collective-permute-start.4 = (bf16[128,256]{1,0:T(8,128)(2,1)S(1)}, bf16[128,256]{1,0:T(8,128)(2,1)S(1)}, u32[]{:S(2)}, u32[]{:S(2)}) collective-permute-start(bf16[128,256]{1,0:T(8,128)(2,1)S(1)} %shard_map.132.refs_0_), channel_id=1, source_target_pairs={{0,1},{1,0},{2,3},{3,2},{4,5},{5,4},{6,7},{7,6},{8,9},{9,8},{10,11... | collective-permute-start | bytes 196616 | tf_op jit(solution)/shard_map/ppermute | solution.py:37
  10.6 7.5 %collective-permute-start.6 = (bf16[64,256]{1,0:T(8,128)(2,1)S(1)}, bf16[64,256]{1,0:T(8,128)(2,1)S(1)}, u32[]{:S(2)}, u32[]{:S(2)}) collective-permute-start(bf16[64,256]{1,0:T(8,128)(2,1)S(1)} %shard_map.133), channel_id=1, source_target_pairs={{0,6},{1,31},{2,4},{3,29},{4,10},{5,3},{6,8},{7,1},{8,14},{9,7},{1... | collective-permute-start | bytes 98312 | tf_op jit(solution)/shard_map/ppermute | solution.py:53
  12.8 6.6 %collective-permute-start.5 = (bf16[64,256]{1,0:T(8,128)(2,1)S(1)}, bf16[64,256]{1,0:T(8,128)(2,1)S(1)}, u32[]{:S(2)}, u32[]{:S(2)}) collective-permute-start(bf16[64,256]{1,0:T(8,128)(2,1)S(1)} %shard_map.133), channel_id=1, source_target_pairs={{0,4},{1,29},{2,6},{3,31},{4,8},{5,1},{6,10},{7,3},{8,12},{9,5},{1... | collective-permute-start | bytes 98312 | tf_op jit(solution)/shard_map/ppermute | solution.py:53
  19.5 2.0 %collective-permute-start.7 = (bf16[512,256]{1,0:T(8,128)(2,1)S(1)}, bf16[512,256]{1,0:T(8,128)(2,1)S(1)}, u32[]{:S(2)}, u32[]{:S(2)}) collective-permute-start(bf16[512,256]{1,0:T(8,128)(2,1)S(1)} %shard_map.135.refs_0_), channel_id=1, source_target_pairs={{0,1},{1,0},{2,3},{3,2},{4,5},{5,4},{6,7},{7,6},{8,9},{9,8},{10,11... | collective-permute-start | bytes 786440 | tf_op jit(solution)/shard_map/ppermute | solution.py:37
  19.6 2.0 %collective-permute-start.8 = (bf16[64,256]{1,0:T(8,128)(2,1)S(1)}, bf16[64,256]{1,0:T(8,128)(2,1)S(1)}, u32[]{:S(2)}, u32[]{:S(2)}) collective-permute-start(bf16[64,256]{1,0:T(8,128)(2,1)S(1)} %shard_map.134.refs_2_), channel_id=1, source_target_pairs={{0,1},{1,0},{2,3},{3,2},{4,5},{5,4},{6,7},{7,6},{8,9},{9,8},{10,11... | collective-permute-start | bytes 98312 | tf_op jit(solution)/shard_map/ppermute | solution.py:37
  20.9 8.3 %collective-permute-start.1 = (bf16[512,256]{1,0:T(8,128)(2,1)S(1)}, bf16[512,256]{1,0:T(8,128)(2,1)S(1)}, u32[]{:S(2)}, u32[]{:S(2)}) collective-permute-start(bf16[512,256]{1,0:T(8,128)(2,1)S(1)} %get-tuple-element.39.refs_2_), channel_id=1, source_target_pairs={{0,2},{1,3},{2,0},{3,1},{4,6},{5,7},{6,4},{7,5},{8,10},{9,11},{10,... | collective-permute-start | bytes 786440 | tf_op jit(solution)/shard_map/ppermute | solution.py:37
  21.6 9.3 %copy-start.1 = (bf16[256,256]{1,0:T(8,128)(2,1)S(1)}, bf16[256,256]{1,0:T(8,128)(2,1)}, u32[]{:S(2)}) copy-start(bf16[256,256]{1,0:T(8,128)(2,1)} %refs_6_.2) | copy-start | bytes 393220
  21.6 9.2 %copy-start.2 = (bf16[256,256]{1,0:T(8,128)(2,1)S(1)}, bf16[256,256]{1,0:T(8,128)(2,1)}, u32[]{:S(2)}) copy-start(bf16[256,256]{1,0:T(8,128)(2,1)} %refs_7_.1) | copy-start | bytes 393220
  29.2 1.6 %collective-permute-start.9 = (bf16[512,256]{1,0:T(8,128)(2,1)S(1)}, bf16[512,256]{1,0:T(8,128)(2,1)S(1)}, u32[]{:S(2)}, u32[]{:S(2)}) collective-permute-start(bf16[512,256]{1,0:T(8,128)(2,1)S(1)} %shard_map.137.refs_0_), channel_id=1, source_target_pairs={{0,1},{1,0},{2,3},{3,2},{4,5},{5,4},{6,7},{7,6},{8,9},{9,8},{10,11... | collective-permute-start | bytes 786440 | tf_op jit(solution)/shard_map/ppermute | solution.py:37
  32.3 5.0 %collective-permute-start.12 = (bf16[144,256]{1,0:T(8,128)(2,1)S(1)}, bf16[144,256]{1,0:T(8,128)(2,1)S(1)}, u32[]{:S(2)}, u32[]{:S(2)}) collective-permute-start(bf16[144,256]{1,0:T(8,128)(2,1)S(1)} %get-tuple-element.54), channel_id=1, source_target_pairs={{0,4},{4,0},{8,12},{12,8},{16,20},{20,16},{24,28},{28,24},{1,5},{5... | collective-permute-start | bytes 221192 | tf_op jit(solution)/shard_map/ppermute | solution.py:37
  33.0 7.0 %collective-permute-start.10 = (bf16[64,256]{1,0:T(8,128)(2,1)S(1)}, bf16[64,256]{1,0:T(8,128)(2,1)S(1)}, u32[]{:S(2)}, u32[]{:S(2)}) collective-permute-start(bf16[64,256]{1,0:T(8,128)(2,1)S(1)} %shard_map.141.refs_3_), channel_id=1, source_target_pairs={{0,4},{1,29},{2,6},{3,31},{4,8},{5,1},{6,10},{7,3},{8,12},{9,5},{1... | collective-permute-start | bytes 98312 | tf_op jit(solution)/shard_map/ppermute | solution.py:53
  37.4 4.4 %collective-permute-start.13 = (bf16[144,256]{1,0:T(8,128)(2,1)S(1)}, bf16[144,256]{1,0:T(8,128)(2,1)S(1)}, u32[]{:S(2)}, u32[]{:S(2)}) collective-permute-start(bf16[144,256]{1,0:T(8,128)(2,1)S(1)} %get-tuple-element.57), channel_id=1, source_target_pairs={{0,8},{4,12},{8,0},{12,4},{16,24},{20,28},{24,16},{28,20},{1,9},{5... | collective-permute-start | bytes 221192 | tf_op jit(solution)/shard_map/ppermute | solution.py:37
  40.0 4.2 %collective-permute-start.11 = (bf16[64,256]{1,0:T(8,128)(2,1)S(1)}, bf16[64,256]{1,0:T(8,128)(2,1)S(1)}, u32[]{:S(2)}, u32[]{:S(2)}) collective-permute-start(bf16[64,256]{1,0:T(8,128)(2,1)S(1)} %collective-permute-done.10.refs_2_), channel_id=1, source_target_pairs={{0,1},{1,0},{2,3},{3,2},{4,5},{5,4},{6,7},{7,6},{8,9},{9,8},{10,11... | collective-permute-start | bytes 98312 | tf_op jit(solution)/shard_map/ppermute | solution.py:37
  41.9 5.5 %collective-permute-start.14 = (bf16[144,256]{1,0:T(8,128)(2,1)S(1)}, bf16[144,256]{1,0:T(8,128)(2,1)S(1)}, u32[]{:S(2)}, u32[]{:S(2)}) collective-permute-start(bf16[144,256]{1,0:T(8,128)(2,1)S(1)} %get-tuple-element.60), channel_id=1, source_target_pairs={{0,16},{4,20},{8,24},{12,28},{16,0},{20,4},{24,8},{28,12},{1,17},{... | collective-permute-start | bytes 221192 | tf_op jit(solution)/shard_map/ppermute | solution.py:37
  47.4 6.1 %collective-permute-start.17 = (bf16[144,256]{1,0:T(8,128)(2,1)S(1)}, bf16[144,256]{1,0:T(8,128)(2,1)S(1)}, u32[]{:S(2)}, u32[]{:S(2)}) collective-permute-start(bf16[144,256]{1,0:T(8,128)(2,1)S(1)} %shard_map.145.refs_0_), channel_id=1, source_target_pairs={{0,6},{1,7},{2,4},{3,5},{4,2},{5,3},{6,0},{7,1},{8,14},{9,15},{10,... | collective-permute-start | bytes 221192 | tf_op jit(solution)/shard_map/ppermute | solution.py:43
  48.2 5.4 %collective-permute-start.16 = (bf16[144,256]{1,0:T(8,128)(2,1)S(1)}, bf16[144,256]{1,0:T(8,128)(2,1)S(1)}, u32[]{:S(2)}, u32[]{:S(2)}) collective-permute-start(bf16[144,256]{1,0:T(8,128)(2,1)S(1)} %shard_map.145.refs_0_), channel_id=1, source_target_pairs={{0,2},{1,3},{2,0},{3,1},{4,6},{5,7},{6,4},{7,5},{8,10},{9,11},{10,... | collective-permute-start | bytes 221192 | tf_op jit(solution)/shard_map/ppermute | solution.py:37
  49.3 4.4 %collective-permute-start.15 = (bf16[144,256]{1,0:T(8,128)(2,1)S(1)}, bf16[144,256]{1,0:T(8,128)(2,1)S(1)}, u32[]{:S(2)}, u32[]{:S(2)}) collective-permute-start(bf16[144,256]{1,0:T(8,128)(2,1)S(1)} %shard_map.145.refs_0_), channel_id=1, source_target_pairs={{0,4},{4,0},{8,12},{12,8},{16,20},{20,16},{24,28},{28,24},{1,5},{5... | collective-permute-start | bytes 221192 | tf_op jit(solution)/shard_map/ppermute | solution.py:37
  53.7 1.6 %collective-permute-start.18 = (bf16[544,256]{1,0:T(8,128)(2,1)S(1)}, bf16[544,256]{1,0:T(8,128)(2,1)S(1)}, u32[]{:S(2)}, u32[]{:S(2)}) collective-permute-start(bf16[544,256]{1,0:T(8,128)(2,1)S(1)} %shard_map.146.refs_0_), channel_id=1, source_target_pairs={{0,1},{1,0},{2,3},{3,2},{4,5},{5,4},{6,7},{7,6},{8,9},{9,8},{10,11... | collective-permute-start | bytes 835592 | tf_op jit(solution)/shard_map/ppermute | solution.py:37

commit v3 on v2

--- a/solution.py
+++ b/solution.py
@@ -43,10 +43,10 @@
     return lax.ppermute(x, ("coarse", "fine"), pairs)
 
 
-def send_sides(x, flip=0):
+def send_sides(x):
     owners, fines = lax.axis_size("coarse"), lax.axis_size("fine")
     pairs = [
-        (g * fines + f, (g + 1 - 2 * (f % 2)) % owners * fines + (f ^ (2 * flip)))
+        (g * fines + f, (g + 1 - 2 * (f % 2)) % owners * fines + f)
         for g in range(owners)
         for f in range(fines)
     ]
@@ -54,7 +54,7 @@
 
 
 def call(body, outs, args, flops, vmem=16, scratch=(), after=()):
-    moved = sum(a.size * a.dtype.itemsize for a in (*args, *outs))
+    moved = sum(a.size * a.dtype.itemsize for a in (*args, *outs)) if flops else 0
     count, waited = len(args), len(after)
 
     def kernel(*refs):
@@ -120,15 +120,8 @@
     out_ref[...] = own[at, :] + other[at, :]
 
 
-def halo_sum_body(*refs):
-    *parts, out_ref, slots = refs
-    chip = lax.axis_index("fine") // 2
-    for offset, part in enumerate(parts):
-        slots[chip ^ offset] = part[...].astype(F32)
-    total = slots[0]
-    for i in range(1, len(parts)):
-        total = total + slots[i]
-    out_ref[...] = total.astype(BF)
+def copy_body(x, out_ref):
+    out_ref[...] = x[...]
 
 
 def chip_body(keep, recv, part_ref, send_ref):
@@ -150,30 +143,35 @@
     return at_own, at_other
 
 
-def forward_body(
-    own_p, other_p, own_halo, other_halo, src_ref, w1_ref, b_ref,
-    ext, hid, slope, feats, token_ref,
-):
+def gather_body(own_p, other_p, src_ref, w1_ref, b_ref, table, base, feats, token_ref):
     half, width = own_p.shape
     cells = 2 * half
-    rows = ext.shape[0]
     at_own, at_other = core_order(half)
-    ext[at_own, :] = own_p[...]
-    ext[at_other, :] = other_p[...]
-    side = own_halo.shape[0]
-    core = lax.axis_index("fine") % 2
-    ext[pl.ds(pl.multiple_of(cells + core * side, PACK), side), :] = own_halo[...]
-    ext[pl.ds(pl.multiple_of(cells + (1 - core) * side, PACK), side), :] = other_halo[...]
+    table[at_own, :] = own_p[...]
+    table[at_other, :] = other_p[...]
     token_ref[...] = jnp.zeros_like(token_ref)
-    base = dot(ext[0:cells, :], w1_ref[0:width, :]) + b_ref[...].astype(F32)
+    base[...] = dot(table[...], w1_ref[0:width, :]) + b_ref[...].astype(F32)
     block = 512
     for k in range(K):
         for t in range(0, cells, block):
-            part = src_ref[k : k + 1, t : t + block]
             at = k * cells + t
-            feats[at : at + block, :] = dot(hot_rows(part, rows), ext[...]).astype(BF)
+            hot = hot_rows(src_ref[k : k + 1, t : t + block], cells)
+            feats[at : at + block, :] = dot(hot, table[...]).astype(BF)
+
+
+def forward_body(base, near, own_halo, other_halo, src_ref, w1_ref, hid, slope, feats, token_ref, halo):
+    token_ref[...] = jnp.zeros_like(token_ref)
+    cells, width = base.shape
+    side = own_halo.shape[0]
+    core = lax.axis_index("fine") % 2
+    halo[pl.ds(pl.multiple_of(core * side, PACK), side), :] = own_halo[...]
+    halo[pl.ds(pl.multiple_of((1 - core) * side, PACK), side), :] = other_halo[...]
+    for k in range(K):
         at = slice(k * cells, (k + 1) * cells)
-        pre = base + dot(feats[at, :], w1_ref[width : 2 * width, :])
+        far = dot(hot_rows(src_ref[k : k + 1, :] - cells, 2 * side), halo[...])
+        rows = (near[at, :].astype(F32) + far).astype(BF)
+        feats[at, :] = rows
+        pre = base[...] + dot(rows, w1_ref[width : 2 * width, :])
         sig = 0.5 * jnp.tanh(0.5 * pre) + 0.5
         hidden = pre * sig
         hid[...] = hidden if k == 0 else hid[...] + hidden
@@ -211,7 +209,7 @@
 
 
 def backward_body(
-    own_g, other_g, ext, feats, hid, slope, wo_ref, wu_ref,
+    own_g, other_g, table, feats, hid, slope, wo_ref, wu_ref,
     act, ga_ref, gn_ref, keep_ref, send_ref, bias_ref,
     gsum, total,
 ):
@@ -244,7 +242,7 @@
                 cols = slice(first, first + n)
                 if which == 0:
                     high, low = split(ga_ref[...])
-                    left = ext[0:cells, cols]
+                    left = table[:, cols]
                     out = dot_tn(left, high) + dot_tn(left, low)
                 elif which == 1:
                     out = dot_tn(feats[:, cols], act[...])
@@ -254,7 +252,7 @@
                 else:
                     high, low = split(hid[...])
                     agg = dot(high, wo_ref[:, cols]) + dot(low, wo_ref[:, cols])
-                    new = (ext[0:cells, cols].astype(F32) + agg).astype(BF)
+                    new = (table[:, cols].astype(F32) + agg).astype(BF)
                     out = dot_tn(new, gsum[...])
                 total[r : r + n, :] = out
 
@@ -370,7 +368,6 @@
     cells = edge_sources.shape[0] // K
     half = cells // 2
     side = halo_lists.shape[0] // 2
-    rows = cells + 2 * side
     fines, coarses = lax.axis_size("fine"), lax.axis_size("coarse")
     fine_bits, coarse_bits = bits_of(fines), bits_of(coarses)
     ids = lax.rem(cluster_ids, cells).reshape(1, nodes)
@@ -393,24 +390,34 @@
 
     part_p, send_p = pool(node_feats)
     part_g, send_g = pool(grad_out)
-    picked = call(pick_body, (sds((2 * side, width), BF),), (send_p, lists), 0, after=(send_g,))[0]
+    own_p = across(part_p, send_p, after=(src, bias))
+    other_p = swap(own_p, "fine", 0)
+    picked = call(pick_body, (sds((2 * side, width), BF),), (own_p, lists), 0)[0]
     sent = call(side_body, (sds((side, width), BF),), (picked, swap(picked, "fine", 0)), 0)[0]
-    own_halo = call(
-        halo_sum_body, (sds((side, width), BF),), [send_sides(sent, d) for d in range(fines // 2)], 0,
-        scratch=(pltpu.VMEM((fines // 2, side, width), F32),),
-    )[0]
-    own_p = across(part_p, send_p, after=(own_halo,))
+    own_halo = send_sides(sent)
+    table, base, near, gather_token = call(
+        gather_body,
+        (
+            sds((cells, width), BF), sds((cells, width), F32),
+            sds((K * cells, width), BF), sds((8, LANES), F32),
+        ),
+        (own_p, other_p, src, w_edge_in, bias),
+        0,
+        vmem=32,
+        after=(sent,),
+    )
+    own_halo = call(copy_body, (sds((side, width), BF),), (own_halo,), 0, after=(gather_token,))[0]
     other_halo = swap(own_halo, "fine", 0)
-    other_p = swap(own_p, "fine", 0)
-    ext, hid, slope, feats, forward_token = call(
+    hid, slope, feats, forward_token = call(
         forward_body,
         (
-            sds((rows, width), BF), sds((cells, width), F32),
-            sds((K * cells, width), F32), sds((K * cells, width), BF), sds((8, LANES), F32),
+            sds((cells, width), F32), sds((K * cells, width), F32),
+            sds((K * cells, width), BF), sds((8, LANES), F32),
         ),
-        (own_p, other_p, own_halo, other_halo, src, w_edge_in, bias),
-        2 * K * cells * width * (rows + width),
+        (base, near, own_halo, other_halo, src, w_edge_in),
+        0,
         vmem=32,
+        scratch=(pltpu.VMEM((2 * side, width), BF),),
     )
     own_g = across(part_g, send_g, after=(forward_token,))
     other_g = swap(own_g, "fine", 0)
@@ -422,7 +429,7 @@
             sds((K * cells, width), BF), sds((cells, width), F32), sds((cells, width), BF),
             sds((first, width), F32), sds((first + PACK, width), BF), sds((8, width), F32),
         ),
-        (own_g, other_g, ext, feats, hid, slope, w_edge_out, w_unpool),
+        (own_g, other_g, table, feats, hid, slope, w_edge_out, w_unpool),
         2 * K * cells * width * width,
         vmem=32,
         scratch=(pltpu.VMEM((cells, width), BF), pltpu.VMEM((per, width), F32)),

time: 56.6 us -> 57.5 us (1.016)
  local copies, waits for them, and re-layouts: 1.99 us -> 3.82 us
  starting transfers between devices: 15.7 us -> 14.5 us
  Pallas kernels: 16.2 us -> 17.1 us
  waiting for transfers between devices: 21 us -> 20.3 us
    ppermute x3 -> x2, waiting for transfers between devices: 6.05 us -> 3.31 us  [send_sides(): return lax.ppermute(x, ('coarse', 'fine'), pairs)]
    ppermute x3 -> x2, starting transfers between devices: 6.07 us -> 3.74 us  [send_sides(): return lax.ppermute(x, ('coarse', 'fine'), pairs)]
    ppermute x15, waiting for transfers between devices: 14.9 us -> 17 us  [swap(): return lax.ppermute(x, axis, [(i, i ^ 1 << bit) for i in range(count)])]
    reshape x2, local copies, waits for them, and re-layouts: 0.72 us -> 2.56 us  [local(): src = edge_sources.reshape(cells, K).T]
    ppermute x15, starting transfers between devices: 8.91 us -> 10.1 us  [swap(): return lax.ppermute(x, axis, [(i, i ^ 1 << bit) for i in range(count)])]
    pallas_call x20 -> x21, Pallas kernels: 16.2 us -> 17.1 us  [call(): pl.pallas_call(kernel, out_shape=outs, in_specs=specs, scratch_shapes=scr...]
  transfers between devices with their start and end apart: 19 -> 18, of which waited for: 12 -> 11; matrix products, arithmetic and copies ran while one was open for 1% -> 4% of each run, Pallas kernels for 22% -> 23%
where the time goes in v3:
time: 57.5 us; the launch traced here: 57.2 us
  waiting for transfers between devices  20.3 us (35%)
  Pallas kernels  17.1 us (30%)
  starting transfers between devices  14.5 us (25%)
  local copies, waits for them, and re-layouts  3.82 us (7%)
  between operations  0.82 us (1%)
  other arithmetic  0.7 us (1%)
    pallas_call x21, Pallas kernels, call(): pl.pallas_call(kernel, out_shape=outs, in_specs=specs, scratch_shapes=scr...  17.1 us
    ppermute x15, waiting for transfers between devices, swap(): return lax.ppermute(x, axis, [(i, i ^ 1 << bit) for i in range(count)])  17 us
    ppermute x15, starting transfers between devices, swap(): return lax.ppermute(x, axis, [(i, i ^ 1 << bit) for i in range(count)])  10.1 us
    ppermute x2, starting transfers between devices, send_sides(): return lax.ppermute(x, ('coarse', 'fine'), pairs)  3.74 us
    ppermute x2, waiting for transfers between devices, send_sides(): return lax.ppermute(x, ('coarse', 'fine'), pairs)  3.31 us
    reshape x2, local copies, waits for them, and re-layouts, local(): src = edge_sources.reshape(cells, K).T  2.56 us
    unnamed x16, local copies, waits for them, and re-layouts  1.26 us
  transfers between devices with their start and end apart: 18, of which 11 were waited for; matrix products, arithmetic and copies ran while one was open for 4% of the time, Pallas kernels for 23%

profile of v3, /device:TPU:0, one launch (start us, length us, event | category | flops | bytes accessed | tf_op | source)
XLA Modules:
  0.0 57.2 jit_solution(11439495609773335717)
XLA Ops:
  0.6 0.7 %negate_select_fusion = s32[2048]{0:T(1024)S(1)} fusion(s32[2048]{0:T(1024)} %param.11), kind=kLoop, calls=%fused_computation | loop fusion | flops 12288 | bytes 16384 | tf_op jit(solution)/shard_map/rem | solution.py:373
  1.3 1.2 %copy-done.4 = bf16[2048,256]{1,0:T(8,128)(2,1)S(1)} copy-done((bf16[2048,256]{1,0:T(8,128)(2,1)S(1)}, bf16[2048,256]{1,0:T(8,128)(2,1)}, u32[]{:S(2)}) %copy-start.4) | copy-done | bytes 1048600
  2.6 1.2 %shard_map.130 = (f32[512,256]{1,0:T(8,128)S(1)}, f32[512,256]{1,0:T(8,128)S(1)}) custom-call(s32[1,2048]{1,0:T(1,128)S(1)} %bitcast.10, bf16[2048,256]{1,0:T(8,128)(2,1)S(1)} %copy-done.4), custom_call_target="tpu_custom_call" | custom-call | flops 1073741824 | bytes 2105344 | tf_op jit(solution)/shard_map/pallas_call | solution.py:64
  3.8 0.5 collective-permute-start.2
  4.4 1.8 %shard_map.128 = (f32[512,256]{1,0:T(8,128)S(1)}, f32[512,256]{1,0:T(8,128)}) custom-call(s32[1,2048]{1,0:T(1,128)S(1)} %bitcast.11, bf16[2048,256]{1,0:T(8,128)(2,1)S(1)} %copy-done.5), custom_call_target="tpu_custom_call" | custom-call | flops 1073741824 | bytes 2105344 | tf_op jit(solution)/shard_map/pallas_call | solution.py:64
  6.3 3.0 %collective-permute-start.3 = (bf16[512,256]{1,0:T(8,128)(2,1)S(1)}, bf16[512,256]{1,0:T(8,128)(2,1)S(1)}, u32[]{:S(2)}, u32[]{:S(2)}) collective-permute-start(bf16[512,256]{1,0:T(8,128)(2,1)S(1)} %get-tuple-element.46), channel_id=1, source_target_pairs={{0,2},{1,3},{2,0},{3,1},{4,6},{5,7},{6,4},{7,5},{8,10},{9,11},{10,... | collective-permute-start | bytes 786440 | tf_op jit(solution)/shard_map/ppermute | solution.py:37
  9.4 1.3 %reshape.26 = s32[1024,4]{1,0:T(8,128)} reshape(s32[4096]{0:T(1024)S(1)} %copy-done.6) | data formatting | bytes 32768 | tf_op jit(solution)/shard_map/reshape | solution.py:375
  10.7 1.2 %copy.14 = s32[1024,4]{0,1:T(4,128)S(1)} copy(s32[1024,4]{1,0:T(8,128)} %reshape.26) | data formatting | bytes 32768 | tf_op jit(solution)/shard_map/reshape | solution.py:375
  11.9 3.9 %collective-permute-done.3.refs_1_ = bf16[512,256]{1,0:T(8,128)(2,1)S(1)} collective-permute-done((bf16[512,256]{1,0:T(8,128)(2,1)S(1)}, bf16[512,256]{1,0:T(8,128)(2,1)S(1)}, u32[]{:S(2)}, u32[]{:S(2)}) %collective-permute-start.3) | collective-permute-done | bytes 262176 | tf_op jit(solution)/shard_map/ppermute | solution.py:37
  16.0 1.8 %collective-permute-start.1 = (bf16[512,256]{1,0:T(8,128)(2,1)S(1)}, bf16[512,256]{1,0:T(8,128)(2,1)S(1)}, u32[]{:S(2)}, u32[]{:S(2)}) collective-permute-start(bf16[512,256]{1,0:T(8,128)(2,1)S(1)} %get-tuple-element.42), channel_id=1, source_target_pairs={{0,2},{1,3},{2,0},{3,1},{4,6},{5,7},{6,4},{7,5},{8,10},{9,11},{10,... | collective-permute-start | bytes 786440 | tf_op jit(solution)/shard_map/ppermute | solution.py:37
  18.4 1.1 %collective-permute-done.5.refs_1_ = bf16[128,256]{1,0:T(8,128)(2,1)S(1)} collective-permute-done((bf16[128,256]{1,0:T(8,128)(2,1)S(1)}, bf16[128,256]{1,0:T(8,128)(2,1)S(1)}, u32[]{:S(2)}, u32[]{:S(2)}) %collective-permute-start.5) | collective-permute-done | bytes 65568 | tf_op jit(solution)/shard_map/ppermute | solution.py:37
  19.4 1.5 %collective-permute-start.6 = (bf16[64,256]{1,0:T(8,128)(2,1)S(1)}, bf16[64,256]{1,0:T(8,128)(2,1)S(1)}, u32[]{:S(2)}, u32[]{:S(2)}) collective-permute-start(bf16[64,256]{1,0:T(8,128)(2,1)S(1)} %shard_map.134.refs_5_), channel_id=1, source_target_pairs={{0,4},{1,29},{2,6},{3,31},{4,8},{5,1},{6,10},{7,3},{8,12},{9,5},{1... | collective-permute-start | bytes 98312 | tf_op jit(solution)/shard_map/ppermute | solution.py:53
  20.9 2.5 %shard_map.135 = (bf16[1024,256]{1,0:T(8,128)(2,1)S(1)}, f32[1024,256]{1,0:T(8,128)S(1)}, bf16[4096,256]{1,0:T(8,128)(2,1)S(1)}, f32[8,128]{1,0:T(8,128)S(1)}) custom-call(bf16[512,256]{1,0:T(8,128)(2,1)S(1)} %shard_map.132.refs_0_, bf16[512,256]{1,0:T(8,128)(2,1)S(1)} %collective-permute-done.4.refs_1_, s32[4,1024]{1,0:T(4,128)S(1)} %bitcast.5, ...), custom_call_target="tpu_custom_call" | custom-call | tf_op jit(solution)/shard_map/pallas_call | solution.py:64
  23.5 2.6 %collective-permute-done.6.refs_0_ = bf16[64,256]{1,0:T(8,128)(2,1)S(1)} collective-permute-done((bf16[64,256]{1,0:T(8,128)(2,1)S(1)}, bf16[64,256]{1,0:T(8,128)(2,1)S(1)}, u32[]{:S(2)}, u32[]{:S(2)}) %collective-permute-start.6) | collective-permute-done | bytes 32800 | tf_op jit(solution)/shard_map/ppermute | solution.py:53
  26.5 0.9 %collective-permute-done.7.refs_3_ = bf16[64,256]{1,0:T(8,128)(2,1)S(1)} collective-permute-done((bf16[64,256]{1,0:T(8,128)(2,1)S(1)}, bf16[64,256]{1,0:T(8,128)(2,1)S(1)}, u32[]{:S(2)}, u32[]{:S(2)}) %collective-permute-start.7) | collective-permute-done | bytes 32800 | tf_op jit(solution)/shard_map/ppermute | solution.py:37
  27.4 2.2 %shard_map.137 = (f32[1024,256]{1,0:T(8,128)S(1)}, f32[4096,256]{1,0:T(8,128)S(1)}, bf16[4096,256]{1,0:T(8,128)(2,1)S(1)}, f32[8,128]{1,0:T(8,128)S(1)}) custom-call(f32[1024,256]{1,0:T(8,128)S(1)} %get-tuple-element.47.refs_0_, bf16[4096,256]{1,0:T(8,128)(2,1)S(1)} %get-tuple-element.48.refs_1_, bf16[64,256]{1,0:T(8,128)(2,1)S(1)} %shard_map.136.refs_2_, ...), custom_call_target="tpu_custom_call" | custom-call | tf_op jit(solution)/shard_map/pallas_call | solution.py:64
  30.0 1.2 %collective-permute-done.8.refs_1_ = bf16[512,256]{1,0:T(8,128)(2,1)S(1)} collective-permute-done((bf16[512,256]{1,0:T(8,128)(2,1)S(1)}, bf16[512,256]{1,0:T(8,128)(2,1)S(1)}, u32[]{:S(2)}, u32[]{:S(2)}) %collective-permute-start.8) | collective-permute-done | bytes 262176 | tf_op jit(solution)/shard_map/ppermute | solution.py:37
  31.2 1.5 %shard_map.139 = (bf16[4096,256]{1,0:T(8,128)(2,1)S(1)}, f32[1024,256]{1,0:T(8,128)S(1)}, bf16[1024,256]{1,0:T(8,128)(2,1)S(1)}, f32[128,256]{1,0:T(8,128)S(1)},...) custom-call(bf16[512,256]{1,0:T(8,128)(2,1)S(1)} %shard_map.138.refs_0_, ...), custom_call_target="tpu_custom_call" | custom-call | flops 536870912 | bytes 12533760 | tf_op jit(solution)/shard_map/pallas_call | solution.py:64
  32.8 0.6 %shard_map.142.refs_3_ = bf16[64,256]{1,0:T(8,128)(2,1)S(1)} custom-call(bf16[4096,256]{1,0:T(8,128)(2,1)S(1)} %get-tuple-element.55.refs_0_, s32[4,1024]{1,0:T(4,128)S(1)} %bitcast.7, bf16[512,256]{1,0:T(8,128)(2,1)S(1)} %copy-done), custom_call_target="tpu_custom_call" | custom-call | flops 268435456 | bytes 2408448 | tf_op jit(solution)/shard_map/pallas_call | solution.py:64
  33.4 2.2 %collective-permute-start.9 = (bf16[64,256]{1,0:T(8,128)(2,1)S(1)}, bf16[64,256]{1,0:T(8,128)(2,1)S(1)}, u32[]{:S(2)}, u32[]{:S(2)}) collective-permute-start(bf16[64,256]{1,0:T(8,128)(2,1)S(1)} %shard_map.142.refs_3_), channel_id=1, source_target_pairs={{0,4},{1,29},{2,6},{3,31},{4,8},{5,1},{6,10},{7,3},{8,12},{9,5},{1... | collective-permute-start | bytes 98312 | tf_op jit(solution)/shard_map/ppermute | solution.py:53
  35.7 2.3 %collective-permute-done.11.refs_1_ = bf16[144,256]{1,0:T(8,128)(2,1)S(1)} collective-permute-done((bf16[144,256]{1,0:T(8,128)(2,1)S(1)}, bf16[144,256]{1,0:T(8,128)(2,1)S(1)}, u32[]{:S(2)}, u32[]{:S(2)}) %collective-permute-start.11) | collective-permute-done | bytes 73760 | tf_op jit(solution)/shard_map/ppermute | solution.py:37
  38.1 1.5 %shard_map.140.refs_0_.refs_3_ = f32[512,256]{1,0:T(8,128)S(1)} custom-call(bf16[4096,256]{1,0:T(8,128)(2,1)S(1)} %get-tuple-element.55.refs_0_, s32[4,1024]{1,0:T(4,128)S(1)} %bitcast.8, f32[1024,256]{1,0:T(8,128)S(1)} %get-tuple-element.56.refs_2_, bf16[1024,256]{1,0:T(8,128)(2,1)S(1)} %get-tuple-element.57.refs_3_, bf16[512,256]{1,0:T(8,128)(2,1)S(1)} %copy-done), custom_call_target="tpu_custom_call" | custom-call | flops 1073741824 | bytes 4472832 | tf_op jit(solution)/shard_map/pallas_call | solution.py:64
  39.6 0.7 %collective-permute-done.9.refs_2_ = bf16[64,256]{1,0:T(8,128)(2,1)S(1)} collective-permute-done((bf16[64,256]{1,0:T(8,128)(2,1)S(1)}, bf16[64,256]{1,0:T(8,128)(2,1)S(1)}, u32[]{:S(2)}, u32[]{:S(2)}) %collective-permute-start.9) | collective-permute-done | bytes 32800 | tf_op jit(solution)/shard_map/ppermute | solution.py:53
  40.3 2.1 %collective-permute-done.12.refs_1_ = bf16[144,256]{1,0:T(8,128)(2,1)S(1)} collective-permute-done((bf16[144,256]{1,0:T(8,128)(2,1)S(1)}, bf16[144,256]{1,0:T(8,128)(2,1)S(1)}, u32[]{:S(2)}, u32[]{:S(2)}) %collective-permute-start.12) | collective-permute-done | bytes 73760 | tf_op jit(solution)/shard_map/ppermute | solution.py:37
  42.8 1.5 %shard_map.141.refs_1_.refs_3_ = f32[512,256]{1,0:T(8,128)S(1)} custom-call(bf16[4096,256]{1,0:T(8,128)(2,1)S(1)} %get-tuple-element.55.refs_0_, s32[4,1024]{1,0:T(4,128)S(1)} %bitcast.9, f32[1024,256]{1,0:T(8,128)S(1)} %get-tuple-element.56.refs_2_, bf16[1024,256]{1,0:T(8,128)(2,1)S(1)} %get-tuple-element.57.refs_3_, bf16[512,256]{1,0:T(8,128)(2,1)S(1)} %copy-done), custom_call_target="tpu_custom_call" | custom-call | flops 1073741824 | bytes 4472832 | tf_op jit(solution)/shard_map/pallas_call | solution.py:64
  44.3 3.7 %collective-permute-done.13.refs_1_ = bf16[144,256]{1,0:T(8,128)(2,1)S(1)} collective-permute-done((bf16[144,256]{1,0:T(8,128)(2,1)S(1)}, bf16[144,256]{1,0:T(8,128)(2,1)S(1)}, u32[]{:S(2)}, u32[]{:S(2)}) %collective-permute-start.13) | collective-permute-done | bytes 73760 | tf_op jit(solution)/shard_map/ppermute | solution.py:37
  48.0 0.6 %collective-permute-start.16 = (bf16[144,256]{1,0:T(8,128)(2,1)S(1)}, bf16[144,256]{1,0:T(8,128)(2,1)S(1)}, u32[]{:S(2)}, u32[]{:S(2)}) collective-permute-start(bf16[144,256]{1,0:T(8,128)(2,1)S(1)} %shard_map.146.refs_0_), channel_id=1, source_target_pairs={{0,6},{1,7},{2,4},{3,5},{4,2},{5,3},{6,0},{7,1},{8,14},{9,15},{10,... | collective-permute-start | bytes 221192 | tf_op jit(solution)/shard_map/ppermute | solution.py:43
  48.6 1.5 %collective-permute-start.15 = (bf16[144,256]{1,0:T(8,128)(2,1)S(1)}, bf16[144,256]{1,0:T(8,128)(2,1)S(1)}, u32[]{:S(2)}, u32[]{:S(2)}) collective-permute-start(bf16[144,256]{1,0:T(8,128)(2,1)S(1)} %shard_map.146.refs_0_), channel_id=1, source_target_pairs={{0,2},{1,3},{2,0},{3,1},{4,6},{5,7},{6,4},{7,5},{8,10},{9,11},{10,... | collective-permute-start | bytes 221192 | tf_op jit(solution)/shard_map/ppermute | solution.py:37
  50.1 1.4 %collective-permute-start.14 = (bf16[144,256]{1,0:T(8,128)(2,1)S(1)}, bf16[144,256]{1,0:T(8,128)(2,1)S(1)}, u32[]{:S(2)}, u32[]{:S(2)}) collective-permute-start(bf16[144,256]{1,0:T(8,128)(2,1)S(1)} %shard_map.146.refs_0_), channel_id=1, source_target_pairs={{0,4},{4,0},{8,12},{12,8},{16,20},{20,16},{24,28},{28,24},{1,5},{5... | collective-permute-start | bytes 221192 | tf_op jit(solution)/shard_map/ppermute | solution.py:37
  51.6 2.5 %shard_map.143 = (bf16[2048,256]{1,0:T(8,128)(2,1)}, f32[8,128]{1,0:T(8,128)S(1)}) custom-call(f32[512,256]{1,0:T(8,128)S(1)} %shard_map.140.refs_0_.refs_3_, f32[512,256]{1,0:T(8,128)S(1)} %shard_map.141.refs_1_.refs_3_, bf16[64,256]{1,0:T(8,128)(2,1)S(1)} %collective-permute-done.9.refs_2_, bf16[64,256]{1,0:T(8,128)(2,1)S(1)} %collective-permute-done.10.refs_3_.refs_4_, ...), custom_call_target="tpu_custom_call" | custom-call | flops 1073741824 | bytes 3224064 | tf_op jit(solution)/shard_map/pallas_call | solution.py:64
  54.6 1.5 %collective-permute-done.17.refs_1_ = bf16[544,256]{1,0:T(8,128)(2,1)S(1)} collective-permute-done((bf16[544,256]{1,0:T(8,128)(2,1)S(1)}, bf16[544,256]{1,0:T(8,128)(2,1)S(1)}, u32[]{:S(2)}, u32[]{:S(2)}) %collective-permute-start.17) | collective-permute-done | bytes 278560 | tf_op jit(solution)/shard_map/ppermute | solution.py:37
  56.2 1.0 %shard_map.148 = (f32[512,256]{1,0:T(8,128)}, f32[1,256]{1,0:T(1,128)}, f32[256,256]{1,0:T(8,128)}, f32[256,256]{1,0:T(8,128)}) custom-call(bf16[544,256]{1,0:T(8,128)(2,1)S(1)} %shard_map.147.refs_0_, bf16[544,256]{1,0:T(8,128)(2,1)S(1)} %collective-permute-done.17.refs_1_), custom_call_target="tpu_custom_call" | custom-call | tf_op jit(solution)/shard_map/pallas_call | solution.py:64
  (45 shorter events, 2.9 us)
Async XLA Ops:
  1.3 1.2 %copy-start.4 = (bf16[2048,256]{1,0:T(8,128)(2,1)S(1)}, bf16[2048,256]{1,0:T(8,128)(2,1)}, u32[]{:S(2)}) copy-start(bf16[2048,256]{1,0:T(8,128)(2,1)} %refs_1_.3) | copy-start | bytes 3145732
  2.6 1.8 %copy-start.5 = (bf16[2048,256]{1,0:T(8,128)(2,1)S(1)}, bf16[2048,256]{1,0:T(8,128)(2,1)}, u32[]{:S(2)}) copy-start(bf16[2048,256]{1,0:T(8,128)(2,1)} %refs_6_.3) | copy-start | bytes 3145732
  3.8 5.5 %copy-start.7 = (bf16[256]{0:T(256)(128)(2,1)S(1)}, bf16[256]{0:T(256)(128)(2,1)}, u32[]{:S(2)}) copy-start(bf16[256]{0:T(256)(128)(2,1)} %param.15) | copy-start | bytes 1540
  3.8 5.5 %copy-start.6 = (s32[4096]{0:T(1024)S(1)}, s32[4096]{0:T(1024)}, u32[]{:S(2)}) copy-start(s32[4096]{0:T(1024)} %param.13) | copy-start | bytes 49156
  3.8 2.4 %collective-permute-start.2 = (f32[512,256]{1,0:T(8,128)S(1)}, f32[512,256]{1,0:T(8,128)S(1)}, u32[]{:S(2)}, u32[]{:S(2)}) collective-permute-start(f32[512,256]{1,0:T(8,128)S(1)} %get-tuple-element.44), channel_id=1, source_target_pairs={{0,1},{1,0},{2,3},{3,2},{4,5},{5,4},{6,7},{7,6},{8,9},{9,8},{10,11... | collective-permute-start | bytes 1572872 | tf_op jit(solution)/shard_map/ppermute | solution.py:37
  6.2 9.8 %collective-permute-start = (f32[512,256]{1,0:T(8,128)}, f32[512,256]{1,0:T(8,128)S(1)}, u32[]{:S(2)}, u32[]{:S(2)}) collective-permute-start(f32[512,256]{1,0:T(8,128)} %get-tuple-element.40), channel_id=1, source_target_pairs={{0,1},{1,0},{2,3},{3,2},{4,5},{5,4},{6,7},{7,6},{8,9},{9,8},{10,11... | collective-permute-start | bytes 1572872 | tf_op jit(solution)/shard_map/ppermute | solution.py:37
  6.2 11.6 %copy-start.3 = (s32[128]{0:T(128)S(1)}, s32[128]{0:T(128)}, u32[]{:S(2)}) copy-start(s32[128]{0:T(128)} %param.12) | copy-start | bytes 1540
  6.3 14.6 %copy-start = (bf16[512,256]{1,0:T(8,128)(2,1)S(1)}, bf16[512,256]{1,0:T(8,128)(2,1)}, u32[]{:S(2)}) copy-start(bf16[512,256]{1,0:T(8,128)(2,1)} %refs_2_.1) | copy-start | bytes 786436
  6.3 9.5 %collective-permute-start.3 = (bf16[512,256]{1,0:T(8,128)(2,1)S(1)}, bf16[512,256]{1,0:T(8,128)(2,1)S(1)}, u32[]{:S(2)}, u32[]{:S(2)}) collective-permute-start(bf16[512,256]{1,0:T(8,128)(2,1)S(1)} %get-tuple-element.46), channel_id=1, source_target_pairs={{0,2},{1,3},{2,0},{3,1},{4,6},{5,7},{6,4},{7,5},{8,10},{9,11},{10,... | collective-permute-start | bytes 786440 | tf_op jit(solution)/shard_map/ppermute | solution.py:37
  15.9 5.0 %collective-permute-start.4 = (bf16[512,256]{1,0:T(8,128)(2,1)S(1)}, bf16[512,256]{1,0:T(8,128)(2,1)S(1)}, u32[]{:S(2)}, u32[]{:S(2)}) collective-permute-start(bf16[512,256]{1,0:T(8,128)(2,1)S(1)} %shard_map.132.refs_0_), channel_id=1, source_target_pairs={{0,1},{1,0},{2,3},{3,2},{4,5},{5,4},{6,7},{7,6},{8,9},{9,8},{10,11... | collective-permute-start | bytes 786440 | tf_op jit(solution)/shard_map/ppermute | solution.py:37
  16.0 13.5 %collective-permute-start.1 = (bf16[512,256]{1,0:T(8,128)(2,1)S(1)}, bf16[512,256]{1,0:T(8,128)(2,1)S(1)}, u32[]{:S(2)}, u32[]{:S(2)}) collective-permute-start(bf16[512,256]{1,0:T(8,128)(2,1)S(1)} %get-tuple-element.42), channel_id=1, source_target_pairs={{0,2},{1,3},{2,0},{3,1},{4,6},{5,7},{6,4},{7,5},{8,10},{9,11},{10,... | collective-permute-start | bytes 786440 | tf_op jit(solution)/shard_map/ppermute | solution.py:37
  18.1 1.3 %collective-permute-start.5 = (bf16[128,256]{1,0:T(8,128)(2,1)S(1)}, bf16[128,256]{1,0:T(8,128)(2,1)S(1)}, u32[]{:S(2)}, u32[]{:S(2)}) collective-permute-start(bf16[128,256]{1,0:T(8,128)(2,1)S(1)} %shard_map.133.refs_0_), channel_id=1, source_target_pairs={{0,1},{1,0},{2,3},{3,2},{4,5},{5,4},{6,7},{7,6},{8,9},{9,8},{10,11... | collective-permute-start | bytes 196616 | tf_op jit(solution)/shard_map/ppermute | solution.py:37
  19.4 6.6 %collective-permute-start.6 = (bf16[64,256]{1,0:T(8,128)(2,1)S(1)}, bf16[64,256]{1,0:T(8,128)(2,1)S(1)}, u32[]{:S(2)}, u32[]{:S(2)}) collective-permute-start(bf16[64,256]{1,0:T(8,128)(2,1)S(1)} %shard_map.134.refs_5_), channel_id=1, source_target_pairs={{0,4},{1,29},{2,6},{3,31},{4,8},{5,1},{6,10},{7,3},{8,12},{9,5},{1... | collective-permute-start | bytes 98312 | tf_op jit(solution)/shard_map/ppermute | solution.py:53
  26.0 1.3 %collective-permute-start.7 = (bf16[64,256]{1,0:T(8,128)(2,1)S(1)}, bf16[64,256]{1,0:T(8,128)(2,1)S(1)}, u32[]{:S(2)}, u32[]{:S(2)}) collective-permute-start(bf16[64,256]{1,0:T(8,128)(2,1)S(1)} %shard_map.136.refs_2_), channel_id=1, source_target_pairs={{0,1},{1,0},{2,3},{3,2},{4,5},{5,4},{6,7},{7,6},{8,9},{9,8},{10,11... | collective-permute-start | bytes 98312 | tf_op jit(solution)/shard_map/ppermute | solution.py:37
  27.4 3.9 %copy-start.1 = (bf16[256,256]{1,0:T(8,128)(2,1)S(1)}, bf16[256,256]{1,0:T(8,128)(2,1)}, u32[]{:S(2)}) copy-start(bf16[256,256]{1,0:T(8,128)(2,1)} %refs_6_.2) | copy-start | bytes 393220
  27.4 3.9 %copy-start.2 = (bf16[256,256]{1,0:T(8,128)(2,1)S(1)}, bf16[256,256]{1,0:T(8,128)(2,1)}, u32[]{:S(2)}) copy-start(bf16[256,256]{1,0:T(8,128)(2,1)} %refs_7_.1) | copy-start | bytes 393220
  29.6 1.6 %collective-permute-start.8 = (bf16[512,256]{1,0:T(8,128)(2,1)S(1)}, bf16[512,256]{1,0:T(8,128)(2,1)S(1)}, u32[]{:S(2)}, u32[]{:S(2)}) collective-permute-start(bf16[512,256]{1,0:T(8,128)(2,1)S(1)} %shard_map.138.refs_0_), channel_id=1, source_target_pairs={{0,1},{1,0},{2,3},{3,2},{4,5},{5,4},{6,7},{7,6},{8,9},{9,8},{10,11... | collective-permute-start | bytes 786440 | tf_op jit(solution)/shard_map/ppermute | solution.py:37
  32.7 5.2 %collective-permute-start.11 = (bf16[144,256]{1,0:T(8,128)(2,1)S(1)}, bf16[144,256]{1,0:T(8,128)(2,1)S(1)}, u32[]{:S(2)}, u32[]{:S(2)}) collective-permute-start(bf16[144,256]{1,0:T(8,128)(2,1)S(1)} %get-tuple-element.60), channel_id=1, source_target_pairs={{0,4},{4,0},{8,12},{12,8},{16,20},{20,16},{24,28},{28,24},{1,5},{5... | collective-permute-start | bytes 221192 | tf_op jit(solution)/shard_map/ppermute | solution.py:37
  33.4 6.9 %collective-permute-start.9 = (bf16[64,256]{1,0:T(8,128)(2,1)S(1)}, bf16[64,256]{1,0:T(8,128)(2,1)S(1)}, u32[]{:S(2)}, u32[]{:S(2)}) collective-permute-start(bf16[64,256]{1,0:T(8,128)(2,1)S(1)} %shard_map.142.refs_3_), channel_id=1, source_target_pairs={{0,4},{1,29},{2,6},{3,31},{4,8},{5,1},{6,10},{7,3},{8,12},{9,5},{1... | collective-permute-start | bytes 98312 | tf_op jit(solution)/shard_map/ppermute | solution.py:53
  38.0 4.4 %collective-permute-start.12 = (bf16[144,256]{1,0:T(8,128)(2,1)S(1)}, bf16[144,256]{1,0:T(8,128)(2,1)S(1)}, u32[]{:S(2)}, u32[]{:S(2)}) collective-permute-start(bf16[144,256]{1,0:T(8,128)(2,1)S(1)} %get-tuple-element.63), channel_id=1, source_target_pairs={{0,8},{4,12},{8,0},{12,4},{16,24},{20,28},{24,16},{28,20},{1,9},{5... | collective-permute-start | bytes 221192 | tf_op jit(solution)/shard_map/ppermute | solution.py:37
  40.3 4.0 %collective-permute-start.10 = (bf16[64,256]{1,0:T(8,128)(2,1)S(1)}, bf16[64,256]{1,0:T(8,128)(2,1)S(1)}, u32[]{:S(2)}, u32[]{:S(2)}) collective-permute-start(bf16[64,256]{1,0:T(8,128)(2,1)S(1)} %collective-permute-done.9.refs_2_), channel_id=1, source_target_pairs={{0,1},{1,0},{2,3},{3,2},{4,5},{5,4},{6,7},{7,6},{8,9},{9,8},{10,11... | collective-permute-start | bytes 98312 | tf_op jit(solution)/shard_map/ppermute | solution.py:37
  42.4 5.5 %collective-permute-start.13 = (bf16[144,256]{1,0:T(8,128)(2,1)S(1)}, bf16[144,256]{1,0:T(8,128)(2,1)S(1)}, u32[]{:S(2)}, u32[]{:S(2)}) collective-permute-start(bf16[144,256]{1,0:T(8,128)(2,1)S(1)} %get-tuple-element.66), channel_id=1, source_target_pairs={{0,16},{4,20},{8,24},{12,28},{16,0},{20,4},{24,8},{28,12},{1,17},{... | collective-permute-start | bytes 221192 | tf_op jit(solution)/shard_map/ppermute | solution.py:37
  48.0 6.1 %collective-permute-start.16 = (bf16[144,256]{1,0:T(8,128)(2,1)S(1)}, bf16[144,256]{1,0:T(8,128)(2,1)S(1)}, u32[]{:S(2)}, u32[]{:S(2)}) collective-permute-start(bf16[144,256]{1,0:T(8,128)(2,1)S(1)} %shard_map.146.refs_0_), channel_id=1, source_target_pairs={{0,6},{1,7},{2,4},{3,5},{4,2},{5,3},{6,0},{7,1},{8,14},{9,15},{10,... | collective-permute-start | bytes 221192 | tf_op jit(solution)/shard_map/ppermute | solution.py:43
  48.6 5.4 %collective-permute-start.15 = (bf16[144,256]{1,0:T(8,128)(2,1)S(1)}, bf16[144,256]{1,0:T(8,128)(2,1)S(1)}, u32[]{:S(2)}, u32[]{:S(2)}) collective-permute-start(bf16[144,256]{1,0:T(8,128)(2,1)S(1)} %shard_map.146.refs_0_), channel_id=1, source_target_pairs={{0,2},{1,3},{2,0},{3,1},{4,6},{5,7},{6,4},{7,5},{8,10},{9,11},{10,... | collective-permute-start | bytes 221192 | tf_op jit(solution)/shard_map/ppermute | solution.py:37
  50.1 4.4 %collective-permute-start.14 = (bf16[144,256]{1,0:T(8,128)(2,1)S(1)}, bf16[144,256]{1,0:T(8,128)(2,1)S(1)}, u32[]{:S(2)}, u32[]{:S(2)}) collective-permute-start(bf16[144,256]{1,0:T(8,128)(2,1)S(1)} %shard_map.146.refs_0_), channel_id=1, source_target_pairs={{0,4},{4,0},{8,12},{12,8},{16,20},{20,16},{24,28},{28,24},{1,5},{5... | collective-permute-start | bytes 221192 | tf_op jit(solution)/shard_map/ppermute | solution.py:37
  54.5 1.6 %collective-permute-start.17 = (bf16[544,256]{1,0:T(8,128)(2,1)S(1)}, bf16[544,256]{1,0:T(8,128)(2,1)S(1)}, u32[]{:S(2)}, u32[]{:S(2)}) collective-permute-start(bf16[544,256]{1,0:T(8,128)(2,1)S(1)} %shard_map.147.refs_0_), channel_id=1, source_target_pairs={{0,1},{1,0},{2,3},{3,2},{4,5},{5,4},{6,7},{7,6},{8,9},{9,8},{10,11... | collective-permute-start | bytes 835592 | tf_op jit(solution)/shard_map/ppermute | solution.py:37

commit v4 on v2

--- a/solution.py
+++ b/solution.py
@@ -54,7 +54,7 @@
 
 
 def call(body, outs, args, flops, vmem=16, scratch=(), after=()):
-    moved = sum(a.size * a.dtype.itemsize for a in (*args, *outs))
+    moved = sum(a.size * a.dtype.itemsize for a in (*args, *outs)) if flops else 0
     count, waited = len(args), len(after)
 
     def kernel(*refs):
@@ -150,33 +150,36 @@
     return at_own, at_other
 
 
-def forward_body(
-    own_p, other_p, own_halo, other_halo, src_ref, w1_ref, b_ref,
-    ext, hid, slope, feats, token_ref,
-):
+def extend_body(*refs):
+    *others, own_p, own_halo, other_halo, w1_ref, b_ref, ext, base = refs
     half, width = own_p.shape
     cells = 2 * half
-    rows = ext.shape[0]
-    at_own, at_other = core_order(half)
-    ext[at_own, :] = own_p[...]
-    ext[at_other, :] = other_p[...]
     side = own_halo.shape[0]
     core = lax.axis_index("fine") % 2
+    ext[pl.ds(pl.multiple_of(core * half, half), half), :] = own_p[...]
+    n = half // len(others)
+    for i, other in enumerate(others):
+        ext[pl.ds(pl.multiple_of((1 - core) * half + i * n, n), n), :] = other[...]
     ext[pl.ds(pl.multiple_of(cells + core * side, PACK), side), :] = own_halo[...]
     ext[pl.ds(pl.multiple_of(cells + (1 - core) * side, PACK), side), :] = other_halo[...]
+    base[...] = dot(ext[0:cells, :], w1_ref[0:width, :]) + b_ref[...].astype(F32)
+
+
+def forward_body(ext, base, src_ref, w1_ref, hid, slope, feats, token_ref, *, first):
+    cells, width = base.shape
+    rows = ext.shape[0]
     token_ref[...] = jnp.zeros_like(token_ref)
-    base = dot(ext[0:cells, :], w1_ref[0:width, :]) + b_ref[...].astype(F32)
     block = 512
-    for k in range(K):
+    for i in range(slope.shape[0] // cells):
         for t in range(0, cells, block):
-            part = src_ref[k : k + 1, t : t + block]
-            at = k * cells + t
+            part = src_ref[first + i : first + i + 1, t : t + block]
+            at = i * cells + t
             feats[at : at + block, :] = dot(hot_rows(part, rows), ext[...]).astype(BF)
-        at = slice(k * cells, (k + 1) * cells)
-        pre = base + dot(feats[at, :], w1_ref[width : 2 * width, :])
+        at = slice(i * cells, (i + 1) * cells)
+        pre = base[...] + dot(feats[at, :], w1_ref[width : 2 * width, :])
         sig = 0.5 * jnp.tanh(0.5 * pre) + 0.5
         hidden = pre * sig
-        hid[...] = hidden if k == 0 else hid[...] + hidden
+        hid[...] = hidden if i == 0 else hid[...] + hidden
         slope[at, :] = sig + hidden * (1.0 - sig)
 
 
@@ -211,7 +214,7 @@
 
 
 def backward_body(
-    own_g, other_g, ext, feats, hid, slope, wo_ref, wu_ref,
+    own_g, other_g, ext, hid_1, slope_1, feats_1, hid_2, slope_2, feats_2, wo_ref, wu_ref,
     act, ga_ref, gn_ref, keep_ref, send_ref, bias_ref,
     gsum, total,
 ):
@@ -227,7 +230,8 @@
     ga = jnp.zeros((cells, width), F32)
     for k in range(K):
         at = slice(k * cells, (k + 1) * cells)
-        part = (grad * slope[at, :]).astype(BF)
+        slope, here = (slope_1, k) if k < K // 2 else (slope_2, k - K // 2)
+        part = (grad * slope[here * cells : (here + 1) * cells, :]).astype(BF)
         act[at, :] = part
         ga = ga + part.astype(F32)
     ga_ref[...] = ga
@@ -247,12 +251,13 @@
                     left = ext[0:cells, cols]
                     out = dot_tn(left, high) + dot_tn(left, low)
                 elif which == 1:
-                    out = dot_tn(feats[:, cols], act[...])
+                    n_1 = feats_1.shape[0]
+                    out = dot_tn(feats_1[:, cols], act[0:n_1, :]) + dot_tn(feats_2[:, cols], act[n_1:, :])
                 elif which == 2:
-                    high, low = split(hid[:, cols])
+                    high, low = split(hid_1[:, cols] + hid_2[:, cols])
                     out = dot_tn(high, gn_ref[...]) + dot_tn(low, gn_ref[...])
                 else:
-                    high, low = split(hid[...])
+                    high, low = split(hid_1[...] + hid_2[...])
                     agg = dot(high, wo_ref[:, cols]) + dot(low, wo_ref[:, cols])
                     new = (ext[0:cells, cols].astype(F32) + agg).astype(BF)
                     out = dot_tn(new, gsum[...])
@@ -399,21 +404,31 @@
         halo_sum_body, (sds((side, width), BF),), [send_sides(sent, d) for d in range(fines // 2)], 0,
         scratch=(pltpu.VMEM((fines // 2, side, width), F32),),
     )[0]
-    own_p = across(part_p, send_p, after=(own_halo,))
+    own_p = across(part_p, send_p, after=(own_halo, src, bias))
     other_halo = swap(own_halo, "fine", 0)
-    other_p = swap(own_p, "fine", 0)
-    ext, hid, slope, feats, forward_token = call(
-        forward_body,
-        (
-            sds((rows, width), BF), sds((cells, width), F32),
-            sds((K * cells, width), F32), sds((K * cells, width), BF), sds((8, LANES), F32),
-        ),
-        (own_p, other_p, own_halo, other_halo, src, w_edge_in, bias),
-        2 * K * cells * width * (rows + width),
-        vmem=32,
+    others = [swap(x, "fine", 0) for x in (own_p[: half // 2], own_p[half // 2 :])]
+    ext, base = call(
+        extend_body,
+        (sds((rows, width), BF), sds((cells, width), F32)),
+        (*others, own_p, own_halo, other_halo, w_edge_in, bias),
+        0,
     )
-    own_g = across(part_g, send_g, after=(forward_token,))
+
+    def forward(first, after=()):
+        edges = K // 2 * cells
+        return call(
+            functools.partial(forward_body, first=first),
+            (sds((cells, width), F32), sds((edges, width), F32), sds((edges, width), BF), sds((8, LANES), F32)),
+            (ext, base, src, w_edge_in),
+            0,
+            vmem=32,
+            after=after,
+        )
+
+    *front, front_token = forward(0)
+    own_g = across(part_g, send_g, after=(front_token,))
     other_g = swap(own_g, "fine", 0)
+    *rear, _ = forward(K // 2, after=(own_g,))
     per = 4 * width // fines
     first = per // 2
     act, ga, gn, keep, send, bias_sum = call(
@@ -422,7 +437,7 @@
             sds((K * cells, width), BF), sds((cells, width), F32), sds((cells, width), BF),
             sds((first, width), F32), sds((first + PACK, width), BF), sds((8, width), F32),
         ),
-        (own_g, other_g, ext, feats, hid, slope, w_edge_out, w_unpool),
+        (own_g, other_g, ext, *front, *rear, w_edge_out, w_unpool),
         2 * K * cells * width * width,
         vmem=32,
         scratch=(pltpu.VMEM((cells, width), BF), pltpu.VMEM((per, width), F32)),

time: 56.6 us -> 55.4 us (0.979)
  waiting for transfers between devices: 21 us -> 16.4 us
  local copies, waits for them, and re-layouts: 1.99 us -> 3.84 us
  Pallas kernels: 16.2 us -> 17.1 us
    ppermute x15 -> x16, waiting for transfers between devices: 14.9 us -> 11.4 us  [swap(): return lax.ppermute(x, axis, [(i, i ^ 1 << bit) for i in range(count)])]
    reshape x2, local copies, waits for them, and re-layouts: 0.72 us -> 2.56 us  [local(): src = edge_sources.reshape(cells, K).T]
    ppermute x15 -> x16, starting transfers between devices: 8.91 us -> 10.7 us  [swap(): return lax.ppermute(x, axis, [(i, i ^ 1 << bit) for i in range(count)])]
    ppermute x3, starting transfers between devices: 6.07 us -> 4.61 us  [send_sides(): return lax.ppermute(x, ('coarse', 'fine'), pairs)]
    ppermute x3, waiting for transfers between devices: 6.05 us -> 4.98 us  [send_sides(): return lax.ppermute(x, ('coarse', 'fine'), pairs)]
    pallas_call x20 -> x22, Pallas kernels: 16.2 us -> 17.1 us  [call(): pl.pallas_call(kernel, out_shape=outs, in_specs=specs, scratch_shapes=scr...]
  transfers between devices with their start and end apart: 19 -> 20, of which waited for: 12 -> 11; matrix products, arithmetic and copies ran while one was open for 1% -> 5% of each run, Pallas kernels for 22% -> 24%
where the time goes in v4:
time: 55.4 us; the launch traced here: 55.1 us
  Pallas kernels  17.1 us (31%)
  waiting for transfers between devices  16.4 us (30%)
  starting transfers between devices  16.2 us (29%)
  local copies, waits for them, and re-layouts  3.84 us (7%)
  between operations  0.85 us (2%)
  other arithmetic  0.7 us (1%)
    pallas_call x22, Pallas kernels, call(): pl.pallas_call(kernel, out_shape=outs, in_specs=specs, scratch_shapes=scr...  17.1 us
    ppermute x16, waiting for transfers between devices, swap(): return lax.ppermute(x, axis, [(i, i ^ 1 << bit) for i in range(count)])  11.4 us
    ppermute x16, starting transfers between devices, swap(): return lax.ppermute(x, axis, [(i, i ^ 1 << bit) for i in range(count)])  10.7 us
    ppermute x3, waiting for transfers between devices, send_sides(): return lax.ppermute(x, ('coarse', 'fine'), pairs)  4.98 us
    ppermute x3, starting transfers between devices, send_sides(): return lax.ppermute(x, ('coarse', 'fine'), pairs)  4.61 us
    reshape x2, local copies, waits for them, and re-layouts, local(): src = edge_sources.reshape(cells, K).T  2.56 us
    unnamed x16, local copies, waits for them, and re-layouts  1.26 us
  transfers between devices with their start and end apart: 20, of which 11 were waited for; matrix products, arithmetic and copies ran while one was open for 5% of the time, Pallas kernels for 24%

profile of v4, /device:TPU:0, one launch (start us, length us, event | category | flops | bytes accessed | tf_op | source)
XLA Modules:
  0.0 55.1 jit_solution(7740539146766724183)
XLA Ops:
  0.6 0.7 %negate_select_fusion = s32[2048]{0:T(1024)S(1)} fusion(s32[2048]{0:T(1024)} %param.11), kind=kLoop, calls=%fused_computation | loop fusion | flops 12288 | bytes 16384 | tf_op jit(solution)/shard_map/rem | solution.py:381
  1.3 1.2 %copy-done.4 = bf16[2048,256]{1,0:T(8,128)(2,1)S(1)} copy-done((bf16[2048,256]{1,0:T(8,128)(2,1)S(1)}, bf16[2048,256]{1,0:T(8,128)(2,1)}, u32[]{:S(2)}) %copy-start.4) | copy-done | bytes 1048600
  2.6 1.2 %shard_map.130 = (f32[512,256]{1,0:T(8,128)S(1)}, f32[512,256]{1,0:T(8,128)S(1)}) custom-call(s32[1,2048]{1,0:T(1,128)S(1)} %bitcast.10, bf16[2048,256]{1,0:T(8,128)(2,1)S(1)} %copy-done.4), custom_call_target="tpu_custom_call" | custom-call | flops 1073741824 | bytes 2105344 | tf_op jit(solution)/shard_map/pallas_call | solution.py:64
  4.3 1.2 %shard_map.128 = (f32[512,256]{1,0:T(8,128)S(1)}, f32[512,256]{1,0:T(8,128)S(1)}) custom-call(s32[1,2048]{1,0:T(1,128)S(1)} %bitcast.11, bf16[2048,256]{1,0:T(8,128)(2,1)S(1)} %copy-done.5), custom_call_target="tpu_custom_call" | custom-call | flops 1073741824 | bytes 2105344 | tf_op jit(solution)/shard_map/pallas_call | solution.py:64
  5.9 3.0 %collective-permute-start.3 = (bf16[512,256]{1,0:T(8,128)(2,1)S(1)}, bf16[512,256]{1,0:T(8,128)(2,1)S(1)}, u32[]{:S(2)}, u32[]{:S(2)}) collective-permute-start(bf16[512,256]{1,0:T(8,128)(2,1)S(1)} %get-tuple-element.47.refs_0_), channel_id=1, source_target_pairs={{0,2},{1,3},{2,0},{3,1},{4,6},{5,7},{6,4},{7,5},{8,10},{9,11},{10,... | collective-permute-start | bytes 786440 | tf_op jit(solution)/shard_map/ppermute | solution.py:37
  9.3 1.2 %collective-permute-done.4.refs_1_ = bf16[128,256]{1,0:T(8,128)(2,1)S(1)} collective-permute-done((bf16[128,256]{1,0:T(8,128)(2,1)S(1)}, bf16[128,256]{1,0:T(8,128)(2,1)S(1)}, u32[]{:S(2)}, u32[]{:S(2)}) %collective-permute-start.4) | collective-permute-done | bytes 65568 | tf_op jit(solution)/shard_map/ppermute | solution.py:37
  10.5 2.3 %collective-permute-start.6 = (bf16[64,256]{1,0:T(8,128)(2,1)S(1)}, bf16[64,256]{1,0:T(8,128)(2,1)S(1)}, u32[]{:S(2)}, u32[]{:S(2)}) collective-permute-start(bf16[64,256]{1,0:T(8,128)(2,1)S(1)} %shard_map.133), channel_id=1, source_target_pairs={{0,6},{1,31},{2,4},{3,29},{4,10},{5,3},{6,8},{7,1},{8,14},{9,7},{1... | collective-permute-start | bytes 98312 | tf_op jit(solution)/shard_map/ppermute | solution.py:53
  12.8 1.5 %collective-permute-start.5 = (bf16[64,256]{1,0:T(8,128)(2,1)S(1)}, bf16[64,256]{1,0:T(8,128)(2,1)S(1)}, u32[]{:S(2)}, u32[]{:S(2)}) collective-permute-start(bf16[64,256]{1,0:T(8,128)(2,1)S(1)} %shard_map.133), channel_id=1, source_target_pairs={{0,4},{1,29},{2,6},{3,31},{4,8},{5,1},{6,10},{7,3},{8,12},{9,5},{1... | collective-permute-start | bytes 98312 | tf_op jit(solution)/shard_map/ppermute | solution.py:53
  14.4 1.3 %reshape.27 = s32[1024,4]{1,0:T(8,128)} reshape(s32[4096]{0:T(1024)S(1)} %copy-done.6) | data formatting | bytes 32768 | tf_op jit(solution)/shard_map/reshape | solution.py:383
  15.7 1.2 %copy.14 = s32[1024,4]{0,1:T(4,128)S(1)} copy(s32[1024,4]{1,0:T(8,128)} %reshape.27) | data formatting | bytes 32768 | tf_op jit(solution)/shard_map/reshape | solution.py:383
  17.0 0.7 %collective-permute-start.1 = (bf16[512,256]{1,0:T(8,128)(2,1)S(1)}, bf16[512,256]{1,0:T(8,128)(2,1)S(1)}, u32[]{:S(2)}, u32[]{:S(2)}) collective-permute-start(bf16[512,256]{1,0:T(8,128)(2,1)S(1)} %get-tuple-element.43.refs_2_), channel_id=1, source_target_pairs={{0,2},{1,3},{2,0},{3,1},{4,6},{5,7},{6,4},{7,5},{8,10},{9,11},{10,... | collective-permute-start | bytes 786440 | tf_op jit(solution)/shard_map/ppermute | solution.py:37
  18.1 1.4 %collective-permute-done.5.refs_0_ = bf16[64,256]{1,0:T(8,128)(2,1)S(1)} collective-permute-done((bf16[64,256]{1,0:T(8,128)(2,1)S(1)}, bf16[64,256]{1,0:T(8,128)(2,1)S(1)}, u32[]{:S(2)}, u32[]{:S(2)}) %collective-permute-start.5) | collective-permute-done | bytes 32800 | tf_op jit(solution)/shard_map/ppermute | solution.py:53
  20.2 1.1 %collective-permute-done.9.refs_4_ = bf16[64,256]{1,0:T(8,128)(2,1)S(1)} collective-permute-done((bf16[64,256]{1,0:T(8,128)(2,1)S(1)}, bf16[64,256]{1,0:T(8,128)(2,1)S(1)}, u32[]{:S(2)}, u32[]{:S(2)}) %collective-permute-start.9) | collective-permute-done | bytes 32800 | tf_op jit(solution)/shard_map/ppermute | solution.py:37
  21.7 2.2 %shard_map.137 = (f32[1024,256]{1,0:T(8,128)S(1)}, f32[2048,256]{1,0:T(8,128)S(1)}, bf16[2048,256]{1,0:T(8,128)(2,1)S(1)}, f32[8,128]{1,0:T(8,128)S(1)}) custom-call(bf16[1152,256]{1,0:T(8,128)(2,1)S(1)} %get-tuple-element.48.refs_0_.refs_2_, f32[1024,256]{1,0:T(8,128)S(1)} %get-tuple-element.49.refs_1_, s32[4,1024]{1,0:T(4,128)S(1)} %bitcast.5, ...), custom_call_target="tpu_custom_call" | custom-call | tf_op jit(solution)/shard_map/pallas_call | solution.py:64
  24.0 1.4 %collective-permute-done.1.refs_1_ = bf16[512,256]{1,0:T(8,128)(2,1)S(1)} collective-permute-done((bf16[512,256]{1,0:T(8,128)(2,1)S(1)}, bf16[512,256]{1,0:T(8,128)(2,1)S(1)}, u32[]{:S(2)}, u32[]{:S(2)}) %collective-permute-start.1) | collective-permute-done | bytes 262176 | tf_op jit(solution)/shard_map/ppermute | solution.py:37
  25.4 0.7 %collective-permute-start.10 = (bf16[512,256]{1,0:T(8,128)(2,1)S(1)}, bf16[512,256]{1,0:T(8,128)(2,1)S(1)}, u32[]{:S(2)}, u32[]{:S(2)}) collective-permute-start(bf16[512,256]{1,0:T(8,128)(2,1)S(1)} %shard_map.138.refs_4_.refs_0_), channel_id=1, source_target_pairs={{0,1},{1,0},{2,3},{3,2},{4,5},{5,4},{6,7},{7,6},{8,9},{9,8},{10,11... | collective-permute-start | bytes 786440 | tf_op jit(solution)/shard_map/ppermute | solution.py:37
  26.1 2.8 %shard_map.139 = (f32[1024,256]{1,0:T(8,128)S(1)}, f32[2048,256]{1,0:T(8,128)S(1)}, bf16[2048,256]{1,0:T(8,128)(2,1)S(1)}, f32[8,128]{1,0:T(8,128)}) custom-call(bf16[1152,256]{1,0:T(8,128)(2,1)S(1)} %get-tuple-element.48.refs_0_.refs_2_, f32[1024,256]{1,0:T(8,128)S(1)} %get-tuple-element.49.refs_1_, s32[4,1024]{1,0:T(4,128)S(1)} %bitcast.6, ...), custom_call_target="tpu_custom_call" | custom-call | tf_op jit(solution)/shard_map/pallas_call | solution.py:64
  28.9 1.5 %shard_map.140 = (bf16[4096,256]{1,0:T(8,128)(2,1)S(1)}, f32[1024,256]{1,0:T(8,128)S(1)}, bf16[1024,256]{1,0:T(8,128)(2,1)S(1)}, f32[128,256]{1,0:T(8,128)S(1)},...) custom-call(bf16[512,256]{1,0:T(8,128)(2,1)S(1)} %shard_map.138.refs_4_.refs_0_, ...), custom_call_target="tpu_custom_call" | custom-call | flops 536870912 | bytes 13647872 | tf_op jit(solution)/shard_map/pallas_call | solution.py:64
  30.4 1.6 %collective-permute-start.13 = (bf16[144,256]{1,0:T(8,128)(2,1)S(1)}, bf16[144,256]{1,0:T(8,128)(2,1)S(1)}, u32[]{:S(2)}, u32[]{:S(2)}) collective-permute-start(bf16[144,256]{1,0:T(8,128)(2,1)S(1)} %get-tuple-element.62), channel_id=1, source_target_pairs={{0,4},{4,0},{8,12},{12,8},{16,20},{20,16},{24,28},{28,24},{1,5},{5... | collective-permute-start | bytes 221192 | tf_op jit(solution)/shard_map/ppermute | solution.py:37
  32.6 0.8 %collective-permute-start.11 = (bf16[64,256]{1,0:T(8,128)(2,1)S(1)}, bf16[64,256]{1,0:T(8,128)(2,1)S(1)}, u32[]{:S(2)}, u32[]{:S(2)}) collective-permute-start(bf16[64,256]{1,0:T(8,128)(2,1)S(1)} %shard_map.143.refs_3_), channel_id=1, source_target_pairs={{0,4},{1,29},{2,6},{3,31},{4,8},{5,1},{6,10},{7,3},{8,12},{9,5},{1... | collective-permute-start | bytes 98312 | tf_op jit(solution)/shard_map/ppermute | solution.py:53
  33.4 1.6 %collective-permute-done.13.refs_1_ = bf16[144,256]{1,0:T(8,128)(2,1)S(1)} collective-permute-done((bf16[144,256]{1,0:T(8,128)(2,1)S(1)}, bf16[144,256]{1,0:T(8,128)(2,1)S(1)}, u32[]{:S(2)}, u32[]{:S(2)}) %collective-permute-start.13) | collective-permute-done | bytes 73760 | tf_op jit(solution)/shard_map/ppermute | solution.py:37
  35.1 1.5 %shard_map.141.refs_0_.refs_3_ = f32[512,256]{1,0:T(8,128)S(1)} custom-call(bf16[4096,256]{1,0:T(8,128)(2,1)S(1)} %get-tuple-element.57.refs_0_, s32[4,1024]{1,0:T(4,128)S(1)} %bitcast.8, f32[1024,256]{1,0:T(8,128)S(1)} %get-tuple-element.58.refs_2_, bf16[1024,256]{1,0:T(8,128)(2,1)S(1)} %get-tuple-element.59.refs_3_, bf16[512,256]{1,0:T(8,128)(2,1)S(1)} %copy-done), custom_call_target="tpu_custom_call" | custom-call | flops 1073741824 | bytes 4472832 | tf_op jit(solution)/shard_map/pallas_call | solution.py:64
  36.6 3.2 %collective-permute-done.11.refs_2_ = bf16[64,256]{1,0:T(8,128)(2,1)S(1)} collective-permute-done((bf16[64,256]{1,0:T(8,128)(2,1)S(1)}, bf16[64,256]{1,0:T(8,128)(2,1)S(1)}, u32[]{:S(2)}, u32[]{:S(2)}) %collective-permute-start.11) | collective-permute-done | bytes 32800 | tf_op jit(solution)/shard_map/ppermute | solution.py:53
  39.8 0.6 %collective-permute-start.15 = (bf16[144,256]{1,0:T(8,128)(2,1)S(1)}, bf16[144,256]{1,0:T(8,128)(2,1)S(1)}, u32[]{:S(2)}, u32[]{:S(2)}) collective-permute-start(bf16[144,256]{1,0:T(8,128)(2,1)S(1)} %get-tuple-element.68), channel_id=1, source_target_pairs={{0,16},{4,20},{8,24},{12,28},{16,0},{20,4},{24,8},{28,12},{1,17},{... | collective-permute-start | bytes 221192 | tf_op jit(solution)/shard_map/ppermute | solution.py:37
  40.5 1.5 %shard_map.142.refs_1_.refs_3_ = f32[512,256]{1,0:T(8,128)S(1)} custom-call(bf16[4096,256]{1,0:T(8,128)(2,1)S(1)} %get-tuple-element.57.refs_0_, s32[4,1024]{1,0:T(4,128)S(1)} %bitcast.9, f32[1024,256]{1,0:T(8,128)S(1)} %get-tuple-element.58.refs_2_, bf16[1024,256]{1,0:T(8,128)(2,1)S(1)} %get-tuple-element.59.refs_3_, bf16[512,256]{1,0:T(8,128)(2,1)S(1)} %copy-done), custom_call_target="tpu_custom_call" | custom-call | flops 1073741824 | bytes 4472832 | tf_op jit(solution)/shard_map/pallas_call | solution.py:64
  42.0 3.8 %collective-permute-done.15.refs_1_ = bf16[144,256]{1,0:T(8,128)(2,1)S(1)} collective-permute-done((bf16[144,256]{1,0:T(8,128)(2,1)S(1)}, bf16[144,256]{1,0:T(8,128)(2,1)S(1)}, u32[]{:S(2)}, u32[]{:S(2)}) %collective-permute-start.15) | collective-permute-done | bytes 73760 | tf_op jit(solution)/shard_map/ppermute | solution.py:37
  45.8 0.9 %collective-permute-start.18 = (bf16[144,256]{1,0:T(8,128)(2,1)S(1)}, bf16[144,256]{1,0:T(8,128)(2,1)S(1)}, u32[]{:S(2)}, u32[]{:S(2)}) collective-permute-start(bf16[144,256]{1,0:T(8,128)(2,1)S(1)} %shard_map.147.refs_0_), channel_id=1, source_target_pairs={{0,6},{1,7},{2,4},{3,5},{4,2},{5,3},{6,0},{7,1},{8,14},{9,15},{10,... | collective-permute-start | bytes 221192 | tf_op jit(solution)/shard_map/ppermute | solution.py:43
  46.8 1.3 %collective-permute-start.17 = (bf16[144,256]{1,0:T(8,128)(2,1)S(1)}, bf16[144,256]{1,0:T(8,128)(2,1)S(1)}, u32[]{:S(2)}, u32[]{:S(2)}) collective-permute-start(bf16[144,256]{1,0:T(8,128)(2,1)S(1)} %shard_map.147.refs_0_), channel_id=1, source_target_pairs={{0,2},{1,3},{2,0},{3,1},{4,6},{5,7},{6,4},{7,5},{8,10},{9,11},{10,... | collective-permute-start | bytes 221192 | tf_op jit(solution)/shard_map/ppermute | solution.py:37
  48.1 1.3 %collective-permute-start.16 = (bf16[144,256]{1,0:T(8,128)(2,1)S(1)}, bf16[144,256]{1,0:T(8,128)(2,1)S(1)}, u32[]{:S(2)}, u32[]{:S(2)}) collective-permute-start(bf16[144,256]{1,0:T(8,128)(2,1)S(1)} %shard_map.147.refs_0_), channel_id=1, source_target_pairs={{0,4},{4,0},{8,12},{12,8},{16,20},{20,16},{24,28},{28,24},{1,5},{5... | collective-permute-start | bytes 221192 | tf_op jit(solution)/shard_map/ppermute | solution.py:37
  49.4 2.5 %shard_map.144 = (bf16[2048,256]{1,0:T(8,128)(2,1)}, f32[8,128]{1,0:T(8,128)S(1)}) custom-call(f32[512,256]{1,0:T(8,128)S(1)} %shard_map.141.refs_0_.refs_3_, f32[512,256]{1,0:T(8,128)S(1)} %shard_map.142.refs_1_.refs_3_, bf16[64,256]{1,0:T(8,128)(2,1)S(1)} %collective-permute-done.11.refs_2_, bf16[64,256]{1,0:T(8,128)(2,1)S(1)} %collective-permute-done.12.refs_3_.refs_4_, ...), custom_call_target="tpu_custom_call" | custom-call | flops 1073741824 | bytes 3224064 | tf_op jit(solution)/shard_map/pallas_call | solution.py:64
  52.5 1.5 %collective-permute-done.19.refs_1_ = bf16[544,256]{1,0:T(8,128)(2,1)S(1)} collective-permute-done((bf16[544,256]{1,0:T(8,128)(2,1)S(1)}, bf16[544,256]{1,0:T(8,128)(2,1)S(1)}, u32[]{:S(2)}, u32[]{:S(2)}) %collective-permute-start.19) | collective-permute-done | bytes 278560 | tf_op jit(solution)/shard_map/ppermute | solution.py:37
  54.1 1.0 %shard_map.149 = (f32[512,256]{1,0:T(8,128)}, f32[1,256]{1,0:T(1,128)}, f32[256,256]{1,0:T(8,128)}, f32[256,256]{1,0:T(8,128)}) custom-call(bf16[544,256]{1,0:T(8,128)(2,1)S(1)} %shard_map.148.refs_0_, bf16[544,256]{1,0:T(8,128)(2,1)S(1)} %collective-permute-done.19.refs_1_), custom_call_target="tpu_custom_call" | custom-call | tf_op jit(solution)/shard_map/pallas_call | solution.py:64
  (51 shorter events, 4.3 us)
Async XLA Ops:
  1.3 1.2 %copy-start.4 = (bf16[2048,256]{1,0:T(8,128)(2,1)S(1)}, bf16[2048,256]{1,0:T(8,128)(2,1)}, u32[]{:S(2)}) copy-start(bf16[2048,256]{1,0:T(8,128)(2,1)} %refs_1_.3) | copy-start | bytes 3145732
  2.6 1.8 %copy-start.5 = (bf16[2048,256]{1,0:T(8,128)(2,1)S(1)}, bf16[2048,256]{1,0:T(8,128)(2,1)}, u32[]{:S(2)}) copy-start(bf16[2048,256]{1,0:T(8,128)(2,1)} %refs_6_.1) | copy-start | bytes 3145732
  3.8 5.2 %copy-start.3 = (s32[128]{0:T(128)S(1)}, s32[128]{0:T(128)}, u32[]{:S(2)}) copy-start(s32[128]{0:T(128)} %param.12) | copy-start | bytes 1540
  3.8 2.1 %collective-permute-start.2 = (f32[512,256]{1,0:T(8,128)S(1)}, f32[512,256]{1,0:T(8,128)S(1)}, u32[]{:S(2)}, u32[]{:S(2)}) collective-permute-start(f32[512,256]{1,0:T(8,128)S(1)} %get-tuple-element.45), channel_id=1, source_target_pairs={{0,1},{1,0},{2,3},{3,2},{4,5},{5,4},{6,7},{7,6},{8,9},{9,8},{10,11... | collective-permute-start | bytes 1572872 | tf_op jit(solution)/shard_map/ppermute | solution.py:37
  5.6 8.8 %copy-start.7 = (bf16[256]{0:T(256)(128)(2,1)S(1)}, bf16[256]{0:T(256)(128)(2,1)}, u32[]{:S(2)}) copy-start(bf16[256]{0:T(256)(128)(2,1)} %param.15) | copy-start | bytes 1540
  5.6 8.8 %copy-start.6 = (s32[4096]{0:T(1024)S(1)}, s32[4096]{0:T(1024)}, u32[]{:S(2)}) copy-start(s32[4096]{0:T(1024)} %param.13) | copy-start | bytes 49156
  5.6 3.3 %collective-permute-start = (f32[512,256]{1,0:T(8,128)S(1)}, f32[512,256]{1,0:T(8,128)S(1)}, u32[]{:S(2)}, u32[]{:S(2)}) collective-permute-start(f32[512,256]{1,0:T(8,128)S(1)} %get-tuple-element.41), channel_id=1, source_target_pairs={{0,1},{1,0},{2,3},{3,2},{4,5},{5,4},{6,7},{7,6},{8,9},{9,8},{10,11... | collective-permute-start | bytes 1572872 | tf_op jit(solution)/shard_map/ppermute | solution.py:37
  5.9 13.5 %collective-permute-start.3 = (bf16[512,256]{1,0:T(8,128)(2,1)S(1)}, bf16[512,256]{1,0:T(8,128)(2,1)S(1)}, u32[]{:S(2)}, u32[]{:S(2)}) collective-permute-start(bf16[512,256]{1,0:T(8,128)(2,1)S(1)} %get-tuple-element.47.refs_0_), channel_id=1, source_target_pairs={{0,2},{1,3},{2,0},{3,1},{4,6},{5,7},{6,4},{7,5},{8,10},{9,11},{10,... | collective-permute-start | bytes 786440 | tf_op jit(solution)/shard_map/ppermute | solution.py:37
  8.9 12.5 %copy-start = (bf16[512,256]{1,0:T(8,128)(2,1)S(1)}, bf16[512,256]{1,0:T(8,128)(2,1)}, u32[]{:S(2)}) copy-start(bf16[512,256]{1,0:T(8,128)(2,1)} %refs_2_.1) | copy-start | bytes 786436
  9.2 1.3 %collective-permute-start.4 = (bf16[128,256]{1,0:T(8,128)(2,1)S(1)}, bf16[128,256]{1,0:T(8,128)(2,1)S(1)}, u32[]{:S(2)}, u32[]{:S(2)}) collective-permute-start(bf16[128,256]{1,0:T(8,128)(2,1)S(1)} %shard_map.132.refs_0_), channel_id=1, source_target_pairs={{0,1},{1,0},{2,3},{3,2},{4,5},{5,4},{6,7},{7,6},{8,9},{9,8},{10,11... | collective-permute-start | bytes 196616 | tf_op jit(solution)/shard_map/ppermute | solution.py:37
  10.5 7.5 %collective-permute-start.6 = (bf16[64,256]{1,0:T(8,128)(2,1)S(1)}, bf16[64,256]{1,0:T(8,128)(2,1)S(1)}, u32[]{:S(2)}, u32[]{:S(2)}) collective-permute-start(bf16[64,256]{1,0:T(8,128)(2,1)S(1)} %shard_map.133), channel_id=1, source_target_pairs={{0,6},{1,31},{2,4},{3,29},{4,10},{5,3},{6,8},{7,1},{8,14},{9,7},{1... | collective-permute-start | bytes 98312 | tf_op jit(solution)/shard_map/ppermute | solution.py:53
  12.8 6.6 %collective-permute-start.5 = (bf16[64,256]{1,0:T(8,128)(2,1)S(1)}, bf16[64,256]{1,0:T(8,128)(2,1)S(1)}, u32[]{:S(2)}, u32[]{:S(2)}) collective-permute-start(bf16[64,256]{1,0:T(8,128)(2,1)S(1)} %shard_map.133), channel_id=1, source_target_pairs={{0,4},{1,29},{2,6},{3,31},{4,8},{5,1},{6,10},{7,3},{8,12},{9,5},{1... | collective-permute-start | bytes 98312 | tf_op jit(solution)/shard_map/ppermute | solution.py:53
  17.0 8.4 %collective-permute-start.1 = (bf16[512,256]{1,0:T(8,128)(2,1)S(1)}, bf16[512,256]{1,0:T(8,128)(2,1)S(1)}, u32[]{:S(2)}, u32[]{:S(2)}) collective-permute-start(bf16[512,256]{1,0:T(8,128)(2,1)S(1)} %get-tuple-element.43.refs_2_), channel_id=1, source_target_pairs={{0,2},{1,3},{2,0},{3,1},{4,6},{5,7},{6,4},{7,5},{8,10},{9,11},{10,... | collective-permute-start | bytes 786440 | tf_op jit(solution)/shard_map/ppermute | solution.py:37
  19.6 1.8 %collective-permute-start.8 = (bf16[256,256]{1,0:T(8,128)(2,1)S(1)}, bf16[256,256]{1,0:T(8,128)(2,1)S(1)}, u32[]{:S(2)}, u32[]{:S(2)}) collective-permute-start(bf16[256,256]{1,0:T(8,128)(2,1)S(1)} %get-tuple-element.75), channel_id=1, source_target_pairs={{0,1},{1,0},{2,3},{3,2},{4,5},{5,4},{6,7},{7,6},{8,9},{9,8},{10,11... | collective-permute-start | bytes 393224 | tf_op jit(solution)/shard_map/ppermute | solution.py:37
  19.7 1.7 %collective-permute-start.7 = (bf16[256,256]{1,0:T(8,128)(2,1)S(1)}, bf16[256,256]{1,0:T(8,128)(2,1)S(1)}, u32[]{:S(2)}, u32[]{:S(2)}) collective-permute-start(bf16[256,256]{1,0:T(8,128)(2,1)S(1)} %get-tuple-element.76), channel_id=1, source_target_pairs={{0,1},{1,0},{2,3},{3,2},{4,5},{5,4},{6,7},{7,6},{8,9},{9,8},{10,11... | collective-permute-start | bytes 393224 | tf_op jit(solution)/shard_map/ppermute | solution.py:37
  20.1 1.2 %collective-permute-start.9 = (bf16[64,256]{1,0:T(8,128)(2,1)S(1)}, bf16[64,256]{1,0:T(8,128)(2,1)S(1)}, u32[]{:S(2)}, u32[]{:S(2)}) collective-permute-start(bf16[64,256]{1,0:T(8,128)(2,1)S(1)} %shard_map.134.refs_2_.refs_3_), channel_id=1, source_target_pairs={{0,1},{1,0},{2,3},{3,2},{4,5},{5,4},{6,7},{7,6},{8,9},{9,8},{10,11... | collective-permute-start | bytes 98312 | tf_op jit(solution)/shard_map/ppermute | solution.py:37
  23.9 5.0 %copy-start.1 = (bf16[256,256]{1,0:T(8,128)(2,1)S(1)}, bf16[256,256]{1,0:T(8,128)(2,1)}, u32[]{:S(2)}) copy-start(bf16[256,256]{1,0:T(8,128)(2,1)} %refs_9_.1) | copy-start | bytes 393220
  23.9 4.9 %copy-start.2 = (bf16[256,256]{1,0:T(8,128)(2,1)S(1)}, bf16[256,256]{1,0:T(8,128)(2,1)}, u32[]{:S(2)}) copy-start(bf16[256,256]{1,0:T(8,128)(2,1)} %refs_10_.1) | copy-start | bytes 393220
  25.4 3.5 %collective-permute-start.10 = (bf16[512,256]{1,0:T(8,128)(2,1)S(1)}, bf16[512,256]{1,0:T(8,128)(2,1)S(1)}, u32[]{:S(2)}, u32[]{:S(2)}) collective-permute-start(bf16[512,256]{1,0:T(8,128)(2,1)S(1)} %shard_map.138.refs_4_.refs_0_), channel_id=1, source_target_pairs={{0,1},{1,0},{2,3},{3,2},{4,5},{5,4},{6,7},{7,6},{8,9},{9,8},{10,11... | collective-permute-start | bytes 786440 | tf_op jit(solution)/shard_map/ppermute | solution.py:37
  30.4 4.5 %collective-permute-start.13 = (bf16[144,256]{1,0:T(8,128)(2,1)S(1)}, bf16[144,256]{1,0:T(8,128)(2,1)S(1)}, u32[]{:S(2)}, u32[]{:S(2)}) collective-permute-start(bf16[144,256]{1,0:T(8,128)(2,1)S(1)} %get-tuple-element.62), channel_id=1, source_target_pairs={{0,4},{4,0},{8,12},{12,8},{16,20},{20,16},{24,28},{28,24},{1,5},{5... | collective-permute-start | bytes 221192 | tf_op jit(solution)/shard_map/ppermute | solution.py:37
  32.6 7.2 %collective-permute-start.11 = (bf16[64,256]{1,0:T(8,128)(2,1)S(1)}, bf16[64,256]{1,0:T(8,128)(2,1)S(1)}, u32[]{:S(2)}, u32[]{:S(2)}) collective-permute-start(bf16[64,256]{1,0:T(8,128)(2,1)S(1)} %shard_map.143.refs_3_), channel_id=1, source_target_pairs={{0,4},{1,29},{2,6},{3,31},{4,8},{5,1},{6,10},{7,3},{8,12},{9,5},{1... | collective-permute-start | bytes 98312 | tf_op jit(solution)/shard_map/ppermute | solution.py:53
  35.0 4.8 %collective-permute-start.14 = (bf16[144,256]{1,0:T(8,128)(2,1)S(1)}, bf16[144,256]{1,0:T(8,128)(2,1)S(1)}, u32[]{:S(2)}, u32[]{:S(2)}) collective-permute-start(bf16[144,256]{1,0:T(8,128)(2,1)S(1)} %get-tuple-element.65), channel_id=1, source_target_pairs={{0,8},{4,12},{8,0},{12,4},{16,24},{20,28},{24,16},{28,20},{1,9},{5... | collective-permute-start | bytes 221192 | tf_op jit(solution)/shard_map/ppermute | solution.py:37
  39.8 2.2 %collective-permute-start.12 = (bf16[64,256]{1,0:T(8,128)(2,1)S(1)}, bf16[64,256]{1,0:T(8,128)(2,1)S(1)}, u32[]{:S(2)}, u32[]{:S(2)}) collective-permute-start(bf16[64,256]{1,0:T(8,128)(2,1)S(1)} %collective-permute-done.11.refs_2_), channel_id=1, source_target_pairs={{0,1},{1,0},{2,3},{3,2},{4,5},{5,4},{6,7},{7,6},{8,9},{9,8},{10,11... | collective-permute-start | bytes 98312 | tf_op jit(solution)/shard_map/ppermute | solution.py:37
  39.8 6.0 %collective-permute-start.15 = (bf16[144,256]{1,0:T(8,128)(2,1)S(1)}, bf16[144,256]{1,0:T(8,128)(2,1)S(1)}, u32[]{:S(2)}, u32[]{:S(2)}) collective-permute-start(bf16[144,256]{1,0:T(8,128)(2,1)S(1)} %get-tuple-element.68), channel_id=1, source_target_pairs={{0,16},{4,20},{8,24},{12,28},{16,0},{20,4},{24,8},{28,12},{1,17},{... | collective-permute-start | bytes 221192 | tf_op jit(solution)/shard_map/ppermute | solution.py:37
  45.8 6.0 %collective-permute-start.18 = (bf16[144,256]{1,0:T(8,128)(2,1)S(1)}, bf16[144,256]{1,0:T(8,128)(2,1)S(1)}, u32[]{:S(2)}, u32[]{:S(2)}) collective-permute-start(bf16[144,256]{1,0:T(8,128)(2,1)S(1)} %shard_map.147.refs_0_), channel_id=1, source_target_pairs={{0,6},{1,7},{2,4},{3,5},{4,2},{5,3},{6,0},{7,1},{8,14},{9,15},{10,... | collective-permute-start | bytes 221192 | tf_op jit(solution)/shard_map/ppermute | solution.py:43
  46.8 5.1 %collective-permute-start.17 = (bf16[144,256]{1,0:T(8,128)(2,1)S(1)}, bf16[144,256]{1,0:T(8,128)(2,1)S(1)}, u32[]{:S(2)}, u32[]{:S(2)}) collective-permute-start(bf16[144,256]{1,0:T(8,128)(2,1)S(1)} %shard_map.147.refs_0_), channel_id=1, source_target_pairs={{0,2},{1,3},{2,0},{3,1},{4,6},{5,7},{6,4},{7,5},{8,10},{9,11},{10,... | collective-permute-start | bytes 221192 | tf_op jit(solution)/shard_map/ppermute | solution.py:37
  48.1 4.4 %collective-permute-start.16 = (bf16[144,256]{1,0:T(8,128)(2,1)S(1)}, bf16[144,256]{1,0:T(8,128)(2,1)S(1)}, u32[]{:S(2)}, u32[]{:S(2)}) collective-permute-start(bf16[144,256]{1,0:T(8,128)(2,1)S(1)} %shard_map.147.refs_0_), channel_id=1, source_target_pairs={{0,4},{4,0},{8,12},{12,8},{16,20},{20,16},{24,28},{28,24},{1,5},{5... | collective-permute-start | bytes 221192 | tf_op jit(solution)/shard_map/ppermute | solution.py:37
  52.4 1.6 %collective-permute-start.19 = (bf16[544,256]{1,0:T(8,128)(2,1)S(1)}, bf16[544,256]{1,0:T(8,128)(2,1)S(1)}, u32[]{:S(2)}, u32[]{:S(2)}) collective-permute-start(bf16[544,256]{1,0:T(8,128)(2,1)S(1)} %shard_map.148.refs_0_), channel_id=1, source_target_pairs={{0,1},{1,0},{2,3},{3,2},{4,5},{5,4},{6,7},{7,6},{8,9},{9,8},{10,11... | collective-permute-start | bytes 835592 | tf_op jit(solution)/shard_map/ppermute | solution.py:37

commit v5 on v4

--- a/solution.py
+++ b/solution.py
@@ -53,22 +53,28 @@
     return lax.ppermute(x, ("coarse", "fine"), pairs)
 
 
-def call(body, outs, args, flops, vmem=16, scratch=(), after=()):
+def call(body, outs, args, flops, vmem=16, scratch=(), after=(), into=None, far=0):
     moved = sum(a.size * a.dtype.itemsize for a in (*args, *outs)) if flops else 0
-    count, waited = len(args), len(after)
+    count = len(args)
+    unseen = (*after, into) if into is not None else after
+    waited = len(unseen)
 
     def kernel(*refs):
         body(*refs[:count], *refs[count + waited :])
 
-    specs = [pl.BlockSpec(memory_space=pltpu.VMEM)] * count + [pl.BlockSpec(memory_space=pl.ANY)] * waited
+    anywhere = pl.BlockSpec(memory_space=pl.ANY)
+    in_vmem = pl.BlockSpec(memory_space=pltpu.VMEM)
+    places = tuple([anywhere] * far + [in_vmem] * (len(outs) - far))
     return pl.pallas_call(
         kernel,
         out_shape=outs,
-        in_specs=specs,
+        in_specs=[in_vmem] * count + [anywhere] * waited,
+        out_specs=places,
         scratch_shapes=scratch,
+        input_output_aliases={} if into is None else {count + waited - 1: 0},
         compiler_params=pltpu.CompilerParams(vmem_limit_bytes=vmem * MIB),
         cost_estimate=pl.CostEstimate(flops=int(flops), bytes_accessed=int(moved), transcendentals=0),
-    )(*args, *after)
+    )(*args, *unseen)
 
 
 def sds(shape, dtype):
@@ -94,6 +100,28 @@
     shape = (height, row.shape[1])
     at = lax.broadcasted_iota(jnp.int32, shape, 0)
     return jnp.where(at == row - start, 1.0, 0.0).astype(BF)
+
+
+def source_body(src_ref, out_ref, mixed):
+    per = LANES // K
+    src = src_ref[...]
+    at = lax.broadcasted_iota(jnp.int32, (LANES, LANES), 0)
+    to = lax.broadcasted_iota(jnp.int32, (LANES, LANES), 1)
+    order = jnp.where(to == (at % K) * per + at // K, 1.0, 0.0).astype(BF)
+    high = lax.shift_right_logical(src, 6)
+    low = (src - 64 * high).astype(F32).astype(BF)
+    high = high.astype(F32).astype(BF)
+    mixed[...] = (64.0 * dot(high, order) + dot(low, order)).astype(jnp.int32)
+    count = mixed.shape[0] // K
+    lane = lax.broadcasted_iota(jnp.int32, (count, LANES), 1) // per
+    quarters = [mixed[pl.ds(j, count, stride=K), :] for j in range(K)]
+    for k in range(K):
+        rows = jnp.zeros((count, LANES), jnp.int32)
+        for j in range(K):
+            turned = quarters[j] if j == k else pltpu.roll(quarters[j], (j - k) % K * per, 1)
+            rows = jnp.where(lane == j, turned, rows)
+        for q in range(count):
+            out_ref[k : k + 1, q * LANES : (q + 1) * LANES] = rows[q : q + 1, :]
 
 
 def pool_body(ids_ref, x_ref, keep_ref, send_ref):
@@ -347,11 +375,8 @@
             out_ref[start + row : start + row + n, :] = value[r : r + n] * scale
 
 
-def feats_body(*refs):
-    *pool_refs, own_back, other_back, lists_ref, ids_ref, grad_ref, out_ref, token_ref, table = refs
-    token_ref[...] = jnp.zeros_like(token_ref)
-    cells = table.shape[0]
-    nodes = grad_ref.shape[0]
+def table_body(*refs):
+    *pool_refs, own_back, other_back, lists_ref, table = refs
     lists = lists_ref[...]
     core = lax.axis_index("fine") % 2
     side = own_back.shape[0]
@@ -362,10 +387,20 @@
     for i, pool_ref in enumerate(pool_refs):
         add = dot(hot_columns(lists, step, i * step), returned)
         table[i * step : (i + 1) * step, :] = (pool_ref[...] + add).astype(BF)
+
+
+def feats_body(table, ids_ref, grad_ref, *rest, first, count):
+    out_hbm, token_ref, out, sem = rest[-4:]
+    token_ref[...] = jnp.zeros_like(token_ref)
+    cells = table.shape[0]
     block = 256
-    for t in range(0, nodes, block):
-        rows = dot(hot_rows(ids_ref[:, t : t + block], cells), table[...])
-        out_ref[t : t + block, :] = (grad_ref[t : t + block, :].astype(F32) + rows).astype(BF)
+    for t in range(0, count, block):
+        at = slice(first + t, first + t + block)
+        rows = dot(hot_rows(ids_ref[:, at], cells), table[...])
+        out[t : t + block, :] = (grad_ref[at, :].astype(F32) + rows).astype(BF)
+    copy = pltpu.make_async_copy(out, out_hbm.at[first : first + count, :], sem)
+    copy.start()
+    copy.wait()
 
 
 def local(
@@ -380,7 +415,10 @@
     fine_bits, coarse_bits = bits_of(fines), bits_of(coarses)
     ids = lax.rem(cluster_ids, cells).reshape(1, nodes)
     lists = halo_lists.reshape(1, 2 * side)
-    src = edge_sources.reshape(cells, K).T
+    flat = edge_sources.reshape(cells * K // LANES, LANES)
+    src = call(
+        source_body, (sds((K, cells), jnp.int32),), (flat,), 0, scratch=(pltpu.VMEM(flat.shape, jnp.int32),)
+    )[0]
     bias = b_edge_in.reshape(1, width)
 
     def pool(x):
@@ -398,7 +436,7 @@
 
     part_p, send_p = pool(node_feats)
     part_g, send_g = pool(grad_out)
-    picked = call(pick_body, (sds((2 * side, width), BF),), (send_p, lists), 0, after=(send_g,))[0]
+    picked = call(pick_body, (sds((2 * side, width), BF),), (send_p, lists), 0)[0]
     sent = call(side_body, (sds((side, width), BF),), (picked, swap(picked, "fine", 0)), 0)[0]
     own_halo = call(
         halo_sum_body, (sds((side, width), BF),), [send_sides(sent, d) for d in range(fines // 2)], 0,
@@ -458,14 +496,22 @@
         )[0]
         for at in (0, half)
     ]
-    grad_feats, feats_token = call(
-        feats_body,
-        (sds((nodes, width), BF), sds((8, LANES), F32)),
-        (*cell_grads, own_back, other_back, lists, ids, grad_out),
-        2 * nodes * cells * width,
-        vmem=24,
-        scratch=(pltpu.VMEM((cells, width), BF),),
-    )
+    table = call(
+        table_body, (sds((cells, width), BF),), (*cell_grads, own_back, other_back, lists), 0
+    )[0]
+
+    def feats(first, count, after=(), into=None):
+        return call(
+            functools.partial(feats_body, first=first, count=count),
+            (sds((nodes, width), BF), sds((8, LANES), F32)),
+            (table, ids, grad_out),
+            2 * count * cells * width,
+            vmem=24,
+            scratch=(pltpu.VMEM((count, width), BF), pltpu.SemaphoreType.DMA(())),
+            after=after,
+            into=into,
+            far=1,
+        )
 
     after = {1: (back,), 2: (cell_grads[0],)}
     for bit in range(1, coarse_bits):
@@ -483,6 +529,8 @@
         end_body, (sds((first + PACK, width), BF),), (keep, recv, bias_sum), 0,
         after=(cell_grads[1], other_back),
     )[0]
+    front_rows = nodes // 2
+    grad_feats, feats_token = feats(0, front_rows)
     near = [swap(part, "coarse", 0), swap(part, "fine", 1), swap_both(part)]
     part = call(
         square_body, (sds((2 * (per + PACK), width), BF),), (part, *near), 0, after=(feats_token,)
@@ -492,6 +540,7 @@
         body = functools.partial(merge_body, bit=bit)
         part = call(body, (sds((2 * part.shape[0], width), BF),), (part, other), 0)[0]
     other = swap(part, "fine", 0)
+    grad_feats, feats_token = feats(front_rows, nodes - front_rows, after=(part,), into=grad_feats)
     total_cells = cells * coarses
     scales = dict(edge_scale=float(total_cells * K) ** -0.5, cell_scale=float(total_cells) ** -0.5)
     grad_w1, grad_b, grad_wo, grad_up = call(
@@ -501,6 +550,7 @@
         ),
         (part, other),
         0,
+        after=(feats_token,),
     )
     return grad_feats, grad_w1, grad_b.reshape(width), grad_wo, grad_up
 

time: 55.4 us -> 53 us (0.957)
  local copies, waits for them, and re-layouts: 3.84 us -> 1.29 us
  waiting for transfers between devices: 16.4 us -> 14.4 us
  Pallas kernels: 17.1 us -> 18.4 us
  starting transfers between devices: 16.2 us -> 17 us
    reshape x2 -> x0, local copies, waits for them, and re-layouts: 2.56 us -> none  [local(): src = edge_sources.reshape(cells, K).T]
    ppermute x16, waiting for transfers between devices: 11.4 us -> 9.67 us  [swap(): return lax.ppermute(x, axis, [(i, i ^ 1 << bit) for i in range(count)])]
    pallas_call x22 -> x25, Pallas kernels: 17.1 us -> 18.4 us  [call(): pl.pallas_call(kernel, out_shape=outs, in_specs=[in_vmem] * count + [anyw...]
    ppermute x1, starting transfers between devices: 0.92 us -> 1.9 us  [swap_both(): return lax.ppermute(x, ('coarse', 'fine'), pairs)]
  transfers between devices with their start and end apart: 20 -> 20, of which waited for: 11 -> 11; matrix products, arithmetic and copies ran while one was open for 5% -> 0% of each run, Pallas kernels for 24% -> 27%
where the time goes in v5:
time: 53 us; the launch traced here: 52.8 us
  Pallas kernels  18.4 us (35%)
  starting transfers between devices  17 us (32%)
  waiting for transfers between devices  14.4 us (27%)
  local copies, waits for them, and re-layouts  1.29 us (2%)
  between operations  0.89 us (2%)
  other arithmetic  0.79 us (1%)
    pallas_call x25, Pallas kernels, call(): pl.pallas_call(kernel, out_shape=outs, in_specs=[in_vmem] * count + [anyw...  18.4 us
    ppermute x16, starting transfers between devices, swap(): return lax.ppermute(x, axis, [(i, i ^ 1 << bit) for i in range(count)])  11 us
    ppermute x16, waiting for transfers between devices, swap(): return lax.ppermute(x, axis, [(i, i ^ 1 << bit) for i in range(count)])  9.67 us
    ppermute x3, waiting for transfers between devices, send_sides(): return lax.ppermute(x, ('coarse', 'fine'), pairs)  4.75 us
    ppermute x3, starting transfers between devices, send_sides(): return lax.ppermute(x, ('coarse', 'fine'), pairs)  4.11 us
    ppermute x1, starting transfers between devices, swap_both(): return lax.ppermute(x, ('coarse', 'fine'), pairs)  1.9 us
    unnamed x16, local copies, waits for them, and re-layouts  1.26 us
  transfers between devices with their start and end apart: 20, of which 11 were waited for; matrix products, arithmetic and copies ran while one was open for 0% of the time, Pallas kernels for 27%

profile of v5, /device:TPU:0, one launch (start us, length us, event | category | flops | bytes accessed | tf_op | source)
XLA Modules:
  0.0 52.8 jit_solution(5821267475624120696)
XLA Ops:
  0.6 0.8 %negate_select_fusion = s32[2048]{0:T(1024)S(1)} fusion(s32[2048]{0:T(1024)} %param.11), kind=kLoop, calls=%fused_computation | loop fusion | flops 12288 | bytes 16384 | tf_op jit(solution)/shard_map/rem | solution.py:416
  1.4 1.2 %copy-done.6 = bf16[2048,256]{1,0:T(8,128)(2,1)S(1)} copy-done((bf16[2048,256]{1,0:T(8,128)(2,1)S(1)}, bf16[2048,256]{1,0:T(8,128)(2,1)}, u32[]{:S(2)}) %copy-start.6) | copy-done | bytes 1048600
  2.7 1.2 %shard_map.130 = (f32[512,256]{1,0:T(8,128)S(1)}, f32[512,256]{1,0:T(8,128)S(1)}) custom-call(s32[1,2048]{1,0:T(1,128)S(1)} %bitcast.4, bf16[2048,256]{1,0:T(8,128)(2,1)S(1)} %copy-done.6), custom_call_target="tpu_custom_call" | custom-call | flops 1073741824 | bytes 2105344 | tf_op jit(solution)/shard_map/pallas_call | solution.py:68
  3.9 0.5 collective-permute-start.2
  4.5 1.2 %shard_map.128 = (f32[512,256]{1,0:T(8,128)S(1)}, f32[512,256]{1,0:T(8,128)S(1)}) custom-call(s32[1,2048]{1,0:T(1,128)S(1)} %bitcast.5, bf16[2048,256]{1,0:T(8,128)(2,1)S(1)} %copy-done.1), custom_call_target="tpu_custom_call" | custom-call | flops 1073741824 | bytes 2105344 | tf_op jit(solution)/shard_map/pallas_call | solution.py:68
  6.1 3.0 %collective-permute-start.3 = (bf16[512,256]{1,0:T(8,128)(2,1)S(1)}, bf16[512,256]{1,0:T(8,128)(2,1)S(1)}, u32[]{:S(2)}, u32[]{:S(2)}) collective-permute-start(bf16[512,256]{1,0:T(8,128)(2,1)S(1)} %get-tuple-element.49.refs_0_), channel_id=1, source_target_pairs={{0,2},{1,3},{2,0},{3,1},{4,6},{5,7},{6,4},{7,5},{8,10},{9,11},{10,... | collective-permute-start | bytes 786440 | tf_op jit(solution)/shard_map/ppermute | solution.py:37
  9.3 1.2 %collective-permute-done.4.refs_1_ = bf16[128,256]{1,0:T(8,128)(2,1)S(1)} collective-permute-done((bf16[128,256]{1,0:T(8,128)(2,1)S(1)}, bf16[128,256]{1,0:T(8,128)(2,1)S(1)}, u32[]{:S(2)}, u32[]{:S(2)}) %collective-permute-start.4) | collective-permute-done | bytes 65568 | tf_op jit(solution)/shard_map/ppermute | solution.py:37
  10.6 1.4 %collective-permute-start.6 = (bf16[64,256]{1,0:T(8,128)(2,1)S(1)}, bf16[64,256]{1,0:T(8,128)(2,1)S(1)}, u32[]{:S(2)}, u32[]{:S(2)}) collective-permute-start(bf16[64,256]{1,0:T(8,128)(2,1)S(1)} %shard_map.133), channel_id=1, source_target_pairs={{0,6},{1,31},{2,4},{3,29},{4,10},{5,3},{6,8},{7,1},{8,14},{9,7},{1... | collective-permute-start | bytes 98312 | tf_op jit(solution)/shard_map/ppermute | solution.py:53
  12.0 1.5 %collective-permute-start.5 = (bf16[64,256]{1,0:T(8,128)(2,1)S(1)}, bf16[64,256]{1,0:T(8,128)(2,1)S(1)}, u32[]{:S(2)}, u32[]{:S(2)}) collective-permute-start(bf16[64,256]{1,0:T(8,128)(2,1)S(1)} %shard_map.133), channel_id=1, source_target_pairs={{0,4},{1,29},{2,6},{3,31},{4,8},{5,1},{6,10},{7,3},{8,12},{9,5},{1... | collective-permute-start | bytes 98312 | tf_op jit(solution)/shard_map/ppermute | solution.py:53
  13.9 1.6 %collective-permute-start.1 = (bf16[512,256]{1,0:T(8,128)(2,1)S(1)}, bf16[512,256]{1,0:T(8,128)(2,1)S(1)}, u32[]{:S(2)}, u32[]{:S(2)}) collective-permute-start(bf16[512,256]{1,0:T(8,128)(2,1)S(1)} %get-tuple-element.45), channel_id=1, source_target_pairs={{0,2},{1,3},{2,0},{3,1},{4,6},{5,7},{6,4},{7,5},{8,10},{9,11},{10,... | collective-permute-start | bytes 786440 | tf_op jit(solution)/shard_map/ppermute | solution.py:37
  15.5 2.7 %collective-permute-done.6.refs_1_ = bf16[64,256]{1,0:T(8,128)(2,1)S(1)} collective-permute-done((bf16[64,256]{1,0:T(8,128)(2,1)S(1)}, bf16[64,256]{1,0:T(8,128)(2,1)S(1)}, u32[]{:S(2)}, u32[]{:S(2)}) %collective-permute-start.6) | collective-permute-done | bytes 32800 | tf_op jit(solution)/shard_map/ppermute | solution.py:53
  18.8 0.5 collective-permute-start.7
  19.4 1.1 %collective-permute-done.9.refs_4_ = bf16[64,256]{1,0:T(8,128)(2,1)S(1)} collective-permute-done((bf16[64,256]{1,0:T(8,128)(2,1)S(1)}, bf16[64,256]{1,0:T(8,128)(2,1)S(1)}, u32[]{:S(2)}, u32[]{:S(2)}) %collective-permute-start.9) | collective-permute-done | bytes 32800 | tf_op jit(solution)/shard_map/ppermute | solution.py:37
  20.9 2.2 %shard_map.138 = (f32[1024,256]{1,0:T(8,128)S(1)}, f32[2048,256]{1,0:T(8,128)S(1)}, bf16[2048,256]{1,0:T(8,128)(2,1)S(1)}, f32[8,128]{1,0:T(8,128)S(1)}) custom-call(bf16[1152,256]{1,0:T(8,128)(2,1)S(1)} %get-tuple-element.50.refs_0_.refs_2_, f32[1024,256]{1,0:T(8,128)S(1)} %get-tuple-element.51.refs_1_, s32[4,1024]{1,0:T(4,128)S(1)} %shard_map.135.refs_3_.refs_2_.refs_1_, ...), custom_call_target="tpu_custom_call" | custom-call | tf_op jit(solution)/shard_map/pallas_call | solution.py:68
  23.5 2.8 %shard_map.140 = (f32[1024,256]{1,0:T(8,128)S(1)}, f32[2048,256]{1,0:T(8,128)S(1)}, bf16[2048,256]{1,0:T(8,128)(2,1)S(1)}, f32[8,128]{1,0:T(8,128)}) custom-call(bf16[1152,256]{1,0:T(8,128)(2,1)S(1)} %get-tuple-element.50.refs_0_.refs_2_, f32[1024,256]{1,0:T(8,128)S(1)} %get-tuple-element.51.refs_1_, s32[4,1024]{1,0:T(4,128)S(1)} %shard_map.135.refs_3_.refs_2_.refs_1_, ...), custom_call_target="tpu_custom_call" | custom-call | tf_op jit(solution)/shard_map/pallas_call | solution.py:68
  26.3 1.5 %shard_map.141 = (bf16[4096,256]{1,0:T(8,128)(2,1)S(1)}, f32[1024,256]{1,0:T(8,128)S(1)}, bf16[1024,256]{1,0:T(8,128)(2,1)S(1)}, f32[128,256]{1,0:T(8,128)S(1)},...) custom-call(bf16[512,256]{1,0:T(8,128)(2,1)S(1)} %shard_map.139.refs_4_.refs_0_, ...), custom_call_target="tpu_custom_call" | custom-call | flops 536870912 | bytes 13647872 | tf_op jit(solution)/shard_map/pallas_call | solution.py:68
  27.8 1.2 %collective-permute-start.13 = (bf16[144,256]{1,0:T(8,128)(2,1)S(1)}, bf16[144,256]{1,0:T(8,128)(2,1)S(1)}, u32[]{:S(2)}, u32[]{:S(2)}) collective-permute-start(bf16[144,256]{1,0:T(8,128)(2,1)S(1)} %get-tuple-element.63), channel_id=1, source_target_pairs={{0,4},{4,0},{8,12},{12,8},{16,20},{20,16},{24,28},{28,24},{1,5},{5... | collective-permute-start | bytes 221192 | tf_op jit(solution)/shard_map/ppermute | solution.py:37
  29.0 0.6 %shard_map.144.refs_3_ = bf16[64,256]{1,0:T(8,128)(2,1)S(1)} custom-call(bf16[4096,256]{1,0:T(8,128)(2,1)S(1)} %get-tuple-element.59.refs_0_, s32[4,1024]{1,0:T(4,128)S(1)} %shard_map.135.refs_3_.refs_2_.refs_1_, bf16[512,256]{1,0:T(8,128)(2,1)S(1)} %copy-done), custom_call_target="tpu_custom_call" | custom-call | flops 268435456 | bytes 2408448 | tf_op jit(solution)/shard_map/pallas_call | solution.py:68
  29.6 1.1 %collective-permute-start.11 = (bf16[64,256]{1,0:T(8,128)(2,1)S(1)}, bf16[64,256]{1,0:T(8,128)(2,1)S(1)}, u32[]{:S(2)}, u32[]{:S(2)}) collective-permute-start(bf16[64,256]{1,0:T(8,128)(2,1)S(1)} %shard_map.144.refs_3_), channel_id=1, source_target_pairs={{0,4},{1,29},{2,6},{3,31},{4,8},{5,1},{6,10},{7,3},{8,12},{9,5},{1... | collective-permute-start | bytes 98312 | tf_op jit(solution)/shard_map/ppermute | solution.py:53
  30.7 2.1 %collective-permute-done.13.refs_1_ = bf16[144,256]{1,0:T(8,128)(2,1)S(1)} collective-permute-done((bf16[144,256]{1,0:T(8,128)(2,1)S(1)}, bf16[144,256]{1,0:T(8,128)(2,1)S(1)}, u32[]{:S(2)}, u32[]{:S(2)}) %collective-permute-start.13) | collective-permute-done | bytes 73760 | tf_op jit(solution)/shard_map/ppermute | solution.py:37
  33.3 1.5 %shard_map.142.refs_0_.refs_3_ = f32[512,256]{1,0:T(8,128)S(1)} custom-call(bf16[4096,256]{1,0:T(8,128)(2,1)S(1)} %get-tuple-element.59.refs_0_, s32[4,1024]{1,0:T(4,128)S(1)} %shard_map.135.refs_3_.refs_2_.refs_1_, f32[1024,256]{1,0:T(8,128)S(1)} %get-tuple-element.60.refs_2_, bf16[1024,256]{1,0:T(8,128)(2,1)S(1)} %get-tuple-element.61.refs_3_, ...), custom_call_target="tpu_custom_call" | custom-call | flops 1073741824 | bytes 4472832 | tf_op jit(solution)/shard_map/pallas_call | solution.py:68
  34.8 1.6 %collective-permute-done.11.refs_2_ = bf16[64,256]{1,0:T(8,128)(2,1)S(1)} collective-permute-done((bf16[64,256]{1,0:T(8,128)(2,1)S(1)}, bf16[64,256]{1,0:T(8,128)(2,1)S(1)}, u32[]{:S(2)}, u32[]{:S(2)}) %collective-permute-start.11) | collective-permute-done | bytes 32800 | tf_op jit(solution)/shard_map/ppermute | solution.py:53
  36.4 0.8 %collective-permute-done.14.refs_1_ = bf16[144,256]{1,0:T(8,128)(2,1)S(1)} collective-permute-done((bf16[144,256]{1,0:T(8,128)(2,1)S(1)}, bf16[144,256]{1,0:T(8,128)(2,1)S(1)}, u32[]{:S(2)}, u32[]{:S(2)}) %collective-permute-start.14) | collective-permute-done | bytes 73760 | tf_op jit(solution)/shard_map/ppermute | solution.py:37
  37.3 1.5 %collective-permute-start.15 = (bf16[144,256]{1,0:T(8,128)(2,1)S(1)}, bf16[144,256]{1,0:T(8,128)(2,1)S(1)}, u32[]{:S(2)}, u32[]{:S(2)}) collective-permute-start(bf16[144,256]{1,0:T(8,128)(2,1)S(1)} %get-tuple-element.69), channel_id=1, source_target_pairs={{0,16},{4,20},{8,24},{12,28},{16,0},{20,4},{24,8},{28,12},{1,17},{... | collective-permute-start | bytes 221192 | tf_op jit(solution)/shard_map/ppermute | solution.py:37
  38.8 1.5 %shard_map.143.refs_1_.refs_3_ = f32[512,256]{1,0:T(8,128)S(1)} custom-call(bf16[4096,256]{1,0:T(8,128)(2,1)S(1)} %get-tuple-element.59.refs_0_, s32[4,1024]{1,0:T(4,128)S(1)} %shard_map.135.refs_3_.refs_2_.refs_1_, f32[1024,256]{1,0:T(8,128)S(1)} %get-tuple-element.60.refs_2_, bf16[1024,256]{1,0:T(8,128)(2,1)S(1)} %get-tuple-element.61.refs_3_, ...), custom_call_target="tpu_custom_call" | custom-call | flops 1073741824 | bytes 4472832 | tf_op jit(solution)/shard_map/pallas_call | solution.py:68
  40.3 2.9 %collective-permute-done.15.refs_1_ = bf16[144,256]{1,0:T(8,128)(2,1)S(1)} collective-permute-done((bf16[144,256]{1,0:T(8,128)(2,1)S(1)}, bf16[144,256]{1,0:T(8,128)(2,1)S(1)}, u32[]{:S(2)}, u32[]{:S(2)}) %collective-permute-start.15) | collective-permute-done | bytes 73760 | tf_op jit(solution)/shard_map/ppermute | solution.py:37
  43.3 1.9 %collective-permute-start.18 = (bf16[144,256]{1,0:T(8,128)(2,1)S(1)}, bf16[144,256]{1,0:T(8,128)(2,1)S(1)}, u32[]{:S(2)}, u32[]{:S(2)}) collective-permute-start(bf16[144,256]{1,0:T(8,128)(2,1)S(1)} %shard_map.148.refs_0_), channel_id=1, source_target_pairs={{0,6},{1,7},{2,4},{3,5},{4,2},{5,3},{6,0},{7,1},{8,14},{9,15},{10,... | collective-permute-start | bytes 221192 | tf_op jit(solution)/shard_map/ppermute | solution.py:43
  45.6 1.2 %collective-permute-start.16 = (bf16[144,256]{1,0:T(8,128)(2,1)S(1)}, bf16[144,256]{1,0:T(8,128)(2,1)S(1)}, u32[]{:S(2)}, u32[]{:S(2)}) collective-permute-start(bf16[144,256]{1,0:T(8,128)(2,1)S(1)} %shard_map.148.refs_0_), channel_id=1, source_target_pairs={{0,4},{4,0},{8,12},{12,8},{16,20},{20,16},{24,28},{28,24},{1,5},{5... | collective-permute-start | bytes 221192 | tf_op jit(solution)/shard_map/ppermute | solution.py:37
  47.2 1.6 %shard_map.149 = (bf16[2048,256]{1,0:T(8,128)(2,1)}, f32[8,128]{1,0:T(8,128)S(1)}) custom-call(bf16[1024,256]{1,0:T(8,128)(2,1)S(1)} %shard_map.145.refs_0_, s32[1,2048]{1,0:T(1,128)S(1)} %bitcast.6, bf16[2048,256]{1,0:T(8,128)(2,1)S(1)} %copy-done.1), custom_call_target="tpu_custom_call" | custom-call | flops 536870912 | bytes 2633728 | tf_op jit(solution)/shard_map/pallas_call | solution.py:68
  48.7 0.8 %collective-permute-done.17.refs_2_ = bf16[144,256]{1,0:T(8,128)(2,1)S(1)} collective-permute-done((bf16[144,256]{1,0:T(8,128)(2,1)S(1)}, bf16[144,256]{1,0:T(8,128)(2,1)S(1)}, u32[]{:S(2)}, u32[]{:S(2)}) %collective-permute-start.17) | collective-permute-done | bytes 73760 | tf_op jit(solution)/shard_map/ppermute | solution.py:37
  50.1 1.6 %shard_map.151 = (bf16[2048,256]{1,0:T(8,128)(2,1)}, f32[8,128]{1,0:T(8,128)S(1)}) custom-call(bf16[1024,256]{1,0:T(8,128)(2,1)S(1)} %shard_map.145.refs_0_, s32[1,2048]{1,0:T(1,128)S(1)} %bitcast.7, bf16[2048,256]{1,0:T(8,128)(2,1)S(1)} %copy-done.1, bf16[544,256]{1,0:T(8,128)(2,1)S(1)} %shard_map.150.refs_3_.refs_0_, ...), custom_call_target="tpu_custom_call", output_to_operand_aliasing={{0}: (4, {})} | custom-call | flops 536870912 | bytes 2633728 | tf_op jit(solution)/shard_map/pallas_call | solution.py:68
  51.7 1.1 %shard_map.152 = (f32[512,256]{1,0:T(8,128)}, f32[1,256]{1,0:T(1,128)}, f32[256,256]{1,0:T(8,128)}, f32[256,256]{1,0:T(8,128)}) custom-call(bf16[544,256]{1,0:T(8,128)(2,1)S(1)} %shard_map.150.refs_3_.refs_0_, bf16[544,256]{1,0:T(8,128)(2,1)S(1)} %collective-permute-done.19.refs_1_, f32[8,128]{1,0:T(8,128)S(1)} %get-tuple-element.74.refs_2_), custom_call_target="tpu_custom_call" | custom-call | tf_op jit(solution)/shard_map/pallas_call | solution.py:68
  (52 shorter events, 4.4 us)
Async XLA Ops:
  0.6 3.8 %copy-start.1 = (bf16[2048,256]{1,0:T(8,128)(2,1)S(1)}, bf16[2048,256]{1,0:T(8,128)(2,1)}, u32[]{:S(2)}) copy-start(bf16[2048,256]{1,0:T(8,128)(2,1)} %refs_2_.5) | copy-start | bytes 3145732
  1.4 1.2 %copy-start.6 = (bf16[2048,256]{1,0:T(8,128)(2,1)S(1)}, bf16[2048,256]{1,0:T(8,128)(2,1)}, u32[]{:S(2)}) copy-start(bf16[2048,256]{1,0:T(8,128)(2,1)} %refs_1_.3) | copy-start | bytes 3145732
  3.9 5.1 %copy-start.5 = (s32[128]{0:T(128)S(1)}, s32[128]{0:T(128)}, u32[]{:S(2)}) copy-start(s32[128]{0:T(128)} %param.12) | copy-start | bytes 1540
  3.9 9.7 %copy-start.7 = (bf16[256]{0:T(256)(128)(2,1)S(1)}, bf16[256]{0:T(256)(128)(2,1)}, u32[]{:S(2)}) copy-start(bf16[256]{0:T(256)(128)(2,1)} %param.15) | copy-start | bytes 1540
  3.9 9.7 %copy-start.4 = (s32[4096]{0:T(1024)S(1)}, s32[4096]{0:T(1024)}, u32[]{:S(2)}) copy-start(s32[4096]{0:T(1024)} %param.13) | copy-start | bytes 49156
  3.9 2.1 %collective-permute-start.2 = (f32[512,256]{1,0:T(8,128)S(1)}, f32[512,256]{1,0:T(8,128)S(1)}, u32[]{:S(2)}, u32[]{:S(2)}) collective-permute-start(f32[512,256]{1,0:T(8,128)S(1)} %get-tuple-element.47), channel_id=1, source_target_pairs={{0,1},{1,0},{2,3},{3,2},{4,5},{5,4},{6,7},{7,6},{8,9},{9,8},{10,11... | collective-permute-start | bytes 1572872 | tf_op jit(solution)/shard_map/ppermute | solution.py:37
  5.7 8.1 %collective-permute-start = (f32[512,256]{1,0:T(8,128)S(1)}, f32[512,256]{1,0:T(8,128)S(1)}, u32[]{:S(2)}, u32[]{:S(2)}) collective-permute-start(f32[512,256]{1,0:T(8,128)S(1)} %get-tuple-element.43), channel_id=1, source_target_pairs={{0,1},{1,0},{2,3},{3,2},{4,5},{5,4},{6,7},{7,6},{8,9},{9,8},{10,11... | collective-permute-start | bytes 1572872 | tf_op jit(solution)/shard_map/ppermute | solution.py:37
  6.0 14.6 %copy-start = (bf16[512,256]{1,0:T(8,128)(2,1)S(1)}, bf16[512,256]{1,0:T(8,128)(2,1)}, u32[]{:S(2)}) copy-start(bf16[512,256]{1,0:T(8,128)(2,1)} %refs_2_.3) | copy-start | bytes 786436
  6.1 12.6 %collective-permute-start.3 = (bf16[512,256]{1,0:T(8,128)(2,1)S(1)}, bf16[512,256]{1,0:T(8,128)(2,1)S(1)}, u32[]{:S(2)}, u32[]{:S(2)}) collective-permute-start(bf16[512,256]{1,0:T(8,128)(2,1)S(1)} %get-tuple-element.49.refs_0_), channel_id=1, source_target_pairs={{0,2},{1,3},{2,0},{3,1},{4,6},{5,7},{6,4},{7,5},{8,10},{9,11},{10,... | collective-permute-start | bytes 786440 | tf_op jit(solution)/shard_map/ppermute | solution.py:37
  9.3 1.3 %collective-permute-start.4 = (bf16[128,256]{1,0:T(8,128)(2,1)S(1)}, bf16[128,256]{1,0:T(8,128)(2,1)S(1)}, u32[]{:S(2)}, u32[]{:S(2)}) collective-permute-start(bf16[128,256]{1,0:T(8,128)(2,1)S(1)} %shard_map.132.refs_0_), channel_id=1, source_target_pairs={{0,1},{1,0},{2,3},{3,2},{4,5},{5,4},{6,7},{7,6},{8,9},{9,8},{10,11... | collective-permute-start | bytes 196616 | tf_op jit(solution)/shard_map/ppermute | solution.py:37
  10.6 7.6 %collective-permute-start.6 = (bf16[64,256]{1,0:T(8,128)(2,1)S(1)}, bf16[64,256]{1,0:T(8,128)(2,1)S(1)}, u32[]{:S(2)}, u32[]{:S(2)}) collective-permute-start(bf16[64,256]{1,0:T(8,128)(2,1)S(1)} %shard_map.133), channel_id=1, source_target_pairs={{0,6},{1,31},{2,4},{3,29},{4,10},{5,3},{6,8},{7,1},{8,14},{9,7},{1... | collective-permute-start | bytes 98312 | tf_op jit(solution)/shard_map/ppermute | solution.py:53
  12.0 6.6 %collective-permute-start.5 = (bf16[64,256]{1,0:T(8,128)(2,1)S(1)}, bf16[64,256]{1,0:T(8,128)(2,1)S(1)}, u32[]{:S(2)}, u32[]{:S(2)}) collective-permute-start(bf16[64,256]{1,0:T(8,128)(2,1)S(1)} %shard_map.133), channel_id=1, source_target_pairs={{0,4},{1,29},{2,6},{3,31},{4,8},{5,1},{6,10},{7,3},{8,12},{9,5},{1... | collective-permute-start | bytes 98312 | tf_op jit(solution)/shard_map/ppermute | solution.py:53
  13.9 9.3 %collective-permute-start.1 = (bf16[512,256]{1,0:T(8,128)(2,1)S(1)}, bf16[512,256]{1,0:T(8,128)(2,1)S(1)}, u32[]{:S(2)}, u32[]{:S(2)}) collective-permute-start(bf16[512,256]{1,0:T(8,128)(2,1)S(1)} %get-tuple-element.45), channel_id=1, source_target_pairs={{0,2},{1,3},{2,0},{3,1},{4,6},{5,7},{6,4},{7,5},{8,10},{9,11},{10,... | collective-permute-start | bytes 786440 | tf_op jit(solution)/shard_map/ppermute | solution.py:37
  18.8 1.8 %collective-permute-start.8 = (bf16[256,256]{1,0:T(8,128)(2,1)S(1)}, bf16[256,256]{1,0:T(8,128)(2,1)S(1)}, u32[]{:S(2)}, u32[]{:S(2)}) collective-permute-start(bf16[256,256]{1,0:T(8,128)(2,1)S(1)} %get-tuple-element.79), channel_id=1, source_target_pairs={{0,1},{1,0},{2,3},{3,2},{4,5},{5,4},{6,7},{7,6},{8,9},{9,8},{10,11... | collective-permute-start | bytes 393224 | tf_op jit(solution)/shard_map/ppermute | solution.py:37
  18.8 1.7 %collective-permute-start.7 = (bf16[256,256]{1,0:T(8,128)(2,1)S(1)}, bf16[256,256]{1,0:T(8,128)(2,1)S(1)}, u32[]{:S(2)}, u32[]{:S(2)}) collective-permute-start(bf16[256,256]{1,0:T(8,128)(2,1)S(1)} %get-tuple-element.80), channel_id=1, source_target_pairs={{0,1},{1,0},{2,3},{3,2},{4,5},{5,4},{6,7},{7,6},{8,9},{9,8},{10,11... | collective-permute-start | bytes 393224 | tf_op jit(solution)/shard_map/ppermute | solution.py:37
  19.3 1.2 %collective-permute-start.9 = (bf16[64,256]{1,0:T(8,128)(2,1)S(1)}, bf16[64,256]{1,0:T(8,128)(2,1)S(1)}, u32[]{:S(2)}, u32[]{:S(2)}) collective-permute-start(bf16[64,256]{1,0:T(8,128)(2,1)S(1)} %shard_map.134.refs_2_.refs_3_), channel_id=1, source_target_pairs={{0,1},{1,0},{2,3},{3,2},{4,5},{5,4},{6,7},{7,6},{8,9},{9,8},{10,11... | collective-permute-start | bytes 98312 | tf_op jit(solution)/shard_map/ppermute | solution.py:37
  23.1 3.1 %copy-start.2 = (bf16[256,256]{1,0:T(8,128)(2,1)S(1)}, bf16[256,256]{1,0:T(8,128)(2,1)}, u32[]{:S(2)}) copy-start(bf16[256,256]{1,0:T(8,128)(2,1)} %refs_9_.1) | copy-start | bytes 393220
  23.1 3.1 %copy-start.3 = (bf16[256,256]{1,0:T(8,128)(2,1)S(1)}, bf16[256,256]{1,0:T(8,128)(2,1)}, u32[]{:S(2)}) copy-start(bf16[256,256]{1,0:T(8,128)(2,1)} %refs_10_.1) | copy-start | bytes 393220
  23.3 3.0 %collective-permute-start.10 = (bf16[512,256]{1,0:T(8,128)(2,1)S(1)}, bf16[512,256]{1,0:T(8,128)(2,1)S(1)}, u32[]{:S(2)}, u32[]{:S(2)}) collective-permute-start(bf16[512,256]{1,0:T(8,128)(2,1)S(1)} %shard_map.139.refs_4_.refs_0_), channel_id=1, source_target_pairs={{0,1},{1,0},{2,3},{3,2},{4,5},{5,4},{6,7},{7,6},{8,9},{9,8},{10,11... | collective-permute-start | bytes 786440 | tf_op jit(solution)/shard_map/ppermute | solution.py:37
  27.8 5.0 %collective-permute-start.13 = (bf16[144,256]{1,0:T(8,128)(2,1)S(1)}, bf16[144,256]{1,0:T(8,128)(2,1)S(1)}, u32[]{:S(2)}, u32[]{:S(2)}) collective-permute-start(bf16[144,256]{1,0:T(8,128)(2,1)S(1)} %get-tuple-element.63), channel_id=1, source_target_pairs={{0,4},{4,0},{8,12},{12,8},{16,20},{20,16},{24,28},{28,24},{1,5},{5... | collective-permute-start | bytes 221192 | tf_op jit(solution)/shard_map/ppermute | solution.py:37
  29.6 6.8 %collective-permute-start.11 = (bf16[64,256]{1,0:T(8,128)(2,1)S(1)}, bf16[64,256]{1,0:T(8,128)(2,1)S(1)}, u32[]{:S(2)}, u32[]{:S(2)}) collective-permute-start(bf16[64,256]{1,0:T(8,128)(2,1)S(1)} %shard_map.144.refs_3_), channel_id=1, source_target_pairs={{0,4},{1,29},{2,6},{3,31},{4,8},{5,1},{6,10},{7,3},{8,12},{9,5},{1... | collective-permute-start | bytes 98312 | tf_op jit(solution)/shard_map/ppermute | solution.py:53
  32.8 4.4 %collective-permute-start.14 = (bf16[144,256]{1,0:T(8,128)(2,1)S(1)}, bf16[144,256]{1,0:T(8,128)(2,1)S(1)}, u32[]{:S(2)}, u32[]{:S(2)}) collective-permute-start(bf16[144,256]{1,0:T(8,128)(2,1)S(1)} %get-tuple-element.66), channel_id=1, source_target_pairs={{0,8},{4,12},{8,0},{12,4},{16,24},{20,28},{24,16},{28,20},{1,9},{5... | collective-permute-start | bytes 221192 | tf_op jit(solution)/shard_map/ppermute | solution.py:37
  36.4 3.9 %collective-permute-start.12 = (bf16[64,256]{1,0:T(8,128)(2,1)S(1)}, bf16[64,256]{1,0:T(8,128)(2,1)S(1)}, u32[]{:S(2)}, u32[]{:S(2)}) collective-permute-start(bf16[64,256]{1,0:T(8,128)(2,1)S(1)} %collective-permute-done.11.refs_2_), channel_id=1, source_target_pairs={{0,1},{1,0},{2,3},{3,2},{4,5},{5,4},{6,7},{7,6},{8,9},{9,8},{10,11... | collective-permute-start | bytes 98312 | tf_op jit(solution)/shard_map/ppermute | solution.py:37
  37.3 6.0 %collective-permute-start.15 = (bf16[144,256]{1,0:T(8,128)(2,1)S(1)}, bf16[144,256]{1,0:T(8,128)(2,1)S(1)}, u32[]{:S(2)}, u32[]{:S(2)}) collective-permute-start(bf16[144,256]{1,0:T(8,128)(2,1)S(1)} %get-tuple-element.69), channel_id=1, source_target_pairs={{0,16},{4,20},{8,24},{12,28},{16,0},{20,4},{24,8},{28,12},{1,17},{... | collective-permute-start | bytes 221192 | tf_op jit(solution)/shard_map/ppermute | solution.py:37
  43.3 5.5 %collective-permute-start.18 = (bf16[144,256]{1,0:T(8,128)(2,1)S(1)}, bf16[144,256]{1,0:T(8,128)(2,1)S(1)}, u32[]{:S(2)}, u32[]{:S(2)}) collective-permute-start(bf16[144,256]{1,0:T(8,128)(2,1)S(1)} %shard_map.148.refs_0_), channel_id=1, source_target_pairs={{0,6},{1,7},{2,4},{3,5},{4,2},{5,3},{6,0},{7,1},{8,14},{9,15},{10,... | collective-permute-start | bytes 221192 | tf_op jit(solution)/shard_map/ppermute | solution.py:43
  45.2 4.4 %collective-permute-start.17 = (bf16[144,256]{1,0:T(8,128)(2,1)S(1)}, bf16[144,256]{1,0:T(8,128)(2,1)S(1)}, u32[]{:S(2)}, u32[]{:S(2)}) collective-permute-start(bf16[144,256]{1,0:T(8,128)(2,1)S(1)} %shard_map.148.refs_0_), channel_id=1, source_target_pairs={{0,2},{1,3},{2,0},{3,1},{4,6},{5,7},{6,4},{7,5},{8,10},{9,11},{10,... | collective-permute-start | bytes 221192 | tf_op jit(solution)/shard_map/ppermute | solution.py:37
  45.6 4.4 %collective-permute-start.16 = (bf16[144,256]{1,0:T(8,128)(2,1)S(1)}, bf16[144,256]{1,0:T(8,128)(2,1)S(1)}, u32[]{:S(2)}, u32[]{:S(2)}) collective-permute-start(bf16[144,256]{1,0:T(8,128)(2,1)S(1)} %shard_map.148.refs_0_), channel_id=1, source_target_pairs={{0,4},{4,0},{8,12},{12,8},{16,20},{20,16},{24,28},{28,24},{1,5},{5... | collective-permute-start | bytes 221192 | tf_op jit(solution)/shard_map/ppermute | solution.py:37
  50.0 1.7 %collective-permute-start.19 = (bf16[544,256]{1,0:T(8,128)(2,1)S(1)}, bf16[544,256]{1,0:T(8,128)(2,1)S(1)}, u32[]{:S(2)}, u32[]{:S(2)}) collective-permute-start(bf16[544,256]{1,0:T(8,128)(2,1)S(1)} %shard_map.150.refs_3_.refs_0_), channel_id=1, source_target_pairs={{0,1},{1,0},{2,3},{3,2},{4,5},{5,4},{6,7},{7,6},{8,9},{9,8},{10,11... | collective-permute-start | bytes 835592 | tf_op jit(solution)/shard_map/ppermute | solution.py:37

commit v6 on v5

--- a/solution.py
+++ b/solution.py
@@ -8,11 +8,13 @@
 from jax.sharding import PartitionSpec as P
 
 K = 4
+EARLY = 3
 BF = jnp.bfloat16
 F32 = jnp.float32
 LANES = 128
 PACK = 16
 MIB = 1 << 20
+AHEAD = 10**9
 
 
 def dot(a, b):
@@ -100,6 +102,10 @@
     shape = (height, row.shape[1])
     at = lax.broadcasted_iota(jnp.int32, shape, 0)
     return jnp.where(at == row - start, 1.0, 0.0).astype(BF)
+
+
+def local_body(ids_ref, out_ref, *, cells):
+    out_ref[...] = lax.rem(ids_ref[...], cells)
 
 
 def source_body(src_ref, out_ref, mixed):
@@ -178,31 +184,47 @@
     return at_own, at_other
 
 
+def near_body(own_p, src_ref, near):
+    half = own_p.shape[0]
+    cells = 2 * half
+    core = lax.axis_index("fine") % 2
+    block = 512
+    for k in range(K):
+        for t in range(0, cells, block):
+            hot = hot_rows(src_ref[k : k + 1, t : t + block] - core * half, half)
+            near[k * cells + t : k * cells + t + block, :] = dot(hot, own_p[...]).astype(BF)
+
+
 def extend_body(*refs):
-    *others, own_p, own_halo, other_halo, w1_ref, b_ref, ext, base = refs
+    *others, own_p, own_halo, other_halo, w1_ref, b_ref, table, far, base = refs
     half, width = own_p.shape
-    cells = 2 * half
     side = own_halo.shape[0]
     core = lax.axis_index("fine") % 2
-    ext[pl.ds(pl.multiple_of(core * half, half), half), :] = own_p[...]
     n = half // len(others)
     for i, other in enumerate(others):
-        ext[pl.ds(pl.multiple_of((1 - core) * half + i * n, n), n), :] = other[...]
-    ext[pl.ds(pl.multiple_of(cells + core * side, PACK), side), :] = own_halo[...]
-    ext[pl.ds(pl.multiple_of(cells + (1 - core) * side, PACK), side), :] = other_halo[...]
-    base[...] = dot(ext[0:cells, :], w1_ref[0:width, :]) + b_ref[...].astype(F32)
-
-
-def forward_body(ext, base, src_ref, w1_ref, hid, slope, feats, token_ref, *, first):
+        far[i * n : (i + 1) * n, :] = other[...]
+    far[pl.ds(pl.multiple_of(half + core * side, PACK), side), :] = own_halo[...]
+    far[pl.ds(pl.multiple_of(half + (1 - core) * side, PACK), side), :] = other_halo[...]
+    at_own, at_other = core_order(half)
+    table[at_own, :] = own_p[...]
+    table[at_other, :] = far[0:half, :]
+    base[...] = dot(table[...], w1_ref[0:width, :]) + b_ref[...].astype(F32)
+
+
+def forward_body(base, far, near, src_ref, w1_ref, hid, slope, feats, token_ref, *, first):
     cells, width = base.shape
-    rows = ext.shape[0]
+    half = cells // 2
+    core = lax.axis_index("fine") % 2
     token_ref[...] = jnp.zeros_like(token_ref)
     block = 512
     for i in range(slope.shape[0] // cells):
         for t in range(0, cells, block):
-            part = src_ref[first + i : first + i + 1, t : t + block]
-            at = i * cells + t
-            feats[at : at + block, :] = dot(hot_rows(part, rows), ext[...]).astype(BF)
+            src = src_ref[first + i : first + i + 1, t : t + block]
+            mine = jnp.logical_and(src >= core * half, src < (core + 1) * half)
+            place = jnp.where(src >= cells, src - half, src - (1 - core) * half)
+            picked = dot(hot_rows(jnp.where(mine, -1, place), far.shape[0]), far[...])
+            here = slice((first + i) * cells + t, (first + i) * cells + t + block)
+            feats[i * cells + t : i * cells + t + block, :] = (picked + near[here, :].astype(F32)).astype(BF)
         at = slice(i * cells, (i + 1) * cells)
         pre = base[...] + dot(feats[at, :], w1_ref[width : 2 * width, :])
         sig = 0.5 * jnp.tanh(0.5 * pre) + 0.5
@@ -242,7 +264,7 @@
 
 
 def backward_body(
-    own_g, other_g, ext, hid_1, slope_1, feats_1, hid_2, slope_2, feats_2, wo_ref, wu_ref,
+    own_g, other_g, table, hid_1, slope_1, feats_1, hid_2, slope_2, feats_2, wo_ref, wu_ref,
     act, ga_ref, gn_ref, keep_ref, send_ref, bias_ref,
     gsum, total,
 ):
@@ -258,7 +280,7 @@
     ga = jnp.zeros((cells, width), F32)
     for k in range(K):
         at = slice(k * cells, (k + 1) * cells)
-        slope, here = (slope_1, k) if k < K // 2 else (slope_2, k - K // 2)
+        slope, here = (slope_1, k) if k < EARLY else (slope_2, k - EARLY)
         part = (grad * slope[here * cells : (here + 1) * cells, :]).astype(BF)
         act[at, :] = part
         ga = ga + part.astype(F32)
@@ -276,7 +298,7 @@
                 cols = slice(first, first + n)
                 if which == 0:
                     high, low = split(ga_ref[...])
-                    left = ext[0:cells, cols]
+                    left = table[:, cols]
                     out = dot_tn(left, high) + dot_tn(left, low)
                 elif which == 1:
                     n_1 = feats_1.shape[0]
@@ -287,7 +309,7 @@
                 else:
                     high, low = split(hid_1[...] + hid_2[...])
                     agg = dot(high, wo_ref[:, cols]) + dot(low, wo_ref[:, cols])
-                    new = (ext[0:cells, cols].astype(F32) + agg).astype(BF)
+                    new = (table[:, cols].astype(F32) + agg).astype(BF)
                     out = dot_tn(new, gsum[...])
                 total[r : r + n, :] = out
 
@@ -410,10 +432,11 @@
     cells = edge_sources.shape[0] // K
     half = cells // 2
     side = halo_lists.shape[0] // 2
-    rows = cells + 2 * side
     fines, coarses = lax.axis_size("fine"), lax.axis_size("coarse")
     fine_bits, coarse_bits = bits_of(fines), bits_of(coarses)
-    ids = lax.rem(cluster_ids, cells).reshape(1, nodes)
+    ids = call(
+        functools.partial(local_body, cells=cells), (sds((1, nodes), jnp.int32),), (cluster_ids.reshape(1, nodes),), AHEAD
+    )[0]
     lists = halo_lists.reshape(1, 2 * side)
     flat = edge_sources.reshape(cells * K // LANES, LANES)
     src = call(
@@ -445,28 +468,29 @@
     own_p = across(part_p, send_p, after=(own_halo, src, bias))
     other_halo = swap(own_halo, "fine", 0)
     others = [swap(x, "fine", 0) for x in (own_p[: half // 2], own_p[half // 2 :])]
-    ext, base = call(
+    near = call(near_body, (sds((K * cells, width), BF),), (own_p, src), 0, vmem=24)[0]
+    table, far, base = call(
         extend_body,
-        (sds((rows, width), BF), sds((cells, width), F32)),
+        (sds((cells, width), BF), sds((half + 2 * side, width), BF), sds((cells, width), F32)),
         (*others, own_p, own_halo, other_halo, w_edge_in, bias),
         0,
     )
 
-    def forward(first, after=()):
-        edges = K // 2 * cells
+    def forward(first, count, after=()):
+        edges = count * cells
         return call(
             functools.partial(forward_body, first=first),
             (sds((cells, width), F32), sds((edges, width), F32), sds((edges, width), BF), sds((8, LANES), F32)),
-            (ext, base, src, w_edge_in),
+            (base, far, near, src, w_edge_in),
             0,
             vmem=32,
             after=after,
         )
 
-    *front, front_token = forward(0)
+    *front, front_token = forward(0, EARLY)
     own_g = across(part_g, send_g, after=(front_token,))
     other_g = swap(own_g, "fine", 0)
-    *rear, _ = forward(K // 2, after=(own_g,))
+    *rear, _ = forward(EARLY, K - EARLY, after=(own_g,))
     per = 4 * width // fines
     first = per // 2
     act, ga, gn, keep, send, bias_sum = call(
@@ -475,7 +499,7 @@
             sds((K * cells, width), BF), sds((cells, width), F32), sds((cells, width), BF),
             sds((first, width), F32), sds((first + PACK, width), BF), sds((8, width), F32),
         ),
-        (own_g, other_g, ext, *front, *rear, w_edge_out, w_unpool),
+        (own_g, other_g, table, *front, *rear, w_edge_out, w_unpool),
         2 * K * cells * width * width,
         vmem=32,
         scratch=(pltpu.VMEM((cells, width), BF), pltpu.VMEM((per, width), F32)),

time: 53 us -> 51 us (0.962)
  waiting for transfers between devices: 14.4 us -> 13.2 us
  other arithmetic: 0.79 us -> 0 us
  Pallas kernels: 18.4 us -> 19 us
  starting transfers between devices: 17 us -> 16.4 us
    ppermute x1, starting transfers between devices: 1.9 us -> 0.7 us  [swap_both(): return lax.ppermute(x, ('coarse', 'fine'), pairs)]
    ppermute x3, starting transfers between devices: 4.11 us -> 5 us  [send_sides(): return lax.ppermute(x, ('coarse', 'fine'), pairs)]
    ppermute x16, waiting for transfers between devices: 9.67 us -> 8.85 us  [swap(): return lax.ppermute(x, axis, [(i, i ^ 1 << bit) for i in range(count)])]
    rem x1 -> x0, other arithmetic: 0.79 us -> none  [local(): ids = lax.rem(cluster_ids, cells).reshape(1, nodes)]
    pallas_call x25 -> x27, Pallas kernels: 18.4 us -> 19 us  [call(): pl.pallas_call(kernel, out_shape=outs, in_specs=[in_vmem] * count + [anyw...]
    unnamed x16 -> x18, local copies, waits for them, and re-layouts: 1.26 us -> 1.26 us
  transfers between devices with their start and end apart: 20 -> 20, of which waited for: 11 -> 10; matrix products, arithmetic and copies ran while one was open for 0% -> 0% of each run, Pallas kernels for 27% -> 30%
where the time goes in v6:
time: 51 us; the launch traced here: 50.7 us
  Pallas kernels  19 us (37%)
  starting transfers between devices  16.4 us (32%)
  waiting for transfers between devices  13.2 us (26%)
  local copies, waits for them, and re-layouts  1.28 us (3%)
  between operations  0.94 us (2%)
    pallas_call x27, Pallas kernels, call(): pl.pallas_call(kernel, out_shape=outs, in_specs=[in_vmem] * count + [anyw...  19 us
    ppermute x16, starting transfers between devices, swap(): return lax.ppermute(x, axis, [(i, i ^ 1 << bit) for i in range(count)])  10.7 us
    ppermute x16, waiting for transfers between devices, swap(): return lax.ppermute(x, axis, [(i, i ^ 1 << bit) for i in range(count)])  8.85 us
    ppermute x3, starting transfers between devices, send_sides(): return lax.ppermute(x, ('coarse', 'fine'), pairs)  5 us
    ppermute x3, waiting for transfers between devices, send_sides(): return lax.ppermute(x, ('coarse', 'fine'), pairs)  4.29 us
    unnamed x18, local copies, waits for them, and re-layouts  1.26 us
  transfers between devices with their start and end apart: 20, of which 10 were waited for; matrix products, arithmetic and copies ran while one was open for 0% of the time, Pallas kernels for 30%

profile of v6, /device:TPU:0, one launch (start us, length us, event | category | flops | bytes accessed | tf_op | source)
XLA Modules:
  0.0 50.7 jit_solution(12781073309263934120)
XLA Ops:
  0.7 0.8 %copy-done.7 = s32[2048]{0:T(1024)S(1)} copy-done((s32[2048]{0:T(1024)S(1)}, s32[2048]{0:T(1024)}, u32[]{:S(2)}) %copy-start.7) | copy-done | bytes 8216
  1.4 0.4 copy-done.6
  1.9 1.2 %shard_map.131 = (f32[512,256]{1,0:T(8,128)S(1)}, f32[512,256]{1,0:T(8,128)S(1)}) custom-call(s32[1,2048]{1,0:T(1,128)S(1)} %shard_map.128.refs_0_.refs_1_, bf16[2048,256]{1,0:T(8,128)(2,1)S(1)} %copy-done.6), custom_call_target="tpu_custom_call" | custom-call | flops 1073741824 | bytes 2105344 | tf_op jit(solution)/shard_map/pallas_call | solution.py:70
  3.2 0.5 %collective-permute-start.2 = (f32[512,256]{1,0:T(8,128)S(1)}, f32[512,256]{1,0:T(8,128)S(1)}, u32[]{:S(2)}, u32[]{:S(2)}) collective-permute-start(f32[512,256]{1,0:T(8,128)S(1)} %get-tuple-element.48), channel_id=1, source_target_pairs={{0,1},{1,0},{2,3},{3,2},{4,5},{5,4},{6,7},{7,6},{8,9},{9,8},{10,11... | collective-permute-start | bytes 1572872 | tf_op jit(solution)/shard_map/ppermute | solution.py:39
  3.7 1.2 %shard_map.129 = (f32[512,256]{1,0:T(8,128)S(1)}, f32[512,256]{1,0:T(8,128)S(1)}) custom-call(s32[1,2048]{1,0:T(1,128)S(1)} %shard_map.128.refs_0_.refs_1_, bf16[2048,256]{1,0:T(8,128)(2,1)S(1)} %copy-done.1), custom_call_target="tpu_custom_call" | custom-call | flops 1073741824 | bytes 2105344 | tf_op jit(solution)/shard_map/pallas_call | solution.py:70
  5.3 3.0 %collective-permute-start.3 = (bf16[512,256]{1,0:T(8,128)(2,1)S(1)}, bf16[512,256]{1,0:T(8,128)(2,1)S(1)}, u32[]{:S(2)}, u32[]{:S(2)}) collective-permute-start(bf16[512,256]{1,0:T(8,128)(2,1)S(1)} %get-tuple-element.50.refs_0_), channel_id=1, source_target_pairs={{0,2},{1,3},{2,0},{3,1},{4,6},{5,7},{6,4},{7,5},{8,10},{9,11},{10,... | collective-permute-start | bytes 786440 | tf_op jit(solution)/shard_map/ppermute | solution.py:39
  8.6 1.2 %collective-permute-done.4.refs_1_ = bf16[128,256]{1,0:T(8,128)(2,1)S(1)} collective-permute-done((bf16[128,256]{1,0:T(8,128)(2,1)S(1)}, bf16[128,256]{1,0:T(8,128)(2,1)S(1)}, u32[]{:S(2)}, u32[]{:S(2)}) %collective-permute-start.4) | collective-permute-done | bytes 65568 | tf_op jit(solution)/shard_map/ppermute | solution.py:39
  9.8 1.4 %collective-permute-start.6 = (bf16[64,256]{1,0:T(8,128)(2,1)S(1)}, bf16[64,256]{1,0:T(8,128)(2,1)S(1)}, u32[]{:S(2)}, u32[]{:S(2)}) collective-permute-start(bf16[64,256]{1,0:T(8,128)(2,1)S(1)} %shard_map.134), channel_id=1, source_target_pairs={{0,6},{1,31},{2,4},{3,29},{4,10},{5,3},{6,8},{7,1},{8,14},{9,7},{1... | collective-permute-start | bytes 98312 | tf_op jit(solution)/shard_map/ppermute | solution.py:55
  11.2 1.5 %collective-permute-start.5 = (bf16[64,256]{1,0:T(8,128)(2,1)S(1)}, bf16[64,256]{1,0:T(8,128)(2,1)S(1)}, u32[]{:S(2)}, u32[]{:S(2)}) collective-permute-start(bf16[64,256]{1,0:T(8,128)(2,1)S(1)} %shard_map.134), channel_id=1, source_target_pairs={{0,4},{1,29},{2,6},{3,31},{4,8},{5,1},{6,10},{7,3},{8,12},{9,5},{1... | collective-permute-start | bytes 98312 | tf_op jit(solution)/shard_map/ppermute | solution.py:55
  13.2 1.6 %collective-permute-start.1 = (bf16[512,256]{1,0:T(8,128)(2,1)S(1)}, bf16[512,256]{1,0:T(8,128)(2,1)S(1)}, u32[]{:S(2)}, u32[]{:S(2)}) collective-permute-start(bf16[512,256]{1,0:T(8,128)(2,1)S(1)} %get-tuple-element.46), channel_id=1, source_target_pairs={{0,2},{1,3},{2,0},{3,1},{4,6},{5,7},{6,4},{7,5},{8,10},{9,11},{10,... | collective-permute-start | bytes 786440 | tf_op jit(solution)/shard_map/ppermute | solution.py:39
  14.8 2.7 %collective-permute-done.6.refs_1_ = bf16[64,256]{1,0:T(8,128)(2,1)S(1)} collective-permute-done((bf16[64,256]{1,0:T(8,128)(2,1)S(1)}, bf16[64,256]{1,0:T(8,128)(2,1)S(1)}, u32[]{:S(2)}, u32[]{:S(2)}) %collective-permute-start.6) | collective-permute-done | bytes 32800 | tf_op jit(solution)/shard_map/ppermute | solution.py:55
  18.1 0.5 collective-permute-start.7
  18.6 1.5 %shard_map.139.refs_2_ = bf16[4096,256]{1,0:T(8,128)(2,1)S(1)} custom-call(bf16[512,256]{1,0:T(8,128)(2,1)S(1)} %shard_map.137.refs_2_.refs_0_, s32[4,1024]{1,0:T(4,128)S(1)} %shard_map.136.refs_3_.refs_1_), custom_call_target="tpu_custom_call" | custom-call | tf_op jit(solution)/shard_map/pallas_call | solution.py:70
  20.5 2.5 %shard_map.140 = (f32[1024,256]{1,0:T(8,128)S(1)}, f32[3072,256]{1,0:T(8,128)S(1)}, bf16[3072,256]{1,0:T(8,128)(2,1)S(1)}, f32[8,128]{1,0:T(8,128)S(1)}) custom-call(f32[1024,256]{1,0:T(8,128)S(1)} %get-tuple-element.51.refs_0_, bf16[640,256]{1,0:T(8,128)(2,1)S(1)} %get-tuple-element.52.refs_1_, bf16[4096,256]{1,0:T(8,128)(2,1)S(1)} %shard_map.139.refs_2_, ...), custom_call_target="tpu_custom_call" | custom-call | tf_op jit(solution)/shard_map/pallas_call | solution.py:70
  23.1 0.5 collective-permute-start.10
  23.6 1.5 %shard_map.142 = (f32[1024,256]{1,0:T(8,128)S(1)}, f32[1024,256]{1,0:T(8,128)S(1)}, bf16[1024,256]{1,0:T(8,128)(2,1)S(1)}, f32[8,128]{1,0:T(8,128)}) custom-call(f32[1024,256]{1,0:T(8,128)S(1)} %get-tuple-element.51.refs_0_, bf16[640,256]{1,0:T(8,128)(2,1)S(1)} %get-tuple-element.52.refs_1_, bf16[4096,256]{1,0:T(8,128)(2,1)S(1)} %shard_map.139.refs_2_, ...), custom_call_target="tpu_custom_call" | custom-call | tf_op jit(solution)/shard_map/pallas_call | solution.py:70
  25.2 1.5 %shard_map.143 = (bf16[4096,256]{1,0:T(8,128)(2,1)S(1)}, f32[1024,256]{1,0:T(8,128)S(1)}, bf16[1024,256]{1,0:T(8,128)(2,1)S(1)}, f32[128,256]{1,0:T(8,128)S(1)},...) custom-call(bf16[512,256]{1,0:T(8,128)(2,1)S(1)} %shard_map.141.refs_5_.refs_0_, ...), custom_call_target="tpu_custom_call" | custom-call | flops 536870912 | bytes 13582336 | tf_op jit(solution)/shard_map/pallas_call | solution.py:70
  27.0 0.6 %shard_map.146.refs_3_ = bf16[64,256]{1,0:T(8,128)(2,1)S(1)} custom-call(bf16[4096,256]{1,0:T(8,128)(2,1)S(1)} %get-tuple-element.61.refs_0_, s32[4,1024]{1,0:T(4,128)S(1)} %shard_map.136.refs_3_.refs_1_, bf16[512,256]{1,0:T(8,128)(2,1)S(1)} %copy-done), custom_call_target="tpu_custom_call" | custom-call | flops 268435456 | bytes 2408448 | tf_op jit(solution)/shard_map/pallas_call | solution.py:70
  27.6 2.0 %collective-permute-start.11 = (bf16[64,256]{1,0:T(8,128)(2,1)S(1)}, bf16[64,256]{1,0:T(8,128)(2,1)S(1)}, u32[]{:S(2)}, u32[]{:S(2)}) collective-permute-start(bf16[64,256]{1,0:T(8,128)(2,1)S(1)} %shard_map.146.refs_3_), channel_id=1, source_target_pairs={{0,4},{1,29},{2,6},{3,31},{4,8},{5,1},{6,10},{7,3},{8,12},{9,5},{1... | collective-permute-start | bytes 98312 | tf_op jit(solution)/shard_map/ppermute | solution.py:55
  29.7 2.0 %collective-permute-done.13.refs_1_ = bf16[144,256]{1,0:T(8,128)(2,1)S(1)} collective-permute-done((bf16[144,256]{1,0:T(8,128)(2,1)S(1)}, bf16[144,256]{1,0:T(8,128)(2,1)S(1)}, u32[]{:S(2)}, u32[]{:S(2)}) %collective-permute-start.13) | collective-permute-done | bytes 73760 | tf_op jit(solution)/shard_map/ppermute | solution.py:39
  31.8 1.5 %shard_map.144.refs_0_.refs_3_ = f32[512,256]{1,0:T(8,128)S(1)} custom-call(bf16[4096,256]{1,0:T(8,128)(2,1)S(1)} %get-tuple-element.61.refs_0_, s32[4,1024]{1,0:T(4,128)S(1)} %shard_map.136.refs_3_.refs_1_, f32[1024,256]{1,0:T(8,128)S(1)} %get-tuple-element.62.refs_2_, bf16[1024,256]{1,0:T(8,128)(2,1)S(1)} %get-tuple-element.63.refs_3_, ...), custom_call_target="tpu_custom_call" | custom-call | flops 1073741824 | bytes 4472832 | tf_op jit(solution)/shard_map/pallas_call | solution.py:70
  33.3 1.2 %collective-permute-done.11.refs_2_ = bf16[64,256]{1,0:T(8,128)(2,1)S(1)} collective-permute-done((bf16[64,256]{1,0:T(8,128)(2,1)S(1)}, bf16[64,256]{1,0:T(8,128)(2,1)S(1)}, u32[]{:S(2)}, u32[]{:S(2)}) %collective-permute-start.11) | collective-permute-done | bytes 32800 | tf_op jit(solution)/shard_map/ppermute | solution.py:55
  34.5 1.6 %collective-permute-done.14.refs_1_ = bf16[144,256]{1,0:T(8,128)(2,1)S(1)} collective-permute-done((bf16[144,256]{1,0:T(8,128)(2,1)S(1)}, bf16[144,256]{1,0:T(8,128)(2,1)S(1)}, u32[]{:S(2)}, u32[]{:S(2)}) %collective-permute-start.14) | collective-permute-done | bytes 73760 | tf_op jit(solution)/shard_map/ppermute | solution.py:39
  36.1 1.0 %collective-permute-start.15 = (bf16[144,256]{1,0:T(8,128)(2,1)S(1)}, bf16[144,256]{1,0:T(8,128)(2,1)S(1)}, u32[]{:S(2)}, u32[]{:S(2)}) collective-permute-start(bf16[144,256]{1,0:T(8,128)(2,1)S(1)} %get-tuple-element.71), channel_id=1, source_target_pairs={{0,16},{4,20},{8,24},{12,28},{16,0},{20,4},{24,8},{28,12},{1,17},{... | collective-permute-start | bytes 221192 | tf_op jit(solution)/shard_map/ppermute | solution.py:39
  37.1 1.5 %shard_map.145.refs_1_.refs_3_ = f32[512,256]{1,0:T(8,128)S(1)} custom-call(bf16[4096,256]{1,0:T(8,128)(2,1)S(1)} %get-tuple-element.61.refs_0_, s32[4,1024]{1,0:T(4,128)S(1)} %shard_map.136.refs_3_.refs_1_, f32[1024,256]{1,0:T(8,128)S(1)} %get-tuple-element.62.refs_2_, bf16[1024,256]{1,0:T(8,128)(2,1)S(1)} %get-tuple-element.63.refs_3_, ...), custom_call_target="tpu_custom_call" | custom-call | flops 1073741824 | bytes 4472832 | tf_op jit(solution)/shard_map/pallas_call | solution.py:70
  38.6 3.1 %collective-permute-done.15.refs_1_ = bf16[144,256]{1,0:T(8,128)(2,1)S(1)} collective-permute-done((bf16[144,256]{1,0:T(8,128)(2,1)S(1)}, bf16[144,256]{1,0:T(8,128)(2,1)S(1)}, u32[]{:S(2)}, u32[]{:S(2)}) %collective-permute-start.15) | collective-permute-done | bytes 73760 | tf_op jit(solution)/shard_map/ppermute | solution.py:39
  41.8 0.7 %collective-permute-start.18 = (bf16[144,256]{1,0:T(8,128)(2,1)S(1)}, bf16[144,256]{1,0:T(8,128)(2,1)S(1)}, u32[]{:S(2)}, u32[]{:S(2)}) collective-permute-start(bf16[144,256]{1,0:T(8,128)(2,1)S(1)} %shard_map.150.refs_0_), channel_id=1, source_target_pairs={{0,6},{1,7},{2,4},{3,5},{4,2},{5,3},{6,0},{7,1},{8,14},{9,15},{10,... | collective-permute-start | bytes 221192 | tf_op jit(solution)/shard_map/ppermute | solution.py:45
  42.5 1.0 %collective-permute-start.17 = (bf16[144,256]{1,0:T(8,128)(2,1)S(1)}, bf16[144,256]{1,0:T(8,128)(2,1)S(1)}, u32[]{:S(2)}, u32[]{:S(2)}) collective-permute-start(bf16[144,256]{1,0:T(8,128)(2,1)S(1)} %shard_map.150.refs_0_), channel_id=1, source_target_pairs={{0,2},{1,3},{2,0},{3,1},{4,6},{5,7},{6,4},{7,5},{8,10},{9,11},{10,... | collective-permute-start | bytes 221192 | tf_op jit(solution)/shard_map/ppermute | solution.py:39
  43.5 1.9 %collective-permute-start.16 = (bf16[144,256]{1,0:T(8,128)(2,1)S(1)}, bf16[144,256]{1,0:T(8,128)(2,1)S(1)}, u32[]{:S(2)}, u32[]{:S(2)}) collective-permute-start(bf16[144,256]{1,0:T(8,128)(2,1)S(1)} %shard_map.150.refs_0_), channel_id=1, source_target_pairs={{0,4},{4,0},{8,12},{12,8},{16,20},{20,16},{24,28},{28,24},{1,5},{5... | collective-permute-start | bytes 221192 | tf_op jit(solution)/shard_map/ppermute | solution.py:39
  45.7 1.6 %shard_map.151 = (bf16[2048,256]{1,0:T(8,128)(2,1)}, f32[8,128]{1,0:T(8,128)S(1)}) custom-call(bf16[1024,256]{1,0:T(8,128)(2,1)S(1)} %shard_map.147.refs_0_, s32[1,2048]{1,0:T(1,128)S(1)} %shard_map.128.refs_0_.refs_1_, bf16[2048,256]{1,0:T(8,128)(2,1)S(1)} %copy-done.1), custom_call_target="tpu_custom_call" | custom-call | flops 536870912 | bytes 2633728 | tf_op jit(solution)/shard_map/pallas_call | solution.py:70
  48.1 1.6 %shard_map.153 = (bf16[2048,256]{1,0:T(8,128)(2,1)}, f32[8,128]{1,0:T(8,128)S(1)}) custom-call(bf16[1024,256]{1,0:T(8,128)(2,1)S(1)} %shard_map.147.refs_0_, s32[1,2048]{1,0:T(1,128)S(1)} %shard_map.128.refs_0_.refs_1_, bf16[2048,256]{1,0:T(8,128)(2,1)S(1)} %copy-done.1, ...), custom_call_target="tpu_custom_call", output_to_operand_aliasing={{0}: (4, {})} | custom-call | flops 536870912 | bytes 2633728 | tf_op jit(solution)/shard_map/pallas_call | solution.py:70
  49.7 1.1 %shard_map.154 = (f32[512,256]{1,0:T(8,128)}, f32[1,256]{1,0:T(1,128)}, f32[256,256]{1,0:T(8,128)}, f32[256,256]{1,0:T(8,128)}) custom-call(bf16[544,256]{1,0:T(8,128)(2,1)S(1)} %shard_map.152.refs_3_.refs_0_, bf16[544,256]{1,0:T(8,128)(2,1)S(1)} %collective-permute-done.19.refs_1_, f32[8,128]{1,0:T(8,128)S(1)} %get-tuple-element.76.refs_2_), custom_call_target="tpu_custom_call" | custom-call | tf_op jit(solution)/shard_map/pallas_call | solution.py:70
  (55 shorter events, 3.8 us)
Async XLA Ops:
  0.6 1.2 %copy-start.6 = (bf16[2048,256]{1,0:T(8,128)(2,1)S(1)}, bf16[2048,256]{1,0:T(8,128)(2,1)}, u32[]{:S(2)}) copy-start(bf16[2048,256]{1,0:T(8,128)(2,1)} %refs_1_.3) | copy-start | bytes 3145732
  0.6 0.8 %copy-start.7 = (s32[2048]{0:T(1024)S(1)}, s32[2048]{0:T(1024)}, u32[]{:S(2)}) copy-start(s32[2048]{0:T(1024)} %param.11) | copy-start | bytes 24580
  1.9 1.8 %copy-start.1 = (bf16[2048,256]{1,0:T(8,128)(2,1)S(1)}, bf16[2048,256]{1,0:T(8,128)(2,1)}, u32[]{:S(2)}) copy-start(bf16[2048,256]{1,0:T(8,128)(2,1)} %refs_2_.5) | copy-start | bytes 3145732
  3.1 5.1 %copy-start.5 = (s32[128]{0:T(128)S(1)}, s32[128]{0:T(128)}, u32[]{:S(2)}) copy-start(s32[128]{0:T(128)} %param.12) | copy-start | bytes 1540
  3.1 9.7 %copy-start.8 = (bf16[256]{0:T(256)(128)(2,1)S(1)}, bf16[256]{0:T(256)(128)(2,1)}, u32[]{:S(2)}) copy-start(bf16[256]{0:T(256)(128)(2,1)} %param.15) | copy-start | bytes 1540
  3.1 9.7 %copy-start.4 = (s32[4096]{0:T(1024)S(1)}, s32[4096]{0:T(1024)}, u32[]{:S(2)}) copy-start(s32[4096]{0:T(1024)} %param.13) | copy-start | bytes 49156
  3.2 2.1 %collective-permute-start.2 = (f32[512,256]{1,0:T(8,128)S(1)}, f32[512,256]{1,0:T(8,128)S(1)}, u32[]{:S(2)}, u32[]{:S(2)}) collective-permute-start(f32[512,256]{1,0:T(8,128)S(1)} %get-tuple-element.48), channel_id=1, source_target_pairs={{0,1},{1,0},{2,3},{3,2},{4,5},{5,4},{6,7},{7,6},{8,9},{9,8},{10,11... | collective-permute-start | bytes 1572872 | tf_op jit(solution)/shard_map/ppermute | solution.py:39
  4.9 8.1 %collective-permute-start = (f32[512,256]{1,0:T(8,128)S(1)}, f32[512,256]{1,0:T(8,128)S(1)}, u32[]{:S(2)}, u32[]{:S(2)}) collective-permute-start(f32[512,256]{1,0:T(8,128)S(1)} %get-tuple-element.44), channel_id=1, source_target_pairs={{0,1},{1,0},{2,3},{3,2},{4,5},{5,4},{6,7},{7,6},{8,9},{9,8},{10,11... | collective-permute-start | bytes 1572872 | tf_op jit(solution)/shard_map/ppermute | solution.py:39
  5.3 12.6 %collective-permute-start.3 = (bf16[512,256]{1,0:T(8,128)(2,1)S(1)}, bf16[512,256]{1,0:T(8,128)(2,1)S(1)}, u32[]{:S(2)}, u32[]{:S(2)}) collective-permute-start(bf16[512,256]{1,0:T(8,128)(2,1)S(1)} %get-tuple-element.50.refs_0_), channel_id=1, source_target_pairs={{0,2},{1,3},{2,0},{3,1},{4,6},{5,7},{6,4},{7,5},{8,10},{9,11},{10,... | collective-permute-start | bytes 786440 | tf_op jit(solution)/shard_map/ppermute | solution.py:39
  8.5 1.3 %collective-permute-start.4 = (bf16[128,256]{1,0:T(8,128)(2,1)S(1)}, bf16[128,256]{1,0:T(8,128)(2,1)S(1)}, u32[]{:S(2)}, u32[]{:S(2)}) collective-permute-start(bf16[128,256]{1,0:T(8,128)(2,1)S(1)} %shard_map.133.refs_0_), channel_id=1, source_target_pairs={{0,1},{1,0},{2,3},{3,2},{4,5},{5,4},{6,7},{7,6},{8,9},{9,8},{10,11... | collective-permute-start | bytes 196616 | tf_op jit(solution)/shard_map/ppermute | solution.py:39
  9.8 7.6 %collective-permute-start.6 = (bf16[64,256]{1,0:T(8,128)(2,1)S(1)}, bf16[64,256]{1,0:T(8,128)(2,1)S(1)}, u32[]{:S(2)}, u32[]{:S(2)}) collective-permute-start(bf16[64,256]{1,0:T(8,128)(2,1)S(1)} %shard_map.134), channel_id=1, source_target_pairs={{0,6},{1,31},{2,4},{3,29},{4,10},{5,3},{6,8},{7,1},{8,14},{9,7},{1... | collective-permute-start | bytes 98312 | tf_op jit(solution)/shard_map/ppermute | solution.py:55
  11.2 6.6 %collective-permute-start.5 = (bf16[64,256]{1,0:T(8,128)(2,1)S(1)}, bf16[64,256]{1,0:T(8,128)(2,1)S(1)}, u32[]{:S(2)}, u32[]{:S(2)}) collective-permute-start(bf16[64,256]{1,0:T(8,128)(2,1)S(1)} %shard_map.134), channel_id=1, source_target_pairs={{0,4},{1,29},{2,6},{3,31},{4,8},{5,1},{6,10},{7,3},{8,12},{9,5},{1... | collective-permute-start | bytes 98312 | tf_op jit(solution)/shard_map/ppermute | solution.py:55
  13.2 7.0 %copy-start = (bf16[512,256]{1,0:T(8,128)(2,1)S(1)}, bf16[512,256]{1,0:T(8,128)(2,1)}, u32[]{:S(2)}) copy-start(bf16[512,256]{1,0:T(8,128)(2,1)} %refs_2_.3) | copy-start | bytes 786436
  13.2 9.9 %collective-permute-start.1 = (bf16[512,256]{1,0:T(8,128)(2,1)S(1)}, bf16[512,256]{1,0:T(8,128)(2,1)S(1)}, u32[]{:S(2)}, u32[]{:S(2)}) collective-permute-start(bf16[512,256]{1,0:T(8,128)(2,1)S(1)} %get-tuple-element.46), channel_id=1, source_target_pairs={{0,2},{1,3},{2,0},{3,1},{4,6},{5,7},{6,4},{7,5},{8,10},{9,11},{10,... | collective-permute-start | bytes 786440 | tf_op jit(solution)/shard_map/ppermute | solution.py:39
  18.0 2.2 %collective-permute-start.8 = (bf16[256,256]{1,0:T(8,128)(2,1)S(1)}, bf16[256,256]{1,0:T(8,128)(2,1)S(1)}, u32[]{:S(2)}, u32[]{:S(2)}) collective-permute-start(bf16[256,256]{1,0:T(8,128)(2,1)S(1)} %get-tuple-element.81), channel_id=1, source_target_pairs={{0,1},{1,0},{2,3},{3,2},{4,5},{5,4},{6,7},{7,6},{8,9},{9,8},{10,11... | collective-permute-start | bytes 393224 | tf_op jit(solution)/shard_map/ppermute | solution.py:39
  18.1 2.1 %collective-permute-start.7 = (bf16[256,256]{1,0:T(8,128)(2,1)S(1)}, bf16[256,256]{1,0:T(8,128)(2,1)S(1)}, u32[]{:S(2)}, u32[]{:S(2)}) collective-permute-start(bf16[256,256]{1,0:T(8,128)(2,1)S(1)} %get-tuple-element.82), channel_id=1, source_target_pairs={{0,1},{1,0},{2,3},{3,2},{4,5},{5,4},{6,7},{7,6},{8,9},{9,8},{10,11... | collective-permute-start | bytes 393224 | tf_op jit(solution)/shard_map/ppermute | solution.py:39
  18.6 1.6 %collective-permute-start.9 = (bf16[64,256]{1,0:T(8,128)(2,1)S(1)}, bf16[64,256]{1,0:T(8,128)(2,1)S(1)}, u32[]{:S(2)}, u32[]{:S(2)}) collective-permute-start(bf16[64,256]{1,0:T(8,128)(2,1)S(1)} %shard_map.135.refs_2_.refs_3_), channel_id=1, source_target_pairs={{0,1},{1,0},{2,3},{3,2},{4,5},{5,4},{6,7},{7,6},{8,9},{9,8},{10,11... | collective-permute-start | bytes 98312 | tf_op jit(solution)/shard_map/ppermute | solution.py:39
  23.1 2.1 %copy-start.2 = (bf16[256,256]{1,0:T(8,128)(2,1)S(1)}, bf16[256,256]{1,0:T(8,128)(2,1)}, u32[]{:S(2)}) copy-start(bf16[256,256]{1,0:T(8,128)(2,1)} %refs_9_.1) | copy-start | bytes 393220
  23.1 2.1 %copy-start.3 = (bf16[256,256]{1,0:T(8,128)(2,1)S(1)}, bf16[256,256]{1,0:T(8,128)(2,1)}, u32[]{:S(2)}) copy-start(bf16[256,256]{1,0:T(8,128)(2,1)} %refs_10_.1) | copy-start | bytes 393220
  23.1 2.0 %collective-permute-start.10 = (bf16[512,256]{1,0:T(8,128)(2,1)S(1)}, bf16[512,256]{1,0:T(8,128)(2,1)S(1)}, u32[]{:S(2)}, u32[]{:S(2)}) collective-permute-start(bf16[512,256]{1,0:T(8,128)(2,1)S(1)} %shard_map.141.refs_5_.refs_0_), channel_id=1, source_target_pairs={{0,1},{1,0},{2,3},{3,2},{4,5},{5,4},{6,7},{7,6},{8,9},{9,8},{10,11... | collective-permute-start | bytes 786440 | tf_op jit(solution)/shard_map/ppermute | solution.py:39
  26.7 4.9 %collective-permute-start.13 = (bf16[144,256]{1,0:T(8,128)(2,1)S(1)}, bf16[144,256]{1,0:T(8,128)(2,1)S(1)}, u32[]{:S(2)}, u32[]{:S(2)}) collective-permute-start(bf16[144,256]{1,0:T(8,128)(2,1)S(1)} %get-tuple-element.65), channel_id=1, source_target_pairs={{0,4},{4,0},{8,12},{12,8},{16,20},{20,16},{24,28},{28,24},{1,5},{5... | collective-permute-start | bytes 221192 | tf_op jit(solution)/shard_map/ppermute | solution.py:39
  27.6 6.8 %collective-permute-start.11 = (bf16[64,256]{1,0:T(8,128)(2,1)S(1)}, bf16[64,256]{1,0:T(8,128)(2,1)S(1)}, u32[]{:S(2)}, u32[]{:S(2)}) collective-permute-start(bf16[64,256]{1,0:T(8,128)(2,1)S(1)} %shard_map.146.refs_3_), channel_id=1, source_target_pairs={{0,4},{1,29},{2,6},{3,31},{4,8},{5,1},{6,10},{7,3},{8,12},{9,5},{1... | collective-permute-start | bytes 98312 | tf_op jit(solution)/shard_map/ppermute | solution.py:55
  31.7 4.4 %collective-permute-start.14 = (bf16[144,256]{1,0:T(8,128)(2,1)S(1)}, bf16[144,256]{1,0:T(8,128)(2,1)S(1)}, u32[]{:S(2)}, u32[]{:S(2)}) collective-permute-start(bf16[144,256]{1,0:T(8,128)(2,1)S(1)} %get-tuple-element.68), channel_id=1, source_target_pairs={{0,8},{4,12},{8,0},{12,4},{16,24},{20,28},{24,16},{28,20},{1,9},{5... | collective-permute-start | bytes 221192 | tf_op jit(solution)/shard_map/ppermute | solution.py:39
  34.5 4.2 %collective-permute-start.12 = (bf16[64,256]{1,0:T(8,128)(2,1)S(1)}, bf16[64,256]{1,0:T(8,128)(2,1)S(1)}, u32[]{:S(2)}, u32[]{:S(2)}) collective-permute-start(bf16[64,256]{1,0:T(8,128)(2,1)S(1)} %collective-permute-done.11.refs_2_), channel_id=1, source_target_pairs={{0,1},{1,0},{2,3},{3,2},{4,5},{5,4},{6,7},{7,6},{8,9},{9,8},{10,11... | collective-permute-start | bytes 98312 | tf_op jit(solution)/shard_map/ppermute | solution.py:39
  36.1 5.6 %collective-permute-start.15 = (bf16[144,256]{1,0:T(8,128)(2,1)S(1)}, bf16[144,256]{1,0:T(8,128)(2,1)S(1)}, u32[]{:S(2)}, u32[]{:S(2)}) collective-permute-start(bf16[144,256]{1,0:T(8,128)(2,1)S(1)} %get-tuple-element.71), channel_id=1, source_target_pairs={{0,16},{4,20},{8,24},{12,28},{16,0},{20,4},{24,8},{28,12},{1,17},{... | collective-permute-start | bytes 221192 | tf_op jit(solution)/shard_map/ppermute | solution.py:39
  41.8 5.5 %collective-permute-start.18 = (bf16[144,256]{1,0:T(8,128)(2,1)S(1)}, bf16[144,256]{1,0:T(8,128)(2,1)S(1)}, u32[]{:S(2)}, u32[]{:S(2)}) collective-permute-start(bf16[144,256]{1,0:T(8,128)(2,1)S(1)} %shard_map.150.refs_0_), channel_id=1, source_target_pairs={{0,6},{1,7},{2,4},{3,5},{4,2},{5,3},{6,0},{7,1},{8,14},{9,15},{10,... | collective-permute-start | bytes 221192 | tf_op jit(solution)/shard_map/ppermute | solution.py:45
  42.5 5.1 %collective-permute-start.17 = (bf16[144,256]{1,0:T(8,128)(2,1)S(1)}, bf16[144,256]{1,0:T(8,128)(2,1)S(1)}, u32[]{:S(2)}, u32[]{:S(2)}) collective-permute-start(bf16[144,256]{1,0:T(8,128)(2,1)S(1)} %shard_map.150.refs_0_), channel_id=1, source_target_pairs={{0,2},{1,3},{2,0},{3,1},{4,6},{5,7},{6,4},{7,5},{8,10},{9,11},{10,... | collective-permute-start | bytes 221192 | tf_op jit(solution)/shard_map/ppermute | solution.py:39
  43.5 4.5 %collective-permute-start.16 = (bf16[144,256]{1,0:T(8,128)(2,1)S(1)}, bf16[144,256]{1,0:T(8,128)(2,1)S(1)}, u32[]{:S(2)}, u32[]{:S(2)}) collective-permute-start(bf16[144,256]{1,0:T(8,128)(2,1)S(1)} %shard_map.150.refs_0_), channel_id=1, source_target_pairs={{0,4},{4,0},{8,12},{12,8},{16,20},{20,16},{24,28},{28,24},{1,5},{5... | collective-permute-start | bytes 221192 | tf_op jit(solution)/shard_map/ppermute | solution.py:39
  48.0 1.7 %collective-permute-start.19 = (bf16[544,256]{1,0:T(8,128)(2,1)S(1)}, bf16[544,256]{1,0:T(8,128)(2,1)S(1)}, u32[]{:S(2)}, u32[]{:S(2)}) collective-permute-start(bf16[544,256]{1,0:T(8,128)(2,1)S(1)} %shard_map.152.refs_3_.refs_0_), channel_id=1, source_target_pairs={{0,1},{1,0},{2,3},{3,2},{4,5},{5,4},{6,7},{7,6},{8,9},{9,8},{10,11... | collective-permute-start | bytes 835592 | tf_op jit(solution)/shard_map/ppermute | solution.py:39

commit v7 on v6

--- a/solution.py
+++ b/solution.py
@@ -8,7 +8,7 @@
 from jax.sharding import PartitionSpec as P
 
 K = 4
-EARLY = 3
+EARLY = 2
 BF = jnp.bfloat16
 F32 = jnp.float32
 LANES = 128
@@ -130,15 +130,20 @@
             out_ref[k : k + 1, q * LANES : (q + 1) * LANES] = rows[q : q + 1, :]
 
 
-def pool_body(ids_ref, x_ref, keep_ref, send_ref):
+def pool_body(ids_ref, x_ref, keep_ref, *send_refs):
     half = keep_ref.shape[0]
+    n = half // len(send_refs)
     core = lax.axis_index("fine") % 2
     ids = ids_ref[...]
     x = x_ref[...]
+    core_rows = (1 - core) * half
+    for i, ref in enumerate(send_refs):
+        step = min(256, n)
+        for t in range(0, n, step):
+            ref[t : t + step, :] = dot(hot_columns(ids, step, core_rows + i * n + t), x)
     step = min(256, half)
-    for out_ref, base in ((send_ref, (1 - core) * half), (keep_ref, core * half)):
-        for t in range(0, half, step):
-            out_ref[t : t + step, :] = dot(hot_columns(ids, step, base + t), x)
+    for t in range(0, half, step):
+        keep_ref[t : t + step, :] = dot(hot_columns(ids, step, core * half + t), x)
 
 
 def pick_body(part_ref, lists_ref, out_ref):
@@ -165,10 +170,14 @@
     out_ref[...] = total.astype(BF)
 
 
-def chip_body(keep, recv, part_ref, send_ref):
-    total = keep[...] + recv[...]
-    part_ref[...] = total
-    send_ref[...] = total.astype(BF)
+def chip_body(keep, *refs):
+    *recvs, part_ref, send_ref = refs
+    n = keep.shape[0] // len(recvs)
+    for i, recv in enumerate(recvs):
+        at = slice(i * n, (i + 1) * n)
+        total = keep[at, :] + recv[...]
+        part_ref[at, :] = total
+        send_ref[at, :] = total.astype(BF)
 
 
 def across_body(part, recv, *out_refs):
@@ -211,11 +220,12 @@
     base[...] = dot(table[...], w1_ref[0:width, :]) + b_ref[...].astype(F32)
 
 
-def forward_body(base, far, near, src_ref, w1_ref, hid, slope, feats, token_ref, *, first):
+def forward_body(base, far, near, src_ref, w1_ref, hid, slope, feats, *tokens, first):
     cells, width = base.shape
     half = cells // 2
     core = lax.axis_index("fine") % 2
-    token_ref[...] = jnp.zeros_like(token_ref)
+    for ref in tokens:
+        ref[...] = jnp.zeros_like(ref)
     block = 512
     for i in range(slope.shape[0] // cells):
         for t in range(0, cells, block):
@@ -444,10 +454,11 @@
     )[0]
     bias = b_edge_in.reshape(1, width)
 
-    def pool(x):
-        keep, send = call(pool_body, (sds((half, width), F32),) * 2, (ids, x), 2 * nodes * cells * width)
+    def pool(x, pieces):
+        outs = (sds((half, width), F32),) + (sds((half // pieces, width), F32),) * pieces
+        keep, *sends = call(pool_body, outs, (ids, x), 2 * nodes * cells * width)
         outs = (sds((half, width), F32), sds((half, width), BF))
-        return call(chip_body, outs, (keep, swap(send, "fine", 0)), 0)
+        return call(chip_body, outs, (keep, *[swap(send, "fine", 0) for send in sends]), 0)
 
     def across(part, send, after=()):
         for bit in range(1, fine_bits):
@@ -457,8 +468,8 @@
             part, send = (*call(across_body, outs, (part, recv), 0, after=after), None)[:2]
         return part
 
-    part_p, send_p = pool(node_feats)
-    part_g, send_g = pool(grad_out)
+    part_p, send_p = pool(node_feats, 1)
+    part_g, send_g = pool(grad_out, 4)
     picked = call(pick_body, (sds((2 * side, width), BF),), (send_p, lists), 0)[0]
     sent = call(side_body, (sds((side, width), BF),), (picked, swap(picked, "fine", 0)), 0)[0]
     own_halo = call(
@@ -476,21 +487,21 @@
         0,
     )
 
-    def forward(first, count, after=()):
+    def forward(first, count, after=(), tokens=()):
         edges = count * cells
         return call(
             functools.partial(forward_body, first=first),
-            (sds((cells, width), F32), sds((edges, width), F32), sds((edges, width), BF), sds((8, LANES), F32)),
+            (sds((cells, width), F32), sds((edges, width), F32), sds((edges, width), BF), *tokens),
             (base, far, near, src, w_edge_in),
             0,
             vmem=32,
             after=after,
         )
 
-    *front, front_token = forward(0, EARLY)
+    *front, front_token = forward(0, EARLY, tokens=(sds((8, LANES), F32),))
     own_g = across(part_g, send_g, after=(front_token,))
     other_g = swap(own_g, "fine", 0)
-    *rear, _ = forward(EARLY, K - EARLY, after=(own_g,))
+    rear = forward(EARLY, K - EARLY, after=(own_g,))
     per = 4 * width // fines
     first = per // 2
     act, ga, gn, keep, send, bias_sum = call(
@@ -549,12 +560,13 @@
             after=after.get(bit, ()),
         )
     recv = swap(send, "coarse", coarse_bits - 1)
+    front_rows = nodes // 4
+    grad_feats, feats_token = feats(0, front_rows)
     part = call(
         end_body, (sds((first + PACK, width), BF),), (keep, recv, bias_sum), 0,
-        after=(cell_grads[1], other_back),
+        after=(feats_token,),
     )[0]
-    front_rows = nodes // 2
-    grad_feats, feats_token = feats(0, front_rows)
+    grad_feats, feats_token = feats(front_rows, nodes - front_rows, after=(part,), into=grad_feats)
     near = [swap(part, "coarse", 0), swap(part, "fine", 1), swap_both(part)]
     part = call(
         square_body, (sds((2 * (per + PACK), width), BF),), (part, *near), 0, after=(feats_token,)
@@ -564,7 +576,6 @@
         body = functools.partial(merge_body, bit=bit)
         part = call(body, (sds((2 * part.shape[0], width), BF),), (part, other), 0)[0]
     other = swap(part, "fine", 0)
-    grad_feats, feats_token = feats(front_rows, nodes - front_rows, after=(part,), into=grad_feats)
     total_cells = cells * coarses
     scales = dict(edge_scale=float(total_cells * K) ** -0.5, cell_scale=float(total_cells) ** -0.5)
     grad_w1, grad_b, grad_wo, grad_up = call(
@@ -574,7 +585,6 @@
         ),
         (part, other),
         0,
-        after=(feats_token,),
     )
     return grad_feats, grad_w1, grad_b.reshape(width), grad_wo, grad_up
 

time: 51 us -> 52.6 us (1.031)
  waiting for transfers between devices: 13.2 us -> 14.9 us
  Pallas kernels: 19 us -> 18.1 us
  starting transfers between devices: 16.4 us -> 17.1 us
    ppermute x3, waiting for transfers between devices: 4.29 us -> 5.37 us  [send_sides(): return lax.ppermute(x, ('coarse', 'fine'), pairs)]
    ppermute x3, starting transfers between devices: 5 us -> 4.12 us  [send_sides(): return lax.ppermute(x, ('coarse', 'fine'), pairs)]
    pallas_call x27, Pallas kernels: 19 us -> 18.1 us  [call(): pl.pallas_call(kernel, out_shape=outs, in_specs=[in_vmem] * count + [anyw...]
    ppermute x1, starting transfers between devices: 0.7 us -> 1.55 us  [swap_both(): return lax.ppermute(x, ('coarse', 'fine'), pairs)]
    ppermute x16 -> x19, starting transfers between devices: 10.7 us -> 11.4 us  [swap(): return lax.ppermute(x, axis, [(i, i ^ 1 << bit) for i in range(count)])]
    ppermute x16 -> x19, waiting for transfers between devices: 8.85 us -> 9.36 us  [swap(): return lax.ppermute(x, axis, [(i, i ^ 1 << bit) for i in range(count)])]
  transfers between devices with their start and end apart: 20 -> 23, of which waited for: 10 -> 13; matrix products, arithmetic and copies ran while one was open for 0% -> 0% of each run, Pallas kernels for 30% -> 27%
where the time goes in v7:
time: 52.6 us; the launch traced here: 52.4 us
  Pallas kernels  18.1 us (34%)
  starting transfers between devices  17.1 us (33%)
  waiting for transfers between devices  14.9 us (28%)
  local copies, waits for them, and re-layouts  1.28 us (2%)
  between operations  0.98 us (2%)
    pallas_call x27, Pallas kernels, call(): pl.pallas_call(kernel, out_shape=outs, in_specs=[in_vmem] * count + [anyw...  18.1 us
    ppermute x19, starting transfers between devices, swap(): return lax.ppermute(x, axis, [(i, i ^ 1 << bit) for i in range(count)])  11.4 us
    ppermute x19, waiting for transfers between devices, swap(): return lax.ppermute(x, axis, [(i, i ^ 1 << bit) for i in range(count)])  9.36 us
    ppermute x3, waiting for transfers between devices, send_sides(): return lax.ppermute(x, ('coarse', 'fine'), pairs)  5.37 us
    ppermute x3, starting transfers between devices, send_sides(): return lax.ppermute(x, ('coarse', 'fine'), pairs)  4.12 us
    ppermute x1, starting transfers between devices, swap_both(): return lax.ppermute(x, ('coarse', 'fine'), pairs)  1.55 us
    unnamed x18, local copies, waits for them, and re-layouts  1.26 us
  transfers between devices with their start and end apart: 23, of which 13 were waited for; matrix products, arithmetic and copies ran while one was open for 0% of the time, Pallas kernels for 27%

profile of v7, /device:TPU:0, one launch (start us, length us, event | category | flops | bytes accessed | tf_op | source)
XLA Modules:
  0.0 52.4 jit_solution(3130564705752715942)
XLA Ops:
  0.7 0.8 %copy-done.7 = s32[2048]{0:T(1024)S(1)} copy-done((s32[2048]{0:T(1024)S(1)}, s32[2048]{0:T(1024)}, u32[]{:S(2)}) %copy-start.7) | copy-done | bytes 8216
  1.9 1.2 %shard_map.131 = (f32[512,256]{1,0:T(8,128)S(1)}, f32[512,256]{1,0:T(8,128)S(1)}) custom-call(s32[1,2048]{1,0:T(1,128)S(1)} %shard_map.128.refs_0_.refs_1_, bf16[2048,256]{1,0:T(8,128)(2,1)S(1)} %copy-done.6), custom_call_target="tpu_custom_call" | custom-call | flops 1073741824 | bytes 2105344 | tf_op jit(solution)/shard_map/pallas_call | solution.py:70
  3.6 1.5 %collective-permute-done.5.refs_1_ = f32[512,256]{1,0:T(8,128)S(1)} collective-permute-done((f32[512,256]{1,0:T(8,128)S(1)}, f32[512,256]{1,0:T(8,128)S(1)}, u32[]{:S(2)}, u32[]{:S(2)}) %collective-permute-start.5) | collective-permute-done | bytes 524320 | tf_op jit(solution)/shard_map/ppermute | solution.py:39
  5.2 3.0 %collective-permute-start.6 = (bf16[512,256]{1,0:T(8,128)(2,1)S(1)}, bf16[512,256]{1,0:T(8,128)(2,1)S(1)}, u32[]{:S(2)}, u32[]{:S(2)}) collective-permute-start(bf16[512,256]{1,0:T(8,128)(2,1)S(1)} %get-tuple-element.56.refs_0_), channel_id=1, source_target_pairs={{0,2},{1,3},{2,0},{3,1},{4,6},{5,7},{6,4},{7,5},{8,10},{9,11},{10,... | collective-permute-start | bytes 786440 | tf_op jit(solution)/shard_map/ppermute | solution.py:39
  8.6 1.3 %shard_map.129 = (f32[512,256]{1,0:T(8,128)S(1)}, f32[128,256]{1,0:T(8,128)S(1)}, f32[128,256]{1,0:T(8,128)S(1)}, f32[128,256]{1,0:T(8,128)S(1)}, f32[128,256]{1,0:T(8,128)S(1)}) custom-call(s32[1,2048]{1,0:T(1,128)S(1)} %shard_map.128.refs_0_.refs_1_, bf16[2048,256]{1,0:T(8,128)(2,1)S(1)} %copy-done.1), custom_call_target="tpu_custom_call" | custom-call | flops 1073741824 | bytes 2105344 | tf_op jit(solution)/shard_map/pallas_call | solution.py:70
  9.8 0.6 %collective-permute-start = (f32[128,256]{1,0:T(8,128)S(1)}, f32[128,256]{1,0:T(8,128)S(1)}, u32[]{:S(2)}, u32[]{:S(2)}) collective-permute-start(f32[128,256]{1,0:T(8,128)S(1)} %get-tuple-element.47), channel_id=1, source_target_pairs={{0,1},{1,0},{2,3},{3,2},{4,5},{5,4},{6,7},{7,6},{8,9},{9,8},{10,11... | collective-permute-start | bytes 393224 | tf_op jit(solution)/shard_map/ppermute | solution.py:39
  11.4 1.4 %collective-permute-start.9 = (bf16[64,256]{1,0:T(8,128)(2,1)S(1)}, bf16[64,256]{1,0:T(8,128)(2,1)S(1)}, u32[]{:S(2)}, u32[]{:S(2)}) collective-permute-start(bf16[64,256]{1,0:T(8,128)(2,1)S(1)} %shard_map.134), channel_id=1, source_target_pairs={{0,6},{1,31},{2,4},{3,29},{4,10},{5,3},{6,8},{7,1},{8,14},{9,7},{1... | collective-permute-start | bytes 98312 | tf_op jit(solution)/shard_map/ppermute | solution.py:55
  12.8 1.6 %collective-permute-start.8 = (bf16[64,256]{1,0:T(8,128)(2,1)S(1)}, bf16[64,256]{1,0:T(8,128)(2,1)S(1)}, u32[]{:S(2)}, u32[]{:S(2)}) collective-permute-start(bf16[64,256]{1,0:T(8,128)(2,1)S(1)} %shard_map.134), channel_id=1, source_target_pairs={{0,4},{1,29},{2,6},{3,31},{4,8},{5,1},{6,10},{7,3},{8,12},{9,5},{1... | collective-permute-start | bytes 98312 | tf_op jit(solution)/shard_map/ppermute | solution.py:55
  14.7 1.6 %collective-permute-start.4 = (bf16[512,256]{1,0:T(8,128)(2,1)S(1)}, bf16[512,256]{1,0:T(8,128)(2,1)S(1)}, u32[]{:S(2)}, u32[]{:S(2)}) collective-permute-start(bf16[512,256]{1,0:T(8,128)(2,1)S(1)} %get-tuple-element.52), channel_id=1, source_target_pairs={{0,2},{1,3},{2,0},{3,1},{4,6},{5,7},{6,4},{7,5},{8,10},{9,11},{10,... | collective-permute-start | bytes 786440 | tf_op jit(solution)/shard_map/ppermute | solution.py:39
  16.3 2.7 %collective-permute-done.9.refs_1_ = bf16[64,256]{1,0:T(8,128)(2,1)S(1)} collective-permute-done((bf16[64,256]{1,0:T(8,128)(2,1)S(1)}, bf16[64,256]{1,0:T(8,128)(2,1)S(1)}, u32[]{:S(2)}, u32[]{:S(2)}) %collective-permute-start.9) | collective-permute-done | bytes 32800 | tf_op jit(solution)/shard_map/ppermute | solution.py:55
  20.2 1.5 %shard_map.139.refs_2_ = bf16[4096,256]{1,0:T(8,128)(2,1)S(1)} custom-call(bf16[512,256]{1,0:T(8,128)(2,1)S(1)} %shard_map.137.refs_2_.refs_0_, s32[4,1024]{1,0:T(4,128)S(1)} %shard_map.136.refs_3_.refs_1_), custom_call_target="tpu_custom_call" | custom-call | tf_op jit(solution)/shard_map/pallas_call | solution.py:70
  22.0 1.7 %shard_map.140 = (f32[1024,256]{1,0:T(8,128)S(1)}, f32[2048,256]{1,0:T(8,128)S(1)}, bf16[2048,256]{1,0:T(8,128)(2,1)S(1)}, f32[8,128]{1,0:T(8,128)S(1)}) custom-call(f32[1024,256]{1,0:T(8,128)S(1)} %get-tuple-element.57.refs_0_, bf16[640,256]{1,0:T(8,128)(2,1)S(1)} %get-tuple-element.58.refs_1_, bf16[4096,256]{1,0:T(8,128)(2,1)S(1)} %shard_map.139.refs_2_, ...), custom_call_target="tpu_custom_call" | custom-call | tf_op jit(solution)/shard_map/pallas_call | solution.py:70
  24.3 1.7 %shard_map.142 = (f32[1024,256]{1,0:T(8,128)S(1)}, f32[2048,256]{1,0:T(8,128)S(1)}, bf16[2048,256]{1,0:T(8,128)(2,1)S(1)}) custom-call(f32[1024,256]{1,0:T(8,128)S(1)} %get-tuple-element.57.refs_0_, bf16[640,256]{1,0:T(8,128)(2,1)S(1)} %get-tuple-element.58.refs_1_, bf16[4096,256]{1,0:T(8,128)(2,1)S(1)} %shard_map.139.refs_2_, ...), custom_call_target="tpu_custom_call" | custom-call | tf_op jit(solution)/shard_map/pallas_call | solution.py:70
  26.0 1.5 %shard_map.143 = (bf16[4096,256]{1,0:T(8,128)(2,1)S(1)}, f32[1024,256]{1,0:T(8,128)S(1)}, bf16[1024,256]{1,0:T(8,128)(2,1)S(1)}, f32[128,256]{1,0:T(8,128)S(1)},...) custom-call(bf16[512,256]{1,0:T(8,128)(2,1)S(1)} %shard_map.141.refs_5_.refs_0_, ...), custom_call_target="tpu_custom_call" | custom-call | flops 536870912 | bytes 13582336 | tf_op jit(solution)/shard_map/pallas_call | solution.py:70
  27.5 1.2 %collective-permute-start.16 = (bf16[144,256]{1,0:T(8,128)(2,1)S(1)}, bf16[144,256]{1,0:T(8,128)(2,1)S(1)}, u32[]{:S(2)}, u32[]{:S(2)}) collective-permute-start(bf16[144,256]{1,0:T(8,128)(2,1)S(1)} %get-tuple-element.71), channel_id=1, source_target_pairs={{0,4},{4,0},{8,12},{12,8},{16,20},{20,16},{24,28},{28,24},{1,5},{5... | collective-permute-start | bytes 221192 | tf_op jit(solution)/shard_map/ppermute | solution.py:39
  28.7 0.6 %shard_map.146.refs_3_ = bf16[64,256]{1,0:T(8,128)(2,1)S(1)} custom-call(bf16[4096,256]{1,0:T(8,128)(2,1)S(1)} %get-tuple-element.67.refs_0_, s32[4,1024]{1,0:T(4,128)S(1)} %shard_map.136.refs_3_.refs_1_, bf16[512,256]{1,0:T(8,128)(2,1)S(1)} %copy-done), custom_call_target="tpu_custom_call" | custom-call | flops 268435456 | bytes 2408448 | tf_op jit(solution)/shard_map/pallas_call | solution.py:70
  29.3 1.1 %collective-permute-start.14 = (bf16[64,256]{1,0:T(8,128)(2,1)S(1)}, bf16[64,256]{1,0:T(8,128)(2,1)S(1)}, u32[]{:S(2)}, u32[]{:S(2)}) collective-permute-start(bf16[64,256]{1,0:T(8,128)(2,1)S(1)} %shard_map.146.refs_3_), channel_id=1, source_target_pairs={{0,4},{1,29},{2,6},{3,31},{4,8},{5,1},{6,10},{7,3},{8,12},{9,5},{1... | collective-permute-start | bytes 98312 | tf_op jit(solution)/shard_map/ppermute | solution.py:55
  30.4 1.8 %collective-permute-done.16.refs_1_ = bf16[144,256]{1,0:T(8,128)(2,1)S(1)} collective-permute-done((bf16[144,256]{1,0:T(8,128)(2,1)S(1)}, bf16[144,256]{1,0:T(8,128)(2,1)S(1)}, u32[]{:S(2)}, u32[]{:S(2)}) %collective-permute-start.16) | collective-permute-done | bytes 73760 | tf_op jit(solution)/shard_map/ppermute | solution.py:39
  32.4 1.5 %shard_map.144.refs_0_.refs_3_ = f32[512,256]{1,0:T(8,128)S(1)} custom-call(bf16[4096,256]{1,0:T(8,128)(2,1)S(1)} %get-tuple-element.67.refs_0_, s32[4,1024]{1,0:T(4,128)S(1)} %shard_map.136.refs_3_.refs_1_, f32[1024,256]{1,0:T(8,128)S(1)} %get-tuple-element.68.refs_2_, bf16[1024,256]{1,0:T(8,128)(2,1)S(1)} %get-tuple-element.69.refs_3_, ...), custom_call_target="tpu_custom_call" | custom-call | flops 1073741824 | bytes 4472832 | tf_op jit(solution)/shard_map/pallas_call | solution.py:70
  33.9 2.3 %collective-permute-done.14.refs_2_ = bf16[64,256]{1,0:T(8,128)(2,1)S(1)} collective-permute-done((bf16[64,256]{1,0:T(8,128)(2,1)S(1)}, bf16[64,256]{1,0:T(8,128)(2,1)S(1)}, u32[]{:S(2)}, u32[]{:S(2)}) %collective-permute-start.14) | collective-permute-done | bytes 32800 | tf_op jit(solution)/shard_map/ppermute | solution.py:55
  36.1 0.6 %collective-permute-done.17.refs_1_ = bf16[144,256]{1,0:T(8,128)(2,1)S(1)} collective-permute-done((bf16[144,256]{1,0:T(8,128)(2,1)S(1)}, bf16[144,256]{1,0:T(8,128)(2,1)S(1)}, u32[]{:S(2)}, u32[]{:S(2)}) %collective-permute-start.17) | collective-permute-done | bytes 73760 | tf_op jit(solution)/shard_map/ppermute | solution.py:39
  36.7 0.8 %collective-permute-start.18 = (bf16[144,256]{1,0:T(8,128)(2,1)S(1)}, bf16[144,256]{1,0:T(8,128)(2,1)S(1)}, u32[]{:S(2)}, u32[]{:S(2)}) collective-permute-start(bf16[144,256]{1,0:T(8,128)(2,1)S(1)} %get-tuple-element.77), channel_id=1, source_target_pairs={{0,16},{4,20},{8,24},{12,28},{16,0},{20,4},{24,8},{28,12},{1,17},{... | collective-permute-start | bytes 221192 | tf_op jit(solution)/shard_map/ppermute | solution.py:39
  37.5 1.5 %shard_map.145.refs_1_ = f32[512,256]{1,0:T(8,128)S(1)} custom-call(bf16[4096,256]{1,0:T(8,128)(2,1)S(1)} %get-tuple-element.67.refs_0_, s32[4,1024]{1,0:T(4,128)S(1)} %shard_map.136.refs_3_.refs_1_, f32[1024,256]{1,0:T(8,128)S(1)} %get-tuple-element.68.refs_2_, bf16[1024,256]{1,0:T(8,128)(2,1)S(1)} %get-tuple-element.69.refs_3_, bf16[512,256]{1,0:T(8,128)(2,1)S(1)} %copy-done), custom_call_target="tpu_custom_call" | custom-call | flops 1073741824 | bytes 4472832 | tf_op jit(solution)/shard_map/pallas_call | solution.py:70
  39.4 1.2 %shard_map.150 = (bf16[2048,256]{1,0:T(8,128)(2,1)}, f32[8,128]{1,0:T(8,128)S(1)}) custom-call(bf16[1024,256]{1,0:T(8,128)(2,1)S(1)} %shard_map.147.refs_0_, s32[1,2048]{1,0:T(1,128)S(1)} %shard_map.128.refs_0_.refs_1_, bf16[2048,256]{1,0:T(8,128)(2,1)S(1)} %copy-done.1), custom_call_target="tpu_custom_call" | custom-call | flops 268435456 | bytes 2633728 | tf_op jit(solution)/shard_map/pallas_call | solution.py:70
  40.6 2.1 %collective-permute-done.18.refs_1_ = bf16[144,256]{1,0:T(8,128)(2,1)S(1)} collective-permute-done((bf16[144,256]{1,0:T(8,128)(2,1)S(1)}, bf16[144,256]{1,0:T(8,128)(2,1)S(1)}, u32[]{:S(2)}, u32[]{:S(2)}) %collective-permute-start.18) | collective-permute-done | bytes 73760 | tf_op jit(solution)/shard_map/ppermute | solution.py:39
  42.7 1.5 %collective-permute-start.21 = (bf16[144,256]{1,0:T(8,128)(2,1)S(1)}, bf16[144,256]{1,0:T(8,128)(2,1)S(1)}, u32[]{:S(2)}, u32[]{:S(2)}) collective-permute-start(bf16[144,256]{1,0:T(8,128)(2,1)S(1)} %shard_map.151.refs_3_.refs_0_), channel_id=1, source_target_pairs={{0,6},{1,7},{2,4},{3,5},{4,2},{5,3},{6,0},{7,1},{8,14},{9,15},{10,... | collective-permute-start | bytes 221192 | tf_op jit(solution)/shard_map/ppermute | solution.py:45
  44.2 0.9 %collective-permute-start.20 = (bf16[144,256]{1,0:T(8,128)(2,1)S(1)}, bf16[144,256]{1,0:T(8,128)(2,1)S(1)}, u32[]{:S(2)}, u32[]{:S(2)}) collective-permute-start(bf16[144,256]{1,0:T(8,128)(2,1)S(1)} %shard_map.151.refs_3_.refs_0_), channel_id=1, source_target_pairs={{0,2},{1,3},{2,0},{3,1},{4,6},{5,7},{6,4},{7,5},{8,10},{9,11},{10,... | collective-permute-start | bytes 221192 | tf_op jit(solution)/shard_map/ppermute | solution.py:39
  45.2 1.1 %collective-permute-start.19 = (bf16[144,256]{1,0:T(8,128)(2,1)S(1)}, bf16[144,256]{1,0:T(8,128)(2,1)S(1)}, u32[]{:S(2)}, u32[]{:S(2)}) collective-permute-start(bf16[144,256]{1,0:T(8,128)(2,1)S(1)} %shard_map.151.refs_3_.refs_0_), channel_id=1, source_target_pairs={{0,4},{4,0},{8,12},{12,8},{16,20},{20,16},{24,28},{28,24},{1,5},{5... | collective-permute-start | bytes 221192 | tf_op jit(solution)/shard_map/ppermute | solution.py:39
  46.2 1.9 %shard_map.152 = (bf16[2048,256]{1,0:T(8,128)(2,1)}, f32[8,128]{1,0:T(8,128)S(1)}) custom-call(bf16[1024,256]{1,0:T(8,128)(2,1)S(1)} %shard_map.147.refs_0_, s32[1,2048]{1,0:T(1,128)S(1)} %shard_map.128.refs_0_.refs_1_, bf16[2048,256]{1,0:T(8,128)(2,1)S(1)} %copy-done.1, ...), custom_call_target="tpu_custom_call", output_to_operand_aliasing={{0}: (4, {})} | custom-call | flops 805306368 | bytes 2633728 | tf_op jit(solution)/shard_map/pallas_call | solution.py:70
  48.9 0.8 %collective-permute-done.19.refs_1_ = bf16[144,256]{1,0:T(8,128)(2,1)S(1)} collective-permute-done((bf16[144,256]{1,0:T(8,128)(2,1)S(1)}, bf16[144,256]{1,0:T(8,128)(2,1)S(1)}, u32[]{:S(2)}, u32[]{:S(2)}) %collective-permute-start.19) | collective-permute-done | bytes 73760 | tf_op jit(solution)/shard_map/ppermute | solution.py:39
  49.8 1.5 %collective-permute-done.22.refs_1_ = bf16[544,256]{1,0:T(8,128)(2,1)S(1)} collective-permute-done((bf16[544,256]{1,0:T(8,128)(2,1)S(1)}, bf16[544,256]{1,0:T(8,128)(2,1)S(1)}, u32[]{:S(2)}, u32[]{:S(2)}) %collective-permute-start.22) | collective-permute-done | bytes 278560 | tf_op jit(solution)/shard_map/ppermute | solution.py:39
  51.4 1.0 %shard_map.154 = (f32[512,256]{1,0:T(8,128)}, f32[1,256]{1,0:T(1,128)}, f32[256,256]{1,0:T(8,128)}, f32[256,256]{1,0:T(8,128)}) custom-call(bf16[544,256]{1,0:T(8,128)(2,1)S(1)} %shard_map.153.refs_0_, bf16[544,256]{1,0:T(8,128)(2,1)S(1)} %collective-permute-done.22.refs_1_), custom_call_target="tpu_custom_call" | custom-call | tf_op jit(solution)/shard_map/pallas_call | solution.py:70
  (61 shorter events, 6.1 us)
Async XLA Ops:
  0.6 1.2 %copy-start.6 = (bf16[2048,256]{1,0:T(8,128)(2,1)S(1)}, bf16[2048,256]{1,0:T(8,128)(2,1)}, u32[]{:S(2)}) copy-start(bf16[2048,256]{1,0:T(8,128)(2,1)} %refs_1_.3) | copy-start | bytes 3145732
  0.6 0.8 %copy-start.7 = (s32[2048]{0:T(1024)S(1)}, s32[2048]{0:T(1024)}, u32[]{:S(2)}) copy-start(s32[2048]{0:T(1024)} %param.11) | copy-start | bytes 24580
  1.9 6.3 %copy-start.5 = (s32[128]{0:T(128)S(1)}, s32[128]{0:T(128)}, u32[]{:S(2)}) copy-start(s32[128]{0:T(128)} %param.12) | copy-start | bytes 1540
  1.9 6.7 %copy-start.1 = (bf16[2048,256]{1,0:T(8,128)(2,1)S(1)}, bf16[2048,256]{1,0:T(8,128)(2,1)}, u32[]{:S(2)}) copy-start(bf16[2048,256]{1,0:T(8,128)(2,1)} %refs_2_.5) | copy-start | bytes 3145732
  3.1 2.1 %collective-permute-start.5 = (f32[512,256]{1,0:T(8,128)S(1)}, f32[512,256]{1,0:T(8,128)S(1)}, u32[]{:S(2)}, u32[]{:S(2)}) collective-permute-start(f32[512,256]{1,0:T(8,128)S(1)} %get-tuple-element.54), channel_id=1, source_target_pairs={{0,1},{1,0},{2,3},{3,2},{4,5},{5,4},{6,7},{7,6},{8,9},{9,8},{10,11... | collective-permute-start | bytes 1572872 | tf_op jit(solution)/shard_map/ppermute | solution.py:39
  5.2 14.2 %collective-permute-start.6 = (bf16[512,256]{1,0:T(8,128)(2,1)S(1)}, bf16[512,256]{1,0:T(8,128)(2,1)S(1)}, u32[]{:S(2)}, u32[]{:S(2)}) collective-permute-start(bf16[512,256]{1,0:T(8,128)(2,1)S(1)} %get-tuple-element.56.refs_0_), channel_id=1, source_target_pairs={{0,2},{1,3},{2,0},{3,1},{4,6},{5,7},{6,4},{7,5},{8,10},{9,11},{10,... | collective-permute-start | bytes 786440 | tf_op jit(solution)/shard_map/ppermute | solution.py:39
  8.4 5.9 %copy-start.8 = (bf16[256]{0:T(256)(128)(2,1)S(1)}, bf16[256]{0:T(256)(128)(2,1)}, u32[]{:S(2)}) copy-start(bf16[256]{0:T(256)(128)(2,1)} %param.15) | copy-start | bytes 1540
  8.5 5.9 %copy-start.4 = (s32[4096]{0:T(1024)S(1)}, s32[4096]{0:T(1024)}, u32[]{:S(2)}) copy-start(s32[4096]{0:T(1024)} %param.13) | copy-start | bytes 49156
  8.5 2.4 %collective-permute-start.7 = (bf16[128,256]{1,0:T(8,128)(2,1)S(1)}, bf16[128,256]{1,0:T(8,128)(2,1)S(1)}, u32[]{:S(2)}, u32[]{:S(2)}) collective-permute-start(bf16[128,256]{1,0:T(8,128)(2,1)S(1)} %shard_map.133.refs_0_), channel_id=1, source_target_pairs={{0,1},{1,0},{2,3},{3,2},{4,5},{5,4},{6,7},{7,6},{8,9},{9,8},{10,11... | collective-permute-start | bytes 196616 | tf_op jit(solution)/shard_map/ppermute | solution.py:39
  9.8 1.6 %collective-permute-start = (f32[128,256]{1,0:T(8,128)S(1)}, f32[128,256]{1,0:T(8,128)S(1)}, u32[]{:S(2)}, u32[]{:S(2)}) collective-permute-start(f32[128,256]{1,0:T(8,128)S(1)} %get-tuple-element.47), channel_id=1, source_target_pairs={{0,1},{1,0},{2,3},{3,2},{4,5},{5,4},{6,7},{7,6},{8,9},{9,8},{10,11... | collective-permute-start | bytes 393224 | tf_op jit(solution)/shard_map/ppermute | solution.py:39
  10.4 2.4 %collective-permute-start.1 = (f32[128,256]{1,0:T(8,128)S(1)}, f32[128,256]{1,0:T(8,128)S(1)}, u32[]{:S(2)}, u32[]{:S(2)}) collective-permute-start(f32[128,256]{1,0:T(8,128)S(1)} %get-tuple-element.48), channel_id=1, source_target_pairs={{0,1},{1,0},{2,3},{3,2},{4,5},{5,4},{6,7},{7,6},{8,9},{9,8},{10,11... | collective-permute-start | bytes 393224 | tf_op jit(solution)/shard_map/ppermute | solution.py:39
  10.5 4.1 %collective-permute-start.2 = (f32[128,256]{1,0:T(8,128)S(1)}, f32[128,256]{1,0:T(8,128)S(1)}, u32[]{:S(2)}, u32[]{:S(2)}) collective-permute-start(f32[128,256]{1,0:T(8,128)S(1)} %get-tuple-element.49), channel_id=1, source_target_pairs={{0,1},{1,0},{2,3},{3,2},{4,5},{5,4},{6,7},{7,6},{8,9},{9,8},{10,11... | collective-permute-start | bytes 393224 | tf_op jit(solution)/shard_map/ppermute | solution.py:39
  10.9 3.7 %collective-permute-start.3 = (f32[128,256]{1,0:T(8,128)S(1)}, f32[128,256]{1,0:T(8,128)S(1)}, u32[]{:S(2)}, u32[]{:S(2)}) collective-permute-start(f32[128,256]{1,0:T(8,128)S(1)} %get-tuple-element.50), channel_id=1, source_target_pairs={{0,1},{1,0},{2,3},{3,2},{4,5},{5,4},{6,7},{7,6},{8,9},{9,8},{10,11... | collective-permute-start | bytes 393224 | tf_op jit(solution)/shard_map/ppermute | solution.py:39
  11.4 7.6 %collective-permute-start.9 = (bf16[64,256]{1,0:T(8,128)(2,1)S(1)}, bf16[64,256]{1,0:T(8,128)(2,1)S(1)}, u32[]{:S(2)}, u32[]{:S(2)}) collective-permute-start(bf16[64,256]{1,0:T(8,128)(2,1)S(1)} %shard_map.134), channel_id=1, source_target_pairs={{0,6},{1,31},{2,4},{3,29},{4,10},{5,3},{6,8},{7,1},{8,14},{9,7},{1... | collective-permute-start | bytes 98312 | tf_op jit(solution)/shard_map/ppermute | solution.py:55
  12.8 6.6 %collective-permute-start.8 = (bf16[64,256]{1,0:T(8,128)(2,1)S(1)}, bf16[64,256]{1,0:T(8,128)(2,1)S(1)}, u32[]{:S(2)}, u32[]{:S(2)}) collective-permute-start(bf16[64,256]{1,0:T(8,128)(2,1)S(1)} %shard_map.134), channel_id=1, source_target_pairs={{0,4},{1,29},{2,6},{3,31},{4,8},{5,1},{6,10},{7,3},{8,12},{9,5},{1... | collective-permute-start | bytes 98312 | tf_op jit(solution)/shard_map/ppermute | solution.py:55
  14.7 7.0 %copy-start = (bf16[512,256]{1,0:T(8,128)(2,1)S(1)}, bf16[512,256]{1,0:T(8,128)(2,1)}, u32[]{:S(2)}) copy-start(bf16[512,256]{1,0:T(8,128)(2,1)} %refs_2_.3) | copy-start | bytes 786436
  14.7 9.1 %collective-permute-start.4 = (bf16[512,256]{1,0:T(8,128)(2,1)S(1)}, bf16[512,256]{1,0:T(8,128)(2,1)S(1)}, u32[]{:S(2)}, u32[]{:S(2)}) collective-permute-start(bf16[512,256]{1,0:T(8,128)(2,1)S(1)} %get-tuple-element.52), channel_id=1, source_target_pairs={{0,2},{1,3},{2,0},{3,1},{4,6},{5,7},{6,4},{7,5},{8,10},{9,11},{10,... | collective-permute-start | bytes 786440 | tf_op jit(solution)/shard_map/ppermute | solution.py:39
  19.5 2.2 %collective-permute-start.11 = (bf16[256,256]{1,0:T(8,128)(2,1)S(1)}, bf16[256,256]{1,0:T(8,128)(2,1)S(1)}, u32[]{:S(2)}, u32[]{:S(2)}) collective-permute-start(bf16[256,256]{1,0:T(8,128)(2,1)S(1)} %get-tuple-element.87), channel_id=1, source_target_pairs={{0,1},{1,0},{2,3},{3,2},{4,5},{5,4},{6,7},{7,6},{8,9},{9,8},{10,11... | collective-permute-start | bytes 393224 | tf_op jit(solution)/shard_map/ppermute | solution.py:39
  19.6 2.1 %collective-permute-start.10 = (bf16[256,256]{1,0:T(8,128)(2,1)S(1)}, bf16[256,256]{1,0:T(8,128)(2,1)S(1)}, u32[]{:S(2)}, u32[]{:S(2)}) collective-permute-start(bf16[256,256]{1,0:T(8,128)(2,1)S(1)} %get-tuple-element.88), channel_id=1, source_target_pairs={{0,1},{1,0},{2,3},{3,2},{4,5},{5,4},{6,7},{7,6},{8,9},{9,8},{10,11... | collective-permute-start | bytes 393224 | tf_op jit(solution)/shard_map/ppermute | solution.py:39
  20.1 1.6 %collective-permute-start.12 = (bf16[64,256]{1,0:T(8,128)(2,1)S(1)}, bf16[64,256]{1,0:T(8,128)(2,1)S(1)}, u32[]{:S(2)}, u32[]{:S(2)}) collective-permute-start(bf16[64,256]{1,0:T(8,128)(2,1)S(1)} %shard_map.135.refs_2_.refs_3_), channel_id=1, source_target_pairs={{0,1},{1,0},{2,3},{3,2},{4,5},{5,4},{6,7},{7,6},{8,9},{9,8},{10,11... | collective-permute-start | bytes 98312 | tf_op jit(solution)/shard_map/ppermute | solution.py:39
  23.9 2.1 %copy-start.2 = (bf16[256,256]{1,0:T(8,128)(2,1)S(1)}, bf16[256,256]{1,0:T(8,128)(2,1)}, u32[]{:S(2)}) copy-start(bf16[256,256]{1,0:T(8,128)(2,1)} %refs_9_.1) | copy-start | bytes 393220
  23.9 2.1 %copy-start.3 = (bf16[256,256]{1,0:T(8,128)(2,1)S(1)}, bf16[256,256]{1,0:T(8,128)(2,1)}, u32[]{:S(2)}) copy-start(bf16[256,256]{1,0:T(8,128)(2,1)} %refs_10_.1) | copy-start | bytes 393220
  23.9 2.1 %collective-permute-start.13 = (bf16[512,256]{1,0:T(8,128)(2,1)S(1)}, bf16[512,256]{1,0:T(8,128)(2,1)S(1)}, u32[]{:S(2)}, u32[]{:S(2)}) collective-permute-start(bf16[512,256]{1,0:T(8,128)(2,1)S(1)} %shard_map.141.refs_5_.refs_0_), channel_id=1, source_target_pairs={{0,1},{1,0},{2,3},{3,2},{4,5},{5,4},{6,7},{7,6},{8,9},{9,8},{10,11... | collective-permute-start | bytes 786440 | tf_op jit(solution)/shard_map/ppermute | solution.py:39
  27.5 4.8 %collective-permute-start.16 = (bf16[144,256]{1,0:T(8,128)(2,1)S(1)}, bf16[144,256]{1,0:T(8,128)(2,1)S(1)}, u32[]{:S(2)}, u32[]{:S(2)}) collective-permute-start(bf16[144,256]{1,0:T(8,128)(2,1)S(1)} %get-tuple-element.71), channel_id=1, source_target_pairs={{0,4},{4,0},{8,12},{12,8},{16,20},{20,16},{24,28},{28,24},{1,5},{5... | collective-permute-start | bytes 221192 | tf_op jit(solution)/shard_map/ppermute | solution.py:39
  29.3 6.8 %collective-permute-start.14 = (bf16[64,256]{1,0:T(8,128)(2,1)S(1)}, bf16[64,256]{1,0:T(8,128)(2,1)S(1)}, u32[]{:S(2)}, u32[]{:S(2)}) collective-permute-start(bf16[64,256]{1,0:T(8,128)(2,1)S(1)} %shard_map.146.refs_3_), channel_id=1, source_target_pairs={{0,4},{1,29},{2,6},{3,31},{4,8},{5,1},{6,10},{7,3},{8,12},{9,5},{1... | collective-permute-start | bytes 98312 | tf_op jit(solution)/shard_map/ppermute | solution.py:55
  32.3 4.4 %collective-permute-start.17 = (bf16[144,256]{1,0:T(8,128)(2,1)S(1)}, bf16[144,256]{1,0:T(8,128)(2,1)S(1)}, u32[]{:S(2)}, u32[]{:S(2)}) collective-permute-start(bf16[144,256]{1,0:T(8,128)(2,1)S(1)} %get-tuple-element.74), channel_id=1, source_target_pairs={{0,8},{4,12},{8,0},{12,4},{16,24},{20,28},{24,16},{28,20},{1,9},{5... | collective-permute-start | bytes 221192 | tf_op jit(solution)/shard_map/ppermute | solution.py:39
  36.1 2.9 %collective-permute-start.15 = (bf16[64,256]{1,0:T(8,128)(2,1)S(1)}, bf16[64,256]{1,0:T(8,128)(2,1)S(1)}, u32[]{:S(2)}, u32[]{:S(2)}) collective-permute-start(bf16[64,256]{1,0:T(8,128)(2,1)S(1)} %collective-permute-done.14.refs_2_), channel_id=1, source_target_pairs={{0,1},{1,0},{2,3},{3,2},{4,5},{5,4},{6,7},{7,6},{8,9},{9,8},{10,11... | collective-permute-start | bytes 98312 | tf_op jit(solution)/shard_map/ppermute | solution.py:39
  36.7 5.9 %collective-permute-start.18 = (bf16[144,256]{1,0:T(8,128)(2,1)S(1)}, bf16[144,256]{1,0:T(8,128)(2,1)S(1)}, u32[]{:S(2)}, u32[]{:S(2)}) collective-permute-start(bf16[144,256]{1,0:T(8,128)(2,1)S(1)} %get-tuple-element.77), channel_id=1, source_target_pairs={{0,16},{4,20},{8,24},{12,28},{16,0},{20,4},{24,8},{28,12},{1,17},{... | collective-permute-start | bytes 221192 | tf_op jit(solution)/shard_map/ppermute | solution.py:39
  42.7 5.7 %collective-permute-start.21 = (bf16[144,256]{1,0:T(8,128)(2,1)S(1)}, bf16[144,256]{1,0:T(8,128)(2,1)S(1)}, u32[]{:S(2)}, u32[]{:S(2)}) collective-permute-start(bf16[144,256]{1,0:T(8,128)(2,1)S(1)} %shard_map.151.refs_3_.refs_0_), channel_id=1, source_target_pairs={{0,6},{1,7},{2,4},{3,5},{4,2},{5,3},{6,0},{7,1},{8,14},{9,15},{10,... | collective-permute-start | bytes 221192 | tf_op jit(solution)/shard_map/ppermute | solution.py:45
  44.2 4.6 %collective-permute-start.20 = (bf16[144,256]{1,0:T(8,128)(2,1)S(1)}, bf16[144,256]{1,0:T(8,128)(2,1)S(1)}, u32[]{:S(2)}, u32[]{:S(2)}) collective-permute-start(bf16[144,256]{1,0:T(8,128)(2,1)S(1)} %shard_map.151.refs_3_.refs_0_), channel_id=1, source_target_pairs={{0,2},{1,3},{2,0},{3,1},{4,6},{5,7},{6,4},{7,5},{8,10},{9,11},{10,... | collective-permute-start | bytes 221192 | tf_op jit(solution)/shard_map/ppermute | solution.py:39
  45.2 4.5 %collective-permute-start.19 = (bf16[144,256]{1,0:T(8,128)(2,1)S(1)}, bf16[144,256]{1,0:T(8,128)(2,1)S(1)}, u32[]{:S(2)}, u32[]{:S(2)}) collective-permute-start(bf16[144,256]{1,0:T(8,128)(2,1)S(1)} %shard_map.151.refs_3_.refs_0_), channel_id=1, source_target_pairs={{0,4},{4,0},{8,12},{12,8},{16,20},{20,16},{24,28},{28,24},{1,5},{5... | collective-permute-start | bytes 221192 | tf_op jit(solution)/shard_map/ppermute | solution.py:39
  49.7 1.6 %collective-permute-start.22 = (bf16[544,256]{1,0:T(8,128)(2,1)S(1)}, bf16[544,256]{1,0:T(8,128)(2,1)S(1)}, u32[]{:S(2)}, u32[]{:S(2)}) collective-permute-start(bf16[544,256]{1,0:T(8,128)(2,1)S(1)} %shard_map.153.refs_0_), channel_id=1, source_target_pairs={{0,1},{1,0},{2,3},{3,2},{4,5},{5,4},{6,7},{7,6},{8,9},{9,8},{10,11... | collective-permute-start | bytes 835592 | tf_op jit(solution)/shard_map/ppermute | solution.py:39

commit v8 on v7

--- a/solution.py
+++ b/solution.py
@@ -130,20 +130,14 @@
             out_ref[k : k + 1, q * LANES : (q + 1) * LANES] = rows[q : q + 1, :]
 
 
-def pool_body(ids_ref, x_ref, keep_ref, *send_refs):
-    half = keep_ref.shape[0]
-    n = half // len(send_refs)
-    core = lax.axis_index("fine") % 2
-    ids = ids_ref[...]
-    x = x_ref[...]
-    core_rows = (1 - core) * half
-    for i, ref in enumerate(send_refs):
-        step = min(256, n)
-        for t in range(0, n, step):
-            ref[t : t + step, :] = dot(hot_columns(ids, step, core_rows + i * n + t), x)
+def pool_body(ids_ref, x_ref, out_ref, *, other):
+    half = out_ref.shape[0]
+    core = lax.axis_index("fine") % 2
+    first = ((1 - core) if other else core) * half
+    ids = ids_ref[...] - first
     step = min(256, half)
     for t in range(0, half, step):
-        keep_ref[t : t + step, :] = dot(hot_columns(ids, step, core * half + t), x)
+        out_ref[t : t + step, :] = dot(hot_columns(ids, step, t), x_ref[...])
 
 
 def pick_body(part_ref, lists_ref, out_ref):
@@ -170,14 +164,10 @@
     out_ref[...] = total.astype(BF)
 
 
-def chip_body(keep, *refs):
-    *recvs, part_ref, send_ref = refs
-    n = keep.shape[0] // len(recvs)
-    for i, recv in enumerate(recvs):
-        at = slice(i * n, (i + 1) * n)
-        total = keep[at, :] + recv[...]
-        part_ref[at, :] = total
-        send_ref[at, :] = total.astype(BF)
+def chip_body(keep, recv, part_ref, send_ref):
+    total = keep[...] + recv[...]
+    part_ref[...] = total
+    send_ref[...] = total.astype(BF)
 
 
 def across_body(part, recv, *out_refs):
@@ -454,11 +444,13 @@
     )[0]
     bias = b_edge_in.reshape(1, width)
 
-    def pool(x, pieces):
-        outs = (sds((half, width), F32),) + (sds((half // pieces, width), F32),) * pieces
-        keep, *sends = call(pool_body, outs, (ids, x), 2 * nodes * cells * width)
+    def half_sums(x, other, after=()):
+        body = functools.partial(pool_body, other=other)
+        return call(body, (sds((half, width), F32),), (ids, x), nodes * cells * width, after=after)[0]
+
+    def chip_sums(keep, recv, after=()):
         outs = (sds((half, width), F32), sds((half, width), BF))
-        return call(chip_body, outs, (keep, *[swap(send, "fine", 0) for send in sends]), 0)
+        return call(chip_body, outs, (keep, recv), 0, after=after)
 
     def across(part, send, after=()):
         for bit in range(1, fine_bits):
@@ -468,10 +460,12 @@
             part, send = (*call(across_body, outs, (part, recv), 0, after=after), None)[:2]
         return part
 
-    part_p, send_p = pool(node_feats, 1)
-    part_g, send_g = pool(grad_out, 4)
+    recv_p = swap(half_sums(node_feats, True), "fine", 0)
+    recv_g = swap(half_sums(grad_out, True), "fine", 0)
+    part_p, send_p = chip_sums(half_sums(node_feats, False), recv_p)
     picked = call(pick_body, (sds((2 * side, width), BF),), (send_p, lists), 0)[0]
     sent = call(side_body, (sds((side, width), BF),), (picked, swap(picked, "fine", 0)), 0)[0]
+    part_g, send_g = chip_sums(half_sums(grad_out, False, after=(send_p,)), recv_g)
     own_halo = call(
         halo_sum_body, (sds((side, width), BF),), [send_sides(sent, d) for d in range(fines // 2)], 0,
         scratch=(pltpu.VMEM((fines // 2, side, width), F32),),

time: 52.6 us -> 51.1 us (0.971)
  waiting for transfers between devices: 14.9 us -> 12.8 us
    ppermute x19 -> x16, waiting for transfers between devices: 9.36 us -> 7.39 us  [swap(): return lax.ppermute(x, axis, [(i, i ^ 1 << bit) for i in range(count)])]
    ppermute x1, starting transfers between devices: 1.55 us -> 2.23 us  [swap_both(): return lax.ppermute(x, ('coarse', 'fine'), pairs)]
    ppermute x3, waiting for transfers between devices: 5.37 us -> 4.83 us  [send_sides(): return lax.ppermute(x, ('coarse', 'fine'), pairs)]
    pallas_call x27 -> x29, Pallas kernels: 18.1 us -> 18.4 us  [call(): pl.pallas_call(kernel, out_shape=outs, in_specs=[in_vmem] * count + [anyw...]
    ppermute x19 -> x16, starting transfers between devices: 11.4 us -> 11.3 us  [swap(): return lax.ppermute(x, axis, [(i, i ^ 1 << bit) for i in range(count)])]
  transfers between devices with their start and end apart: 23 -> 20, of which waited for: 13 -> 12; matrix products, arithmetic and copies ran while one was open for 0% -> 0% of each run, Pallas kernels for 27% -> 30%
where the time goes in v8:
time: 51.1 us; the launch traced here: 50.9 us
  Pallas kernels  18.4 us (36%)
  starting transfers between devices  17.3 us (34%)
  waiting for transfers between devices  12.8 us (25%)
  local copies, waits for them, and re-layouts  1.28 us (3%)
  between operations  1.01 us (2%)
    pallas_call x29, Pallas kernels, call(): pl.pallas_call(kernel, out_shape=outs, in_specs=[in_vmem] * count + [anyw...  18.4 us
    ppermute x16, starting transfers between devices, swap(): return lax.ppermute(x, axis, [(i, i ^ 1 << bit) for i in range(count)])  11.3 us
    ppermute x16, waiting for transfers between devices, swap(): return lax.ppermute(x, axis, [(i, i ^ 1 << bit) for i in range(count)])  7.39 us
    ppermute x3, waiting for transfers between devices, send_sides(): return lax.ppermute(x, ('coarse', 'fine'), pairs)  4.83 us
    ppermute x3, starting transfers between devices, send_sides(): return lax.ppermute(x, ('coarse', 'fine'), pairs)  3.84 us
    ppermute x1, starting transfers between devices, swap_both(): return lax.ppermute(x, ('coarse', 'fine'), pairs)  2.23 us
    unnamed x18, local copies, waits for them, and re-layouts  1.26 us
  transfers between devices with their start and end apart: 20, of which 12 were waited for; matrix products, arithmetic and copies ran while one was open for 0% of the time, Pallas kernels for 30%

profile of v8, /device:TPU:0, one launch (start us, length us, event | category | flops | bytes accessed | tf_op | source)
XLA Modules:
  0.0 50.9 jit_solution(12989231512427404733)
XLA Ops:
  0.7 0.8 %copy-done.7 = s32[2048]{0:T(1024)S(1)} copy-done((s32[2048]{0:T(1024)S(1)}, s32[2048]{0:T(1024)}, u32[]{:S(2)}) %copy-start.7) | copy-done | bytes 8216
  1.9 0.7 %shard_map.130 = f32[512,256]{1,0:T(8,128)S(1)} custom-call(s32[1,2048]{1,0:T(1,128)S(1)} %shard_map.128.refs_0_.refs_1_, bf16[2048,256]{1,0:T(8,128)(2,1)S(1)} %copy-done.6), custom_call_target="tpu_custom_call" | custom-call | flops 536870912 | bytes 1581056 | tf_op jit(solution)/shard_map/pallas_call | solution.py:70
  3.1 0.7 %shard_map.133 = f32[512,256]{1,0:T(8,128)S(1)} custom-call(s32[1,2048]{1,0:T(1,128)S(1)} %shard_map.128.refs_0_.refs_1_, bf16[2048,256]{1,0:T(8,128)(2,1)S(1)} %copy-done.1), custom_call_target="tpu_custom_call" | custom-call | flops 536870912 | bytes 1581056 | tf_op jit(solution)/shard_map/pallas_call | solution.py:70
  4.0 0.7 %shard_map.129.refs_0_ = f32[512,256]{1,0:T(8,128)S(1)} custom-call(s32[1,2048]{1,0:T(1,128)S(1)} %shard_map.128.refs_0_.refs_1_, bf16[2048,256]{1,0:T(8,128)(2,1)S(1)} %copy-done.6), custom_call_target="tpu_custom_call" | custom-call | flops 536870912 | bytes 1581056 | tf_op jit(solution)/shard_map/pallas_call | solution.py:70
  4.8 3.0 %collective-permute-start.3 = (bf16[512,256]{1,0:T(8,128)(2,1)S(1)}, bf16[512,256]{1,0:T(8,128)(2,1)S(1)}, u32[]{:S(2)}, u32[]{:S(2)}) collective-permute-start(bf16[512,256]{1,0:T(8,128)(2,1)S(1)} %get-tuple-element.39.refs_2_.refs_0_), channel_id=1, source_target_pairs={{0,2},{1,3},{2,0},{3,1},{4,6},{5,7},{6,4},{7,5},{8,10},{9,11},{10,... | collective-permute-start | bytes 786440 | tf_op jit(solution)/shard_map/ppermute | solution.py:39
  8.4 1.0 %collective-permute-done.4.refs_1_ = bf16[128,256]{1,0:T(8,128)(2,1)S(1)} collective-permute-done((bf16[128,256]{1,0:T(8,128)(2,1)S(1)}, bf16[128,256]{1,0:T(8,128)(2,1)S(1)}, u32[]{:S(2)}, u32[]{:S(2)}) %collective-permute-start.4) | collective-permute-done | bytes 65568 | tf_op jit(solution)/shard_map/ppermute | solution.py:39
  9.4 1.4 %collective-permute-start.6 = (bf16[64,256]{1,0:T(8,128)(2,1)S(1)}, bf16[64,256]{1,0:T(8,128)(2,1)S(1)}, u32[]{:S(2)}, u32[]{:S(2)}) collective-permute-start(bf16[64,256]{1,0:T(8,128)(2,1)S(1)} %shard_map.136), channel_id=1, source_target_pairs={{0,6},{1,31},{2,4},{3,29},{4,10},{5,3},{6,8},{7,1},{8,14},{9,7},{1... | collective-permute-start | bytes 98312 | tf_op jit(solution)/shard_map/ppermute | solution.py:55
  10.8 1.5 %collective-permute-start.5 = (bf16[64,256]{1,0:T(8,128)(2,1)S(1)}, bf16[64,256]{1,0:T(8,128)(2,1)S(1)}, u32[]{:S(2)}, u32[]{:S(2)}) collective-permute-start(bf16[64,256]{1,0:T(8,128)(2,1)S(1)} %shard_map.136), channel_id=1, source_target_pairs={{0,4},{1,29},{2,6},{3,31},{4,8},{5,1},{6,10},{7,3},{8,12},{9,5},{1... | collective-permute-start | bytes 98312 | tf_op jit(solution)/shard_map/ppermute | solution.py:55
  12.3 0.7 %shard_map.132.refs_0_ = f32[512,256]{1,0:T(8,128)S(1)} custom-call(s32[1,2048]{1,0:T(1,128)S(1)} %shard_map.128.refs_0_.refs_1_, bf16[2048,256]{1,0:T(8,128)(2,1)S(1)} %copy-done.1, bf16[512,256]{1,0:T(8,128)(2,1)S(1)} %get-tuple-element.39.refs_2_.refs_0_), custom_call_target="tpu_custom_call" | custom-call | flops 536870912 | bytes 1581056 | tf_op jit(solution)/shard_map/pallas_call | solution.py:70
  13.1 1.6 %collective-permute-start.2 = (bf16[512,256]{1,0:T(8,128)(2,1)S(1)}, bf16[512,256]{1,0:T(8,128)(2,1)S(1)}, u32[]{:S(2)}, u32[]{:S(2)}) collective-permute-start(bf16[512,256]{1,0:T(8,128)(2,1)S(1)} %get-tuple-element.41), channel_id=1, source_target_pairs={{0,2},{1,3},{2,0},{3,1},{4,6},{5,7},{6,4},{7,5},{8,10},{9,11},{10,... | collective-permute-start | bytes 786440 | tf_op jit(solution)/shard_map/ppermute | solution.py:39
  14.7 2.1 %collective-permute-done.6.refs_1_ = bf16[64,256]{1,0:T(8,128)(2,1)S(1)} collective-permute-done((bf16[64,256]{1,0:T(8,128)(2,1)S(1)}, bf16[64,256]{1,0:T(8,128)(2,1)S(1)}, u32[]{:S(2)}, u32[]{:S(2)}) %collective-permute-start.6) | collective-permute-done | bytes 32800 | tf_op jit(solution)/shard_map/ppermute | solution.py:55
  18.2 1.5 %shard_map.141.refs_2_ = bf16[4096,256]{1,0:T(8,128)(2,1)S(1)} custom-call(bf16[512,256]{1,0:T(8,128)(2,1)S(1)} %shard_map.139.refs_2_.refs_0_, s32[4,1024]{1,0:T(4,128)S(1)} %shard_map.138.refs_3_.refs_1_), custom_call_target="tpu_custom_call" | custom-call | tf_op jit(solution)/shard_map/pallas_call | solution.py:70
  20.0 1.7 %shard_map.142 = (f32[1024,256]{1,0:T(8,128)S(1)}, f32[2048,256]{1,0:T(8,128)S(1)}, bf16[2048,256]{1,0:T(8,128)(2,1)S(1)}, f32[8,128]{1,0:T(8,128)S(1)}) custom-call(f32[1024,256]{1,0:T(8,128)S(1)} %get-tuple-element.43.refs_0_, bf16[640,256]{1,0:T(8,128)(2,1)S(1)} %get-tuple-element.44.refs_1_, bf16[4096,256]{1,0:T(8,128)(2,1)S(1)} %shard_map.141.refs_2_, ...), custom_call_target="tpu_custom_call" | custom-call | tf_op jit(solution)/shard_map/pallas_call | solution.py:70
  22.4 1.7 %shard_map.144 = (f32[1024,256]{1,0:T(8,128)S(1)}, f32[2048,256]{1,0:T(8,128)S(1)}, bf16[2048,256]{1,0:T(8,128)(2,1)S(1)}) custom-call(f32[1024,256]{1,0:T(8,128)S(1)} %get-tuple-element.43.refs_0_, bf16[640,256]{1,0:T(8,128)(2,1)S(1)} %get-tuple-element.44.refs_1_, bf16[4096,256]{1,0:T(8,128)(2,1)S(1)} %shard_map.141.refs_2_, ...), custom_call_target="tpu_custom_call" | custom-call | tf_op jit(solution)/shard_map/pallas_call | solution.py:70
  24.1 1.5 %shard_map.145 = (bf16[4096,256]{1,0:T(8,128)(2,1)S(1)}, f32[1024,256]{1,0:T(8,128)S(1)}, bf16[1024,256]{1,0:T(8,128)(2,1)S(1)}, f32[128,256]{1,0:T(8,128)S(1)},...) custom-call(bf16[512,256]{1,0:T(8,128)(2,1)S(1)} %shard_map.143.refs_5_.refs_0_, ...), custom_call_target="tpu_custom_call" | custom-call | flops 536870912 | bytes 13582336 | tf_op jit(solution)/shard_map/pallas_call | solution.py:70
  25.6 1.5 %collective-permute-start.13 = (bf16[144,256]{1,0:T(8,128)(2,1)S(1)}, bf16[144,256]{1,0:T(8,128)(2,1)S(1)}, u32[]{:S(2)}, u32[]{:S(2)}) collective-permute-start(bf16[144,256]{1,0:T(8,128)(2,1)S(1)} %get-tuple-element.57), channel_id=1, source_target_pairs={{0,4},{4,0},{8,12},{12,8},{16,20},{20,16},{24,28},{28,24},{1,5},{5... | collective-permute-start | bytes 221192 | tf_op jit(solution)/shard_map/ppermute | solution.py:39
  27.1 0.6 %shard_map.148.refs_3_ = bf16[64,256]{1,0:T(8,128)(2,1)S(1)} custom-call(bf16[4096,256]{1,0:T(8,128)(2,1)S(1)} %get-tuple-element.53.refs_0_, s32[4,1024]{1,0:T(4,128)S(1)} %shard_map.138.refs_3_.refs_1_, bf16[512,256]{1,0:T(8,128)(2,1)S(1)} %copy-done), custom_call_target="tpu_custom_call" | custom-call | flops 268435456 | bytes 2408448 | tf_op jit(solution)/shard_map/pallas_call | solution.py:70
  27.7 0.9 %collective-permute-start.11 = (bf16[64,256]{1,0:T(8,128)(2,1)S(1)}, bf16[64,256]{1,0:T(8,128)(2,1)S(1)}, u32[]{:S(2)}, u32[]{:S(2)}) collective-permute-start(bf16[64,256]{1,0:T(8,128)(2,1)S(1)} %shard_map.148.refs_3_), channel_id=1, source_target_pairs={{0,4},{1,29},{2,6},{3,31},{4,8},{5,1},{6,10},{7,3},{8,12},{9,5},{1... | collective-permute-start | bytes 98312 | tf_op jit(solution)/shard_map/ppermute | solution.py:55
  28.6 1.8 %collective-permute-done.13.refs_1_ = bf16[144,256]{1,0:T(8,128)(2,1)S(1)} collective-permute-done((bf16[144,256]{1,0:T(8,128)(2,1)S(1)}, bf16[144,256]{1,0:T(8,128)(2,1)S(1)}, u32[]{:S(2)}, u32[]{:S(2)}) %collective-permute-start.13) | collective-permute-done | bytes 73760 | tf_op jit(solution)/shard_map/ppermute | solution.py:39
  30.9 1.5 %shard_map.146.refs_0_.refs_3_ = f32[512,256]{1,0:T(8,128)S(1)} custom-call(bf16[4096,256]{1,0:T(8,128)(2,1)S(1)} %get-tuple-element.53.refs_0_, s32[4,1024]{1,0:T(4,128)S(1)} %shard_map.138.refs_3_.refs_1_, f32[1024,256]{1,0:T(8,128)S(1)} %get-tuple-element.54.refs_2_, bf16[1024,256]{1,0:T(8,128)(2,1)S(1)} %get-tuple-element.55.refs_3_, ...), custom_call_target="tpu_custom_call" | custom-call | flops 1073741824 | bytes 4472832 | tf_op jit(solution)/shard_map/pallas_call | solution.py:70
  32.4 2.1 %collective-permute-done.11.refs_2_ = bf16[64,256]{1,0:T(8,128)(2,1)S(1)} collective-permute-done((bf16[64,256]{1,0:T(8,128)(2,1)S(1)}, bf16[64,256]{1,0:T(8,128)(2,1)S(1)}, u32[]{:S(2)}, u32[]{:S(2)}) %collective-permute-start.11) | collective-permute-done | bytes 32800 | tf_op jit(solution)/shard_map/ppermute | solution.py:55
  34.8 1.5 %collective-permute-start.15 = (bf16[144,256]{1,0:T(8,128)(2,1)S(1)}, bf16[144,256]{1,0:T(8,128)(2,1)S(1)}, u32[]{:S(2)}, u32[]{:S(2)}) collective-permute-start(bf16[144,256]{1,0:T(8,128)(2,1)S(1)} %get-tuple-element.63), channel_id=1, source_target_pairs={{0,16},{4,20},{8,24},{12,28},{16,0},{20,4},{24,8},{28,12},{1,17},{... | collective-permute-start | bytes 221192 | tf_op jit(solution)/shard_map/ppermute | solution.py:39
  36.4 1.5 %shard_map.147.refs_1_ = f32[512,256]{1,0:T(8,128)S(1)} custom-call(bf16[4096,256]{1,0:T(8,128)(2,1)S(1)} %get-tuple-element.53.refs_0_, s32[4,1024]{1,0:T(4,128)S(1)} %shard_map.138.refs_3_.refs_1_, f32[1024,256]{1,0:T(8,128)S(1)} %get-tuple-element.54.refs_2_, bf16[1024,256]{1,0:T(8,128)(2,1)S(1)} %get-tuple-element.55.refs_3_, bf16[512,256]{1,0:T(8,128)(2,1)S(1)} %copy-done), custom_call_target="tpu_custom_call" | custom-call | flops 1073741824 | bytes 4472832 | tf_op jit(solution)/shard_map/pallas_call | solution.py:70
  38.2 1.2 %shard_map.152 = (bf16[2048,256]{1,0:T(8,128)(2,1)}, f32[8,128]{1,0:T(8,128)S(1)}) custom-call(bf16[1024,256]{1,0:T(8,128)(2,1)S(1)} %shard_map.149.refs_0_, s32[1,2048]{1,0:T(1,128)S(1)} %shard_map.128.refs_0_.refs_1_, bf16[2048,256]{1,0:T(8,128)(2,1)S(1)} %copy-done.1), custom_call_target="tpu_custom_call" | custom-call | flops 268435456 | bytes 2633728 | tf_op jit(solution)/shard_map/pallas_call | solution.py:70
  39.4 1.6 %collective-permute-done.15.refs_1_ = bf16[144,256]{1,0:T(8,128)(2,1)S(1)} collective-permute-done((bf16[144,256]{1,0:T(8,128)(2,1)S(1)}, bf16[144,256]{1,0:T(8,128)(2,1)S(1)}, u32[]{:S(2)}, u32[]{:S(2)}) %collective-permute-start.15) | collective-permute-done | bytes 73760 | tf_op jit(solution)/shard_map/ppermute | solution.py:39
  41.1 2.2 %collective-permute-start.18 = (bf16[144,256]{1,0:T(8,128)(2,1)S(1)}, bf16[144,256]{1,0:T(8,128)(2,1)S(1)}, u32[]{:S(2)}, u32[]{:S(2)}) collective-permute-start(bf16[144,256]{1,0:T(8,128)(2,1)S(1)} %shard_map.153.refs_3_.refs_0_), channel_id=1, source_target_pairs={{0,6},{1,7},{2,4},{3,5},{4,2},{5,3},{6,0},{7,1},{8,14},{9,15},{10,... | collective-permute-start | bytes 221192 | tf_op jit(solution)/shard_map/ppermute | solution.py:45
  43.8 0.8 %collective-permute-start.16 = (bf16[144,256]{1,0:T(8,128)(2,1)S(1)}, bf16[144,256]{1,0:T(8,128)(2,1)S(1)}, u32[]{:S(2)}, u32[]{:S(2)}) collective-permute-start(bf16[144,256]{1,0:T(8,128)(2,1)S(1)} %shard_map.153.refs_3_.refs_0_), channel_id=1, source_target_pairs={{0,4},{4,0},{8,12},{12,8},{16,20},{20,16},{24,28},{28,24},{1,5},{5... | collective-permute-start | bytes 221192 | tf_op jit(solution)/shard_map/ppermute | solution.py:39
  44.6 1.9 %shard_map.154 = (bf16[2048,256]{1,0:T(8,128)(2,1)}, f32[8,128]{1,0:T(8,128)S(1)}) custom-call(bf16[1024,256]{1,0:T(8,128)(2,1)S(1)} %shard_map.149.refs_0_, s32[1,2048]{1,0:T(1,128)S(1)} %shard_map.128.refs_0_.refs_1_, bf16[2048,256]{1,0:T(8,128)(2,1)S(1)} %copy-done.1, ...), custom_call_target="tpu_custom_call", output_to_operand_aliasing={{0}: (4, {})} | custom-call | flops 805306368 | bytes 2633728 | tf_op jit(solution)/shard_map/pallas_call | solution.py:70
  46.6 0.6 %collective-permute-done.18.refs_3_ = bf16[144,256]{1,0:T(8,128)(2,1)S(1)} collective-permute-done((bf16[144,256]{1,0:T(8,128)(2,1)S(1)}, bf16[144,256]{1,0:T(8,128)(2,1)S(1)}, u32[]{:S(2)}, u32[]{:S(2)}) %collective-permute-start.18) | collective-permute-done | bytes 73760 | tf_op jit(solution)/shard_map/ppermute | solution.py:45
  47.2 0.7 %collective-permute-done.17.refs_2_ = bf16[144,256]{1,0:T(8,128)(2,1)S(1)} collective-permute-done((bf16[144,256]{1,0:T(8,128)(2,1)S(1)}, bf16[144,256]{1,0:T(8,128)(2,1)S(1)}, u32[]{:S(2)}, u32[]{:S(2)}) %collective-permute-start.17) | collective-permute-done | bytes 73760 | tf_op jit(solution)/shard_map/ppermute | solution.py:39
  48.3 1.5 %collective-permute-done.19.refs_1_ = bf16[544,256]{1,0:T(8,128)(2,1)S(1)} collective-permute-done((bf16[544,256]{1,0:T(8,128)(2,1)S(1)}, bf16[544,256]{1,0:T(8,128)(2,1)S(1)}, u32[]{:S(2)}, u32[]{:S(2)}) %collective-permute-start.19) | collective-permute-done | bytes 278560 | tf_op jit(solution)/shard_map/ppermute | solution.py:39
  49.8 1.0 %shard_map.156 = (f32[512,256]{1,0:T(8,128)}, f32[1,256]{1,0:T(1,128)}, f32[256,256]{1,0:T(8,128)}, f32[256,256]{1,0:T(8,128)}) custom-call(bf16[544,256]{1,0:T(8,128)(2,1)S(1)} %shard_map.155.refs_0_, bf16[544,256]{1,0:T(8,128)(2,1)S(1)} %collective-permute-done.19.refs_1_), custom_call_target="tpu_custom_call" | custom-call | tf_op jit(solution)/shard_map/pallas_call | solution.py:70
  (57 shorter events, 6.3 us)
Async XLA Ops:
  0.6 1.2 %copy-start.6 = (bf16[2048,256]{1,0:T(8,128)(2,1)S(1)}, bf16[2048,256]{1,0:T(8,128)(2,1)}, u32[]{:S(2)}) copy-start(bf16[2048,256]{1,0:T(8,128)(2,1)} %refs_1_.5) | copy-start | bytes 3145732
  0.6 0.8 %copy-start.7 = (s32[2048]{0:T(1024)S(1)}, s32[2048]{0:T(1024)}, u32[]{:S(2)}) copy-start(s32[2048]{0:T(1024)} %param.11) | copy-start | bytes 24580
  1.4 1.7 %copy-start.1 = (bf16[2048,256]{1,0:T(8,128)(2,1)S(1)}, bf16[2048,256]{1,0:T(8,128)(2,1)}, u32[]{:S(2)}) copy-start(bf16[2048,256]{1,0:T(8,128)(2,1)} %refs_2_.5) | copy-start | bytes 3145732
  2.6 5.2 %copy-start.5 = (s32[128]{0:T(128)S(1)}, s32[128]{0:T(128)}, u32[]{:S(2)}) copy-start(s32[128]{0:T(128)} %param.12) | copy-start | bytes 1540
  2.6 2.1 %collective-permute-start = (f32[512,256]{1,0:T(8,128)S(1)}, f32[512,256]{1,0:T(8,128)S(1)}, u32[]{:S(2)}, u32[]{:S(2)}) collective-permute-start(f32[512,256]{1,0:T(8,128)S(1)} %shard_map.130), channel_id=1, source_target_pairs={{0,1},{1,0},{2,3},{3,2},{4,5},{5,4},{6,7},{7,6},{8,9},{9,8},{10,11... | collective-permute-start | bytes 1572872 | tf_op jit(solution)/shard_map/ppermute | solution.py:39
  3.8 4.3 %copy-start.8 = (bf16[256]{0:T(256)(128)(2,1)S(1)}, bf16[256]{0:T(256)(128)(2,1)}, u32[]{:S(2)}) copy-start(bf16[256]{0:T(256)(128)(2,1)} %param.15) | copy-start | bytes 1540
  3.8 4.3 %copy-start.4 = (s32[4096]{0:T(1024)S(1)}, s32[4096]{0:T(1024)}, u32[]{:S(2)}) copy-start(s32[4096]{0:T(1024)} %param.13) | copy-start | bytes 49156
  3.8 9.2 %collective-permute-start.1 = (f32[512,256]{1,0:T(8,128)S(1)}, f32[512,256]{1,0:T(8,128)S(1)}, u32[]{:S(2)}, u32[]{:S(2)}) collective-permute-start(f32[512,256]{1,0:T(8,128)S(1)} %shard_map.133), channel_id=1, source_target_pairs={{0,1},{1,0},{2,3},{3,2},{4,5},{5,4},{6,7},{7,6},{8,9},{9,8},{10,11... | collective-permute-start | bytes 1572872 | tf_op jit(solution)/shard_map/ppermute | solution.py:39
  4.8 12.7 %collective-permute-start.3 = (bf16[512,256]{1,0:T(8,128)(2,1)S(1)}, bf16[512,256]{1,0:T(8,128)(2,1)S(1)}, u32[]{:S(2)}, u32[]{:S(2)}) collective-permute-start(bf16[512,256]{1,0:T(8,128)(2,1)S(1)} %get-tuple-element.39.refs_2_.refs_0_), channel_id=1, source_target_pairs={{0,2},{1,3},{2,0},{3,1},{4,6},{5,7},{6,4},{7,5},{8,10},{9,11},{10,... | collective-permute-start | bytes 786440 | tf_op jit(solution)/shard_map/ppermute | solution.py:39
  8.0 1.3 %collective-permute-start.4 = (bf16[128,256]{1,0:T(8,128)(2,1)S(1)}, bf16[128,256]{1,0:T(8,128)(2,1)S(1)}, u32[]{:S(2)}, u32[]{:S(2)}) collective-permute-start(bf16[128,256]{1,0:T(8,128)(2,1)S(1)} %shard_map.135.refs_0_), channel_id=1, source_target_pairs={{0,1},{1,0},{2,3},{3,2},{4,5},{5,4},{6,7},{7,6},{8,9},{9,8},{10,11... | collective-permute-start | bytes 196616 | tf_op jit(solution)/shard_map/ppermute | solution.py:39
  9.4 7.5 %collective-permute-start.6 = (bf16[64,256]{1,0:T(8,128)(2,1)S(1)}, bf16[64,256]{1,0:T(8,128)(2,1)S(1)}, u32[]{:S(2)}, u32[]{:S(2)}) collective-permute-start(bf16[64,256]{1,0:T(8,128)(2,1)S(1)} %shard_map.136), channel_id=1, source_target_pairs={{0,6},{1,31},{2,4},{3,29},{4,10},{5,3},{6,8},{7,1},{8,14},{9,7},{1... | collective-permute-start | bytes 98312 | tf_op jit(solution)/shard_map/ppermute | solution.py:55
  10.8 6.6 %collective-permute-start.5 = (bf16[64,256]{1,0:T(8,128)(2,1)S(1)}, bf16[64,256]{1,0:T(8,128)(2,1)S(1)}, u32[]{:S(2)}, u32[]{:S(2)}) collective-permute-start(bf16[64,256]{1,0:T(8,128)(2,1)S(1)} %shard_map.136), channel_id=1, source_target_pairs={{0,4},{1,29},{2,6},{3,31},{4,8},{5,1},{6,10},{7,3},{8,12},{9,5},{1... | collective-permute-start | bytes 98312 | tf_op jit(solution)/shard_map/ppermute | solution.py:55
  13.1 6.6 %copy-start = (bf16[512,256]{1,0:T(8,128)(2,1)S(1)}, bf16[512,256]{1,0:T(8,128)(2,1)}, u32[]{:S(2)}) copy-start(bf16[512,256]{1,0:T(8,128)(2,1)} %refs_2_.3) | copy-start | bytes 786436
  13.1 8.8 %collective-permute-start.2 = (bf16[512,256]{1,0:T(8,128)(2,1)S(1)}, bf16[512,256]{1,0:T(8,128)(2,1)S(1)}, u32[]{:S(2)}, u32[]{:S(2)}) collective-permute-start(bf16[512,256]{1,0:T(8,128)(2,1)S(1)} %get-tuple-element.41), channel_id=1, source_target_pairs={{0,2},{1,3},{2,0},{3,1},{4,6},{5,7},{6,4},{7,5},{8,10},{9,11},{10,... | collective-permute-start | bytes 786440 | tf_op jit(solution)/shard_map/ppermute | solution.py:39
  17.5 2.2 %collective-permute-start.8 = (bf16[256,256]{1,0:T(8,128)(2,1)S(1)}, bf16[256,256]{1,0:T(8,128)(2,1)S(1)}, u32[]{:S(2)}, u32[]{:S(2)}) collective-permute-start(bf16[256,256]{1,0:T(8,128)(2,1)S(1)} %get-tuple-element.73), channel_id=1, source_target_pairs={{0,1},{1,0},{2,3},{3,2},{4,5},{5,4},{6,7},{7,6},{8,9},{9,8},{10,11... | collective-permute-start | bytes 393224 | tf_op jit(solution)/shard_map/ppermute | solution.py:39
  17.6 2.1 %collective-permute-start.7 = (bf16[256,256]{1,0:T(8,128)(2,1)S(1)}, bf16[256,256]{1,0:T(8,128)(2,1)S(1)}, u32[]{:S(2)}, u32[]{:S(2)}) collective-permute-start(bf16[256,256]{1,0:T(8,128)(2,1)S(1)} %get-tuple-element.74), channel_id=1, source_target_pairs={{0,1},{1,0},{2,3},{3,2},{4,5},{5,4},{6,7},{7,6},{8,9},{9,8},{10,11... | collective-permute-start | bytes 393224 | tf_op jit(solution)/shard_map/ppermute | solution.py:39
  18.1 1.6 %collective-permute-start.9 = (bf16[64,256]{1,0:T(8,128)(2,1)S(1)}, bf16[64,256]{1,0:T(8,128)(2,1)S(1)}, u32[]{:S(2)}, u32[]{:S(2)}) collective-permute-start(bf16[64,256]{1,0:T(8,128)(2,1)S(1)} %shard_map.137.refs_2_.refs_3_), channel_id=1, source_target_pairs={{0,1},{1,0},{2,3},{3,2},{4,5},{5,4},{6,7},{7,6},{8,9},{9,8},{10,11... | collective-permute-start | bytes 98312 | tf_op jit(solution)/shard_map/ppermute | solution.py:39
  22.0 2.1 %copy-start.2 = (bf16[256,256]{1,0:T(8,128)(2,1)S(1)}, bf16[256,256]{1,0:T(8,128)(2,1)}, u32[]{:S(2)}) copy-start(bf16[256,256]{1,0:T(8,128)(2,1)} %refs_9_.1) | copy-start | bytes 393220
  22.0 2.1 %copy-start.3 = (bf16[256,256]{1,0:T(8,128)(2,1)S(1)}, bf16[256,256]{1,0:T(8,128)(2,1)}, u32[]{:S(2)}) copy-start(bf16[256,256]{1,0:T(8,128)(2,1)} %refs_10_.1) | copy-start | bytes 393220
  22.1 2.1 %collective-permute-start.10 = (bf16[512,256]{1,0:T(8,128)(2,1)S(1)}, bf16[512,256]{1,0:T(8,128)(2,1)S(1)}, u32[]{:S(2)}, u32[]{:S(2)}) collective-permute-start(bf16[512,256]{1,0:T(8,128)(2,1)S(1)} %shard_map.143.refs_5_.refs_0_), channel_id=1, source_target_pairs={{0,1},{1,0},{2,3},{3,2},{4,5},{5,4},{6,7},{7,6},{8,9},{9,8},{10,11... | collective-permute-start | bytes 786440 | tf_op jit(solution)/shard_map/ppermute | solution.py:39
  25.6 4.7 %collective-permute-start.13 = (bf16[144,256]{1,0:T(8,128)(2,1)S(1)}, bf16[144,256]{1,0:T(8,128)(2,1)S(1)}, u32[]{:S(2)}, u32[]{:S(2)}) collective-permute-start(bf16[144,256]{1,0:T(8,128)(2,1)S(1)} %get-tuple-element.57), channel_id=1, source_target_pairs={{0,4},{4,0},{8,12},{12,8},{16,20},{20,16},{24,28},{28,24},{1,5},{5... | collective-permute-start | bytes 221192 | tf_op jit(solution)/shard_map/ppermute | solution.py:39
  27.7 6.8 %collective-permute-start.11 = (bf16[64,256]{1,0:T(8,128)(2,1)S(1)}, bf16[64,256]{1,0:T(8,128)(2,1)S(1)}, u32[]{:S(2)}, u32[]{:S(2)}) collective-permute-start(bf16[64,256]{1,0:T(8,128)(2,1)S(1)} %shard_map.148.refs_3_), channel_id=1, source_target_pairs={{0,4},{1,29},{2,6},{3,31},{4,8},{5,1},{6,10},{7,3},{8,12},{9,5},{1... | collective-permute-start | bytes 98312 | tf_op jit(solution)/shard_map/ppermute | solution.py:55
  30.4 4.4 %collective-permute-start.14 = (bf16[144,256]{1,0:T(8,128)(2,1)S(1)}, bf16[144,256]{1,0:T(8,128)(2,1)S(1)}, u32[]{:S(2)}, u32[]{:S(2)}) collective-permute-start(bf16[144,256]{1,0:T(8,128)(2,1)S(1)} %get-tuple-element.60), channel_id=1, source_target_pairs={{0,8},{4,12},{8,0},{12,4},{16,24},{20,28},{24,16},{28,20},{1,9},{5... | collective-permute-start | bytes 221192 | tf_op jit(solution)/shard_map/ppermute | solution.py:39
  34.6 3.3 %collective-permute-start.12 = (bf16[64,256]{1,0:T(8,128)(2,1)S(1)}, bf16[64,256]{1,0:T(8,128)(2,1)S(1)}, u32[]{:S(2)}, u32[]{:S(2)}) collective-permute-start(bf16[64,256]{1,0:T(8,128)(2,1)S(1)} %collective-permute-done.11.refs_2_), channel_id=1, source_target_pairs={{0,1},{1,0},{2,3},{3,2},{4,5},{5,4},{6,7},{7,6},{8,9},{9,8},{10,11... | collective-permute-start | bytes 98312 | tf_op jit(solution)/shard_map/ppermute | solution.py:39
  34.8 6.2 %collective-permute-start.15 = (bf16[144,256]{1,0:T(8,128)(2,1)S(1)}, bf16[144,256]{1,0:T(8,128)(2,1)S(1)}, u32[]{:S(2)}, u32[]{:S(2)}) collective-permute-start(bf16[144,256]{1,0:T(8,128)(2,1)S(1)} %get-tuple-element.63), channel_id=1, source_target_pairs={{0,16},{4,20},{8,24},{12,28},{16,0},{20,4},{24,8},{28,12},{1,17},{... | collective-permute-start | bytes 221192 | tf_op jit(solution)/shard_map/ppermute | solution.py:39
  41.1 6.1 %collective-permute-start.18 = (bf16[144,256]{1,0:T(8,128)(2,1)S(1)}, bf16[144,256]{1,0:T(8,128)(2,1)S(1)}, u32[]{:S(2)}, u32[]{:S(2)}) collective-permute-start(bf16[144,256]{1,0:T(8,128)(2,1)S(1)} %shard_map.153.refs_3_.refs_0_), channel_id=1, source_target_pairs={{0,6},{1,7},{2,4},{3,5},{4,2},{5,3},{6,0},{7,1},{8,14},{9,15},{10,... | collective-permute-start | bytes 221192 | tf_op jit(solution)/shard_map/ppermute | solution.py:45
  43.3 4.5 %collective-permute-start.17 = (bf16[144,256]{1,0:T(8,128)(2,1)S(1)}, bf16[144,256]{1,0:T(8,128)(2,1)S(1)}, u32[]{:S(2)}, u32[]{:S(2)}) collective-permute-start(bf16[144,256]{1,0:T(8,128)(2,1)S(1)} %shard_map.153.refs_3_.refs_0_), channel_id=1, source_target_pairs={{0,2},{1,3},{2,0},{3,1},{4,6},{5,7},{6,4},{7,5},{8,10},{9,11},{10,... | collective-permute-start | bytes 221192 | tf_op jit(solution)/shard_map/ppermute | solution.py:39
  43.8 4.4 %collective-permute-start.16 = (bf16[144,256]{1,0:T(8,128)(2,1)S(1)}, bf16[144,256]{1,0:T(8,128)(2,1)S(1)}, u32[]{:S(2)}, u32[]{:S(2)}) collective-permute-start(bf16[144,256]{1,0:T(8,128)(2,1)S(1)} %shard_map.153.refs_3_.refs_0_), channel_id=1, source_target_pairs={{0,4},{4,0},{8,12},{12,8},{16,20},{20,16},{24,28},{28,24},{1,5},{5... | collective-permute-start | bytes 221192 | tf_op jit(solution)/shard_map/ppermute | solution.py:39
  48.2 1.6 %collective-permute-start.19 = (bf16[544,256]{1,0:T(8,128)(2,1)S(1)}, bf16[544,256]{1,0:T(8,128)(2,1)S(1)}, u32[]{:S(2)}, u32[]{:S(2)}) collective-permute-start(bf16[544,256]{1,0:T(8,128)(2,1)S(1)} %shard_map.155.refs_0_), channel_id=1, source_target_pairs={{0,1},{1,0},{2,3},{3,2},{4,5},{5,4},{6,7},{7,6},{8,9},{9,8},{10,11... | collective-permute-start | bytes 835592 | tf_op jit(solution)/shard_map/ppermute | solution.py:39

commit v9 on v8

--- a/solution.py
+++ b/solution.py
@@ -37,6 +37,10 @@
 def swap(x, axis, bit):
     count = lax.axis_size(axis)
     return lax.ppermute(x, axis, [(i, i ^ (1 << bit)) for i in range(count)])
+
+
+def swap_owners(x):
+    return lax.ppermute(x, "coarse", [(i, i ^ 3) for i in range(lax.axis_size("coarse"))])
 
 
 def swap_both(x):
@@ -248,15 +252,10 @@
     return lax.rem(lax.axis_index(axis) // (1 << bit), 2)
 
 
-def emit(total_ref, bias, bit, keep_ref, send_ref, bias_ref):
+def emit(total, bias, keep_ref, send_ref, bias_ref):
     n = keep_ref.shape[0]
-    if n == total_ref.shape[0]:
-        sent = total_ref[...].astype(BF)
-        keep_ref[...] = sent.astype(F32)
-    else:
-        side = axis_bit("coarse", bit)
-        keep_ref[...] = total_ref[pl.ds(pl.multiple_of(side * n, n), n), :]
-        sent = total_ref[pl.ds(pl.multiple_of((1 - side) * n, n), n), :].astype(BF)
+    sent = total.astype(BF)
+    keep_ref[...] = sent.astype(F32)
     rows, bias = bias_rows(bias)
     send_ref[0:n, :] = sent
     send_ref[n : n + PACK, :] = rows
@@ -265,7 +264,7 @@
 
 def backward_body(
     own_g, other_g, table, hid_1, slope_1, feats_1, hid_2, slope_2, feats_2, wo_ref, wu_ref,
-    act, ga_ref, gn_ref, keep_ref, send_ref, bias_ref,
+    act, ga_ref, gn_ref, mine_ref, by_one, by_two, by_both,
     gsum, total,
 ):
     half, width = own_g.shape
@@ -313,17 +312,31 @@
                     out = dot_tn(new, gsum[...])
                 total[r : r + n, :] = out
 
-    emit(total, jnp.sum(ga_ref[...], axis=0, keepdims=True), 0, keep_ref, send_ref, bias_ref)
+    rows = bias_rows(jnp.sum(ga_ref[...], axis=0, keepdims=True))[0]
+    half = axis_bit("coarse", 0)
+    n = per // 2
+    for ref, at in ((mine_ref, half), (by_one, 1 - half), (by_two, half), (by_both, 1 - half)):
+        ref[0:n, :] = total[pl.ds(pl.multiple_of(at * n, n), n), :].astype(BF)
+        ref[n : n + PACK, :] = rows
+
+
+def square_sum_body(own, by_both, by_two, by_one, keep_ref, send_ref, bias_ref, slots):
+    n = keep_ref.shape[0]
+    me = lax.rem(lax.axis_index("coarse"), 4)
+    for i, ref in enumerate((own, by_one, by_two, by_both)):
+        slots[me ^ i] = ref[...].astype(F32)
+    total = slots[0] + slots[1] + slots[2] + slots[3]
+    emit(total[0:n], total[n : n + 1] + total[n + 1 : n + 2], keep_ref, send_ref, bias_ref)
 
 
 def received_bias(recv, n):
     return recv[n : n + 1, :].astype(F32) + recv[n + 1 : n + 2, :].astype(F32)
 
 
-def stage_body(keep_in, recv, bias_in, keep_ref, send_ref, bias_ref, total, *, bit):
+def stage_body(keep_in, recv, bias_in, keep_ref, send_ref, bias_ref):
     n = keep_in.shape[0]
-    total[...] = keep_in[...] + recv[0:n, :].astype(F32)
-    emit(total, bias_in[0:1, :] + received_bias(recv, n), bit, keep_ref, send_ref, bias_ref)
+    total = keep_in[...] + recv[0:n, :].astype(F32)
+    emit(total, bias_in[0:1, :] + received_bias(recv, n), keep_ref, send_ref, bias_ref)
 
 
 def end_body(keep_in, recv, bias_in, out_ref):
@@ -498,11 +511,12 @@
     rear = forward(EARLY, K - EARLY, after=(own_g,))
     per = 4 * width // fines
     first = per // 2
-    act, ga, gn, keep, send, bias_sum = call(
+    message = sds((first + PACK, width), BF)
+    act, ga, gn, mine, *sends = call(
         backward_body,
         (
             sds((K * cells, width), BF), sds((cells, width), F32), sds((cells, width), BF),
-            sds((first, width), F32), sds((first + PACK, width), BF), sds((8, width), F32),
+            message, message, message, message,
         ),
         (own_g, other_g, table, *front, *rear, w_edge_out, w_unpool),
         2 * K * cells * width * width,
@@ -511,20 +525,26 @@
     )
 
     back = call(
-        back_body, (sds((side, width), BF),), (act, src, w_edge_in), 4 * K * side * cells * width,
+        back_body, (sds((side, width), BF),), (act, src, w_edge_in), 0,
         scratch=(pltpu.VMEM((2 * side, width), F32),),
     )[0]
     own_back = send_sides(back)
-    other_back = swap(own_back, "fine", 0)
     cell_grads = [
         call(
             functools.partial(cell_grad_body, first=at),
             (sds((half, width), F32),),
             (act, src, ga, gn, w_edge_in),
-            2 * K * half * cells * width,
+            0,
         )[0]
         for at in (0, half)
     ]
+    recvs = swap_owners(sends[2]), swap(sends[1], "coarse", 1), swap(sends[0], "coarse", 0)
+    outs = (sds((first, width), F32), message, sds((8, width), F32))
+    keep, send, bias_sum = call(
+        square_sum_body, outs, (mine, *recvs), 0, after=(own_back, cell_grads[1]),
+        scratch=(pltpu.VMEM((4, first + PACK, width), F32),),
+    )
+    other_back = swap(own_back, "fine", 0)
     table = call(
         table_body, (sds((cells, width), BF),), (*cell_grads, own_back, other_back, lists), 0
     )[0]
@@ -542,25 +562,13 @@
             far=1,
         )
 
-    after = {1: (back,), 2: (cell_grads[0],)}
-    for bit in range(1, coarse_bits):
-        recv = swap(send, "coarse", bit - 1)
-        keep, send, bias_sum = call(
-            functools.partial(stage_body, bit=bit),
-            (sds((first, width), F32), sds((first + PACK, width), BF), sds((8, width), F32)),
-            (keep, recv, bias_sum),
-            0,
-            scratch=(pltpu.VMEM((first, width), F32),),
-            after=after.get(bit, ()),
-        )
+    for bit in range(2, coarse_bits - 1):
+        recv = swap(send, "coarse", bit)
+        keep, send, bias_sum = call(stage_body, outs, (keep, recv, bias_sum), 0)
     recv = swap(send, "coarse", coarse_bits - 1)
-    front_rows = nodes // 4
+    part = call(end_body, (message,), (keep, recv, bias_sum), 0, after=(other_back, cell_grads[0]))[0]
+    front_rows = nodes // 8 * 5
     grad_feats, feats_token = feats(0, front_rows)
-    part = call(
-        end_body, (sds((first + PACK, width), BF),), (keep, recv, bias_sum), 0,
-        after=(feats_token,),
-    )[0]
-    grad_feats, feats_token = feats(front_rows, nodes - front_rows, after=(part,), into=grad_feats)
     near = [swap(part, "coarse", 0), swap(part, "fine", 1), swap_both(part)]
     part = call(
         square_body, (sds((2 * (per + PACK), width), BF),), (part, *near), 0, after=(feats_token,)
@@ -570,6 +578,7 @@
         body = functools.partial(merge_body, bit=bit)
         part = call(body, (sds((2 * part.shape[0], width), BF),), (part, other), 0)[0]
     other = swap(part, "fine", 0)
+    grad_feats, feats_token = feats(front_rows, nodes - front_rows, after=(part,), into=grad_feats)
     total_cells = cells * coarses
     scales = dict(edge_scale=float(total_cells * K) ** -0.5, cell_scale=float(total_cells) ** -0.5)
     grad_w1, grad_b, grad_wo, grad_up = call(
@@ -579,6 +588,7 @@
         ),
         (part, other),
         0,
+        after=(feats_token,),
     )
     return grad_feats, grad_w1, grad_b.reshape(width), grad_wo, grad_up
 

time: 51.1 us -> 51.2 us (level)
  starting transfers between devices: 17.3 us -> 18.3 us
  waiting for transfers between devices: 12.8 us -> 11.8 us
    ppermute x16, waiting for transfers between devices: 7.39 us -> 5.41 us  [swap(): return lax.ppermute(x, axis, [(i, i ^ 1 << bit) for i in range(count)])]
    ppermute x3, waiting for transfers between devices: 4.83 us -> 6.38 us  [send_sides(): return lax.ppermute(x, ('coarse', 'fine'), pairs)]
    ppermute x0 -> x1, starting transfers between devices: none -> 1.14 us  [swap_owners(): lax.ppermute(x, 'coarse', [(i, i ^ 3) for i in range(lax.axis_size('coars...]
    ppermute x1, starting transfers between devices: 2.23 us -> 1.21 us  [swap_both(): return lax.ppermute(x, ('coarse', 'fine'), pairs)]
    ppermute x3, starting transfers between devices: 3.84 us -> 4.61 us  [send_sides(): return lax.ppermute(x, ('coarse', 'fine'), pairs)]
    ppermute x1, waiting for transfers between devices: 0.59 us -> 0.01 us  [swap_both(): return lax.ppermute(x, ('coarse', 'fine'), pairs)]
    pallas_call x29 -> x28, Pallas kernels: 18.4 us -> 18.5 us  [call(): pl.pallas_call(kernel, out_shape=outs, in_specs=[in_vmem] * count + [anyw...]
  transfers between devices with their start and end apart: 20 -> 21, of which waited for: 12 -> 8; matrix products, arithmetic and copies ran while one was open for 0% -> 0% of each run, Pallas kernels for 30% -> 30%
where the time goes in v9:
time: 51.2 us; the launch traced here: 51 us
  Pallas kernels  18.5 us (36%)
  starting transfers between devices  18.3 us (36%)
  waiting for transfers between devices  11.8 us (23%)
  local copies, waits for them, and re-layouts  1.28 us (2%)
  between operations  1.04 us (2%)
    pallas_call x28, Pallas kernels, call(): pl.pallas_call(kernel, out_shape=outs, in_specs=[in_vmem] * count + [anyw...  18.5 us
    ppermute x16, starting transfers between devices, swap(): return lax.ppermute(x, axis, [(i, i ^ 1 << bit) for i in range(count)])  11.3 us
    ppermute x3, waiting for transfers between devices, send_sides(): return lax.ppermute(x, ('coarse', 'fine'), pairs)  6.38 us
    ppermute x16, waiting for transfers between devices, swap(): return lax.ppermute(x, axis, [(i, i ^ 1 << bit) for i in range(count)])  5.41 us
    ppermute x3, starting transfers between devices, send_sides(): return lax.ppermute(x, ('coarse', 'fine'), pairs)  4.61 us
    unnamed x18, local copies, waits for them, and re-layouts  1.26 us
    ppermute x1, starting transfers between devices, swap_both(): return lax.ppermute(x, ('coarse', 'fine'), pairs)  1.21 us
    ppermute x1, starting transfers between devices, swap_owners(): lax.ppermute(x, 'coarse', [(i, i ^ 3) for i in range(lax.axis_size('coars...  1.14 us
  transfers between devices with their start and end apart: 21, of which 8 were waited for; matrix products, arithmetic and copies ran while one was open for 0% of the time, Pallas kernels for 30%

profile of v9, /device:TPU:0, one launch (start us, length us, event | category | flops | bytes accessed | tf_op | source)
XLA Modules:
  0.0 51.0 jit_solution(11295438642379385471)
XLA Ops:
  0.7 0.8 %copy-done.7 = s32[2048]{0:T(1024)S(1)} copy-done((s32[2048]{0:T(1024)S(1)}, s32[2048]{0:T(1024)}, u32[]{:S(2)}) %copy-start.7) | copy-done | bytes 8216
  1.9 0.7 %shard_map.130 = f32[512,256]{1,0:T(8,128)S(1)} custom-call(s32[1,2048]{1,0:T(1,128)S(1)} %shard_map.128.refs_0_.refs_1_, bf16[2048,256]{1,0:T(8,128)(2,1)S(1)} %copy-done.6), custom_call_target="tpu_custom_call" | custom-call | flops 536870912 | bytes 1581056 | tf_op jit(solution)/shard_map/pallas_call | solution.py:74
  2.6 0.5 %collective-permute-start = (f32[512,256]{1,0:T(8,128)S(1)}, f32[512,256]{1,0:T(8,128)S(1)}, u32[]{:S(2)}, u32[]{:S(2)}) collective-permute-start(f32[512,256]{1,0:T(8,128)S(1)} %shard_map.130), channel_id=1, source_target_pairs={{0,1},{1,0},{2,3},{3,2},{4,5},{5,4},{6,7},{7,6},{8,9},{9,8},{10,11... | collective-permute-start | bytes 1572872 | tf_op jit(solution)/shard_map/ppermute | solution.py:39
  3.1 0.7 %shard_map.133 = f32[512,256]{1,0:T(8,128)S(1)} custom-call(s32[1,2048]{1,0:T(1,128)S(1)} %shard_map.128.refs_0_.refs_1_, bf16[2048,256]{1,0:T(8,128)(2,1)S(1)} %copy-done.1), custom_call_target="tpu_custom_call" | custom-call | flops 536870912 | bytes 1581056 | tf_op jit(solution)/shard_map/pallas_call | solution.py:74
  4.0 0.7 %shard_map.129.refs_0_ = f32[512,256]{1,0:T(8,128)S(1)} custom-call(s32[1,2048]{1,0:T(1,128)S(1)} %shard_map.128.refs_0_.refs_1_, bf16[2048,256]{1,0:T(8,128)(2,1)S(1)} %copy-done.6), custom_call_target="tpu_custom_call" | custom-call | flops 536870912 | bytes 1581056 | tf_op jit(solution)/shard_map/pallas_call | solution.py:74
  4.8 3.0 %collective-permute-start.3 = (bf16[512,256]{1,0:T(8,128)(2,1)S(1)}, bf16[512,256]{1,0:T(8,128)(2,1)S(1)}, u32[]{:S(2)}, u32[]{:S(2)}) collective-permute-start(bf16[512,256]{1,0:T(8,128)(2,1)S(1)} %get-tuple-element.37.refs_2_.refs_0_), channel_id=1, source_target_pairs={{0,2},{1,3},{2,0},{3,1},{4,6},{5,7},{6,4},{7,5},{8,10},{9,11},{10,... | collective-permute-start | bytes 786440 | tf_op jit(solution)/shard_map/ppermute | solution.py:39
  8.4 1.0 %collective-permute-done.4.refs_1_ = bf16[128,256]{1,0:T(8,128)(2,1)S(1)} collective-permute-done((bf16[128,256]{1,0:T(8,128)(2,1)S(1)}, bf16[128,256]{1,0:T(8,128)(2,1)S(1)}, u32[]{:S(2)}, u32[]{:S(2)}) %collective-permute-start.4) | collective-permute-done | bytes 65568 | tf_op jit(solution)/shard_map/ppermute | solution.py:39
  9.4 1.4 %collective-permute-start.6 = (bf16[64,256]{1,0:T(8,128)(2,1)S(1)}, bf16[64,256]{1,0:T(8,128)(2,1)S(1)}, u32[]{:S(2)}, u32[]{:S(2)}) collective-permute-start(bf16[64,256]{1,0:T(8,128)(2,1)S(1)} %shard_map.136), channel_id=1, source_target_pairs={{0,6},{1,31},{2,4},{3,29},{4,10},{5,3},{6,8},{7,1},{8,14},{9,7},{1... | collective-permute-start | bytes 98312 | tf_op jit(solution)/shard_map/ppermute | solution.py:59
  10.8 1.5 %collective-permute-start.5 = (bf16[64,256]{1,0:T(8,128)(2,1)S(1)}, bf16[64,256]{1,0:T(8,128)(2,1)S(1)}, u32[]{:S(2)}, u32[]{:S(2)}) collective-permute-start(bf16[64,256]{1,0:T(8,128)(2,1)S(1)} %shard_map.136), channel_id=1, source_target_pairs={{0,4},{1,29},{2,6},{3,31},{4,8},{5,1},{6,10},{7,3},{8,12},{9,5},{1... | collective-permute-start | bytes 98312 | tf_op jit(solution)/shard_map/ppermute | solution.py:59
  12.3 0.7 %shard_map.132.refs_0_ = f32[512,256]{1,0:T(8,128)S(1)} custom-call(s32[1,2048]{1,0:T(1,128)S(1)} %shard_map.128.refs_0_.refs_1_, bf16[2048,256]{1,0:T(8,128)(2,1)S(1)} %copy-done.1, bf16[512,256]{1,0:T(8,128)(2,1)S(1)} %get-tuple-element.37.refs_2_.refs_0_), custom_call_target="tpu_custom_call" | custom-call | flops 536870912 | bytes 1581056 | tf_op jit(solution)/shard_map/pallas_call | solution.py:74
  13.1 1.6 %collective-permute-start.2 = (bf16[512,256]{1,0:T(8,128)(2,1)S(1)}, bf16[512,256]{1,0:T(8,128)(2,1)S(1)}, u32[]{:S(2)}, u32[]{:S(2)}) collective-permute-start(bf16[512,256]{1,0:T(8,128)(2,1)S(1)} %get-tuple-element.39), channel_id=1, source_target_pairs={{0,2},{1,3},{2,0},{3,1},{4,6},{5,7},{6,4},{7,5},{8,10},{9,11},{10,... | collective-permute-start | bytes 786440 | tf_op jit(solution)/shard_map/ppermute | solution.py:39
  14.7 2.1 %collective-permute-done.6.refs_1_ = bf16[64,256]{1,0:T(8,128)(2,1)S(1)} collective-permute-done((bf16[64,256]{1,0:T(8,128)(2,1)S(1)}, bf16[64,256]{1,0:T(8,128)(2,1)S(1)}, u32[]{:S(2)}, u32[]{:S(2)}) %collective-permute-start.6) | collective-permute-done | bytes 32800 | tf_op jit(solution)/shard_map/ppermute | solution.py:59
  16.9 0.5 %collective-permute-done.5.refs_0_ = bf16[64,256]{1,0:T(8,128)(2,1)S(1)} collective-permute-done((bf16[64,256]{1,0:T(8,128)(2,1)S(1)}, bf16[64,256]{1,0:T(8,128)(2,1)S(1)}, u32[]{:S(2)}, u32[]{:S(2)}) %collective-permute-start.5) | collective-permute-done | bytes 32800 | tf_op jit(solution)/shard_map/ppermute | solution.py:59
  17.6 0.5 collective-permute-start.7
  18.2 1.5 %shard_map.141.refs_2_ = bf16[4096,256]{1,0:T(8,128)(2,1)S(1)} custom-call(bf16[512,256]{1,0:T(8,128)(2,1)S(1)} %shard_map.139.refs_2_.refs_0_, s32[4,1024]{1,0:T(4,128)S(1)} %shard_map.138.refs_3_.refs_1_), custom_call_target="tpu_custom_call" | custom-call | tf_op jit(solution)/shard_map/pallas_call | solution.py:74
  20.1 1.7 %shard_map.142 = (f32[1024,256]{1,0:T(8,128)S(1)}, f32[2048,256]{1,0:T(8,128)S(1)}, bf16[2048,256]{1,0:T(8,128)(2,1)S(1)}, f32[8,128]{1,0:T(8,128)S(1)}) custom-call(f32[1024,256]{1,0:T(8,128)S(1)} %get-tuple-element.41.refs_0_, bf16[640,256]{1,0:T(8,128)(2,1)S(1)} %get-tuple-element.42.refs_1_, bf16[4096,256]{1,0:T(8,128)(2,1)S(1)} %shard_map.141.refs_2_, ...), custom_call_target="tpu_custom_call" | custom-call | tf_op jit(solution)/shard_map/pallas_call | solution.py:74
  22.4 1.7 %shard_map.144 = (f32[1024,256]{1,0:T(8,128)S(1)}, f32[2048,256]{1,0:T(8,128)S(1)}, bf16[2048,256]{1,0:T(8,128)(2,1)S(1)}) custom-call(f32[1024,256]{1,0:T(8,128)S(1)} %get-tuple-element.41.refs_0_, bf16[640,256]{1,0:T(8,128)(2,1)S(1)} %get-tuple-element.42.refs_1_, bf16[4096,256]{1,0:T(8,128)(2,1)S(1)} %shard_map.141.refs_2_, ...), custom_call_target="tpu_custom_call" | custom-call | tf_op jit(solution)/shard_map/pallas_call | solution.py:74
  24.1 1.5 %shard_map.145 = (bf16[4096,256]{1,0:T(8,128)(2,1)S(1)}, f32[1024,256]{1,0:T(8,128)S(1)}, bf16[1024,256]{1,0:T(8,128)(2,1)S(1)}, bf16[144,256]{1,0:T(8,128)(2,1)...) custom-call(bf16[512,256]{1,0:T(8,128)(2,1)S(1)} %shard_map.143.refs_5_.refs_0_, ...), custom_call_target="tpu_custom_call" | custom-call | flops 536870912 | bytes 13664256 | tf_op jit(solution)/shard_map/pallas_call | solution.py:74
  25.6 1.1 %collective-permute-start.13 = (bf16[144,256]{1,0:T(8,128)(2,1)S(1)}, bf16[144,256]{1,0:T(8,128)(2,1)S(1)}, u32[]{:S(2)}, u32[]{:S(2)}) collective-permute-start(bf16[144,256]{1,0:T(8,128)(2,1)S(1)} %get-tuple-element.55), channel_id=1, source_target_pairs={{0,12},{4,8},{8,4},{12,0},{16,28},{20,24},{24,20},{28,16},{1,13},{... | collective-permute-start | bytes 221192 | tf_op jit(solution)/shard_map/ppermute | solution.py:43
  26.8 1.8 %collective-permute-start.14 = (bf16[144,256]{1,0:T(8,128)(2,1)S(1)}, bf16[144,256]{1,0:T(8,128)(2,1)S(1)}, u32[]{:S(2)}, u32[]{:S(2)}) collective-permute-start(bf16[144,256]{1,0:T(8,128)(2,1)S(1)} %get-tuple-element.56), channel_id=1, source_target_pairs={{0,8},{4,12},{8,0},{12,4},{16,24},{20,28},{24,16},{28,20},{1,9},{5... | collective-permute-start | bytes 221192 | tf_op jit(solution)/shard_map/ppermute | solution.py:39
  28.6 0.6 %collective-permute-start.15 = (bf16[144,256]{1,0:T(8,128)(2,1)S(1)}, bf16[144,256]{1,0:T(8,128)(2,1)S(1)}, u32[]{:S(2)}, u32[]{:S(2)}) collective-permute-start(bf16[144,256]{1,0:T(8,128)(2,1)S(1)} %get-tuple-element.57), channel_id=1, source_target_pairs={{0,4},{4,0},{8,12},{12,8},{16,20},{20,16},{24,28},{28,24},{1,5},{5... | collective-permute-start | bytes 221192 | tf_op jit(solution)/shard_map/ppermute | solution.py:39
  29.2 0.6 %shard_map.148 = bf16[64,256]{1,0:T(8,128)(2,1)S(1)} custom-call(bf16[4096,256]{1,0:T(8,128)(2,1)S(1)} %get-tuple-element.51.refs_0_, s32[4,1024]{1,0:T(4,128)S(1)} %shard_map.138.refs_3_.refs_1_, bf16[512,256]{1,0:T(8,128)(2,1)S(1)} %copy-done), custom_call_target="tpu_custom_call" | custom-call | tf_op jit(solution)/shard_map/pallas_call | solution.py:74
  29.8 1.6 %collective-permute-start.11 = (bf16[64,256]{1,0:T(8,128)(2,1)S(1)}, bf16[64,256]{1,0:T(8,128)(2,1)S(1)}, u32[]{:S(2)}, u32[]{:S(2)}) collective-permute-start(bf16[64,256]{1,0:T(8,128)(2,1)S(1)} %shard_map.148), channel_id=1, source_target_pairs={{0,4},{1,29},{2,6},{3,31},{4,8},{5,1},{6,10},{7,3},{8,12},{9,5},{1... | collective-permute-start | bytes 98312 | tf_op jit(solution)/shard_map/ppermute | solution.py:59
  31.4 1.5 %shard_map.147.refs_1_.refs_5_ = f32[512,256]{1,0:T(8,128)S(1)} custom-call(bf16[4096,256]{1,0:T(8,128)(2,1)S(1)} %get-tuple-element.51.refs_0_, s32[4,1024]{1,0:T(4,128)S(1)} %shard_map.138.refs_3_.refs_1_, f32[1024,256]{1,0:T(8,128)S(1)} %get-tuple-element.52.refs_2_, bf16[1024,256]{1,0:T(8,128)(2,1)S(1)} %get-tuple-element.53.refs_3_, ...), custom_call_target="tpu_custom_call" | custom-call | tf_op jit(solution)/shard_map/pallas_call | solution.py:74
  33.0 3.7 %collective-permute-done.11.refs_2_.refs_4_ = bf16[64,256]{1,0:T(8,128)(2,1)S(1)} collective-permute-done((bf16[64,256]{1,0:T(8,128)(2,1)S(1)}, bf16[64,256]{1,0:T(8,128)(2,1)S(1)}, u32[]{:S(2)}, u32[]{:S(2)}) %collective-permute-start.11) | collective-permute-done | bytes 32800 | tf_op jit(solution)/shard_map/ppermute | solution.py:59
  36.9 1.5 %shard_map.146.refs_0_.refs_4_ = f32[512,256]{1,0:T(8,128)S(1)} custom-call(bf16[4096,256]{1,0:T(8,128)(2,1)S(1)} %get-tuple-element.51.refs_0_, s32[4,1024]{1,0:T(4,128)S(1)} %shard_map.138.refs_3_.refs_1_, f32[1024,256]{1,0:T(8,128)S(1)} %get-tuple-element.52.refs_2_, bf16[1024,256]{1,0:T(8,128)(2,1)S(1)} %get-tuple-element.53.refs_3_, ...), custom_call_target="tpu_custom_call" | custom-call | tf_op jit(solution)/shard_map/pallas_call | solution.py:74
  38.5 3.6 %collective-permute-done.16.refs_1_ = bf16[144,256]{1,0:T(8,128)(2,1)S(1)} collective-permute-done((bf16[144,256]{1,0:T(8,128)(2,1)S(1)}, bf16[144,256]{1,0:T(8,128)(2,1)S(1)}, u32[]{:S(2)}, u32[]{:S(2)}) %collective-permute-start.16) | collective-permute-done | bytes 73760 | tf_op jit(solution)/shard_map/ppermute | solution.py:39
  42.1 1.2 %collective-permute-start.19 = (bf16[144,256]{1,0:T(8,128)(2,1)S(1)}, bf16[144,256]{1,0:T(8,128)(2,1)S(1)}, u32[]{:S(2)}, u32[]{:S(2)}) collective-permute-start(bf16[144,256]{1,0:T(8,128)(2,1)S(1)} %shard_map.151.refs_0_), channel_id=1, source_target_pairs={{0,6},{1,7},{2,4},{3,5},{4,2},{5,3},{6,0},{7,1},{8,14},{9,15},{10,... | collective-permute-start | bytes 221192 | tf_op jit(solution)/shard_map/ppermute | solution.py:49
  43.8 1.9 %collective-permute-start.17 = (bf16[144,256]{1,0:T(8,128)(2,1)S(1)}, bf16[144,256]{1,0:T(8,128)(2,1)S(1)}, u32[]{:S(2)}, u32[]{:S(2)}) collective-permute-start(bf16[144,256]{1,0:T(8,128)(2,1)S(1)} %shard_map.151.refs_0_), channel_id=1, source_target_pairs={{0,4},{4,0},{8,12},{12,8},{16,20},{20,16},{24,28},{28,24},{1,5},{5... | collective-permute-start | bytes 221192 | tf_op jit(solution)/shard_map/ppermute | solution.py:39
  46.0 1.8 %shard_map.152 = (bf16[2048,256]{1,0:T(8,128)(2,1)}, f32[8,128]{1,0:T(8,128)S(1)}) custom-call(bf16[1024,256]{1,0:T(8,128)(2,1)S(1)} %shard_map.149.refs_0_, s32[1,2048]{1,0:T(1,128)S(1)} %shard_map.128.refs_0_.refs_1_, bf16[2048,256]{1,0:T(8,128)(2,1)S(1)} %copy-done.1), custom_call_target="tpu_custom_call" | custom-call | flops 671088640 | bytes 2633728 | tf_op jit(solution)/shard_map/pallas_call | solution.py:74
  48.4 1.4 %shard_map.154 = (bf16[2048,256]{1,0:T(8,128)(2,1)}, f32[8,128]{1,0:T(8,128)S(1)}) custom-call(bf16[1024,256]{1,0:T(8,128)(2,1)S(1)} %shard_map.149.refs_0_, s32[1,2048]{1,0:T(1,128)S(1)} %shard_map.128.refs_0_.refs_1_, bf16[2048,256]{1,0:T(8,128)(2,1)S(1)} %copy-done.1, ...), custom_call_target="tpu_custom_call", output_to_operand_aliasing={{0}: (4, {})} | custom-call | flops 402653184 | bytes 2633728 | tf_op jit(solution)/shard_map/pallas_call | solution.py:74
  49.9 1.0 %shard_map.155 = (f32[512,256]{1,0:T(8,128)}, f32[1,256]{1,0:T(1,128)}, f32[256,256]{1,0:T(8,128)}, f32[256,256]{1,0:T(8,128)}) custom-call(bf16[544,256]{1,0:T(8,128)(2,1)S(1)} %shard_map.153.refs_3_.refs_0_, bf16[544,256]{1,0:T(8,128)(2,1)S(1)} %collective-permute-done.20.refs_1_, f32[8,128]{1,0:T(8,128)S(1)} %get-tuple-element.64.refs_2_), custom_call_target="tpu_custom_call" | custom-call | tf_op jit(solution)/shard_map/pallas_call | solution.py:74
  (58 shorter events, 4.3 us)
Async XLA Ops:
  0.6 1.2 %copy-start.6 = (bf16[2048,256]{1,0:T(8,128)(2,1)S(1)}, bf16[2048,256]{1,0:T(8,128)(2,1)}, u32[]{:S(2)}) copy-start(bf16[2048,256]{1,0:T(8,128)(2,1)} %refs_1_.5) | copy-start | bytes 3145732
  0.6 0.8 %copy-start.7 = (s32[2048]{0:T(1024)S(1)}, s32[2048]{0:T(1024)}, u32[]{:S(2)}) copy-start(s32[2048]{0:T(1024)} %param.11) | copy-start | bytes 24580
  1.4 1.7 %copy-start.1 = (bf16[2048,256]{1,0:T(8,128)(2,1)S(1)}, bf16[2048,256]{1,0:T(8,128)(2,1)}, u32[]{:S(2)}) copy-start(bf16[2048,256]{1,0:T(8,128)(2,1)} %refs_2_.5) | copy-start | bytes 3145732
  2.6 5.2 %copy-start.5 = (s32[128]{0:T(128)S(1)}, s32[128]{0:T(128)}, u32[]{:S(2)}) copy-start(s32[128]{0:T(128)} %param.12) | copy-start | bytes 1540
  2.6 2.1 %collective-permute-start = (f32[512,256]{1,0:T(8,128)S(1)}, f32[512,256]{1,0:T(8,128)S(1)}, u32[]{:S(2)}, u32[]{:S(2)}) collective-permute-start(f32[512,256]{1,0:T(8,128)S(1)} %shard_map.130), channel_id=1, source_target_pairs={{0,1},{1,0},{2,3},{3,2},{4,5},{5,4},{6,7},{7,6},{8,9},{9,8},{10,11... | collective-permute-start | bytes 1572872 | tf_op jit(solution)/shard_map/ppermute | solution.py:39
  3.8 4.3 %copy-start.8 = (bf16[256]{0:T(256)(128)(2,1)S(1)}, bf16[256]{0:T(256)(128)(2,1)}, u32[]{:S(2)}) copy-start(bf16[256]{0:T(256)(128)(2,1)} %param.15) | copy-start | bytes 1540
  3.8 4.3 %copy-start.4 = (s32[4096]{0:T(1024)S(1)}, s32[4096]{0:T(1024)}, u32[]{:S(2)}) copy-start(s32[4096]{0:T(1024)} %param.13) | copy-start | bytes 49156
  3.8 9.2 %collective-permute-start.1 = (f32[512,256]{1,0:T(8,128)S(1)}, f32[512,256]{1,0:T(8,128)S(1)}, u32[]{:S(2)}, u32[]{:S(2)}) collective-permute-start(f32[512,256]{1,0:T(8,128)S(1)} %shard_map.133), channel_id=1, source_target_pairs={{0,1},{1,0},{2,3},{3,2},{4,5},{5,4},{6,7},{7,6},{8,9},{9,8},{10,11... | collective-permute-start | bytes 1572872 | tf_op jit(solution)/shard_map/ppermute | solution.py:39
  4.8 12.7 %collective-permute-start.3 = (bf16[512,256]{1,0:T(8,128)(2,1)S(1)}, bf16[512,256]{1,0:T(8,128)(2,1)S(1)}, u32[]{:S(2)}, u32[]{:S(2)}) collective-permute-start(bf16[512,256]{1,0:T(8,128)(2,1)S(1)} %get-tuple-element.37.refs_2_.refs_0_), channel_id=1, source_target_pairs={{0,2},{1,3},{2,0},{3,1},{4,6},{5,7},{6,4},{7,5},{8,10},{9,11},{10,... | collective-permute-start | bytes 786440 | tf_op jit(solution)/shard_map/ppermute | solution.py:39
  8.0 1.3 %collective-permute-start.4 = (bf16[128,256]{1,0:T(8,128)(2,1)S(1)}, bf16[128,256]{1,0:T(8,128)(2,1)S(1)}, u32[]{:S(2)}, u32[]{:S(2)}) collective-permute-start(bf16[128,256]{1,0:T(8,128)(2,1)S(1)} %shard_map.135.refs_0_), channel_id=1, source_target_pairs={{0,1},{1,0},{2,3},{3,2},{4,5},{5,4},{6,7},{7,6},{8,9},{9,8},{10,11... | collective-permute-start | bytes 196616 | tf_op jit(solution)/shard_map/ppermute | solution.py:39
  9.4 7.5 %collective-permute-start.6 = (bf16[64,256]{1,0:T(8,128)(2,1)S(1)}, bf16[64,256]{1,0:T(8,128)(2,1)S(1)}, u32[]{:S(2)}, u32[]{:S(2)}) collective-permute-start(bf16[64,256]{1,0:T(8,128)(2,1)S(1)} %shard_map.136), channel_id=1, source_target_pairs={{0,6},{1,31},{2,4},{3,29},{4,10},{5,3},{6,8},{7,1},{8,14},{9,7},{1... | collective-permute-start | bytes 98312 | tf_op jit(solution)/shard_map/ppermute | solution.py:59
  10.8 6.6 %collective-permute-start.5 = (bf16[64,256]{1,0:T(8,128)(2,1)S(1)}, bf16[64,256]{1,0:T(8,128)(2,1)S(1)}, u32[]{:S(2)}, u32[]{:S(2)}) collective-permute-start(bf16[64,256]{1,0:T(8,128)(2,1)S(1)} %shard_map.136), channel_id=1, source_target_pairs={{0,4},{1,29},{2,6},{3,31},{4,8},{5,1},{6,10},{7,3},{8,12},{9,5},{1... | collective-permute-start | bytes 98312 | tf_op jit(solution)/shard_map/ppermute | solution.py:59
  13.1 6.6 %copy-start = (bf16[512,256]{1,0:T(8,128)(2,1)S(1)}, bf16[512,256]{1,0:T(8,128)(2,1)}, u32[]{:S(2)}) copy-start(bf16[512,256]{1,0:T(8,128)(2,1)} %refs_2_.3) | copy-start | bytes 786436
  13.1 8.8 %collective-permute-start.2 = (bf16[512,256]{1,0:T(8,128)(2,1)S(1)}, bf16[512,256]{1,0:T(8,128)(2,1)S(1)}, u32[]{:S(2)}, u32[]{:S(2)}) collective-permute-start(bf16[512,256]{1,0:T(8,128)(2,1)S(1)} %get-tuple-element.39), channel_id=1, source_target_pairs={{0,2},{1,3},{2,0},{3,1},{4,6},{5,7},{6,4},{7,5},{8,10},{9,11},{10,... | collective-permute-start | bytes 786440 | tf_op jit(solution)/shard_map/ppermute | solution.py:39
  17.5 2.2 %collective-permute-start.8 = (bf16[256,256]{1,0:T(8,128)(2,1)S(1)}, bf16[256,256]{1,0:T(8,128)(2,1)S(1)}, u32[]{:S(2)}, u32[]{:S(2)}) collective-permute-start(bf16[256,256]{1,0:T(8,128)(2,1)S(1)} %get-tuple-element.69), channel_id=1, source_target_pairs={{0,1},{1,0},{2,3},{3,2},{4,5},{5,4},{6,7},{7,6},{8,9},{9,8},{10,11... | collective-permute-start | bytes 393224 | tf_op jit(solution)/shard_map/ppermute | solution.py:39
  17.6 2.1 %collective-permute-start.7 = (bf16[256,256]{1,0:T(8,128)(2,1)S(1)}, bf16[256,256]{1,0:T(8,128)(2,1)S(1)}, u32[]{:S(2)}, u32[]{:S(2)}) collective-permute-start(bf16[256,256]{1,0:T(8,128)(2,1)S(1)} %get-tuple-element.70), channel_id=1, source_target_pairs={{0,1},{1,0},{2,3},{3,2},{4,5},{5,4},{6,7},{7,6},{8,9},{9,8},{10,11... | collective-permute-start | bytes 393224 | tf_op jit(solution)/shard_map/ppermute | solution.py:39
  18.1 1.6 %collective-permute-start.9 = (bf16[64,256]{1,0:T(8,128)(2,1)S(1)}, bf16[64,256]{1,0:T(8,128)(2,1)S(1)}, u32[]{:S(2)}, u32[]{:S(2)}) collective-permute-start(bf16[64,256]{1,0:T(8,128)(2,1)S(1)} %shard_map.137.refs_2_.refs_3_), channel_id=1, source_target_pairs={{0,1},{1,0},{2,3},{3,2},{4,5},{5,4},{6,7},{7,6},{8,9},{9,8},{10,11... | collective-permute-start | bytes 98312 | tf_op jit(solution)/shard_map/ppermute | solution.py:39
  22.0 2.1 %copy-start.2 = (bf16[256,256]{1,0:T(8,128)(2,1)S(1)}, bf16[256,256]{1,0:T(8,128)(2,1)}, u32[]{:S(2)}) copy-start(bf16[256,256]{1,0:T(8,128)(2,1)} %refs_9_.1) | copy-start | bytes 393220
  22.0 2.1 %copy-start.3 = (bf16[256,256]{1,0:T(8,128)(2,1)S(1)}, bf16[256,256]{1,0:T(8,128)(2,1)}, u32[]{:S(2)}) copy-start(bf16[256,256]{1,0:T(8,128)(2,1)} %refs_10_.1) | copy-start | bytes 393220
  22.1 2.1 %collective-permute-start.10 = (bf16[512,256]{1,0:T(8,128)(2,1)S(1)}, bf16[512,256]{1,0:T(8,128)(2,1)S(1)}, u32[]{:S(2)}, u32[]{:S(2)}) collective-permute-start(bf16[512,256]{1,0:T(8,128)(2,1)S(1)} %shard_map.143.refs_5_.refs_0_), channel_id=1, source_target_pairs={{0,1},{1,0},{2,3},{3,2},{4,5},{5,4},{6,7},{7,6},{8,9},{9,8},{10,11... | collective-permute-start | bytes 786440 | tf_op jit(solution)/shard_map/ppermute | solution.py:39
  25.6 11.0 %collective-permute-start.13 = (bf16[144,256]{1,0:T(8,128)(2,1)S(1)}, bf16[144,256]{1,0:T(8,128)(2,1)S(1)}, u32[]{:S(2)}, u32[]{:S(2)}) collective-permute-start(bf16[144,256]{1,0:T(8,128)(2,1)S(1)} %get-tuple-element.55), channel_id=1, source_target_pairs={{0,12},{4,8},{8,4},{12,0},{16,28},{20,24},{24,20},{28,16},{1,13},{... | collective-permute-start | bytes 221192 | tf_op jit(solution)/shard_map/ppermute | solution.py:43
  26.8 9.9 %collective-permute-start.14 = (bf16[144,256]{1,0:T(8,128)(2,1)S(1)}, bf16[144,256]{1,0:T(8,128)(2,1)S(1)}, u32[]{:S(2)}, u32[]{:S(2)}) collective-permute-start(bf16[144,256]{1,0:T(8,128)(2,1)S(1)} %get-tuple-element.56), channel_id=1, source_target_pairs={{0,8},{4,12},{8,0},{12,4},{16,24},{20,28},{24,16},{28,20},{1,9},{5... | collective-permute-start | bytes 221192 | tf_op jit(solution)/shard_map/ppermute | solution.py:39
  28.6 8.1 %collective-permute-start.15 = (bf16[144,256]{1,0:T(8,128)(2,1)S(1)}, bf16[144,256]{1,0:T(8,128)(2,1)S(1)}, u32[]{:S(2)}, u32[]{:S(2)}) collective-permute-start(bf16[144,256]{1,0:T(8,128)(2,1)S(1)} %get-tuple-element.57), channel_id=1, source_target_pairs={{0,4},{4,0},{8,12},{12,8},{16,20},{20,16},{24,28},{28,24},{1,5},{5... | collective-permute-start | bytes 221192 | tf_op jit(solution)/shard_map/ppermute | solution.py:39
  29.8 6.8 %collective-permute-start.11 = (bf16[64,256]{1,0:T(8,128)(2,1)S(1)}, bf16[64,256]{1,0:T(8,128)(2,1)S(1)}, u32[]{:S(2)}, u32[]{:S(2)}) collective-permute-start(bf16[64,256]{1,0:T(8,128)(2,1)S(1)} %shard_map.148), channel_id=1, source_target_pairs={{0,4},{1,29},{2,6},{3,31},{4,8},{5,1},{6,10},{7,3},{8,12},{9,5},{1... | collective-permute-start | bytes 98312 | tf_op jit(solution)/shard_map/ppermute | solution.py:59
  36.8 5.3 %collective-permute-start.16 = (bf16[144,256]{1,0:T(8,128)(2,1)S(1)}, bf16[144,256]{1,0:T(8,128)(2,1)S(1)}, u32[]{:S(2)}, u32[]{:S(2)}) collective-permute-start(bf16[144,256]{1,0:T(8,128)(2,1)S(1)} %get-tuple-element.59), channel_id=1, source_target_pairs={{0,16},{4,20},{8,24},{12,28},{16,0},{20,4},{24,8},{28,12},{1,17},{... | collective-permute-start | bytes 221192 | tf_op jit(solution)/shard_map/ppermute | solution.py:39
  36.9 1.6 %collective-permute-start.12 = (bf16[64,256]{1,0:T(8,128)(2,1)S(1)}, bf16[64,256]{1,0:T(8,128)(2,1)S(1)}, u32[]{:S(2)}, u32[]{:S(2)}) collective-permute-start(bf16[64,256]{1,0:T(8,128)(2,1)S(1)} %collective-permute-done.11.refs_2_.refs_4_), channel_id=1, source_target_pairs={{0,1},{1,0},{2,3},{3,2},{4,5},{5,4},{6,7},{7,6},{8,9},{9,8},{10,11... | collective-permute-start | bytes 98312 | tf_op jit(solution)/shard_map/ppermute | solution.py:39
  42.1 5.7 %collective-permute-start.19 = (bf16[144,256]{1,0:T(8,128)(2,1)S(1)}, bf16[144,256]{1,0:T(8,128)(2,1)S(1)}, u32[]{:S(2)}, u32[]{:S(2)}) collective-permute-start(bf16[144,256]{1,0:T(8,128)(2,1)S(1)} %shard_map.151.refs_0_), channel_id=1, source_target_pairs={{0,6},{1,7},{2,4},{3,5},{4,2},{5,3},{6,0},{7,1},{8,14},{9,15},{10,... | collective-permute-start | bytes 221192 | tf_op jit(solution)/shard_map/ppermute | solution.py:49
  43.3 4.9 %collective-permute-start.18 = (bf16[144,256]{1,0:T(8,128)(2,1)S(1)}, bf16[144,256]{1,0:T(8,128)(2,1)S(1)}, u32[]{:S(2)}, u32[]{:S(2)}) collective-permute-start(bf16[144,256]{1,0:T(8,128)(2,1)S(1)} %shard_map.151.refs_0_), channel_id=1, source_target_pairs={{0,2},{1,3},{2,0},{3,1},{4,6},{5,7},{6,4},{7,5},{8,10},{9,11},{10,... | collective-permute-start | bytes 221192 | tf_op jit(solution)/shard_map/ppermute | solution.py:39
  43.8 4.4 %collective-permute-start.17 = (bf16[144,256]{1,0:T(8,128)(2,1)S(1)}, bf16[144,256]{1,0:T(8,128)(2,1)S(1)}, u32[]{:S(2)}, u32[]{:S(2)}) collective-permute-start(bf16[144,256]{1,0:T(8,128)(2,1)S(1)} %shard_map.151.refs_0_), channel_id=1, source_target_pairs={{0,4},{4,0},{8,12},{12,8},{16,20},{20,16},{24,28},{28,24},{1,5},{5... | collective-permute-start | bytes 221192 | tf_op jit(solution)/shard_map/ppermute | solution.py:39
  48.3 1.6 %collective-permute-start.20 = (bf16[544,256]{1,0:T(8,128)(2,1)S(1)}, bf16[544,256]{1,0:T(8,128)(2,1)S(1)}, u32[]{:S(2)}, u32[]{:S(2)}) collective-permute-start(bf16[544,256]{1,0:T(8,128)(2,1)S(1)} %shard_map.153.refs_3_.refs_0_), channel_id=1, source_target_pairs={{0,1},{1,0},{2,3},{3,2},{4,5},{5,4},{6,7},{7,6},{8,9},{9,8},{10,11... | collective-permute-start | bytes 835592 | tf_op jit(solution)/shard_map/ppermute | solution.py:39

commit v10 on v9

--- a/solution.py
+++ b/solution.py
@@ -8,7 +8,7 @@
 from jax.sharding import PartitionSpec as P
 
 K = 4
-EARLY = 2
+EARLY = 3
 BF = jnp.bfloat16
 F32 = jnp.float32
 LANES = 128
@@ -354,12 +354,11 @@
     return out
 
 
-def back_body(act, src_ref, w1_ref, out_ref, both):
+def back_body(act, src_ref, w1_ref, out_ref):
     side, width = out_ref.shape
-    rows = scatter(act, src_ref, src_ref.shape[1], 2 * side)
-    both[...] = dot_nt(rows.astype(BF), w1_ref[width : 2 * width, :])
-    core = lax.axis_index("fine") % 2
-    out_ref[...] = both[pl.ds(pl.multiple_of((1 - core) * side, side), side), :].astype(BF)
+    core = lax.axis_index("fine") % 2
+    rows = scatter(act, src_ref, src_ref.shape[1] + (1 - core) * side, side)
+    out_ref[...] = dot_nt(rows.astype(BF), w1_ref[width : 2 * width, :]).astype(BF)
 
 
 def cell_grad_body(act, src_ref, ga_ref, gn_ref, w1_ref, out_ref, *, first):
@@ -424,18 +423,19 @@
         table[i * step : (i + 1) * step, :] = (pool_ref[...] + add).astype(BF)
 
 
-def feats_body(table, ids_ref, grad_ref, *rest, first, count):
-    out_hbm, token_ref, out, sem = rest[-4:]
+def feats_body(table, ids_ref, grad_ref, out_hbm, token_ref, out, sems):
     token_ref[...] = jnp.zeros_like(token_ref)
     cells = table.shape[0]
-    block = 256
-    for t in range(0, count, block):
-        at = slice(first + t, first + t + block)
+    block = out.shape[0] // sems.shape[0]
+    stores = []
+    for i in range(sems.shape[0]):
+        at = slice(i * block, (i + 1) * block)
         rows = dot(hot_rows(ids_ref[:, at], cells), table[...])
-        out[t : t + block, :] = (grad_ref[at, :].astype(F32) + rows).astype(BF)
-    copy = pltpu.make_async_copy(out, out_hbm.at[first : first + count, :], sem)
-    copy.start()
-    copy.wait()
+        out[at, :] = (grad_ref[at, :].astype(F32) + rows).astype(BF)
+        stores.append(pltpu.make_async_copy(out.at[at, :], out_hbm.at[at, :], sems.at[i]))
+        stores[-1].start()
+    for store in stores:
+        store.wait()
 
 
 def local(
@@ -525,8 +525,7 @@
     )
 
     back = call(
-        back_body, (sds((side, width), BF),), (act, src, w_edge_in), 0,
-        scratch=(pltpu.VMEM((2 * side, width), F32),),
+        back_body, (sds((side, width), BF),), (act, src, w_edge_in), 0
     )[0]
     own_back = send_sides(back)
     cell_grads = [
@@ -549,26 +548,15 @@
         table_body, (sds((cells, width), BF),), (*cell_grads, own_back, other_back, lists), 0
     )[0]
 
-    def feats(first, count, after=(), into=None):
-        return call(
-            functools.partial(feats_body, first=first, count=count),
-            (sds((nodes, width), BF), sds((8, LANES), F32)),
-            (table, ids, grad_out),
-            2 * count * cells * width,
-            vmem=24,
-            scratch=(pltpu.VMEM((count, width), BF), pltpu.SemaphoreType.DMA(())),
-            after=after,
-            into=into,
-            far=1,
-        )
-
     for bit in range(2, coarse_bits - 1):
         recv = swap(send, "coarse", bit)
         keep, send, bias_sum = call(stage_body, outs, (keep, recv, bias_sum), 0)
     recv = swap(send, "coarse", coarse_bits - 1)
     part = call(end_body, (message,), (keep, recv, bias_sum), 0, after=(other_back, cell_grads[0]))[0]
-    front_rows = nodes // 8 * 5
-    grad_feats, feats_token = feats(0, front_rows)
+    grad_feats, feats_token = call(
+        feats_body, (sds((nodes, width), BF), sds((8, LANES), F32)), (table, ids, grad_out), 2 * nodes * cells * width,
+        vmem=24, scratch=(pltpu.VMEM((nodes, width), BF), pltpu.SemaphoreType.DMA((nodes // 256,))), far=1,
+    )
     near = [swap(part, "coarse", 0), swap(part, "fine", 1), swap_both(part)]
     part = call(
         square_body, (sds((2 * (per + PACK), width), BF),), (part, *near), 0, after=(feats_token,)
@@ -578,7 +566,6 @@
         body = functools.partial(merge_body, bit=bit)
         part = call(body, (sds((2 * part.shape[0], width), BF),), (part, other), 0)[0]
     other = swap(part, "fine", 0)
-    grad_feats, feats_token = feats(front_rows, nodes - front_rows, after=(part,), into=grad_feats)
     total_cells = cells * coarses
     scales = dict(edge_scale=float(total_cells * K) ** -0.5, cell_scale=float(total_cells) ** -0.5)
     grad_w1, grad_b, grad_wo, grad_up = call(
@@ -588,7 +575,6 @@
         ),
         (part, other),
         0,
-        after=(feats_token,),
     )
     return grad_feats, grad_w1, grad_b.reshape(width), grad_wo, grad_up
 

time: 51.2 us -> 51.5 us (level)
  waiting for transfers between devices: 11.8 us -> 13.6 us
  Pallas kernels: 18.5 us -> 17.7 us
  starting transfers between devices: 18.3 us -> 17.7 us
    ppermute x16, waiting for transfers between devices: 5.41 us -> 6.48 us  [swap(): return lax.ppermute(x, axis, [(i, i ^ 1 << bit) for i in range(count)])]
    ppermute x16, starting transfers between devices: 11.3 us -> 12.2 us  [swap(): return lax.ppermute(x, axis, [(i, i ^ 1 << bit) for i in range(count)])]
    pallas_call x28 -> x27, Pallas kernels: 18.5 us -> 17.7 us  [call(): pl.pallas_call(kernel, out_shape=outs, in_specs=[in_vmem] * count + [anyw...]
    ppermute x3, starting transfers between devices: 4.61 us -> 3.89 us  [send_sides(): return lax.ppermute(x, ('coarse', 'fine'), pairs)]
    ppermute x3, waiting for transfers between devices: 6.38 us -> 7.07 us  [send_sides(): return lax.ppermute(x, ('coarse', 'fine'), pairs)]
    ppermute x1, starting transfers between devices: 1.21 us -> 0.68 us  [swap_both(): return lax.ppermute(x, ('coarse', 'fine'), pairs)]
  transfers between devices with their start and end apart: 21 -> 21, of which waited for: 8 -> 9; matrix products, arithmetic and copies ran while one was open for 0% -> 0% of each run, Pallas kernels for 30% -> 28%
where the time goes in v10:
time: 51.5 us; the launch traced here: 51.3 us
  Pallas kernels  17.7 us (34%)
  starting transfers between devices  17.7 us (34%)
  waiting for transfers between devices  13.6 us (26%)
  local copies, waits for them, and re-layouts  1.28 us (2%)
  between operations  1.01 us (2%)
    pallas_call x27, Pallas kernels, call(): pl.pallas_call(kernel, out_shape=outs, in_specs=[in_vmem] * count + [anyw...  17.7 us
    ppermute x16, starting transfers between devices, swap(): return lax.ppermute(x, axis, [(i, i ^ 1 << bit) for i in range(count)])  12.2 us
    ppermute x3, waiting for transfers between devices, send_sides(): return lax.ppermute(x, ('coarse', 'fine'), pairs)  7.07 us
    ppermute x16, waiting for transfers between devices, swap(): return lax.ppermute(x, axis, [(i, i ^ 1 << bit) for i in range(count)])  6.48 us
    ppermute x3, starting transfers between devices, send_sides(): return lax.ppermute(x, ('coarse', 'fine'), pairs)  3.89 us
    unnamed x18, local copies, waits for them, and re-layouts  1.26 us
  transfers between devices with their start and end apart: 21, of which 9 were waited for; matrix products, arithmetic and copies ran while one was open for 0% of the time, Pallas kernels for 28%

profile of v10, /device:TPU:0, one launch (start us, length us, event | category | flops | bytes accessed | tf_op | source)
XLA Modules:
  0.0 51.3 jit_solution(567680528735044556)
XLA Ops:
  0.7 0.8 %copy-done.7 = s32[2048]{0:T(1024)S(1)} copy-done((s32[2048]{0:T(1024)S(1)}, s32[2048]{0:T(1024)}, u32[]{:S(2)}) %copy-start.7) | copy-done | bytes 8216
  1.9 0.7 %shard_map.130 = f32[512,256]{1,0:T(8,128)S(1)} custom-call(s32[1,2048]{1,0:T(1,128)S(1)} %shard_map.128.refs_0_.refs_1_, bf16[2048,256]{1,0:T(8,128)(2,1)S(1)} %copy-done.5), custom_call_target="tpu_custom_call" | custom-call | flops 536870912 | bytes 1581056 | tf_op jit(solution)/shard_map/pallas_call | solution.py:74
  2.6 0.5 %collective-permute-start = (f32[512,256]{1,0:T(8,128)S(1)}, f32[512,256]{1,0:T(8,128)S(1)}, u32[]{:S(2)}, u32[]{:S(2)}) collective-permute-start(f32[512,256]{1,0:T(8,128)S(1)} %shard_map.130), channel_id=1, source_target_pairs={{0,1},{1,0},{2,3},{3,2},{4,5},{5,4},{6,7},{7,6},{8,9},{9,8},{10,11... | collective-permute-start | bytes 1572872 | tf_op jit(solution)/shard_map/ppermute | solution.py:39
  3.1 0.7 %shard_map.133 = f32[512,256]{1,0:T(8,128)S(1)} custom-call(s32[1,2048]{1,0:T(1,128)S(1)} %shard_map.128.refs_0_.refs_1_, bf16[2048,256]{1,0:T(8,128)(2,1)S(1)} %copy-done.6), custom_call_target="tpu_custom_call" | custom-call | flops 536870912 | bytes 1581056 | tf_op jit(solution)/shard_map/pallas_call | solution.py:74
  4.0 0.7 %shard_map.129.refs_0_ = f32[512,256]{1,0:T(8,128)S(1)} custom-call(s32[1,2048]{1,0:T(1,128)S(1)} %shard_map.128.refs_0_.refs_1_, bf16[2048,256]{1,0:T(8,128)(2,1)S(1)} %copy-done.5), custom_call_target="tpu_custom_call" | custom-call | flops 536870912 | bytes 1581056 | tf_op jit(solution)/shard_map/pallas_call | solution.py:74
  4.8 3.0 %collective-permute-start.3 = (bf16[512,256]{1,0:T(8,128)(2,1)S(1)}, bf16[512,256]{1,0:T(8,128)(2,1)S(1)}, u32[]{:S(2)}, u32[]{:S(2)}) collective-permute-start(bf16[512,256]{1,0:T(8,128)(2,1)S(1)} %get-tuple-element.35.refs_2_.refs_0_), channel_id=1, source_target_pairs={{0,2},{1,3},{2,0},{3,1},{4,6},{5,7},{6,4},{7,5},{8,10},{9,11},{10,... | collective-permute-start | bytes 786440 | tf_op jit(solution)/shard_map/ppermute | solution.py:39
  8.4 1.0 %collective-permute-done.4.refs_1_ = bf16[128,256]{1,0:T(8,128)(2,1)S(1)} collective-permute-done((bf16[128,256]{1,0:T(8,128)(2,1)S(1)}, bf16[128,256]{1,0:T(8,128)(2,1)S(1)}, u32[]{:S(2)}, u32[]{:S(2)}) %collective-permute-start.4) | collective-permute-done | bytes 65568 | tf_op jit(solution)/shard_map/ppermute | solution.py:39
  9.4 1.4 %collective-permute-start.6 = (bf16[64,256]{1,0:T(8,128)(2,1)S(1)}, bf16[64,256]{1,0:T(8,128)(2,1)S(1)}, u32[]{:S(2)}, u32[]{:S(2)}) collective-permute-start(bf16[64,256]{1,0:T(8,128)(2,1)S(1)} %shard_map.136), channel_id=1, source_target_pairs={{0,6},{1,31},{2,4},{3,29},{4,10},{5,3},{6,8},{7,1},{8,14},{9,7},{1... | collective-permute-start | bytes 98312 | tf_op jit(solution)/shard_map/ppermute | solution.py:59
  10.8 1.5 %collective-permute-start.5 = (bf16[64,256]{1,0:T(8,128)(2,1)S(1)}, bf16[64,256]{1,0:T(8,128)(2,1)S(1)}, u32[]{:S(2)}, u32[]{:S(2)}) collective-permute-start(bf16[64,256]{1,0:T(8,128)(2,1)S(1)} %shard_map.136), channel_id=1, source_target_pairs={{0,4},{1,29},{2,6},{3,31},{4,8},{5,1},{6,10},{7,3},{8,12},{9,5},{1... | collective-permute-start | bytes 98312 | tf_op jit(solution)/shard_map/ppermute | solution.py:59
  12.3 0.7 %shard_map.132.refs_0_ = f32[512,256]{1,0:T(8,128)S(1)} custom-call(s32[1,2048]{1,0:T(1,128)S(1)} %shard_map.128.refs_0_.refs_1_, bf16[2048,256]{1,0:T(8,128)(2,1)S(1)} %copy-done.6, bf16[512,256]{1,0:T(8,128)(2,1)S(1)} %get-tuple-element.35.refs_2_.refs_0_), custom_call_target="tpu_custom_call" | custom-call | flops 536870912 | bytes 1581056 | tf_op jit(solution)/shard_map/pallas_call | solution.py:74
  13.2 1.6 %collective-permute-start.2 = (bf16[512,256]{1,0:T(8,128)(2,1)S(1)}, bf16[512,256]{1,0:T(8,128)(2,1)S(1)}, u32[]{:S(2)}, u32[]{:S(2)}) collective-permute-start(bf16[512,256]{1,0:T(8,128)(2,1)S(1)} %get-tuple-element.37), channel_id=1, source_target_pairs={{0,2},{1,3},{2,0},{3,1},{4,6},{5,7},{6,4},{7,5},{8,10},{9,11},{10,... | collective-permute-start | bytes 786440 | tf_op jit(solution)/shard_map/ppermute | solution.py:39
  14.8 2.1 %collective-permute-done.6.refs_1_ = bf16[64,256]{1,0:T(8,128)(2,1)S(1)} collective-permute-done((bf16[64,256]{1,0:T(8,128)(2,1)S(1)}, bf16[64,256]{1,0:T(8,128)(2,1)S(1)}, u32[]{:S(2)}, u32[]{:S(2)}) %collective-permute-start.6) | collective-permute-done | bytes 32800 | tf_op jit(solution)/shard_map/ppermute | solution.py:59
  16.9 0.5 %collective-permute-done.5.refs_0_ = bf16[64,256]{1,0:T(8,128)(2,1)S(1)} collective-permute-done((bf16[64,256]{1,0:T(8,128)(2,1)S(1)}, bf16[64,256]{1,0:T(8,128)(2,1)S(1)}, u32[]{:S(2)}, u32[]{:S(2)}) %collective-permute-start.5) | collective-permute-done | bytes 32800 | tf_op jit(solution)/shard_map/ppermute | solution.py:59
  18.2 1.5 %shard_map.141.refs_2_ = bf16[4096,256]{1,0:T(8,128)(2,1)S(1)} custom-call(bf16[512,256]{1,0:T(8,128)(2,1)S(1)} %shard_map.139.refs_2_.refs_0_, s32[4,1024]{1,0:T(4,128)S(1)} %shard_map.138.refs_3_.refs_1_), custom_call_target="tpu_custom_call" | custom-call | tf_op jit(solution)/shard_map/pallas_call | solution.py:74
  20.1 2.5 %shard_map.142 = (f32[1024,256]{1,0:T(8,128)S(1)}, f32[3072,256]{1,0:T(8,128)S(1)}, bf16[3072,256]{1,0:T(8,128)(2,1)S(1)}, f32[8,128]{1,0:T(8,128)S(1)}) custom-call(f32[1024,256]{1,0:T(8,128)S(1)} %get-tuple-element.39.refs_0_, bf16[640,256]{1,0:T(8,128)(2,1)S(1)} %get-tuple-element.40.refs_1_, bf16[4096,256]{1,0:T(8,128)(2,1)S(1)} %shard_map.141.refs_2_, ...), custom_call_target="tpu_custom_call" | custom-call | tf_op jit(solution)/shard_map/pallas_call | solution.py:74
  23.2 1.0 %shard_map.144 = (f32[1024,256]{1,0:T(8,128)S(1)}, f32[1024,256]{1,0:T(8,128)S(1)}, bf16[1024,256]{1,0:T(8,128)(2,1)S(1)}) custom-call(f32[1024,256]{1,0:T(8,128)S(1)} %get-tuple-element.39.refs_0_, bf16[640,256]{1,0:T(8,128)(2,1)S(1)} %get-tuple-element.40.refs_1_, bf16[4096,256]{1,0:T(8,128)(2,1)S(1)} %shard_map.141.refs_2_, ...), custom_call_target="tpu_custom_call" | custom-call | tf_op jit(solution)/shard_map/pallas_call | solution.py:74
  24.4 1.5 %shard_map.145 = (bf16[4096,256]{1,0:T(8,128)(2,1)S(1)}, f32[1024,256]{1,0:T(8,128)S(1)}, bf16[1024,256]{1,0:T(8,128)(2,1)S(1)}, bf16[144,256]{1,0:T(8,128)(2,1)...) custom-call(bf16[512,256]{1,0:T(8,128)(2,1)S(1)} %shard_map.143.refs_5_.refs_0_, ...), custom_call_target="tpu_custom_call" | custom-call | flops 536870912 | bytes 13664256 | tf_op jit(solution)/shard_map/pallas_call | solution.py:74
  25.9 0.9 %collective-permute-start.13 = (bf16[144,256]{1,0:T(8,128)(2,1)S(1)}, bf16[144,256]{1,0:T(8,128)(2,1)S(1)}, u32[]{:S(2)}, u32[]{:S(2)}) collective-permute-start(bf16[144,256]{1,0:T(8,128)(2,1)S(1)} %get-tuple-element.54), channel_id=1, source_target_pairs={{0,12},{4,8},{8,4},{12,0},{16,28},{20,24},{24,20},{28,16},{1,13},{... | collective-permute-start | bytes 221192 | tf_op jit(solution)/shard_map/ppermute | solution.py:43
  26.8 1.3 %collective-permute-start.14 = (bf16[144,256]{1,0:T(8,128)(2,1)S(1)}, bf16[144,256]{1,0:T(8,128)(2,1)S(1)}, u32[]{:S(2)}, u32[]{:S(2)}) collective-permute-start(bf16[144,256]{1,0:T(8,128)(2,1)S(1)} %get-tuple-element.55), channel_id=1, source_target_pairs={{0,8},{4,12},{8,0},{12,4},{16,24},{20,28},{24,16},{28,20},{1,9},{5... | collective-permute-start | bytes 221192 | tf_op jit(solution)/shard_map/ppermute | solution.py:39
  28.1 1.4 %collective-permute-start.15 = (bf16[144,256]{1,0:T(8,128)(2,1)S(1)}, bf16[144,256]{1,0:T(8,128)(2,1)S(1)}, u32[]{:S(2)}, u32[]{:S(2)}) collective-permute-start(bf16[144,256]{1,0:T(8,128)(2,1)S(1)} %get-tuple-element.56), channel_id=1, source_target_pairs={{0,4},{4,0},{8,12},{12,8},{16,20},{20,16},{24,28},{28,24},{1,5},{5... | collective-permute-start | bytes 221192 | tf_op jit(solution)/shard_map/ppermute | solution.py:39
  29.5 0.6 %shard_map.148 = bf16[64,256]{1,0:T(8,128)(2,1)S(1)} custom-call(bf16[4096,256]{1,0:T(8,128)(2,1)S(1)} %get-tuple-element.49.refs_0_, s32[4,1024]{1,0:T(4,128)S(1)} %shard_map.138.refs_3_.refs_1_, bf16[512,256]{1,0:T(8,128)(2,1)S(1)} %copy-done), custom_call_target="tpu_custom_call" | custom-call | tf_op jit(solution)/shard_map/pallas_call | solution.py:74
  30.1 0.9 %collective-permute-start.11 = (bf16[64,256]{1,0:T(8,128)(2,1)S(1)}, bf16[64,256]{1,0:T(8,128)(2,1)S(1)}, u32[]{:S(2)}, u32[]{:S(2)}) collective-permute-start(bf16[64,256]{1,0:T(8,128)(2,1)S(1)} %shard_map.148), channel_id=1, source_target_pairs={{0,4},{1,29},{2,6},{3,31},{4,8},{5,1},{6,10},{7,3},{8,12},{9,5},{1... | collective-permute-start | bytes 98312 | tf_op jit(solution)/shard_map/ppermute | solution.py:59
  31.0 1.5 %shard_map.147.refs_1_.refs_5_ = f32[512,256]{1,0:T(8,128)S(1)} custom-call(bf16[4096,256]{1,0:T(8,128)(2,1)S(1)} %get-tuple-element.49.refs_0_, s32[4,1024]{1,0:T(4,128)S(1)} %shard_map.138.refs_3_.refs_1_, f32[1024,256]{1,0:T(8,128)S(1)} %get-tuple-element.50.refs_2_, bf16[1024,256]{1,0:T(8,128)(2,1)S(1)} %get-tuple-element.51.refs_3_, ...), custom_call_target="tpu_custom_call" | custom-call | tf_op jit(solution)/shard_map/pallas_call | solution.py:74
  32.5 4.4 %collective-permute-done.11.refs_2_.refs_4_ = bf16[64,256]{1,0:T(8,128)(2,1)S(1)} collective-permute-done((bf16[64,256]{1,0:T(8,128)(2,1)S(1)}, bf16[64,256]{1,0:T(8,128)(2,1)S(1)}, u32[]{:S(2)}, u32[]{:S(2)}) %collective-permute-start.11) | collective-permute-done | bytes 32800 | tf_op jit(solution)/shard_map/ppermute | solution.py:59
  37.2 1.5 %shard_map.146.refs_0_.refs_4_ = f32[512,256]{1,0:T(8,128)S(1)} custom-call(bf16[4096,256]{1,0:T(8,128)(2,1)S(1)} %get-tuple-element.49.refs_0_, s32[4,1024]{1,0:T(4,128)S(1)} %shard_map.138.refs_3_.refs_1_, f32[1024,256]{1,0:T(8,128)S(1)} %get-tuple-element.50.refs_2_, bf16[1024,256]{1,0:T(8,128)(2,1)S(1)} %get-tuple-element.51.refs_3_, ...), custom_call_target="tpu_custom_call" | custom-call | tf_op jit(solution)/shard_map/pallas_call | solution.py:74
  39.1 3.3 %collective-permute-done.16.refs_1_ = bf16[144,256]{1,0:T(8,128)(2,1)S(1)} collective-permute-done((bf16[144,256]{1,0:T(8,128)(2,1)S(1)}, bf16[144,256]{1,0:T(8,128)(2,1)S(1)}, u32[]{:S(2)}, u32[]{:S(2)}) %collective-permute-start.16) | collective-permute-done | bytes 73760 | tf_op jit(solution)/shard_map/ppermute | solution.py:39
  42.4 0.7 %collective-permute-start.19 = (bf16[144,256]{1,0:T(8,128)(2,1)S(1)}, bf16[144,256]{1,0:T(8,128)(2,1)S(1)}, u32[]{:S(2)}, u32[]{:S(2)}) collective-permute-start(bf16[144,256]{1,0:T(8,128)(2,1)S(1)} %shard_map.152.refs_0_), channel_id=1, source_target_pairs={{0,6},{1,7},{2,4},{3,5},{4,2},{5,3},{6,0},{7,1},{8,14},{9,15},{10,... | collective-permute-start | bytes 221192 | tf_op jit(solution)/shard_map/ppermute | solution.py:49
  43.1 1.0 %collective-permute-start.18 = (bf16[144,256]{1,0:T(8,128)(2,1)S(1)}, bf16[144,256]{1,0:T(8,128)(2,1)S(1)}, u32[]{:S(2)}, u32[]{:S(2)}) collective-permute-start(bf16[144,256]{1,0:T(8,128)(2,1)S(1)} %shard_map.152.refs_0_), channel_id=1, source_target_pairs={{0,2},{1,3},{2,0},{3,1},{4,6},{5,7},{6,4},{7,5},{8,10},{9,11},{10,... | collective-permute-start | bytes 221192 | tf_op jit(solution)/shard_map/ppermute | solution.py:39
  44.1 1.9 %collective-permute-start.17 = (bf16[144,256]{1,0:T(8,128)(2,1)S(1)}, bf16[144,256]{1,0:T(8,128)(2,1)S(1)}, u32[]{:S(2)}, u32[]{:S(2)}) collective-permute-start(bf16[144,256]{1,0:T(8,128)(2,1)S(1)} %shard_map.152.refs_0_), channel_id=1, source_target_pairs={{0,4},{4,0},{8,12},{12,8},{16,20},{20,16},{24,28},{28,24},{1,5},{5... | collective-permute-start | bytes 221192 | tf_op jit(solution)/shard_map/ppermute | solution.py:39
  46.0 2.1 %shard_map.150 = (bf16[2048,256]{1,0:T(8,128)(2,1)}, f32[8,128]{1,0:T(8,128)S(1)}) custom-call(bf16[1024,256]{1,0:T(8,128)(2,1)S(1)} %shard_map.149.refs_0_, s32[1,2048]{1,0:T(1,128)S(1)} %shard_map.128.refs_0_.refs_1_, bf16[2048,256]{1,0:T(8,128)(2,1)S(1)} %copy-done.6), custom_call_target="tpu_custom_call" | custom-call | flops 1073741824 | bytes 2633728 | tf_op jit(solution)/shard_map/pallas_call | solution.py:74
  48.7 1.5 %collective-permute-done.20.refs_1_ = bf16[544,256]{1,0:T(8,128)(2,1)S(1)} collective-permute-done((bf16[544,256]{1,0:T(8,128)(2,1)S(1)}, bf16[544,256]{1,0:T(8,128)(2,1)S(1)}, u32[]{:S(2)}, u32[]{:S(2)}) %collective-permute-start.20) | collective-permute-done | bytes 278560 | tf_op jit(solution)/shard_map/ppermute | solution.py:39
  50.2 1.0 %shard_map.154 = (f32[512,256]{1,0:T(8,128)}, f32[1,256]{1,0:T(1,128)}, f32[256,256]{1,0:T(8,128)}, f32[256,256]{1,0:T(8,128)}) custom-call(bf16[544,256]{1,0:T(8,128)(2,1)S(1)} %shard_map.153.refs_0_, bf16[544,256]{1,0:T(8,128)(2,1)S(1)} %collective-permute-done.20.refs_1_), custom_call_target="tpu_custom_call" | custom-call | tf_op jit(solution)/shard_map/pallas_call | solution.py:74
  (57 shorter events, 4.4 us)
Async XLA Ops:
  0.6 1.2 %copy-start.5 = (bf16[2048,256]{1,0:T(8,128)(2,1)S(1)}, bf16[2048,256]{1,0:T(8,128)(2,1)}, u32[]{:S(2)}) copy-start(bf16[2048,256]{1,0:T(8,128)(2,1)} %refs_1_.5) | copy-start | bytes 3145732
  0.6 0.8 %copy-start.7 = (s32[2048]{0:T(1024)S(1)}, s32[2048]{0:T(1024)}, u32[]{:S(2)}) copy-start(s32[2048]{0:T(1024)} %param.11) | copy-start | bytes 24580
  1.4 1.7 %copy-start.6 = (bf16[2048,256]{1,0:T(8,128)(2,1)S(1)}, bf16[2048,256]{1,0:T(8,128)(2,1)}, u32[]{:S(2)}) copy-start(bf16[2048,256]{1,0:T(8,128)(2,1)} %refs_2_.3) | copy-start | bytes 3145732
  2.6 5.2 %copy-start.4 = (s32[128]{0:T(128)S(1)}, s32[128]{0:T(128)}, u32[]{:S(2)}) copy-start(s32[128]{0:T(128)} %param.12) | copy-start | bytes 1540
  2.6 2.1 %collective-permute-start = (f32[512,256]{1,0:T(8,128)S(1)}, f32[512,256]{1,0:T(8,128)S(1)}, u32[]{:S(2)}, u32[]{:S(2)}) collective-permute-start(f32[512,256]{1,0:T(8,128)S(1)} %shard_map.130), channel_id=1, source_target_pairs={{0,1},{1,0},{2,3},{3,2},{4,5},{5,4},{6,7},{7,6},{8,9},{9,8},{10,11... | collective-permute-start | bytes 1572872 | tf_op jit(solution)/shard_map/ppermute | solution.py:39
  3.8 4.3 %copy-start.8 = (bf16[256]{0:T(256)(128)(2,1)S(1)}, bf16[256]{0:T(256)(128)(2,1)}, u32[]{:S(2)}) copy-start(bf16[256]{0:T(256)(128)(2,1)} %param.15) | copy-start | bytes 1540
  3.8 4.3 %copy-start.3 = (s32[4096]{0:T(1024)S(1)}, s32[4096]{0:T(1024)}, u32[]{:S(2)}) copy-start(s32[4096]{0:T(1024)} %param.13) | copy-start | bytes 49156
  3.8 9.2 %collective-permute-start.1 = (f32[512,256]{1,0:T(8,128)S(1)}, f32[512,256]{1,0:T(8,128)S(1)}, u32[]{:S(2)}, u32[]{:S(2)}) collective-permute-start(f32[512,256]{1,0:T(8,128)S(1)} %shard_map.133), channel_id=1, source_target_pairs={{0,1},{1,0},{2,3},{3,2},{4,5},{5,4},{6,7},{7,6},{8,9},{9,8},{10,11... | collective-permute-start | bytes 1572872 | tf_op jit(solution)/shard_map/ppermute | solution.py:39
  4.8 12.7 %collective-permute-start.3 = (bf16[512,256]{1,0:T(8,128)(2,1)S(1)}, bf16[512,256]{1,0:T(8,128)(2,1)S(1)}, u32[]{:S(2)}, u32[]{:S(2)}) collective-permute-start(bf16[512,256]{1,0:T(8,128)(2,1)S(1)} %get-tuple-element.35.refs_2_.refs_0_), channel_id=1, source_target_pairs={{0,2},{1,3},{2,0},{3,1},{4,6},{5,7},{6,4},{7,5},{8,10},{9,11},{10,... | collective-permute-start | bytes 786440 | tf_op jit(solution)/shard_map/ppermute | solution.py:39
  8.0 1.3 %collective-permute-start.4 = (bf16[128,256]{1,0:T(8,128)(2,1)S(1)}, bf16[128,256]{1,0:T(8,128)(2,1)S(1)}, u32[]{:S(2)}, u32[]{:S(2)}) collective-permute-start(bf16[128,256]{1,0:T(8,128)(2,1)S(1)} %shard_map.135.refs_0_), channel_id=1, source_target_pairs={{0,1},{1,0},{2,3},{3,2},{4,5},{5,4},{6,7},{7,6},{8,9},{9,8},{10,11... | collective-permute-start | bytes 196616 | tf_op jit(solution)/shard_map/ppermute | solution.py:39
  9.4 7.5 %collective-permute-start.6 = (bf16[64,256]{1,0:T(8,128)(2,1)S(1)}, bf16[64,256]{1,0:T(8,128)(2,1)S(1)}, u32[]{:S(2)}, u32[]{:S(2)}) collective-permute-start(bf16[64,256]{1,0:T(8,128)(2,1)S(1)} %shard_map.136), channel_id=1, source_target_pairs={{0,6},{1,31},{2,4},{3,29},{4,10},{5,3},{6,8},{7,1},{8,14},{9,7},{1... | collective-permute-start | bytes 98312 | tf_op jit(solution)/shard_map/ppermute | solution.py:59
  10.8 6.6 %collective-permute-start.5 = (bf16[64,256]{1,0:T(8,128)(2,1)S(1)}, bf16[64,256]{1,0:T(8,128)(2,1)S(1)}, u32[]{:S(2)}, u32[]{:S(2)}) collective-permute-start(bf16[64,256]{1,0:T(8,128)(2,1)S(1)} %shard_map.136), channel_id=1, source_target_pairs={{0,4},{1,29},{2,6},{3,31},{4,8},{5,1},{6,10},{7,3},{8,12},{9,5},{1... | collective-permute-start | bytes 98312 | tf_op jit(solution)/shard_map/ppermute | solution.py:59
  13.2 6.6 %copy-start = (bf16[512,256]{1,0:T(8,128)(2,1)S(1)}, bf16[512,256]{1,0:T(8,128)(2,1)}, u32[]{:S(2)}) copy-start(bf16[512,256]{1,0:T(8,128)(2,1)} %refs_2_.2) | copy-start | bytes 786436
  13.2 9.4 %collective-permute-start.2 = (bf16[512,256]{1,0:T(8,128)(2,1)S(1)}, bf16[512,256]{1,0:T(8,128)(2,1)S(1)}, u32[]{:S(2)}, u32[]{:S(2)}) collective-permute-start(bf16[512,256]{1,0:T(8,128)(2,1)S(1)} %get-tuple-element.37), channel_id=1, source_target_pairs={{0,2},{1,3},{2,0},{3,1},{4,6},{5,7},{6,4},{7,5},{8,10},{9,11},{10,... | collective-permute-start | bytes 786440 | tf_op jit(solution)/shard_map/ppermute | solution.py:39
  17.5 2.2 %collective-permute-start.8 = (bf16[256,256]{1,0:T(8,128)(2,1)S(1)}, bf16[256,256]{1,0:T(8,128)(2,1)S(1)}, u32[]{:S(2)}, u32[]{:S(2)}) collective-permute-start(bf16[256,256]{1,0:T(8,128)(2,1)S(1)} %get-tuple-element.65), channel_id=1, source_target_pairs={{0,1},{1,0},{2,3},{3,2},{4,5},{5,4},{6,7},{7,6},{8,9},{9,8},{10,11... | collective-permute-start | bytes 393224 | tf_op jit(solution)/shard_map/ppermute | solution.py:39
  17.6 2.1 %collective-permute-start.7 = (bf16[256,256]{1,0:T(8,128)(2,1)S(1)}, bf16[256,256]{1,0:T(8,128)(2,1)S(1)}, u32[]{:S(2)}, u32[]{:S(2)}) collective-permute-start(bf16[256,256]{1,0:T(8,128)(2,1)S(1)} %get-tuple-element.66), channel_id=1, source_target_pairs={{0,1},{1,0},{2,3},{3,2},{4,5},{5,4},{6,7},{7,6},{8,9},{9,8},{10,11... | collective-permute-start | bytes 393224 | tf_op jit(solution)/shard_map/ppermute | solution.py:39
  18.1 1.6 %collective-permute-start.9 = (bf16[64,256]{1,0:T(8,128)(2,1)S(1)}, bf16[64,256]{1,0:T(8,128)(2,1)S(1)}, u32[]{:S(2)}, u32[]{:S(2)}) collective-permute-start(bf16[64,256]{1,0:T(8,128)(2,1)S(1)} %shard_map.137.refs_2_.refs_3_), channel_id=1, source_target_pairs={{0,1},{1,0},{2,3},{3,2},{4,5},{5,4},{6,7},{7,6},{8,9},{9,8},{10,11... | collective-permute-start | bytes 98312 | tf_op jit(solution)/shard_map/ppermute | solution.py:39
  22.7 1.7 %copy-start.1 = (bf16[256,256]{1,0:T(8,128)(2,1)S(1)}, bf16[256,256]{1,0:T(8,128)(2,1)}, u32[]{:S(2)}) copy-start(bf16[256,256]{1,0:T(8,128)(2,1)} %refs_9_.1) | copy-start | bytes 393220
  22.7 1.7 %copy-start.2 = (bf16[256,256]{1,0:T(8,128)(2,1)S(1)}, bf16[256,256]{1,0:T(8,128)(2,1)}, u32[]{:S(2)}) copy-start(bf16[256,256]{1,0:T(8,128)(2,1)} %refs_10_.1) | copy-start | bytes 393220
  22.7 1.7 %collective-permute-start.10 = (bf16[512,256]{1,0:T(8,128)(2,1)S(1)}, bf16[512,256]{1,0:T(8,128)(2,1)S(1)}, u32[]{:S(2)}, u32[]{:S(2)}) collective-permute-start(bf16[512,256]{1,0:T(8,128)(2,1)S(1)} %shard_map.143.refs_5_.refs_0_), channel_id=1, source_target_pairs={{0,1},{1,0},{2,3},{3,2},{4,5},{5,4},{6,7},{7,6},{8,9},{9,8},{10,11... | collective-permute-start | bytes 786440 | tf_op jit(solution)/shard_map/ppermute | solution.py:39
  25.9 11.1 %collective-permute-start.13 = (bf16[144,256]{1,0:T(8,128)(2,1)S(1)}, bf16[144,256]{1,0:T(8,128)(2,1)S(1)}, u32[]{:S(2)}, u32[]{:S(2)}) collective-permute-start(bf16[144,256]{1,0:T(8,128)(2,1)S(1)} %get-tuple-element.54), channel_id=1, source_target_pairs={{0,12},{4,8},{8,4},{12,0},{16,28},{20,24},{24,20},{28,16},{1,13},{... | collective-permute-start | bytes 221192 | tf_op jit(solution)/shard_map/ppermute | solution.py:43
  26.8 10.1 %collective-permute-start.14 = (bf16[144,256]{1,0:T(8,128)(2,1)S(1)}, bf16[144,256]{1,0:T(8,128)(2,1)S(1)}, u32[]{:S(2)}, u32[]{:S(2)}) collective-permute-start(bf16[144,256]{1,0:T(8,128)(2,1)S(1)} %get-tuple-element.55), channel_id=1, source_target_pairs={{0,8},{4,12},{8,0},{12,4},{16,24},{20,28},{24,16},{28,20},{1,9},{5... | collective-permute-start | bytes 221192 | tf_op jit(solution)/shard_map/ppermute | solution.py:39
  28.1 8.8 %collective-permute-start.15 = (bf16[144,256]{1,0:T(8,128)(2,1)S(1)}, bf16[144,256]{1,0:T(8,128)(2,1)S(1)}, u32[]{:S(2)}, u32[]{:S(2)}) collective-permute-start(bf16[144,256]{1,0:T(8,128)(2,1)S(1)} %get-tuple-element.56), channel_id=1, source_target_pairs={{0,4},{4,0},{8,12},{12,8},{16,20},{20,16},{24,28},{28,24},{1,5},{5... | collective-permute-start | bytes 221192 | tf_op jit(solution)/shard_map/ppermute | solution.py:39
  30.1 6.8 %collective-permute-start.11 = (bf16[64,256]{1,0:T(8,128)(2,1)S(1)}, bf16[64,256]{1,0:T(8,128)(2,1)S(1)}, u32[]{:S(2)}, u32[]{:S(2)}) collective-permute-start(bf16[64,256]{1,0:T(8,128)(2,1)S(1)} %shard_map.148), channel_id=1, source_target_pairs={{0,4},{1,29},{2,6},{3,31},{4,8},{5,1},{6,10},{7,3},{8,12},{9,5},{1... | collective-permute-start | bytes 98312 | tf_op jit(solution)/shard_map/ppermute | solution.py:59
  37.0 5.3 %collective-permute-start.16 = (bf16[144,256]{1,0:T(8,128)(2,1)S(1)}, bf16[144,256]{1,0:T(8,128)(2,1)S(1)}, u32[]{:S(2)}, u32[]{:S(2)}) collective-permute-start(bf16[144,256]{1,0:T(8,128)(2,1)S(1)} %get-tuple-element.58), channel_id=1, source_target_pairs={{0,16},{4,20},{8,24},{12,28},{16,0},{20,4},{24,8},{28,12},{1,17},{... | collective-permute-start | bytes 221192 | tf_op jit(solution)/shard_map/ppermute | solution.py:39
  37.1 1.6 %collective-permute-start.12 = (bf16[64,256]{1,0:T(8,128)(2,1)S(1)}, bf16[64,256]{1,0:T(8,128)(2,1)S(1)}, u32[]{:S(2)}, u32[]{:S(2)}) collective-permute-start(bf16[64,256]{1,0:T(8,128)(2,1)S(1)} %collective-permute-done.11.refs_2_.refs_4_), channel_id=1, source_target_pairs={{0,1},{1,0},{2,3},{3,2},{4,5},{5,4},{6,7},{7,6},{8,9},{9,8},{10,11... | collective-permute-start | bytes 98312 | tf_op jit(solution)/shard_map/ppermute | solution.py:39
  42.4 5.7 %collective-permute-start.19 = (bf16[144,256]{1,0:T(8,128)(2,1)S(1)}, bf16[144,256]{1,0:T(8,128)(2,1)S(1)}, u32[]{:S(2)}, u32[]{:S(2)}) collective-permute-start(bf16[144,256]{1,0:T(8,128)(2,1)S(1)} %shard_map.152.refs_0_), channel_id=1, source_target_pairs={{0,6},{1,7},{2,4},{3,5},{4,2},{5,3},{6,0},{7,1},{8,14},{9,15},{10,... | collective-permute-start | bytes 221192 | tf_op jit(solution)/shard_map/ppermute | solution.py:49
  43.1 5.1 %collective-permute-start.18 = (bf16[144,256]{1,0:T(8,128)(2,1)S(1)}, bf16[144,256]{1,0:T(8,128)(2,1)S(1)}, u32[]{:S(2)}, u32[]{:S(2)}) collective-permute-start(bf16[144,256]{1,0:T(8,128)(2,1)S(1)} %shard_map.152.refs_0_), channel_id=1, source_target_pairs={{0,2},{1,3},{2,0},{3,1},{4,6},{5,7},{6,4},{7,5},{8,10},{9,11},{10,... | collective-permute-start | bytes 221192 | tf_op jit(solution)/shard_map/ppermute | solution.py:39
  44.1 4.5 %collective-permute-start.17 = (bf16[144,256]{1,0:T(8,128)(2,1)S(1)}, bf16[144,256]{1,0:T(8,128)(2,1)S(1)}, u32[]{:S(2)}, u32[]{:S(2)}) collective-permute-start(bf16[144,256]{1,0:T(8,128)(2,1)S(1)} %shard_map.152.refs_0_), channel_id=1, source_target_pairs={{0,4},{4,0},{8,12},{12,8},{16,20},{20,16},{24,28},{28,24},{1,5},{5... | collective-permute-start | bytes 221192 | tf_op jit(solution)/shard_map/ppermute | solution.py:39
  48.6 1.6 %collective-permute-start.20 = (bf16[544,256]{1,0:T(8,128)(2,1)S(1)}, bf16[544,256]{1,0:T(8,128)(2,1)S(1)}, u32[]{:S(2)}, u32[]{:S(2)}) collective-permute-start(bf16[544,256]{1,0:T(8,128)(2,1)S(1)} %shard_map.153.refs_0_), channel_id=1, source_target_pairs={{0,1},{1,0},{2,3},{3,2},{4,5},{5,4},{6,7},{7,6},{8,9},{9,8},{10,11... | collective-permute-start | bytes 835592 | tf_op jit(solution)/shard_map/ppermute | solution.py:39

commit v11 on v10

--- a/solution.py
+++ b/solution.py
@@ -533,7 +533,7 @@
             functools.partial(cell_grad_body, first=at),
             (sds((half, width), F32),),
             (act, src, ga, gn, w_edge_in),
-            0,
+            2 * K * half * cells * width,
         )[0]
         for at in (0, half)
     ]

time: 51.5 us -> 52.4 us (1.017)
  starting transfers between devices: 17.7 us -> 18.9 us
    ppermute x3, waiting for transfers between devices: 7.07 us -> 3.84 us  [send_sides(): return lax.ppermute(x, ('coarse', 'fine'), pairs)]
    ppermute x16, waiting for transfers between devices: 6.48 us -> 9.44 us  [swap(): return lax.ppermute(x, axis, [(i, i ^ 1 << bit) for i in range(count)])]
    ppermute x1, starting transfers between devices: 0.68 us -> 1.71 us  [swap_both(): return lax.ppermute(x, ('coarse', 'fine'), pairs)]
    ppermute x1, starting transfers between devices: 0.93 us -> 1.7 us  [swap_owners(): lax.ppermute(x, 'coarse', [(i, i ^ 3) for i in range(lax.axis_size('coars...]
    ppermute x16, starting transfers between devices: 12.2 us -> 11.6 us  [swap(): return lax.ppermute(x, axis, [(i, i ^ 1 << bit) for i in range(count)])]
  transfers between devices with their start and end apart: 21 -> 21, of which waited for: 9 -> 11; matrix products, arithmetic and copies ran while one was open for 0% -> 0% of each run, Pallas kernels for 28% -> 26%
where the time goes in v11:
time: 52.4 us; the launch traced here: 52.1 us
  starting transfers between devices  18.9 us (36%)
  Pallas kernels  17.7 us (34%)
  waiting for transfers between devices  13.3 us (25%)
  local copies, waits for them, and re-layouts  1.28 us (2%)
  between operations  0.99 us (2%)
    pallas_call x27, Pallas kernels, call(): pl.pallas_call(kernel, out_shape=outs, in_specs=[in_vmem] * count + [anyw...  17.7 us
    ppermute x16, starting transfers between devices, swap(): return lax.ppermute(x, axis, [(i, i ^ 1 << bit) for i in range(count)])  11.6 us
    ppermute x16, waiting for transfers between devices, swap(): return lax.ppermute(x, axis, [(i, i ^ 1 << bit) for i in range(count)])  9.44 us
    ppermute x3, starting transfers between devices, send_sides(): return lax.ppermute(x, ('coarse', 'fine'), pairs)  3.9 us
    ppermute x3, waiting for transfers between devices, send_sides(): return lax.ppermute(x, ('coarse', 'fine'), pairs)  3.84 us
    ppermute x1, starting transfers between devices, swap_both(): return lax.ppermute(x, ('coarse', 'fine'), pairs)  1.71 us
    ppermute x1, starting transfers between devices, swap_owners(): lax.ppermute(x, 'coarse', [(i, i ^ 3) for i in range(lax.axis_size('coars...  1.7 us
    unnamed x18, local copies, waits for them, and re-layouts  1.26 us
  transfers between devices with their start and end apart: 21, of which 11 were waited for; matrix products, arithmetic and copies ran while one was open for 0% of the time, Pallas kernels for 26%

profile of v11, /device:TPU:0, one launch (start us, length us, event | category | flops | bytes accessed | tf_op | source)
XLA Modules:
  0.0 52.1 jit_solution(4472850621978099233)
XLA Ops:
  0.7 0.8 %copy-done.7 = s32[2048]{0:T(1024)S(1)} copy-done((s32[2048]{0:T(1024)S(1)}, s32[2048]{0:T(1024)}, u32[]{:S(2)}) %copy-start.7) | copy-done | bytes 8216
  1.9 0.7 %shard_map.130 = f32[512,256]{1,0:T(8,128)S(1)} custom-call(s32[1,2048]{1,0:T(1,128)S(1)} %shard_map.128.refs_0_.refs_1_, bf16[2048,256]{1,0:T(8,128)(2,1)S(1)} %copy-done.5), custom_call_target="tpu_custom_call" | custom-call | flops 536870912 | bytes 1581056 | tf_op jit(solution)/shard_map/pallas_call | solution.py:74
  3.1 0.7 %shard_map.133 = f32[512,256]{1,0:T(8,128)S(1)} custom-call(s32[1,2048]{1,0:T(1,128)S(1)} %shard_map.128.refs_0_.refs_1_, bf16[2048,256]{1,0:T(8,128)(2,1)S(1)} %copy-done.6), custom_call_target="tpu_custom_call" | custom-call | flops 536870912 | bytes 1581056 | tf_op jit(solution)/shard_map/pallas_call | solution.py:74
  4.0 0.7 %shard_map.129.refs_0_ = f32[512,256]{1,0:T(8,128)S(1)} custom-call(s32[1,2048]{1,0:T(1,128)S(1)} %shard_map.128.refs_0_.refs_1_, bf16[2048,256]{1,0:T(8,128)(2,1)S(1)} %copy-done.5), custom_call_target="tpu_custom_call" | custom-call | flops 536870912 | bytes 1581056 | tf_op jit(solution)/shard_map/pallas_call | solution.py:74
  4.8 3.0 %collective-permute-start.3 = (bf16[512,256]{1,0:T(8,128)(2,1)S(1)}, bf16[512,256]{1,0:T(8,128)(2,1)S(1)}, u32[]{:S(2)}, u32[]{:S(2)}) collective-permute-start(bf16[512,256]{1,0:T(8,128)(2,1)S(1)} %get-tuple-element.35.refs_2_.refs_0_), channel_id=1, source_target_pairs={{0,2},{1,3},{2,0},{3,1},{4,6},{5,7},{6,4},{7,5},{8,10},{9,11},{10,... | collective-permute-start | bytes 786440 | tf_op jit(solution)/shard_map/ppermute | solution.py:39
  8.4 1.0 %collective-permute-done.4.refs_1_ = bf16[128,256]{1,0:T(8,128)(2,1)S(1)} collective-permute-done((bf16[128,256]{1,0:T(8,128)(2,1)S(1)}, bf16[128,256]{1,0:T(8,128)(2,1)S(1)}, u32[]{:S(2)}, u32[]{:S(2)}) %collective-permute-start.4) | collective-permute-done | bytes 65568 | tf_op jit(solution)/shard_map/ppermute | solution.py:39
  9.4 1.4 %collective-permute-start.6 = (bf16[64,256]{1,0:T(8,128)(2,1)S(1)}, bf16[64,256]{1,0:T(8,128)(2,1)S(1)}, u32[]{:S(2)}, u32[]{:S(2)}) collective-permute-start(bf16[64,256]{1,0:T(8,128)(2,1)S(1)} %shard_map.136), channel_id=1, source_target_pairs={{0,6},{1,31},{2,4},{3,29},{4,10},{5,3},{6,8},{7,1},{8,14},{9,7},{1... | collective-permute-start | bytes 98312 | tf_op jit(solution)/shard_map/ppermute | solution.py:59
  10.8 1.5 %collective-permute-start.5 = (bf16[64,256]{1,0:T(8,128)(2,1)S(1)}, bf16[64,256]{1,0:T(8,128)(2,1)S(1)}, u32[]{:S(2)}, u32[]{:S(2)}) collective-permute-start(bf16[64,256]{1,0:T(8,128)(2,1)S(1)} %shard_map.136), channel_id=1, source_target_pairs={{0,4},{1,29},{2,6},{3,31},{4,8},{5,1},{6,10},{7,3},{8,12},{9,5},{1... | collective-permute-start | bytes 98312 | tf_op jit(solution)/shard_map/ppermute | solution.py:59
  12.3 0.7 %shard_map.132.refs_0_ = f32[512,256]{1,0:T(8,128)S(1)} custom-call(s32[1,2048]{1,0:T(1,128)S(1)} %shard_map.128.refs_0_.refs_1_, bf16[2048,256]{1,0:T(8,128)(2,1)S(1)} %copy-done.6, bf16[512,256]{1,0:T(8,128)(2,1)S(1)} %get-tuple-element.35.refs_2_.refs_0_), custom_call_target="tpu_custom_call" | custom-call | flops 536870912 | bytes 1581056 | tf_op jit(solution)/shard_map/pallas_call | solution.py:74
  13.2 1.6 %collective-permute-start.2 = (bf16[512,256]{1,0:T(8,128)(2,1)S(1)}, bf16[512,256]{1,0:T(8,128)(2,1)S(1)}, u32[]{:S(2)}, u32[]{:S(2)}) collective-permute-start(bf16[512,256]{1,0:T(8,128)(2,1)S(1)} %get-tuple-element.37), channel_id=1, source_target_pairs={{0,2},{1,3},{2,0},{3,1},{4,6},{5,7},{6,4},{7,5},{8,10},{9,11},{10,... | collective-permute-start | bytes 786440 | tf_op jit(solution)/shard_map/ppermute | solution.py:39
  14.8 2.1 %collective-permute-done.6.refs_1_ = bf16[64,256]{1,0:T(8,128)(2,1)S(1)} collective-permute-done((bf16[64,256]{1,0:T(8,128)(2,1)S(1)}, bf16[64,256]{1,0:T(8,128)(2,1)S(1)}, u32[]{:S(2)}, u32[]{:S(2)}) %collective-permute-start.6) | collective-permute-done | bytes 32800 | tf_op jit(solution)/shard_map/ppermute | solution.py:59
  18.2 1.5 %shard_map.141.refs_2_ = bf16[4096,256]{1,0:T(8,128)(2,1)S(1)} custom-call(bf16[512,256]{1,0:T(8,128)(2,1)S(1)} %shard_map.139.refs_2_.refs_0_, s32[4,1024]{1,0:T(4,128)S(1)} %shard_map.138.refs_3_.refs_1_), custom_call_target="tpu_custom_call" | custom-call | tf_op jit(solution)/shard_map/pallas_call | solution.py:74
  20.1 2.5 %shard_map.142 = (f32[1024,256]{1,0:T(8,128)S(1)}, f32[3072,256]{1,0:T(8,128)S(1)}, bf16[3072,256]{1,0:T(8,128)(2,1)S(1)}, f32[8,128]{1,0:T(8,128)S(1)}) custom-call(f32[1024,256]{1,0:T(8,128)S(1)} %get-tuple-element.39.refs_0_, bf16[640,256]{1,0:T(8,128)(2,1)S(1)} %get-tuple-element.40.refs_1_, bf16[4096,256]{1,0:T(8,128)(2,1)S(1)} %shard_map.141.refs_2_, ...), custom_call_target="tpu_custom_call" | custom-call | tf_op jit(solution)/shard_map/pallas_call | solution.py:74
  23.2 1.0 %shard_map.144 = (f32[1024,256]{1,0:T(8,128)S(1)}, f32[1024,256]{1,0:T(8,128)S(1)}, bf16[1024,256]{1,0:T(8,128)(2,1)S(1)}) custom-call(f32[1024,256]{1,0:T(8,128)S(1)} %get-tuple-element.39.refs_0_, bf16[640,256]{1,0:T(8,128)(2,1)S(1)} %get-tuple-element.40.refs_1_, bf16[4096,256]{1,0:T(8,128)(2,1)S(1)} %shard_map.141.refs_2_, ...), custom_call_target="tpu_custom_call" | custom-call | tf_op jit(solution)/shard_map/pallas_call | solution.py:74
  24.4 1.5 %shard_map.145 = (bf16[4096,256]{1,0:T(8,128)(2,1)S(1)}, f32[1024,256]{1,0:T(8,128)S(1)}, bf16[1024,256]{1,0:T(8,128)(2,1)S(1)}, bf16[144,256]{1,0:T(8,128)(2,1)...) custom-call(bf16[512,256]{1,0:T(8,128)(2,1)S(1)} %shard_map.143.refs_5_.refs_0_, ...), custom_call_target="tpu_custom_call" | custom-call | flops 536870912 | bytes 13664256 | tf_op jit(solution)/shard_map/pallas_call | solution.py:74
  25.9 0.6 %shard_map.148 = bf16[64,256]{1,0:T(8,128)(2,1)S(1)} custom-call(bf16[4096,256]{1,0:T(8,128)(2,1)S(1)} %get-tuple-element.49.refs_0_, s32[4,1024]{1,0:T(4,128)S(1)} %shard_map.138.refs_3_.refs_1_, bf16[512,256]{1,0:T(8,128)(2,1)S(1)} %copy-done), custom_call_target="tpu_custom_call" | custom-call | tf_op jit(solution)/shard_map/pallas_call | solution.py:74
  26.5 0.9 %collective-permute-start.11 = (bf16[64,256]{1,0:T(8,128)(2,1)S(1)}, bf16[64,256]{1,0:T(8,128)(2,1)S(1)}, u32[]{:S(2)}, u32[]{:S(2)}) collective-permute-start(bf16[64,256]{1,0:T(8,128)(2,1)S(1)} %shard_map.148), channel_id=1, source_target_pairs={{0,4},{1,29},{2,6},{3,31},{4,8},{5,1},{6,10},{7,3},{8,12},{9,5},{1... | collective-permute-start | bytes 98312 | tf_op jit(solution)/shard_map/ppermute | solution.py:59
  27.4 1.7 %collective-permute-start.13 = (bf16[144,256]{1,0:T(8,128)(2,1)S(1)}, bf16[144,256]{1,0:T(8,128)(2,1)S(1)}, u32[]{:S(2)}, u32[]{:S(2)}) collective-permute-start(bf16[144,256]{1,0:T(8,128)(2,1)S(1)} %get-tuple-element.54), channel_id=1, source_target_pairs={{0,12},{4,8},{8,4},{12,0},{16,28},{20,24},{24,20},{28,16},{1,13},{... | collective-permute-start | bytes 221192 | tf_op jit(solution)/shard_map/ppermute | solution.py:43
  29.1 0.6 %collective-permute-start.14 = (bf16[144,256]{1,0:T(8,128)(2,1)S(1)}, bf16[144,256]{1,0:T(8,128)(2,1)S(1)}, u32[]{:S(2)}, u32[]{:S(2)}) collective-permute-start(bf16[144,256]{1,0:T(8,128)(2,1)S(1)} %get-tuple-element.55), channel_id=1, source_target_pairs={{0,8},{4,12},{8,0},{12,4},{16,24},{20,28},{24,16},{28,20},{1,9},{5... | collective-permute-start | bytes 221192 | tf_op jit(solution)/shard_map/ppermute | solution.py:39
  29.7 1.2 %collective-permute-start.15 = (bf16[144,256]{1,0:T(8,128)(2,1)S(1)}, bf16[144,256]{1,0:T(8,128)(2,1)S(1)}, u32[]{:S(2)}, u32[]{:S(2)}) collective-permute-start(bf16[144,256]{1,0:T(8,128)(2,1)S(1)} %get-tuple-element.56), channel_id=1, source_target_pairs={{0,4},{4,0},{8,12},{12,8},{16,20},{20,16},{24,28},{28,24},{1,5},{5... | collective-permute-start | bytes 221192 | tf_op jit(solution)/shard_map/ppermute | solution.py:39
  30.9 1.5 %shard_map.147.refs_1_.refs_5_ = f32[512,256]{1,0:T(8,128)S(1)} custom-call(bf16[4096,256]{1,0:T(8,128)(2,1)S(1)} %get-tuple-element.49.refs_0_, s32[4,1024]{1,0:T(4,128)S(1)} %shard_map.138.refs_3_.refs_1_, f32[1024,256]{1,0:T(8,128)S(1)} %get-tuple-element.50.refs_2_, bf16[1024,256]{1,0:T(8,128)(2,1)S(1)} %get-tuple-element.51.refs_3_, ...), custom_call_target="tpu_custom_call" | custom-call | flops 1073741824 | bytes 4472832 | tf_op jit(solution)/shard_map/pallas_call | solution.py:74
  32.4 1.2 %collective-permute-done.11.refs_2_.refs_4_ = bf16[64,256]{1,0:T(8,128)(2,1)S(1)} collective-permute-done((bf16[64,256]{1,0:T(8,128)(2,1)S(1)}, bf16[64,256]{1,0:T(8,128)(2,1)S(1)}, u32[]{:S(2)}, u32[]{:S(2)}) %collective-permute-start.11) | collective-permute-done | bytes 32800 | tf_op jit(solution)/shard_map/ppermute | solution.py:59
  34.3 1.3 %collective-permute-done.15.refs_3_ = bf16[144,256]{1,0:T(8,128)(2,1)S(1)} collective-permute-done((bf16[144,256]{1,0:T(8,128)(2,1)S(1)}, bf16[144,256]{1,0:T(8,128)(2,1)S(1)}, u32[]{:S(2)}, u32[]{:S(2)}) %collective-permute-start.15) | collective-permute-done | bytes 73760 | tf_op jit(solution)/shard_map/ppermute | solution.py:39
  35.8 0.9 %collective-permute-start.16 = (bf16[144,256]{1,0:T(8,128)(2,1)S(1)}, bf16[144,256]{1,0:T(8,128)(2,1)S(1)}, u32[]{:S(2)}, u32[]{:S(2)}) collective-permute-start(bf16[144,256]{1,0:T(8,128)(2,1)S(1)} %get-tuple-element.58), channel_id=1, source_target_pairs={{0,16},{4,20},{8,24},{12,28},{16,0},{20,4},{24,8},{28,12},{1,17},{... | collective-permute-start | bytes 221192 | tf_op jit(solution)/shard_map/ppermute | solution.py:39
  36.7 1.5 %shard_map.146.refs_0_.refs_4_ = f32[512,256]{1,0:T(8,128)S(1)} custom-call(bf16[4096,256]{1,0:T(8,128)(2,1)S(1)} %get-tuple-element.49.refs_0_, s32[4,1024]{1,0:T(4,128)S(1)} %shard_map.138.refs_3_.refs_1_, f32[1024,256]{1,0:T(8,128)S(1)} %get-tuple-element.50.refs_2_, bf16[1024,256]{1,0:T(8,128)(2,1)S(1)} %get-tuple-element.51.refs_3_, ...), custom_call_target="tpu_custom_call" | custom-call | flops 1073741824 | bytes 4472832 | tf_op jit(solution)/shard_map/pallas_call | solution.py:74
  38.5 3.7 %collective-permute-done.16.refs_1_ = bf16[144,256]{1,0:T(8,128)(2,1)S(1)} collective-permute-done((bf16[144,256]{1,0:T(8,128)(2,1)S(1)}, bf16[144,256]{1,0:T(8,128)(2,1)S(1)}, u32[]{:S(2)}, u32[]{:S(2)}) %collective-permute-start.16) | collective-permute-done | bytes 73760 | tf_op jit(solution)/shard_map/ppermute | solution.py:39
  42.3 1.7 %collective-permute-start.19 = (bf16[144,256]{1,0:T(8,128)(2,1)S(1)}, bf16[144,256]{1,0:T(8,128)(2,1)S(1)}, u32[]{:S(2)}, u32[]{:S(2)}) collective-permute-start(bf16[144,256]{1,0:T(8,128)(2,1)S(1)} %shard_map.152.refs_0_), channel_id=1, source_target_pairs={{0,6},{1,7},{2,4},{3,5},{4,2},{5,3},{6,0},{7,1},{8,14},{9,15},{10,... | collective-permute-start | bytes 221192 | tf_op jit(solution)/shard_map/ppermute | solution.py:49
  44.4 1.5 %collective-permute-start.17 = (bf16[144,256]{1,0:T(8,128)(2,1)S(1)}, bf16[144,256]{1,0:T(8,128)(2,1)S(1)}, u32[]{:S(2)}, u32[]{:S(2)}) collective-permute-start(bf16[144,256]{1,0:T(8,128)(2,1)S(1)} %shard_map.152.refs_0_), channel_id=1, source_target_pairs={{0,4},{4,0},{8,12},{12,8},{16,20},{20,16},{24,28},{28,24},{1,5},{5... | collective-permute-start | bytes 221192 | tf_op jit(solution)/shard_map/ppermute | solution.py:39
  45.9 2.1 %shard_map.150 = (bf16[2048,256]{1,0:T(8,128)(2,1)}, f32[8,128]{1,0:T(8,128)S(1)}) custom-call(bf16[1024,256]{1,0:T(8,128)(2,1)S(1)} %shard_map.149.refs_0_, s32[1,2048]{1,0:T(1,128)S(1)} %shard_map.128.refs_0_.refs_1_, bf16[2048,256]{1,0:T(8,128)(2,1)S(1)} %copy-done.6), custom_call_target="tpu_custom_call" | custom-call | flops 1073741824 | bytes 2633728 | tf_op jit(solution)/shard_map/pallas_call | solution.py:74
  48.5 0.9 %collective-permute-done.17.refs_1_ = bf16[144,256]{1,0:T(8,128)(2,1)S(1)} collective-permute-done((bf16[144,256]{1,0:T(8,128)(2,1)S(1)}, bf16[144,256]{1,0:T(8,128)(2,1)S(1)}, u32[]{:S(2)}, u32[]{:S(2)}) %collective-permute-start.17) | collective-permute-done | bytes 73760 | tf_op jit(solution)/shard_map/ppermute | solution.py:39
  49.5 1.5 %collective-permute-done.20.refs_1_ = bf16[544,256]{1,0:T(8,128)(2,1)S(1)} collective-permute-done((bf16[544,256]{1,0:T(8,128)(2,1)S(1)}, bf16[544,256]{1,0:T(8,128)(2,1)S(1)}, u32[]{:S(2)}, u32[]{:S(2)}) %collective-permute-start.20) | collective-permute-done | bytes 278560 | tf_op jit(solution)/shard_map/ppermute | solution.py:39
  51.1 1.0 %shard_map.154 = (f32[512,256]{1,0:T(8,128)}, f32[1,256]{1,0:T(1,128)}, f32[256,256]{1,0:T(8,128)}, f32[256,256]{1,0:T(8,128)}) custom-call(bf16[544,256]{1,0:T(8,128)(2,1)S(1)} %shard_map.153.refs_0_, bf16[544,256]{1,0:T(8,128)(2,1)S(1)} %collective-permute-done.20.refs_1_), custom_call_target="tpu_custom_call" | custom-call | tf_op jit(solution)/shard_map/pallas_call | solution.py:74
  (57 shorter events, 6.4 us)
Async XLA Ops:
  0.6 1.2 %copy-start.5 = (bf16[2048,256]{1,0:T(8,128)(2,1)S(1)}, bf16[2048,256]{1,0:T(8,128)(2,1)}, u32[]{:S(2)}) copy-start(bf16[2048,256]{1,0:T(8,128)(2,1)} %refs_1_.5) | copy-start | bytes 3145732
  0.6 0.8 %copy-start.7 = (s32[2048]{0:T(1024)S(1)}, s32[2048]{0:T(1024)}, u32[]{:S(2)}) copy-start(s32[2048]{0:T(1024)} %param.11) | copy-start | bytes 24580
  1.4 1.7 %copy-start.6 = (bf16[2048,256]{1,0:T(8,128)(2,1)S(1)}, bf16[2048,256]{1,0:T(8,128)(2,1)}, u32[]{:S(2)}) copy-start(bf16[2048,256]{1,0:T(8,128)(2,1)} %refs_2_.3) | copy-start | bytes 3145732
  2.6 5.2 %copy-start.4 = (s32[128]{0:T(128)S(1)}, s32[128]{0:T(128)}, u32[]{:S(2)}) copy-start(s32[128]{0:T(128)} %param.12) | copy-start | bytes 1540
  2.6 2.1 %collective-permute-start = (f32[512,256]{1,0:T(8,128)S(1)}, f32[512,256]{1,0:T(8,128)S(1)}, u32[]{:S(2)}, u32[]{:S(2)}) collective-permute-start(f32[512,256]{1,0:T(8,128)S(1)} %shard_map.130), channel_id=1, source_target_pairs={{0,1},{1,0},{2,3},{3,2},{4,5},{5,4},{6,7},{7,6},{8,9},{9,8},{10,11... | collective-permute-start | bytes 1572872 | tf_op jit(solution)/shard_map/ppermute | solution.py:39
  3.8 4.3 %copy-start.8 = (bf16[256]{0:T(256)(128)(2,1)S(1)}, bf16[256]{0:T(256)(128)(2,1)}, u32[]{:S(2)}) copy-start(bf16[256]{0:T(256)(128)(2,1)} %param.15) | copy-start | bytes 1540
  3.8 4.3 %copy-start.3 = (s32[4096]{0:T(1024)S(1)}, s32[4096]{0:T(1024)}, u32[]{:S(2)}) copy-start(s32[4096]{0:T(1024)} %param.13) | copy-start | bytes 49156
  3.8 9.2 %collective-permute-start.1 = (f32[512,256]{1,0:T(8,128)S(1)}, f32[512,256]{1,0:T(8,128)S(1)}, u32[]{:S(2)}, u32[]{:S(2)}) collective-permute-start(f32[512,256]{1,0:T(8,128)S(1)} %shard_map.133), channel_id=1, source_target_pairs={{0,1},{1,0},{2,3},{3,2},{4,5},{5,4},{6,7},{7,6},{8,9},{9,8},{10,11... | collective-permute-start | bytes 1572872 | tf_op jit(solution)/shard_map/ppermute | solution.py:39
  4.8 12.7 %collective-permute-start.3 = (bf16[512,256]{1,0:T(8,128)(2,1)S(1)}, bf16[512,256]{1,0:T(8,128)(2,1)S(1)}, u32[]{:S(2)}, u32[]{:S(2)}) collective-permute-start(bf16[512,256]{1,0:T(8,128)(2,1)S(1)} %get-tuple-element.35.refs_2_.refs_0_), channel_id=1, source_target_pairs={{0,2},{1,3},{2,0},{3,1},{4,6},{5,7},{6,4},{7,5},{8,10},{9,11},{10,... | collective-permute-start | bytes 786440 | tf_op jit(solution)/shard_map/ppermute | solution.py:39
  8.0 1.3 %collective-permute-start.4 = (bf16[128,256]{1,0:T(8,128)(2,1)S(1)}, bf16[128,256]{1,0:T(8,128)(2,1)S(1)}, u32[]{:S(2)}, u32[]{:S(2)}) collective-permute-start(bf16[128,256]{1,0:T(8,128)(2,1)S(1)} %shard_map.135.refs_0_), channel_id=1, source_target_pairs={{0,1},{1,0},{2,3},{3,2},{4,5},{5,4},{6,7},{7,6},{8,9},{9,8},{10,11... | collective-permute-start | bytes 196616 | tf_op jit(solution)/shard_map/ppermute | solution.py:39
  9.4 7.5 %collective-permute-start.6 = (bf16[64,256]{1,0:T(8,128)(2,1)S(1)}, bf16[64,256]{1,0:T(8,128)(2,1)S(1)}, u32[]{:S(2)}, u32[]{:S(2)}) collective-permute-start(bf16[64,256]{1,0:T(8,128)(2,1)S(1)} %shard_map.136), channel_id=1, source_target_pairs={{0,6},{1,31},{2,4},{3,29},{4,10},{5,3},{6,8},{7,1},{8,14},{9,7},{1... | collective-permute-start | bytes 98312 | tf_op jit(solution)/shard_map/ppermute | solution.py:59
  10.8 6.6 %collective-permute-start.5 = (bf16[64,256]{1,0:T(8,128)(2,1)S(1)}, bf16[64,256]{1,0:T(8,128)(2,1)S(1)}, u32[]{:S(2)}, u32[]{:S(2)}) collective-permute-start(bf16[64,256]{1,0:T(8,128)(2,1)S(1)} %shard_map.136), channel_id=1, source_target_pairs={{0,4},{1,29},{2,6},{3,31},{4,8},{5,1},{6,10},{7,3},{8,12},{9,5},{1... | collective-permute-start | bytes 98312 | tf_op jit(solution)/shard_map/ppermute | solution.py:59
  13.2 6.6 %copy-start = (bf16[512,256]{1,0:T(8,128)(2,1)S(1)}, bf16[512,256]{1,0:T(8,128)(2,1)}, u32[]{:S(2)}) copy-start(bf16[512,256]{1,0:T(8,128)(2,1)} %refs_2_.2) | copy-start | bytes 786436
  13.2 9.4 %collective-permute-start.2 = (bf16[512,256]{1,0:T(8,128)(2,1)S(1)}, bf16[512,256]{1,0:T(8,128)(2,1)S(1)}, u32[]{:S(2)}, u32[]{:S(2)}) collective-permute-start(bf16[512,256]{1,0:T(8,128)(2,1)S(1)} %get-tuple-element.37), channel_id=1, source_target_pairs={{0,2},{1,3},{2,0},{3,1},{4,6},{5,7},{6,4},{7,5},{8,10},{9,11},{10,... | collective-permute-start | bytes 786440 | tf_op jit(solution)/shard_map/ppermute | solution.py:39
  17.5 2.2 %collective-permute-start.8 = (bf16[256,256]{1,0:T(8,128)(2,1)S(1)}, bf16[256,256]{1,0:T(8,128)(2,1)S(1)}, u32[]{:S(2)}, u32[]{:S(2)}) collective-permute-start(bf16[256,256]{1,0:T(8,128)(2,1)S(1)} %get-tuple-element.65), channel_id=1, source_target_pairs={{0,1},{1,0},{2,3},{3,2},{4,5},{5,4},{6,7},{7,6},{8,9},{9,8},{10,11... | collective-permute-start | bytes 393224 | tf_op jit(solution)/shard_map/ppermute | solution.py:39
  17.6 2.1 %collective-permute-start.7 = (bf16[256,256]{1,0:T(8,128)(2,1)S(1)}, bf16[256,256]{1,0:T(8,128)(2,1)S(1)}, u32[]{:S(2)}, u32[]{:S(2)}) collective-permute-start(bf16[256,256]{1,0:T(8,128)(2,1)S(1)} %get-tuple-element.66), channel_id=1, source_target_pairs={{0,1},{1,0},{2,3},{3,2},{4,5},{5,4},{6,7},{7,6},{8,9},{9,8},{10,11... | collective-permute-start | bytes 393224 | tf_op jit(solution)/shard_map/ppermute | solution.py:39
  18.1 1.6 %collective-permute-start.9 = (bf16[64,256]{1,0:T(8,128)(2,1)S(1)}, bf16[64,256]{1,0:T(8,128)(2,1)S(1)}, u32[]{:S(2)}, u32[]{:S(2)}) collective-permute-start(bf16[64,256]{1,0:T(8,128)(2,1)S(1)} %shard_map.137.refs_2_.refs_3_), channel_id=1, source_target_pairs={{0,1},{1,0},{2,3},{3,2},{4,5},{5,4},{6,7},{7,6},{8,9},{9,8},{10,11... | collective-permute-start | bytes 98312 | tf_op jit(solution)/shard_map/ppermute | solution.py:39
  22.7 1.7 %copy-start.1 = (bf16[256,256]{1,0:T(8,128)(2,1)S(1)}, bf16[256,256]{1,0:T(8,128)(2,1)}, u32[]{:S(2)}) copy-start(bf16[256,256]{1,0:T(8,128)(2,1)} %refs_9_.1) | copy-start | bytes 393220
  22.7 1.7 %copy-start.2 = (bf16[256,256]{1,0:T(8,128)(2,1)S(1)}, bf16[256,256]{1,0:T(8,128)(2,1)}, u32[]{:S(2)}) copy-start(bf16[256,256]{1,0:T(8,128)(2,1)} %refs_10_.1) | copy-start | bytes 393220
  22.7 1.7 %collective-permute-start.10 = (bf16[512,256]{1,0:T(8,128)(2,1)S(1)}, bf16[512,256]{1,0:T(8,128)(2,1)S(1)}, u32[]{:S(2)}, u32[]{:S(2)}) collective-permute-start(bf16[512,256]{1,0:T(8,128)(2,1)S(1)} %shard_map.143.refs_5_.refs_0_), channel_id=1, source_target_pairs={{0,1},{1,0},{2,3},{3,2},{4,5},{5,4},{6,7},{7,6},{8,9},{9,8},{10,11... | collective-permute-start | bytes 786440 | tf_op jit(solution)/shard_map/ppermute | solution.py:39
  26.5 7.1 %collective-permute-start.11 = (bf16[64,256]{1,0:T(8,128)(2,1)S(1)}, bf16[64,256]{1,0:T(8,128)(2,1)S(1)}, u32[]{:S(2)}, u32[]{:S(2)}) collective-permute-start(bf16[64,256]{1,0:T(8,128)(2,1)S(1)} %shard_map.148), channel_id=1, source_target_pairs={{0,4},{1,29},{2,6},{3,31},{4,8},{5,1},{6,10},{7,3},{8,12},{9,5},{1... | collective-permute-start | bytes 98312 | tf_op jit(solution)/shard_map/ppermute | solution.py:59
  27.4 6.7 %collective-permute-start.13 = (bf16[144,256]{1,0:T(8,128)(2,1)S(1)}, bf16[144,256]{1,0:T(8,128)(2,1)S(1)}, u32[]{:S(2)}, u32[]{:S(2)}) collective-permute-start(bf16[144,256]{1,0:T(8,128)(2,1)S(1)} %get-tuple-element.54), channel_id=1, source_target_pairs={{0,12},{4,8},{8,4},{12,0},{16,28},{20,24},{24,20},{28,16},{1,13},{... | collective-permute-start | bytes 221192 | tf_op jit(solution)/shard_map/ppermute | solution.py:43
  29.1 5.2 %collective-permute-start.14 = (bf16[144,256]{1,0:T(8,128)(2,1)S(1)}, bf16[144,256]{1,0:T(8,128)(2,1)S(1)}, u32[]{:S(2)}, u32[]{:S(2)}) collective-permute-start(bf16[144,256]{1,0:T(8,128)(2,1)S(1)} %get-tuple-element.55), channel_id=1, source_target_pairs={{0,8},{4,12},{8,0},{12,4},{16,24},{20,28},{24,16},{28,20},{1,9},{5... | collective-permute-start | bytes 221192 | tf_op jit(solution)/shard_map/ppermute | solution.py:39
  29.7 6.0 %collective-permute-start.15 = (bf16[144,256]{1,0:T(8,128)(2,1)S(1)}, bf16[144,256]{1,0:T(8,128)(2,1)S(1)}, u32[]{:S(2)}, u32[]{:S(2)}) collective-permute-start(bf16[144,256]{1,0:T(8,128)(2,1)S(1)} %get-tuple-element.56), channel_id=1, source_target_pairs={{0,4},{4,0},{8,12},{12,8},{16,20},{20,16},{24,28},{28,24},{1,5},{5... | collective-permute-start | bytes 221192 | tf_op jit(solution)/shard_map/ppermute | solution.py:39
  33.6 4.6 %collective-permute-start.12 = (bf16[64,256]{1,0:T(8,128)(2,1)S(1)}, bf16[64,256]{1,0:T(8,128)(2,1)S(1)}, u32[]{:S(2)}, u32[]{:S(2)}) collective-permute-start(bf16[64,256]{1,0:T(8,128)(2,1)S(1)} %collective-permute-done.11.refs_2_.refs_4_), channel_id=1, source_target_pairs={{0,1},{1,0},{2,3},{3,2},{4,5},{5,4},{6,7},{7,6},{8,9},{9,8},{10,11... | collective-permute-start | bytes 98312 | tf_op jit(solution)/shard_map/ppermute | solution.py:39
  35.8 6.5 %collective-permute-start.16 = (bf16[144,256]{1,0:T(8,128)(2,1)S(1)}, bf16[144,256]{1,0:T(8,128)(2,1)S(1)}, u32[]{:S(2)}, u32[]{:S(2)}) collective-permute-start(bf16[144,256]{1,0:T(8,128)(2,1)S(1)} %get-tuple-element.58), channel_id=1, source_target_pairs={{0,16},{4,20},{8,24},{12,28},{16,0},{20,4},{24,8},{28,12},{1,17},{... | collective-permute-start | bytes 221192 | tf_op jit(solution)/shard_map/ppermute | solution.py:39
  42.3 5.7 %collective-permute-start.19 = (bf16[144,256]{1,0:T(8,128)(2,1)S(1)}, bf16[144,256]{1,0:T(8,128)(2,1)S(1)}, u32[]{:S(2)}, u32[]{:S(2)}) collective-permute-start(bf16[144,256]{1,0:T(8,128)(2,1)S(1)} %shard_map.152.refs_0_), channel_id=1, source_target_pairs={{0,6},{1,7},{2,4},{3,5},{4,2},{5,3},{6,0},{7,1},{8,14},{9,15},{10,... | collective-permute-start | bytes 221192 | tf_op jit(solution)/shard_map/ppermute | solution.py:49
  44.0 4.5 %collective-permute-start.18 = (bf16[144,256]{1,0:T(8,128)(2,1)S(1)}, bf16[144,256]{1,0:T(8,128)(2,1)S(1)}, u32[]{:S(2)}, u32[]{:S(2)}) collective-permute-start(bf16[144,256]{1,0:T(8,128)(2,1)S(1)} %shard_map.152.refs_0_), channel_id=1, source_target_pairs={{0,2},{1,3},{2,0},{3,1},{4,6},{5,7},{6,4},{7,5},{8,10},{9,11},{10,... | collective-permute-start | bytes 221192 | tf_op jit(solution)/shard_map/ppermute | solution.py:39
  44.4 5.0 %collective-permute-start.17 = (bf16[144,256]{1,0:T(8,128)(2,1)S(1)}, bf16[144,256]{1,0:T(8,128)(2,1)S(1)}, u32[]{:S(2)}, u32[]{:S(2)}) collective-permute-start(bf16[144,256]{1,0:T(8,128)(2,1)S(1)} %shard_map.152.refs_0_), channel_id=1, source_target_pairs={{0,4},{4,0},{8,12},{12,8},{16,20},{20,16},{24,28},{28,24},{1,5},{5... | collective-permute-start | bytes 221192 | tf_op jit(solution)/shard_map/ppermute | solution.py:39
  49.5 1.6 %collective-permute-start.20 = (bf16[544,256]{1,0:T(8,128)(2,1)S(1)}, bf16[544,256]{1,0:T(8,128)(2,1)S(1)}, u32[]{:S(2)}, u32[]{:S(2)}) collective-permute-start(bf16[544,256]{1,0:T(8,128)(2,1)S(1)} %shard_map.153.refs_0_), channel_id=1, source_target_pairs={{0,1},{1,0},{2,3},{3,2},{4,5},{5,4},{6,7},{7,6},{8,9},{9,8},{10,11... | collective-permute-start | bytes 835592 | tf_op jit(solution)/shard_map/ppermute | solution.py:39
